TPU v7x, 512 devices: a whole 4x4x16 slice. The times are simulated.
512 devices in a mesh: gx: 8 (over x, z_hi), gy: 8 (over y, core), gz: 8 (over z_lo).
Axes of the slice: x: 4, y: 4, z: 16 (z_hi: 2, z_lo: 8; z = z_hi * 8 + z_lo), core: 2. Of those that a mesh axis runs over, the one named last changes fastest.
Arguments:
- tokens: bfloat16 [256, 12288], P(('gx', 'gy'), 'gz'), may hold values from -6 to 6
- up_proj: bfloat16 [12288, 24576], P(None, ('gx', 'gy', 'gz')), may hold values from -0.0546875 to 0.0546875
- down_proj: bfloat16 [24576, 12288], P(('gx', 'gy', 'gz')), may hold values from -0.0390625 to 0.0390625
- out_grad: bfloat16 [256, 12288], P(('gx', 'gy'), 'gz'), may hold values from -6 to 6
Outputs:
- output: bfloat16 [256, 12288], P(('gx', 'gy'), 'gz')
- input_grad: bfloat16 [256, 12288], P(('gx', 'gy'), 'gz')
- up_grad: bfloat16 [12288, 24576], P('gz', ('gx', 'gy'))
- down_grad: bfloat16 [24576, 12288], P(('gx', 'gy'), 'gz')
All inputs are finite; a program needn't handle non-finite values.
Results may differ from a plain program's by a relative error of at most 0.0049.
Values may be sent and summed in bfloat16 or wider, within the bound.
No kernel may reach another device: no remote copies, remote signals or barrier semaphores. Data moves between devices by JAX's collectives and lax.ppermute only.
A program may use at most 64 MiB of HBM per device.

v0:
```python
import jax
import jax.numpy as jnp
from jax import lax
from jax.sharding import PartitionSpec as P


def activate(values):
    return jax.nn.gelu(values, approximate=True)


def gelu_slope(pre_act, cotangent):
    unused, pullback = jax.vjp(activate, pre_act)
    return pullback(cotangent)[0]


def contract_rows(left, right):
    return lax.dot_general(
        left, right, (((0,), (0,)), ((), ())), preferred_element_type=jnp.float32
    )


def contract_cols(left, right):
    return lax.dot_general(
        left, right, (((1,), (1,)), ((), ())), preferred_element_type=jnp.float32
    )


def feature_sum(partial_value):
    return lax.psum_scatter(partial_value, ("gx", "gy"), scatter_dimension=0, tiled=True)


def local(tokens, up_proj, down_proj, out_grad):
    up_cube = lax.all_to_all(up_proj, "gz", split_axis=0, concat_axis=1, tiled=True)
    down_cube = lax.all_to_all(down_proj, "gz", split_axis=1, concat_axis=0, tiled=True)
    inputs = lax.all_gather(tokens, ("gx", "gy"), axis=0, tiled=True)
    partial_value = jnp.dot(inputs, up_cube, preferred_element_type=jnp.float32)
    pre_act = lax.psum_scatter(partial_value, "gz", scatter_dimension=0, tiled=True)
    acted = lax.all_gather(activate(pre_act).astype(jnp.bfloat16), "gz", axis=0, tiled=True)
    output = feature_sum(jnp.dot(acted, down_cube, preferred_element_type=jnp.float32)).astype(
        jnp.bfloat16
    )
    gathered_grad = lax.all_gather(out_grad, ("gx", "gy"), axis=0, tiled=True)
    down_grad = contract_rows(acted, gathered_grad).astype(jnp.bfloat16)
    act_part = contract_cols(gathered_grad, down_cube)
    act_share = lax.psum_scatter(act_part, "gz", scatter_dimension=0, tiled=True)
    pre_grad = lax.all_gather(
        gelu_slope(pre_act, act_share).astype(jnp.bfloat16), "gz", axis=0, tiled=True
    )
    up_grad = contract_rows(inputs, pre_grad).astype(jnp.bfloat16)
    input_grad = feature_sum(contract_cols(pre_grad, up_cube)).astype(jnp.bfloat16)
    return (output, input_grad, up_grad, down_grad)


def solution(mesh):
    placed = (
        P(("gx", "gy"), "gz"),
        P(None, ("gx", "gy", "gz")),
        P(("gx", "gy", "gz"), None),
        P(("gx", "gy"), "gz"),
    )
    return jax.shard_map(
        local,
        mesh=mesh,
        in_specs=placed,
        out_specs=(
            P(("gx", "gy"), "gz"),
            P(("gx", "gy"), "gz"),
            P("gz", ("gx", "gy")),
            P(("gx", "gy"), "gz"),
        ),
        check_vma=False,
    )
```

profile of v0, /device:TPU:0, one launch (start us, length us, event | category | flops | bytes accessed | tf_op | source)
XLA Modules:
  0.0 1203.4 jit_solution(7071339045004234929)
XLA Ops:
  7.2 2.4 copy.21
  9.6 7.3 all-to-all-start
  16.8 1.1 copy.20
  18.0 55.7 %all-to-all-done = bf16[8,1536,48]{1,2,0:T(8,128)(2,1)S(1)} async-done(((bf16[8,1536,48]{1,2,0:T(8,128)(2,1)}), bf16[8,1536,48]{1,2,0:T(8,128)(2,1)S(1)}, u32[]{:S(2)}, u32[]{:S(2)}) %all-to-all-start) | async-done | bytes 1179680 | tf_op jit(solution)/shard_map/all_to_all | solution.py:33
  73.7 4.4 all-to-all-start.1
  78.1 175.0 %all-gather = bf16[64,4,1536]{2,1,0:T(4,128)(2,1)} all-gather(bf16[1,4,1536]{2,1,0:T(4,128)(2,1)S(1)} %bitcast.38), channel_id=1, replica_groups=mesh['gx'=8,'gy'=8,'gz'=8] {'gx','gy'}, dimensions={0}, use_global_device_ids=true | all-gather | bytes 798720 | tf_op jit(solution)/shard_map/all_gather | solution.py:35
  253.2 1.6 reshape.15
  254.8 1.4 fusion.8
  256.2 0.0 reduce-scatter.5.cloned.1.call-start
  256.2 153.8 %all-gather.1 = bf16[64,4,1536]{2,1,0:T(4,128)(2,1)} all-gather(bf16[1,4,1536]{2,1,0:T(4,128)(2,1)S(1)} %bitcast.39), channel_id=1, replica_groups=mesh['gx'=8,'gy'=8,'gz'=8] {'gx','gy'}, dimensions={0}, use_global_device_ids=true | all-gather | bytes 798720 | tf_op jit(solution)/shard_map/all_gather | solution.py:42
  410.0 2.3 reshape.17
  412.3 2.5 fusion.10
  414.8 1.3 dynamic-slice
  416.8 82.6 %reduce-scatter.5.cloned.1.call-done = f32[32,384]{1,0:T(8,128)} async-done(((f32[256,384]{1,0:T(8,128)}), f32[32,384]{1,0:T(8,128)}) %reduce-scatter.5.cloned.1.call-update) | async-done | bytes 49168 | tf_op jit(solution)/shard_map/reduce_scatter | solution.py:45
  499.4 0.9 fusion.7
  500.2 46.6 %all_gather.15 = bf16[256,384]{1,0:T(8,128)(2,1)S(1)} all-gather(bf16[32,384]{1,0:T(8,128)(2,1)S(1)} %get-tuple-element.22), channel_id=1, replica_groups=mesh['gx'=8,'gy'=8,'gz'=8] {'gz'}, dimensions={0}, use_global_device_ids=true | all-gather | bytes 221184 | tf_op jit(solution)/shard_map/all_gather | solution.py:46
  546.8 1.7 fusion.11
  548.5 1.5 fusion
  550.0 46.5 %all_gather.13 = bf16[256,384]{1,0:T(8,128)(2,1)S(1)} all-gather(bf16[32,384]{1,0:T(8,128)(2,1)S(1)} %get-tuple-element.23), channel_id=1, replica_groups=mesh['gx'=8,'gy'=8,'gz'=8] {'gz'}, dimensions={0}, use_global_device_ids=true | all-gather | bytes 221184 | tf_op jit(solution)/shard_map/all_gather | solution.py:38
  596.5 1.7 fusion.9
  598.2 1.5 convolution_convert_fusion
  599.7 2.5 copy.15
  602.2 593.7 %all-reduce.4 = (bf16[256,1536]{1,0:T(8,128)(2,1)S(1)}, bf16[256,1536]{1,0:T(8,128)(2,1)S(1)}) all-reduce(f32[256,1536]{1,0:T(8,128)} %fusion.9, f32[256,1536]{1,0:T(8,128)S(1)} %copy-done.1), channel_id=3, replica_groups=mesh['gx'=8,'gy'=8,'gz'=8] {'gx','gy'}, use_global_device_ids=true, to_apply=%region_1.0.clone | all-reduce | flops 786432 | bytes 4718592
  1196.0 0.6 dynamic-slice_convert_fusion
  (15 shorter events, 0.1 us)
Async XLA Ops:
  9.6 7.3 copy-start.2
  9.6 64.1 %all-to-all-start = ((bf16[8,1536,48]{1,2,0:T(8,128)(2,1)}), bf16[8,1536,48]{1,2,0:T(8,128)(2,1)S(1)}, u32[]{:S(2)}, u32[]{:S(2)}) async-start(bf16[8,1536,48]{1,2,0:T(8,128)(2,1)} %bitcast.30), calls=%async_computation | async-start | bytes 2359296 | tf_op jit(solution)/shard_map/all_to_all | solution.py:33
  73.7 4.5 copy-start.3
  73.7 338.6 %all-to-all-start.1 = ((bf16[48,8,1536]{2,0,1:T(8,128)(2,1)}), bf16[48,8,1536]{2,0,1:T(8,128)(2,1)S(1)}, u32[]{:S(2)}, u32[]{:S(2)}) async-start(bf16[48,8,1536]{2,0,1:T(8,128)(2,1)} %bitcast.35), calls=%async_computation.2 | async-start | bytes 2359296 | tf_op jit(solution)/shard_map/all_to_all | solution.py:34
  78.1 338.7 %reduce-scatter.3.cloned.1.call-start = ((), (), s32[]{:S(2)}) async-start(), calls=%async_computation.4 | async-start | bytes 442368 | tf_op jit(solution)/shard_map/reduce_scatter | solution.py:37
  254.8 1.4 copy-start.4
  256.2 243.2 %reduce-scatter.5.cloned.1.call-start = ((), (), s32[]{:S(2)}) async-start(), calls=%async_computation.5 | async-start | bytes 442368 | tf_op jit(solution)/shard_map/reduce_scatter | solution.py:45
  596.5 1.7 copy-start
  599.7 2.5 copy-start.1
Sparse Core Ops, SparseCore 0:
  256.3 83.5 reduce-scatter.2
  414.9 84.3 reduce-scatter.4
where the time goes:
time: 1200 us
  blocking collectives  1020 us (85%)
  waiting for transfers between devices  138 us (12%)
  between operations  14.8 us (1%)
    unnamed x1, blocking collectives  594 us
    all_gather x1, blocking collectives, local(): inputs = lax.all_gather(tokens, ('gx', 'gy'), axis=0, tiled=True)  175 us
    all_gather x1, blocking collectives, local(): gathered_grad = lax.all_gather(out_grad, ('gx', 'gy'), axis=0, tiled=True)  154 us
    reduce_scatter x1, waiting for transfers between devices, local(): lax.psum_scatter(act_part, 'gz', scatter_dimension=0, tiled=True)  82.6 us
    all_to_all x1, waiting for transfers between devices, local(): lax.all_to_all(up_proj, 'gz', split_axis=0, concat_axis=1, tiled=True)  55.7 us
    all_gather x1, blocking collectives, local(): lax.all_gather(gelu_slope(pre_act, act_share).astype(jnp.bfloat16), 'gz',...  46.6 us
    all_gather x1, blocking collectives, local(): lax.all_gather(activate(pre_act).astype(jnp.bfloat16), 'gz', axis=0, tile...  46.5 us
  transfers between devices with their start and end apart: 4, of which 2 were waited for; matrix products, arithmetic and copies ran while one was open for 1% of the time, Pallas kernels for 0%

commit v1 on v0

v1 whole, which is shorter than its diff:
```python
import jax
import jax.numpy as jnp
from jax import lax
from jax.sharding import Mesh, PartitionSpec as P

BF16 = jnp.bfloat16
F32 = jnp.float32


def activate(values):
    return jax.nn.gelu(values, approximate=True)


def gelu_slope(pre_act, cotangent):
    unused, pullback = jax.vjp(activate, pre_act)
    return pullback(cotangent)[0]


def exchange(value, axes):
    return lax.all_to_all(value, axes, split_axis=0, concat_axis=0, tiled=True)


def spread(value, axes, count):
    return exchange(jnp.broadcast_to(value[None], (count,) + value.shape), axes)


def other_core(value):
    return lax.ppermute(value, "c", [(0, 1), (1, 0)])


def dot(left, right, left_dim, right_dim):
    return lax.dot_general(
        left, right, (((left_dim,), (right_dim,)), ((), ())), preferred_element_type=F32
    )


PLANE = ("xh", "xp", "y")
COLUMN = ("zh", "z2", "z1")
GROUP = ("xp", "zp")
LINE = ("z2", "z1", "zp")


def local(tokens, up_proj, down_proj, out_grad):
    width = tokens.shape[1]
    units = down_proj.shape[0]

    def regroup(weight):
        blocks = weight.reshape(units, 2, 2, 2, width)
        sent = blocks.transpose(2, 3, 0, 1, 4)
        own = exchange(sent.reshape(4, units, 2 * width), GROUP)
        own = own.reshape(4 * units, 2 * width)
        return own, other_core(own)

    both = jnp.concatenate([tokens, out_grad], axis=0)
    column = spread(both, COLUMN, 8).reshape(2, 2, 2, 2, 4, width)
    sent = column.transpose(2, 1, 3, 0, 4, 5).reshape(1, 2, 1, 2, 2, 8, width)
    sent = jnp.broadcast_to(sent, (2, 2, 4, 2, 2, 8, width)).reshape(16, 2, 2, 8, width)
    plane = exchange(sent, PLANE)
    rows = plane.transpose(2, 0, 3, 1, 4).reshape(2, 128, 2 * width)

    up = regroup(up_proj.T)
    down = regroup(down_proj)

    parts = jnp.stack(
        [
            jnp.stack([dot(weight, rows[at], 1, 1).reshape(4, units, 128) for weight in pair], 1)
            for at, pair in ((0, up), (1, down))
        ],
        1,
    )
    sums = jnp.sum(exchange(parts, GROUP).reshape(4, 2, 2, units, 128), axis=0)
    acted = activate(sums[0]).astype(BF16)
    pre_grad = gelu_slope(sums[0], sums[1]).astype(BF16)
    hidden = jnp.stack([acted, pre_grad])
    shared = spread(hidden, GROUP, 4).reshape(4, 2, 2, units, 128)

    def partial_rows(kind, pair):
        total = sum(
            dot(shared[:, kind, at].reshape(4 * units, 128), pair[at], 0, 0) for at in range(2)
        )
        return total.astype(BF16).reshape(16, 8, 2 * width)

    partials = jnp.stack([partial_rows(0, down), partial_rows(1, up)], 1)
    arrived = exchange(partials, PLANE).reshape(2, 2, 4, 2, 8, 2 * width)
    summed = jnp.sum(arrived.astype(F32), axis=(0, 2))
    summed = summed.astype(BF16).reshape(2, 2, 2, 4, 2, width)
    summed = summed.transpose(2, 4, 0, 1, 3, 5).reshape(8, 2, 4, width)
    ends = jnp.sum(exchange(summed, COLUMN).astype(F32), axis=0).astype(BF16)

    mine = lax.dynamic_index_in_dim(
        column.reshape(2, 4, 2, 4, width), lax.axis_index(("z2", "z1")), 1, keepdims=False
    )
    mine = mine.transpose(1, 0, 2, 3).reshape(2, 8, width)
    flat = spread(mine, PLANE, 16).reshape(16, 2, 8, width).transpose(1, 0, 2, 3).reshape(2, 128, width)
    flat = jnp.concatenate([flat, other_core(flat)], axis=1)
    units_all = jnp.concatenate([hidden[:, 0], other_core(hidden[:, 1])], axis=2)
    units_all = spread(units_all, LINE, 8).reshape(8, 2, units, 256)
    down_grad = dot(units_all[:, 0].reshape(8 * units, 256), flat[1], 1, 0).astype(BF16)
    up_grad = dot(flat[0], units_all[:, 1].reshape(8 * units, 256), 0, 1).astype(BF16)
    return (ends[0], ends[1], up_grad, down_grad)


def solution(mesh):
    fine = Mesh(
        mesh.devices.reshape(2, 2, 2, 4, 2, 2, 2, 2),
        ("xh", "xp", "zh", "y", "c", "z2", "z1", "zp"),
    )
    owners = ("xh", "xp", "zh", "y", "c")
    features = ("z2", "z1", "zp")
    return jax.shard_map(
        local,
        mesh=fine,
        in_specs=(
            P(owners, features),
            P(None, owners + features),
            P(owners + features, None),
            P(owners, features),
        ),
        out_specs=(
            P(owners, features),
            P(owners, features),
            P(features, owners),
            P(owners, features),
        ),
        check_vma=False,
    )
```

time: 1200 us -> 213 us (0.18)
  the two profiles are of different devices: /device:TPU:0 before, /device:TPU:6 now
where the time goes in v1:
time: 213 us; the launch traced here: 210 us
  waiting for transfers between devices  89.8 us (42%)
  starting transfers between devices  70.9 us (33%)
  local copies, waits for them, and re-layouts  25 us (12%)
  matrix products  9.18 us (4%)
  blocking collectives  8.99 us (4%)
  other arithmetic  5.71 us (3%)
    all_to_all x9, waiting for transfers between devices, exchange(): return lax.all_to_all(value, axes, split_axis=0, concat_axis=0, tiled=True)  88.7 us
    all_to_all x9, starting transfers between devices, exchange(): return lax.all_to_all(value, axes, split_axis=0, concat_axis=0, tiled=True)  62.7 us
    dot_general x10, matrix products, dot(): lax.dot_general(left, right, (((left_dim,), (right_dim,)), ((), ())), pre...  9.18 us
    all_to_all x1, blocking collectives, exchange(): return lax.all_to_all(value, axes, split_axis=0, concat_axis=0, tiled=True)  8.99 us
    ppermute x4, starting transfers between devices, other_core(): return lax.ppermute(value, 'c', [(0, 1), (1, 0)])  8.16 us
    reshape x4, local copies, waits for them, and re-layouts, regroup(): blocks = weight.reshape(units, 2, 2, 2, width)  5.71 us
    broadcast_in_dim x5, local copies, waits for them, and re-layouts, spread(): return exchange(jnp.broadcast_to(value[None], (count,) + value.shape), axes)  4.54 us
  transfers between devices with their start and end apart: 13, of which 10 were waited for; matrix products, arithmetic and copies ran while one was open for 14% of the time, Pallas kernels for 0%

profile of v1, /device:TPU:6, one launch (start us, length us, event | category | flops | bytes accessed | tf_op | source)
XLA Modules:
  0.0 210.4 jit_solution(16100019632622814252)
XLA Ops:
  2.1 15.1 %all-to-all-start = ((bf16[8,8,1536]{2,1,0:T(8,128)(2,1)}), bf16[8,8,1536]{2,1,0:T(8,128)(2,1)S(1)}, u32[]{:S(2)}, u32[]{:S(2)}) async-start(bf16[8,8,1536]{2,1,0:T(8,128)(2,1)} %broadcast_in_dim.14), calls=%async_computation | async-start | bytes 393216 | tf_op jit(solution)/shard_map/all_to_all | solution.py:20
  17.2 1.9 reshape.57
  21.7 14.1 %all-to-all-done = bf16[8,8,1536]{2,1,0:T(8,128)(2,1)S(1)} async-done(((bf16[8,8,1536]{2,1,0:T(8,128)(2,1)}), bf16[8,8,1536]{2,1,0:T(8,128)(2,1)S(1)}, u32[]{:S(2)}, u32[]{:S(2)}) %all-to-all-start) | async-done | bytes 196640 | tf_op jit(solution)/shard_map/all_to_all | solution.py:20
  36.5 4.3 %all-to-all-start.2 = ((bf16[4,48,3072]{2,1,0:T(8,128)(2,1)}), bf16[4,48,3072]{2,1,0:T(8,128)(2,1)S(1)}, u32[]{:S(2)}, u32[]{:S(2)}) async-start(bf16[4,48,3072]{2,1,0:T(8,128)(2,1)} %reshape.58), calls=%async_computation.2 | async-start | bytes 2359296 | tf_op jit(solution)/shard_map/all_to_all | solution.py:20
  40.8 1.9 reshape.60
  45.4 6.4 %all-to-all-done.2 = bf16[4,48,3072]{2,1,0:T(8,128)(2,1)S(1)} async-done(((bf16[4,48,3072]{2,1,0:T(8,128)(2,1)}), bf16[4,48,3072]{2,1,0:T(8,128)(2,1)S(1)}, u32[]{:S(2)}, u32[]{:S(2)}) %all-to-all-start.2) | async-done | bytes 1179680 | tf_op jit(solution)/shard_map/all_to_all | solution.py:20
  51.8 4.1 %all-to-all-start.3 = ((bf16[4,48,3072]{2,1,0:T(8,128)(2,1)}), bf16[4,48,3072]{2,1,0:T(8,128)(2,1)S(1)}, u32[]{:S(2)}, u32[]{:S(2)}) async-start(bf16[4,48,3072]{2,1,0:T(8,128)(2,1)} %reshape.61), calls=%async_computation.3 | async-start | bytes 2359296 | tf_op jit(solution)/shard_map/all_to_all | solution.py:20
  56.1 12.8 %all-to-all-done.3 = bf16[4,48,3072]{2,1,0:T(8,128)(2,1)S(1)} async-done(((bf16[4,48,3072]{2,1,0:T(8,128)(2,1)}), bf16[4,48,3072]{2,1,0:T(8,128)(2,1)S(1)}, u32[]{:S(2)}, u32[]{:S(2)}) %all-to-all-start.3) | async-done | bytes 1179680 | tf_op jit(solution)/shard_map/all_to_all | solution.py:20
  70.3 7.2 %all-to-all-start.1 = ((bf16[16,2,2,8,1536]{4,3,2,1,0:T(8,128)(2,1)}), bf16[16,2,2,8,1536]{4,3,2,1,0:T(8,128)(2,1)}, u32[]{:S(2)}, u32[]{:S(2)}) async-start(bf16[16,2,2,8,1536]{4,3,2,1,0:T(8,128)(2,1)} %bitcast.115), calls=%async_computation.1 | async-start | bytes 3145728 | tf_op jit(solution)/shard_map/all_to_all | solution.py:20
  77.4 1.9 collective-permute-start
  79.4 2.4 %collective-permute-start.1 = (bf16[192,3072]{1,0:T(8,128)(2,1)S(1)}, bf16[192,3072]{1,0:T(8,128)(2,1)S(1)}, u32[]{:S(2)}, u32[]{:S(2)}) collective-permute-start(bf16[192,3072]{1,0:T(8,128)(2,1)S(1)} %bitcast.107), channel_id=1, source_target_pairs={{0,8},{8,0},{1,9},{9,1},{2,10},{10,2},{3,11},{11,3},{4,12},{12,4},... | collective-permute-start | bytes 3538952 | tf_op jit(solution)/shard_map/ppermute | solution.py:28
  81.8 16.2 %all-to-all-done.1 = bf16[16,2,2,8,1536]{4,3,2,1,0:T(8,128)(2,1)} async-done(((bf16[16,2,2,8,1536]{4,3,2,1,0:T(8,128)(2,1)}), bf16[16,2,2,8,1536]{4,3,2,1,0:T(8,128)(2,1)}, u32[]{:S(2)}, u32[]{:S(2)}) %all-to-all-start.1) | async-done | bytes 1572896 | tf_op jit(solution)/shard_map/all_to_all | solution.py:20
  102.8 9.0 %all_to_all.50 = f32[4,2,2,48,128]{4,3,2,1,0:T(8,128)} all-to-all(f32[4,2,2,48,128]{4,3,2,1,0:T(8,128)S(1)} %pad_maximum_fusion.2), channel_id=1, replica_groups=mesh['xh'=2,'xp'=2,'zh'=2,'y'=4,'c'=2,'z2'=2,'z1'=2,'zp'=2] {'xp','zp'}, dimensions={0} | all-to-all | bytes 786432 | tf_op jit(solution)/shard_map/all_to_all | solution.py:20
  115.6 5.1 %all-to-all-start.5 = ((bf16[4,2,2,48,128]{4,3,2,1,0:T(8,128)(2,1)}), bf16[4,2,2,48,128]{4,3,2,1,0:T(8,128)(2,1)}, u32[]{:S(2)}, u32[]{:S(2)}) async-start(bf16[4,2,2,48,128]{4,3,2,1,0:T(8,128)(2,1)} %broadcast_in_dim.17), calls=%async_computation.5 | async-start | bytes 393216 | tf_op jit(solution)/shard_map/all_to_all | solution.py:20
  126.8 7.0 %all-to-all-start.8 = ((bf16[16,2,8,1536]{3,2,1,0:T(8,128)(2,1)}), bf16[16,2,8,1536]{3,2,1,0:T(8,128)(2,1)}, u32[]{:S(2)}, u32[]{:S(2)}) async-start(bf16[16,2,8,1536]{3,2,1,0:T(8,128)(2,1)} %broadcast_in_dim.37), calls=%async_computation.8 | async-start | bytes 1572864 | tf_op jit(solution)/shard_map/all_to_all | solution.py:20
  138.9 4.4 %all-to-all-done.8 = bf16[16,2,8,1536]{3,2,1,0:T(8,128)(2,1)} async-done(((bf16[16,2,8,1536]{3,2,1,0:T(8,128)(2,1)}), bf16[16,2,8,1536]{3,2,1,0:T(8,128)(2,1)}, u32[]{:S(2)}, u32[]{:S(2)}) %all-to-all-start.8) | async-done | bytes 786464 | tf_op jit(solution)/shard_map/all_to_all | solution.py:20
  143.3 5.8 %all-to-all-start.6 = ((bf16[16,2,8,3072]{3,2,1,0:T(8,128)(2,1)}), bf16[16,2,8,3072]{3,2,1,0:T(8,128)(2,1)S(1)}, u32[]{:S(2)}, u32[]{:S(2)}) async-start(bf16[16,2,8,3072]{3,2,1,0:T(8,128)(2,1)} %pad_maximum_fusion), calls=%async_computation.6 | async-start | bytes 3145728 | tf_op jit(solution)/shard_map/all_to_all | solution.py:20
  149.2 1.9 collective-permute-start.3
  152.3 11.2 %all-to-all-done.6 = bf16[16,2,8,3072]{3,2,1,0:T(8,128)(2,1)S(1)} async-done(((bf16[16,2,8,3072]{3,2,1,0:T(8,128)(2,1)}), bf16[16,2,8,3072]{3,2,1,0:T(8,128)(2,1)S(1)}, u32[]{:S(2)}, u32[]{:S(2)}) %all-to-all-start.6) | async-done | bytes 1572896 | tf_op jit(solution)/shard_map/all_to_all | solution.py:20
  164.2 5.5 %all-to-all-start.9 = ((bf16[8,2,48,256]{3,2,1,0:T(8,128)(2,1)}), bf16[8,2,48,256]{3,2,1,0:T(8,128)(2,1)S(1)}, u32[]{:S(2)}, u32[]{:S(2)}) async-start(bf16[8,2,48,256]{3,2,1,0:T(8,128)(2,1)} %broadcast_in_dim.38), calls=%async_computation.9 | async-start | bytes 786432 | tf_op jit(solution)/shard_map/all_to_all | solution.py:20
  171.0 1.9 collective-permute-start.2
  175.6 9.1 %all-to-all-done.9 = bf16[8,2,48,256]{3,2,1,0:T(8,128)(2,1)S(1)} async-done(((bf16[8,2,48,256]{3,2,1,0:T(8,128)(2,1)}), bf16[8,2,48,256]{3,2,1,0:T(8,128)(2,1)S(1)}, u32[]{:S(2)}, u32[]{:S(2)}) %all-to-all-start.9) | async-done | bytes 393248 | tf_op jit(solution)/shard_map/all_to_all | solution.py:20
  184.7 8.6 %all-to-all-start.7 = ((bf16[8,2,4,1536]{3,2,1,0:T(4,128)(2,1)}), bf16[8,2,4,1536]{3,2,1,0:T(4,128)(2,1)S(1)}, u32[]{:S(2)}, u32[]{:S(2)}) async-start(bf16[8,2,4,1536]{3,2,1,0:T(4,128)(2,1)} %bitcast.36), calls=%async_computation.7 | async-start | bytes 393216 | tf_op jit(solution)/shard_map/all_to_all | solution.py:20
  196.5 13.2 %all-to-all-done.7 = bf16[8,2,4,1536]{3,2,1,0:T(4,128)(2,1)S(1)} async-done(((bf16[8,2,4,1536]{3,2,1,0:T(4,128)(2,1)}), bf16[8,2,4,1536]{3,2,1,0:T(4,128)(2,1)S(1)}, u32[]{:S(2)}, u32[]{:S(2)}) %all-to-all-start.7) | async-done | bytes 196640 | tf_op jit(solution)/shard_map/all_to_all | solution.py:20
  (61 shorter events, 38.4 us)
Async XLA Ops:
  2.1 33.8 %all-to-all-start = ((bf16[8,8,1536]{2,1,0:T(8,128)(2,1)}), bf16[8,8,1536]{2,1,0:T(8,128)(2,1)S(1)}, u32[]{:S(2)}, u32[]{:S(2)}) async-start(bf16[8,8,1536]{2,1,0:T(8,128)(2,1)} %broadcast_in_dim.14), calls=%async_computation | async-start | bytes 393216 | tf_op jit(solution)/shard_map/all_to_all | solution.py:20
  35.8 0.7 copy-start
  36.5 15.3 %all-to-all-start.2 = ((bf16[4,48,3072]{2,1,0:T(8,128)(2,1)}), bf16[4,48,3072]{2,1,0:T(8,128)(2,1)S(1)}, u32[]{:S(2)}, u32[]{:S(2)}) async-start(bf16[4,48,3072]{2,1,0:T(8,128)(2,1)} %reshape.58), calls=%async_computation.2 | async-start | bytes 2359296 | tf_op jit(solution)/shard_map/all_to_all | solution.py:20
  45.4 10.5 %copy-start.1 = (bf16[8,8,1536]{2,1,0:T(8,128)(2,1)S(1)}, bf16[8,8,1536]{2,1,0:T(8,128)(2,1)}, u32[]{:S(2)}) copy-start(bf16[8,8,1536]{2,1,0:T(8,128)(2,1)} %copy-done) | copy-start | bytes 589828
  51.8 17.1 %all-to-all-start.3 = ((bf16[4,48,3072]{2,1,0:T(8,128)(2,1)}), bf16[4,48,3072]{2,1,0:T(8,128)(2,1)S(1)}, u32[]{:S(2)}, u32[]{:S(2)}) async-start(bf16[4,48,3072]{2,1,0:T(8,128)(2,1)} %reshape.61), calls=%async_computation.3 | async-start | bytes 2359296 | tf_op jit(solution)/shard_map/all_to_all | solution.py:20
  70.3 27.7 %all-to-all-start.1 = ((bf16[16,2,2,8,1536]{4,3,2,1,0:T(8,128)(2,1)}), bf16[16,2,2,8,1536]{4,3,2,1,0:T(8,128)(2,1)}, u32[]{:S(2)}, u32[]{:S(2)}) async-start(bf16[16,2,2,8,1536]{4,3,2,1,0:T(8,128)(2,1)} %bitcast.115), calls=%async_computation.1 | async-start | bytes 3145728 | tf_op jit(solution)/shard_map/all_to_all | solution.py:20
  77.4 23.0 %collective-permute-start = (bf16[192,3072]{1,0:T(8,128)(2,1)S(1)}, bf16[192,3072]{1,0:T(8,128)(2,1)}, u32[]{:S(2)}, u32[]{:S(2)}) collective-permute-start(bf16[192,3072]{1,0:T(8,128)(2,1)S(1)} %bitcast.104), channel_id=1, source_target_pairs={{0,8},{8,0},{1,9},{9,1},{2,10},{10,2},{3,11},{11,3},{4,12},{12,4},... | collective-permute-start | bytes 3538952 | tf_op jit(solution)/shard_map/ppermute | solution.py:28
  79.4 22.9 %collective-permute-start.1 = (bf16[192,3072]{1,0:T(8,128)(2,1)S(1)}, bf16[192,3072]{1,0:T(8,128)(2,1)S(1)}, u32[]{:S(2)}, u32[]{:S(2)}) collective-permute-start(bf16[192,3072]{1,0:T(8,128)(2,1)S(1)} %bitcast.107), channel_id=1, source_target_pairs={{0,8},{8,0},{1,9},{9,1},{2,10},{10,2},{3,11},{11,3},{4,12},{12,4},... | collective-permute-start | bytes 3538952 | tf_op jit(solution)/shard_map/ppermute | solution.py:28
  114.3 0.6 copy-start.2
  114.3 0.6 copy-start.4
  115.6 9.4 %all-to-all-start.5 = ((bf16[4,2,2,48,128]{4,3,2,1,0:T(8,128)(2,1)}), bf16[4,2,2,48,128]{4,3,2,1,0:T(8,128)(2,1)}, u32[]{:S(2)}, u32[]{:S(2)}) async-start(bf16[4,2,2,48,128]{4,3,2,1,0:T(8,128)(2,1)} %broadcast_in_dim.17), calls=%async_computation.5 | async-start | bytes 393216 | tf_op jit(solution)/shard_map/all_to_all | solution.py:20
  126.8 16.5 %all-to-all-start.8 = ((bf16[16,2,8,1536]{3,2,1,0:T(8,128)(2,1)}), bf16[16,2,8,1536]{3,2,1,0:T(8,128)(2,1)}, u32[]{:S(2)}, u32[]{:S(2)}) async-start(bf16[16,2,8,1536]{3,2,1,0:T(8,128)(2,1)} %broadcast_in_dim.37), calls=%async_computation.8 | async-start | bytes 1572864 | tf_op jit(solution)/shard_map/all_to_all | solution.py:20
  138.9 10.2 %copy-start.3 = (bf16[1,2,48,128]{3,2,1,0:T(8,128)(2,1)S(1)}, bf16[1,2,48,128]{3,2,1,0:T(8,128)(2,1)}, u32[]{:S(2)}) copy-start(bf16[1,2,48,128]{3,2,1,0:T(8,128)(2,1)} %copy-done.2) | copy-start | bytes 73732
  138.9 10.2 %copy-start.5 = (bf16[1,2,48,128]{3,2,1,0:T(8,128)(2,1)S(1)}, bf16[1,2,48,128]{3,2,1,0:T(8,128)(2,1)}, u32[]{:S(2)}) copy-start(bf16[1,2,48,128]{3,2,1,0:T(8,128)(2,1)} %copy-done.4) | copy-start | bytes 73732
  143.3 20.1 %all-to-all-start.6 = ((bf16[16,2,8,3072]{3,2,1,0:T(8,128)(2,1)}), bf16[16,2,8,3072]{3,2,1,0:T(8,128)(2,1)S(1)}, u32[]{:S(2)}, u32[]{:S(2)}) async-start(bf16[16,2,8,3072]{3,2,1,0:T(8,128)(2,1)} %pad_maximum_fusion), calls=%async_computation.6 | async-start | bytes 3145728 | tf_op jit(solution)/shard_map/all_to_all | solution.py:20
  149.2 3.1 %collective-permute-start.3 = (bf16[2,48,128]{2,1,0:T(8,128)(2,1)S(1)}, bf16[2,48,128]{2,1,0:T(8,128)(2,1)S(1)}, u32[]{:S(2)}, u32[]{:S(2)}) collective-permute-start(bf16[2,48,128]{2,1,0:T(8,128)(2,1)S(1)} %get-tuple-element.15), channel_id=1, source_target_pairs={{0,8},{8,0},{1,9},{9,1},{2,10},{10,2},{3,11},{11,3},{4,12},{12,4},... | collective-permute-start | bytes 73736 | tf_op jit(solution)/shard_map/ppermute | solution.py:28
  164.2 20.5 %all-to-all-start.9 = ((bf16[8,2,48,256]{3,2,1,0:T(8,128)(2,1)}), bf16[8,2,48,256]{3,2,1,0:T(8,128)(2,1)S(1)}, u32[]{:S(2)}, u32[]{:S(2)}) async-start(bf16[8,2,48,256]{3,2,1,0:T(8,128)(2,1)} %broadcast_in_dim.38), calls=%async_computation.9 | async-start | bytes 786432 | tf_op jit(solution)/shard_map/all_to_all | solution.py:20
  171.0 22.4 %collective-permute-start.2 = (bf16[2,128,1536]{2,1,0:T(8,128)(2,1)S(1)}, bf16[2,128,1536]{2,1,0:T(8,128)(2,1)S(1)}, u32[]{:S(2)}, u32[]{:S(2)}) collective-permute-start(bf16[2,128,1536]{2,1,0:T(8,128)(2,1)S(1)} %bitcast.118), channel_id=1, source_target_pairs={{0,8},{8,0},{1,9},{9,1},{2,10},{10,2},{3,11},{11,3},{4,12},{12,4},... | collective-permute-start | bytes 2359304 | tf_op jit(solution)/shard_map/ppermute | solution.py:28
  184.7 25.0 %all-to-all-start.7 = ((bf16[8,2,4,1536]{3,2,1,0:T(4,128)(2,1)}), bf16[8,2,4,1536]{3,2,1,0:T(4,128)(2,1)S(1)}, u32[]{:S(2)}, u32[]{:S(2)}) async-start(bf16[8,2,4,1536]{3,2,1,0:T(4,128)(2,1)} %bitcast.36), calls=%async_computation.7 | async-start | bytes 393216 | tf_op jit(solution)/shard_map/all_to_all | solution.py:20

commit v2 on v1

v2 whole, which is shorter than its diff:
```python
import jax
import jax.numpy as jnp
from jax import lax
from jax.experimental import pallas as pl
from jax.experimental.pallas import tpu as pltpu
from jax.sharding import Mesh, PartitionSpec as P

BF16 = jnp.bfloat16
F32 = jnp.float32
VMEM_BYTES = 48 * 1024 * 1024

PLANE = ("xh", "xp", "y")
COLUMN = ("zh", "z2", "z1")
GROUP = ("xp", "zp")


def activate(values):
    return jax.nn.gelu(values, approximate=True)


def gelu_slope(pre_act, cotangent):
    unused, pullback = jax.vjp(activate, pre_act)
    return pullback(cotangent)[0]


def exchange(value, axes):
    return lax.all_to_all(value, axes, split_axis=0, concat_axis=0, tiled=True)


def spread(value, axes, count):
    return exchange(jnp.broadcast_to(value[None], (count,) + value.shape), axes)


def partner(value, axes, count, step):
    return lax.ppermute(value, axes, [(at, at ^ step) for at in range(count)])


def other_core(value):
    return partner(value, "c", 2, 1)


def gather_ring(value, axes, count, dim):
    here = lax.axis_index(axes)
    shape = list(value.shape)
    shape[dim] = count
    start = [0] * len(shape)
    whole = jnp.zeros(shape, value.dtype)
    for step in range(count):
        block = partner(value, axes, count, step) if step else value
        start[dim] = here ^ step
        whole = lax.dynamic_update_slice(whole, block, tuple(start))
    return whole


def after(value, *others):
    return lax.optimization_barrier((value,) + others)[0]


def dot(left, right, left_dim, right_dim):
    return lax.dot_general(
        left, right, (((left_dim,), (right_dim,)), ((), ())), preferred_element_type=F32
    )


def cut_kernel(member_ref, up_ref, down_ref, *refs):
    pieces, sems = refs[:4], refs[4]
    width = pieces[0].shape[2] // 2
    copies = []
    for step in range(4):
        for kind, source in enumerate((up_ref, down_ref)):
            for far in range(2):
                column = pl.multiple_of((far * 4 + (member_ref[0] ^ step)) * width, width)
                copies.append(
                    pltpu.make_async_copy(
                        source.at[:, pl.ds(column, width)],
                        pieces[step].at[kind, :, pl.ds(far * width, width)],
                        sems.at[len(copies)],
                    )
                )
                copies[-1].start()
    for copy in copies:
        copy.wait()


def cut(member, up_rows, down_rows):
    units, features = up_rows.shape
    piece = jax.ShapeDtypeStruct((2, units, features // 4), BF16)
    return pl.pallas_call(
        cut_kernel,
        out_shape=[piece] * 4,
        in_specs=[pl.BlockSpec(memory_space=pltpu.SMEM)] + [pl.BlockSpec(memory_space=pl.ANY)] * 2,
        out_specs=[pl.BlockSpec(memory_space=pl.ANY)] * 4,
        scratch_shapes=[pltpu.SemaphoreType.DMA((16,))],
        cost_estimate=pl.CostEstimate(flops=0, bytes_accessed=16 * units * features, transcendentals=0),
        name="cut_weights",
    )(member, up_rows, down_rows)


def hidden_kernel(member_ref, rows_ref, *refs):
    own, beside, out_ref = refs[:4], refs[4:8], refs[8]
    units = own[0].shape[1]
    width = rows_ref.shape[4]
    for kind in range(2):
        rows = [rows_ref[:, far, kind].reshape(-1, width) for far in range(2)]
        for core, pieces in enumerate((own, beside)):
            total = None
            for far in range(2):
                weight = jnp.concatenate(
                    [piece[kind, :, far * width : (far + 1) * width] for piece in pieces], axis=0
                )
                term = dot(weight, rows[far], 1, 1)
                total = term if total is None else total + term
            for step in range(4):
                out_ref[member_ref[0] ^ step, kind, core] = total[step * units : (step + 1) * units]


def hidden_parts(member, rows, own, beside):
    units = own[0].shape[1]
    tokens = rows.shape[0] * rows.shape[3]
    return pl.pallas_call(
        hidden_kernel,
        out_shape=jax.ShapeDtypeStruct((4, 2, 2, units, tokens), F32),
        in_specs=[pl.BlockSpec(memory_space=pltpu.SMEM)] + [pl.BlockSpec(memory_space=pltpu.VMEM)] * 9,
        out_specs=pl.BlockSpec(memory_space=pltpu.VMEM),
        compiler_params=pltpu.CompilerParams(vmem_limit_bytes=VMEM_BYTES),
        cost_estimate=pl.CostEstimate(flops=604_000_000, bytes_accessed=6_700_000, transcendentals=0),
        name="hidden_parts",
    )(member, rows, *own, *beside)


def gelu_kernel(parts_ref, own_ref, spread_ref):
    pre_act = parts_ref[0, 0] + parts_ref[1, 0] + parts_ref[2, 0] + parts_ref[3, 0]
    act_grad = parts_ref[0, 1] + parts_ref[1, 1] + parts_ref[2, 1] + parts_ref[3, 1]
    for kind, value in enumerate((activate(pre_act), gelu_slope(pre_act, act_grad))):
        value = value.astype(BF16)
        own_ref[kind] = value
        for at in range(4):
            spread_ref[at, kind] = value


def gelu_both(parts):
    shape = parts.shape
    return pl.pallas_call(
        gelu_kernel,
        out_shape=[jax.ShapeDtypeStruct(shape[1:], BF16), jax.ShapeDtypeStruct(shape, BF16)],
        in_specs=[pl.BlockSpec(memory_space=pltpu.VMEM)],
        out_specs=[pl.BlockSpec(memory_space=pltpu.VMEM)] * 2,
        cost_estimate=pl.CostEstimate(flops=1_000_000, bytes_accessed=700_000, transcendentals=12_288),
        name="gelu_both",
    )(parts)


def output_kernel(member_ref, shared_ref, *refs):
    own, beside, out_ref = refs[:4], refs[4:8], refs[8]
    features = own[0].shape[2]
    count, unused, rows, unused = out_ref.shape
    step_of = features // 4
    for result in range(2):
        units = jnp.concatenate(
            [shared_ref[member_ref[0] ^ step, result, core] for core in range(2) for step in range(4)],
            axis=0,
        )
        for at in range(4):
            columns = slice(at * step_of, (at + 1) * step_of)
            weight = jnp.concatenate(
                [piece[1 - result, :, columns] for piece in (*own, *beside)], axis=0
            )
            total = dot(units, weight, 0, 0)
            out_ref[:, result, :, columns] = total.astype(BF16).reshape(count, rows, step_of)


def output_parts(member, shared, own, beside, count):
    features = own[0].shape[2]
    rows = shared.shape[4] // count
    return pl.pallas_call(
        output_kernel,
        out_shape=jax.ShapeDtypeStruct((count, 2, rows, features), BF16),
        in_specs=[pl.BlockSpec(memory_space=pltpu.SMEM)] + [pl.BlockSpec(memory_space=pltpu.VMEM)] * 9,
        out_specs=pl.BlockSpec(memory_space=pltpu.VMEM),
        compiler_params=pltpu.CompilerParams(vmem_limit_bytes=VMEM_BYTES),
        cost_estimate=pl.CostEstimate(flops=604_000_000, bytes_accessed=6_700_000, transcendentals=0),
        name="output_parts",
    )(member, shared, *own, *beside)


def local(tokens, up_proj, down_proj, out_grad):
    width = tokens.shape[1]
    units = down_proj.shape[0]
    member = lax.axis_index(GROUP).reshape(1).astype(jnp.int32)

    both = jnp.concatenate([tokens, out_grad], axis=0)
    column = spread(both, COLUMN, 8).reshape(2, 2, 2, 2, 4, width)
    sent = column.transpose(2, 1, 3, 0, 4, 5).reshape(1, 2, 1, 2, 2, 8, width)
    sent = jnp.broadcast_to(sent, (2, 2, 4, 2, 2, 8, width)).reshape(16, 2, 2, 8, width)
    plane = exchange(sent, PLANE)

    pieces = cut(member, up_proj.T, down_proj)
    own = [pieces[0]] + [partner(pieces[step], GROUP, 4, step) for step in range(1, 4)]
    beside = [other_core(piece) for piece in own]

    parts = hidden_parts(member, plane, own, beside)
    hidden, shared = gelu_both(exchange(parts, GROUP))
    shared = exchange(shared, GROUP)

    partials = output_parts(member, shared, own, beside, 16)
    arrived = exchange(partials, PLANE)
    summed = jnp.sum(arrived.reshape(2, 2, 4, 2, 8, 2 * width).astype(F32), axis=(0, 2))
    summed = summed.astype(BF16).reshape(2, 2, 2, 4, 2, width)
    summed = summed.transpose(2, 4, 0, 1, 3, 5).reshape(8, 2, 4, width)
    ends = jnp.sum(exchange(summed, COLUMN).astype(F32), axis=0).astype(BF16)

    mine = lax.dynamic_index_in_dim(
        column.reshape(2, 4, 2, 4, width), lax.axis_index(("z2", "z1")), 1, keepdims=False
    )
    mine = mine.transpose(1, 0, 2, 3).reshape(2, 1, 1, 8, width)
    flat = gather_ring(mine, "y", 4, 2)
    flat = gather_ring(after(flat, partials), ("xh", "xp"), 4, 1).reshape(2, 128, width)
    flat = jnp.concatenate([flat, other_core(flat)], axis=1)
    units_all = jnp.concatenate([hidden[:, 0], other_core(hidden[:, 1])], axis=2)
    units_all = gather_ring(after(units_all, partials)[:, None], "z2", 2, 1)
    units_all = gather_ring(units_all[:, :, None], "z1", 2, 2)
    units_all = gather_ring(after(units_all, arrived)[:, :, :, None], "zp", 2, 3)
    units_all = units_all.reshape(2, 8 * units, 256)
    down_grad = dot(units_all[0], flat[1], 1, 0).astype(BF16)
    up_grad = dot(flat[0], units_all[1], 0, 1).astype(BF16)
    return (ends[0], ends[1], up_grad, down_grad)


def solution(mesh):
    fine = Mesh(
        mesh.devices.reshape(2, 2, 2, 4, 2, 2, 2, 2),
        ("xh", "xp", "zh", "y", "c", "z2", "z1", "zp"),
    )
    owners = ("xh", "xp", "zh", "y", "c")
    features = ("z2", "z1", "zp")
    return jax.shard_map(
        local,
        mesh=fine,
        in_specs=(
            P(owners, features),
            P(None, owners + features),
            P(owners + features, None),
            P(owners, features),
        ),
        out_specs=(
            P(owners, features),
            P(owners, features),
            P(features, owners),
            P(owners, features),
        ),
        check_vma=False,
    )
```

time: 213 us -> 265 us (1.24)
  Pallas kernels: 0 us -> 80.8 us
  waiting for transfers between devices: 89.8 us -> 38 us
  blocking collectives: 8.99 us -> 33.6 us
  starting transfers between devices: 70.9 us -> 81.9 us
  local copies, waits for them, and re-layouts: 25 us -> 19 us
  matrix products: 9.18 us -> 5.11 us
  other arithmetic: 5.71 us -> 1.72 us
    all_to_all x9 -> x5, waiting for transfers between devices: 88.7 us -> 0.82 us  [exchange(): return lax.all_to_all(value, axes, split_axis=0, concat_axis=0, tiled=True)]
    pallas_call x0 -> x4, Pallas kernels: none -> 80.8 us  [the longest x1 72.7 us: cut(): pl.pallas_call(cut_kernel, out_shape=[piece] * 4, in_specs=[pl.BlockSpec(...]
    ppermute x4 -> x18, starting transfers between devices: 8.16 us -> 51.2 us  [partner(): return lax.ppermute(value, axes, [(at, at ^ step) for at in range(count)])]
    ppermute x4 -> x18, waiting for transfers between devices: 1.17 us -> 37.1 us  [partner(): return lax.ppermute(value, axes, [(at, at ^ step) for at in range(count)])]
    all_to_all x9 -> x5, starting transfers between devices: 62.7 us -> 30.8 us  [exchange(): return lax.all_to_all(value, axes, split_axis=0, concat_axis=0, tiled=True)]
    all_to_all x1, blocking collectives: 8.99 us -> 33.6 us  [exchange(): return lax.all_to_all(value, axes, split_axis=0, concat_axis=0, tiled=True)]
    reshape x6 -> x0, local copies, waits for them, and re-layouts: 9.09 us -> none  [the longest x4 5.71 us: regroup(): blocks = weight.reshape(units, 2, 2, 2, width)]
    dynamic_update_slice x0 -> x14, local copies, waits for them, and re-layouts: none -> 6.8 us  [gather_ring(): whole = lax.dynamic_update_slice(whole, block, tuple(start))]
  transfers between devices with their start and end apart: 13 -> 23, of which waited for: 10 -> 8; matrix products, arithmetic and copies ran while one was open for 14% -> 7% of each run, Pallas kernels for 0% -> 30%
where the time goes in v2:
time: 265 us; the launch traced here: 261 us
  starting transfers between devices  81.9 us (31%)
  Pallas kernels  80.8 us (30%)
  waiting for transfers between devices  38 us (14%)
  blocking collectives  33.6 us (13%)
  local copies, waits for them, and re-layouts  19 us (7%)
  matrix products  5.11 us (2%)
    pallas_call x1, Pallas kernels, cut(): pl.pallas_call(cut_kernel, out_shape=[piece] * 4, in_specs=[pl.BlockSpec(...  72.7 us
    ppermute x18, starting transfers between devices, partner(): return lax.ppermute(value, axes, [(at, at ^ step) for at in range(count)])  51.2 us
    ppermute x18, waiting for transfers between devices, partner(): return lax.ppermute(value, axes, [(at, at ^ step) for at in range(count)])  37.1 us
    all_to_all x1, blocking collectives, exchange(): return lax.all_to_all(value, axes, split_axis=0, concat_axis=0, tiled=True)  33.6 us
    all_to_all x5, starting transfers between devices, exchange(): return lax.all_to_all(value, axes, split_axis=0, concat_axis=0, tiled=True)  30.8 us
    dynamic_update_slice x14, local copies, waits for them, and re-layouts, gather_ring(): whole = lax.dynamic_update_slice(whole, block, tuple(start))  6.8 us
  transfers between devices with their start and end apart: 23, of which 8 were waited for; matrix products, arithmetic and copies ran while one was open for 7% of the time, Pallas kernels for 30%

profile of v2, /device:TPU:6, one launch (start us, length us, event | category | flops | bytes accessed | tf_op | source)
XLA Modules:
  0.0 261.2 jit_solution(12946258608301270091)
XLA Ops:
  1.4 33.6 %all_to_all.30 = bf16[8,8,1536]{2,1,0:T(8,128)(2,1)S(1)} all-to-all(bf16[8,8,1536]{2,1,0:T(8,128)(2,1)S(1)} %broadcast_in_dim.39), channel_id=1, replica_groups=mesh['xh'=2,'xp'=2,'zh'=2,'y'=4,'c'=2,'z2'=2,'z1'=2,'zp'=2] {'zh','z2','..., dimensions={0} | all-to-all | bytes 393216 | tf_op jit(solution)/shard_map/all_to_all | solution.py:27
  36.5 7.4 %all-to-all-start.1 = ((bf16[16,2,2,8,1536]{4,3,2,1,0:T(8,128)(2,1)}), bf16[16,2,2,8,1536]{4,3,2,1,0:T(8,128)(2,1)}, u32[]{:S(2)}, u32[]{:S(2)}) async-start(bf16[16,2,2,8,1536]{4,3,2,1,0:T(8,128)(2,1)} %bitcast.3), calls=%async_computation.1 | async-start | bytes 3145728 | tf_op jit(solution)/shard_map/all_to_all | solution.py:27
  44.0 72.7 %cut_weights.1 = (bf16[2,48,3072]{2,1,0:T(8,128)(2,1)}, bf16[2,48,3072]{2,1,0:T(8,128)(2,1)}, bf16[2,48,3072]{2,1,0:T(8,128)(2,1)}, bf16[2,48,3072]{2,1,0:T(8,128)(2,1)}) custom-call(s32[1]{0:T(128)} %bitcast.member_ref, bf16[48,12288]{1,0:T(8,128)(2,1)} %bitcast.49, bf16[48,12288]{1,0:T(8,128)(2,1)} %down_ref.1), custom_call_target="tpu_custom_call" | custom-call | bytes 9437184 | tf_op jit(solution)/shard_map/cut_weights/pallas_call | solution.py:88
  119.1 2.8 %collective-permute-start.1 = (bf16[2,48,3072]{2,1,0:T(8,128)(2,1)}, bf16[2,48,3072]{2,1,0:T(8,128)(2,1)S(1)}, u32[]{:S(2)}, u32[]{:S(2)}) collective-permute-start(bf16[2,48,3072]{2,1,0:T(8,128)(2,1)} %get-tuple-element.15), channel_id=1, source_target_pairs={{0,128},{1,129},{128,0},{129,1},{2,130},{3,131},{130,2},{131,3},{4... | collective-permute-start | bytes 1769480 | tf_op jit(solution)/shard_map/ppermute | solution.py:35
  121.8 4.1 %collective-permute-start.2 = (bf16[2,48,3072]{2,1,0:T(8,128)(2,1)}, bf16[2,48,3072]{2,1,0:T(8,128)(2,1)S(1)}, u32[]{:S(2)}, u32[]{:S(2)}) collective-permute-start(bf16[2,48,3072]{2,1,0:T(8,128)(2,1)} %get-tuple-element.16), channel_id=1, source_target_pairs={{0,129},{1,128},{128,1},{129,0},{2,131},{3,130},{130,3},{131,2},{4... | collective-permute-start | bytes 1769480 | tf_op jit(solution)/shard_map/ppermute | solution.py:35
  127.8 7.2 %collective-permute-done.refs_1_ = bf16[2,48,3072]{2,1,0:T(8,128)(2,1)S(1)} collective-permute-done((bf16[2,48,3072]{2,1,0:T(8,128)(2,1)}, bf16[2,48,3072]{2,1,0:T(8,128)(2,1)S(1)}, u32[]{:S(2)}, u32[]{:S(2)}) %collective-permute-start) | collective-permute-done | bytes 589856 | tf_op jit(solution)/shard_map/ppermute | solution.py:35
  137.0 7.5 %collective-permute-done.1.refs_2_ = bf16[2,48,3072]{2,1,0:T(8,128)(2,1)S(1)} collective-permute-done((bf16[2,48,3072]{2,1,0:T(8,128)(2,1)}, bf16[2,48,3072]{2,1,0:T(8,128)(2,1)S(1)}, u32[]{:S(2)}, u32[]{:S(2)}) %collective-permute-start.1) | collective-permute-done | bytes 589856 | tf_op jit(solution)/shard_map/ppermute | solution.py:35
  152.0 3.4 %collective-permute-start.7 = (bf16[2,1,1,8,1536]{4,0,3,2,1:T(2,128)(2,1)}, bf16[2,1,1,8,1536]{4,0,3,2,1:T(2,128)(2,1)}, u32[]{:S(2)}, u32[]{:S(2)}) collective-permute-start(bf16[2,1,1,8,1536]{4,0,3,2,1:T(2,128)(2,1)} %bitcast.12), channel_id=1, source_target_pairs={{0,16},{16,0},{32,48},{48,32},{1,17},{17,1},{33,49},{49,33},{2,18}... | collective-permute-start | bytes 147464 | tf_op jit(solution)/shard_map/ppermute | solution.py:35
  155.4 4.6 %collective-permute-start.8 = (bf16[2,1,1,8,1536]{4,0,3,2,1:T(2,128)(2,1)}, bf16[2,1,1,8,1536]{4,0,3,2,1:T(2,128)(2,1)}, u32[]{:S(2)}, u32[]{:S(2)}) collective-permute-start(bf16[2,1,1,8,1536]{4,0,3,2,1:T(2,128)(2,1)} %bitcast.12), channel_id=1, source_target_pairs={{0,32},{16,48},{32,0},{48,16},{1,33},{17,49},{33,1},{49,17},{2,34}... | collective-permute-start | bytes 147464 | tf_op jit(solution)/shard_map/ppermute | solution.py:35
  163.5 2.9 %hidden_parts.1 = f32[4,2,2,48,128]{4,3,2,1,0:T(8,128)S(1)} custom-call(s32[1]{0:T(128)} %bitcast.member_ref, bf16[16,2,2,8,1536]{4,3,2,1,0:T(8,128)(2,1)} %all-to-all-done.1.rows_ref, bf16[2,48,3072]{2,1,0:T(8,128)(2,1)S(1)} %copy-done, bf16[2,48,3072]{2,1,0:T(8,128)(2,1)S(1)} %collective-permute-done.refs_1_, ...), custom_call_target="tpu_custom_call" | custom-call | flops 604000000 | bytes 6700000 | tf_op jit(solution)/shard_map/hidden_parts/pallas_call | solution.py:120
  168.1 5.0 %all-to-all-start.2 = ((f32[4,2,2,48,128]{4,3,2,1,0:T(8,128)}), f32[4,2,2,48,128]{4,3,2,1,0:T(8,128)}, u32[]{:S(2)}, u32[]{:S(2)}) async-start(f32[4,2,2,48,128]{4,3,2,1,0:T(8,128)} %copy-done.4), calls=%async_computation.2 | async-start | bytes 786432 | tf_op jit(solution)/shard_map/all_to_all | solution.py:27
  180.6 4.5 %all-to-all-start.3 = ((bf16[4,2,2,48,128]{4,3,2,1,0:T(8,128)(2,1)}), bf16[4,2,2,48,128]{4,3,2,1,0:T(8,128)(2,1)}, u32[]{:S(2)}, u32[]{:S(2)}) async-start(bf16[4,2,2,48,128]{4,3,2,1,0:T(8,128)(2,1)} %get-tuple-element.17), calls=%async_computation.3 | async-start | bytes 393216 | tf_op jit(solution)/shard_map/all_to_all | solution.py:27
  192.1 3.4 %output_parts.1 = bf16[16,2,8,3072]{3,2,1,0:T(8,128)(2,1)} custom-call(s32[1]{0:T(128)} %bitcast.member_ref, bf16[4,2,2,48,128]{4,3,2,1,0:T(8,128)(2,1)} %all-to-all-done.3.shared_ref, bf16[2,48,3072]{2,1,0:T(8,128)(2,1)S(1)} %copy-done.1, bf16[2,48,3072]{2,1,0:T(8,128)(2,1)S(1)} %collective-permute-done.refs_1_, ...), custom_call_target="tpu_custom_call" | custom-call | flops 604000000 | bytes 6700000 | tf_op jit(solution)/shard_map/output_parts/pallas_call | solution.py:175
  195.5 6.8 %all-to-all-start.4 = ((bf16[16,2,8,3072]{3,2,1,0:T(8,128)(2,1)}), bf16[16,2,8,3072]{3,2,1,0:T(8,128)(2,1)S(1)}, u32[]{:S(2)}, u32[]{:S(2)}) async-start(bf16[16,2,8,3072]{3,2,1,0:T(8,128)(2,1)} %output_parts.1), calls=%async_computation.4 | async-start | bytes 3145728 | tf_op jit(solution)/shard_map/all_to_all | solution.py:27
  202.2 2.8 %collective-permute-start.10 = (bf16[2,1,4,8,1536]{4,3,2,1,0:T(8,128)(2,1)}, bf16[2,1,4,8,1536]{4,3,2,1,0:T(8,128)(2,1)S(1)}, u32[]{:S(2)}, u32[]{:S(2)}) collective-permute-start(bf16[2,1,4,8,1536]{4,3,2,1,0:T(8,128)(2,1)} %copy_dynamic-update-slice_fusion), channel_id=1, source_target_pairs={{0,128},{128,0},{256,384},{384,256},{1,129},{129,1},{257,385},{385... | collective-permute-start | bytes 589832 | tf_op jit(solution)/shard_map/ppermute | solution.py:35
  205.0 2.6 %collective-permute-start.11 = (bf16[2,1,4,8,1536]{4,3,2,1,0:T(8,128)(2,1)}, bf16[2,1,4,8,1536]{4,3,2,1,0:T(8,128)(2,1)S(1)}, u32[]{:S(2)}, u32[]{:S(2)}) collective-permute-start(bf16[2,1,4,8,1536]{4,3,2,1,0:T(8,128)(2,1)} %copy_dynamic-update-slice_fusion), channel_id=1, source_target_pairs={{0,256},{128,384},{256,0},{384,128},{1,257},{129,385},{257,1},{385... | collective-permute-start | bytes 589832 | tf_op jit(solution)/shard_map/ppermute | solution.py:35
  207.6 5.0 %collective-permute-start.12 = (bf16[2,1,4,8,1536]{4,3,2,1,0:T(8,128)(2,1)}, bf16[2,1,4,8,1536]{4,3,2,1,0:T(8,128)(2,1)S(1)}, u32[]{:S(2)}, u32[]{:S(2)}) collective-permute-start(bf16[2,1,4,8,1536]{4,3,2,1,0:T(8,128)(2,1)} %copy_dynamic-update-slice_fusion), channel_id=1, source_target_pairs={{0,384},{128,256},{256,128},{384,0},{1,385},{129,257},{257,129},{3... | collective-permute-start | bytes 589832 | tf_op jit(solution)/shard_map/ppermute | solution.py:35
  212.7 3.6 %collective-permute-start.15 = (bf16[2,1,48,256]{3,2,0,1:T(8,128)(2,1)S(1)}, bf16[2,1,48,256]{3,2,0,1:T(8,128)(2,1)S(1)}, u32[]{:S(2)}, u32[]{:S(2)}) collective-permute-start(bf16[2,1,48,256]{3,2,0,1:T(8,128)(2,1)S(1)} %bitcast.55), channel_id=1, source_target_pairs={{0,4},{4,0},{1,5},{5,1},{2,6},{6,2},{3,7},{7,3},{8,12},{12,8},{9,1... | collective-permute-start | bytes 147464 | tf_op jit(solution)/shard_map/ppermute | solution.py:35
  217.3 6.8 %collective-permute-done.15 = bf16[2,1,48,256]{3,2,0,1:T(8,128)(2,1)S(1)} collective-permute-done((bf16[2,1,48,256]{3,2,0,1:T(8,128)(2,1)S(1)}, bf16[2,1,48,256]{3,2,0,1:T(8,128)(2,1)S(1)}, u32[]{:S(2)}, u32[]{:S(2)}) %collective-permute-start.15) | collective-permute-done | bytes 49184 | tf_op jit(solution)/shard_map/ppermute | solution.py:35
  226.6 3.0 %collective-permute-done.11 = bf16[2,1,4,8,1536]{4,3,2,1,0:T(8,128)(2,1)S(1)} collective-permute-done((bf16[2,1,4,8,1536]{4,3,2,1,0:T(8,128)(2,1)}, bf16[2,1,4,8,1536]{4,3,2,1,0:T(8,128)(2,1)S(1)}, u32[]{:S(2)}, u32[]{:S(2)}) %collective-permute-start.11) | collective-permute-done | bytes 196640 | tf_op jit(solution)/shard_map/ppermute | solution.py:35
  233.1 7.1 %all-to-all-start.5 = ((bf16[8,2,4,1536]{3,2,1,0:T(4,128)(2,1)}), bf16[8,2,4,1536]{3,2,1,0:T(4,128)(2,1)S(1)}, u32[]{:S(2)}, u32[]{:S(2)}) async-start(bf16[8,2,4,1536]{3,2,1,0:T(4,128)(2,1)} %bitcast.7), calls=%async_computation.5 | async-start | bytes 393216 | tf_op jit(solution)/shard_map/all_to_all | solution.py:27
  240.1 3.1 %collective-permute-start.17 = (bf16[2,2,2,1,48,256]{5,4,3,2,1,0:T(8,128)(2,1)S(1)}, bf16[2,2,2,1,48,256]{5,4,3,2,1,0:T(8,128)(2,1)S(1)}, u32[]{:S(2)}, u32[]{:S(2)}) collective-permute-start(bf16[2,2,2,1,48,256]{5,4,3,2,1,0:T(8,128)(2,1)S(1)} %bitcast.52), channel_id=1, source_target_pairs={{0,1},{1,0},{2,3},{3,2},{4,5},{5,4},{6,7},{7,6},{8,9},{9,8},{10,11... | collective-permute-start | bytes 589832 | tf_op jit(solution)/shard_map/ppermute | solution.py:35
  243.3 12.0 %collective-permute-done.17 = bf16[2,2,2,1,48,256]{5,4,3,2,1,0:T(8,128)(2,1)S(1)} collective-permute-done((bf16[2,2,2,1,48,256]{5,4,3,2,1,0:T(8,128)(2,1)S(1)}, bf16[2,2,2,1,48,256]{5,4,3,2,1,0:T(8,128)(2,1)S(1)}, u32[]{:S(2)}, u32[]{:S(2)}) %collective-permute-start.17) | collective-permute-done | bytes 196640 | tf_op jit(solution)/shard_map/ppermute | solution.py:35
  255.3 2.6 %convolution_convert_fusion.1 = bf16[1536,384]{1,0:T(8,128)(2,1)} fusion(bf16[384,256]{1,0:T(8,128)(2,1)S(1)} %bitcast.56, bf16[2,128,1536]{2,1,0:T(8,128)(2,1)S(1)} %bitcast.47, bf16[2,128,1536]{2,1,0:T(8,128)(2,1)} %collective-permute-done.13), kind=kOutput, calls=%fused_computation.1 | convolution fusion | flops 304152576 | bytes 2949120 | tf_op jit(solution)/shard_map/dot_general | solution.py:60
  (80 shorter events, 45.7 us)
Async XLA Ops:
  36.5 125.9 %all-to-all-start.1 = ((bf16[16,2,2,8,1536]{4,3,2,1,0:T(8,128)(2,1)}), bf16[16,2,2,8,1536]{4,3,2,1,0:T(8,128)(2,1)}, u32[]{:S(2)}, u32[]{:S(2)}) async-start(bf16[16,2,2,8,1536]{4,3,2,1,0:T(8,128)(2,1)} %bitcast.3), calls=%async_computation.1 | async-start | bytes 3145728 | tf_op jit(solution)/shard_map/all_to_all | solution.py:27
  116.7 18.4 %collective-permute-start = (bf16[2,48,3072]{2,1,0:T(8,128)(2,1)}, bf16[2,48,3072]{2,1,0:T(8,128)(2,1)S(1)}, u32[]{:S(2)}, u32[]{:S(2)}) collective-permute-start(bf16[2,48,3072]{2,1,0:T(8,128)(2,1)} %get-tuple-element.14), channel_id=1, source_target_pairs={{0,1},{1,0},{128,129},{129,128},{2,3},{3,2},{130,131},{131,130},{4... | collective-permute-start | bytes 1769480 | tf_op jit(solution)/shard_map/ppermute | solution.py:35
  119.1 25.4 %collective-permute-start.1 = (bf16[2,48,3072]{2,1,0:T(8,128)(2,1)}, bf16[2,48,3072]{2,1,0:T(8,128)(2,1)S(1)}, u32[]{:S(2)}, u32[]{:S(2)}) collective-permute-start(bf16[2,48,3072]{2,1,0:T(8,128)(2,1)} %get-tuple-element.15), channel_id=1, source_target_pairs={{0,128},{1,129},{128,0},{129,1},{2,130},{3,131},{130,2},{131,3},{4... | collective-permute-start | bytes 1769480 | tf_op jit(solution)/shard_map/ppermute | solution.py:35
  121.8 24.5 %collective-permute-start.2 = (bf16[2,48,3072]{2,1,0:T(8,128)(2,1)}, bf16[2,48,3072]{2,1,0:T(8,128)(2,1)S(1)}, u32[]{:S(2)}, u32[]{:S(2)}) collective-permute-start(bf16[2,48,3072]{2,1,0:T(8,128)(2,1)} %get-tuple-element.16), channel_id=1, source_target_pairs={{0,129},{1,128},{128,1},{129,0},{2,131},{3,130},{130,3},{131,2},{4... | collective-permute-start | bytes 1769480 | tf_op jit(solution)/shard_map/ppermute | solution.py:35
  125.9 29.5 %collective-permute-start.3 = (bf16[2,48,3072]{2,1,0:T(8,128)(2,1)}, bf16[2,48,3072]{2,1,0:T(8,128)(2,1)S(1)}, u32[]{:S(2)}, u32[]{:S(2)}) collective-permute-start(bf16[2,48,3072]{2,1,0:T(8,128)(2,1)} %get-tuple-element.13.refs_0_), channel_id=1, source_target_pairs={{0,8},{8,0},{1,9},{9,1},{2,10},{10,2},{3,11},{11,3},{4,12},{12,4},... | collective-permute-start | bytes 1769480 | tf_op jit(solution)/shard_map/ppermute | solution.py:35
  135.0 24.9 %collective-permute-start.4 = (bf16[2,48,3072]{2,1,0:T(8,128)(2,1)S(1)}, bf16[2,48,3072]{2,1,0:T(8,128)(2,1)S(1)}, u32[]{:S(2)}, u32[]{:S(2)}) collective-permute-start(bf16[2,48,3072]{2,1,0:T(8,128)(2,1)S(1)} %collective-permute-done.refs_1_), channel_id=1, source_target_pairs={{0,8},{8,0},{1,9},{9,1},{2,10},{10,2},{3,11},{11,3},{4,12},{12,4},... | collective-permute-start | bytes 1769480 | tf_op jit(solution)/shard_map/ppermute | solution.py:35
  144.4 18.0 %collective-permute-start.5 = (bf16[2,48,3072]{2,1,0:T(8,128)(2,1)S(1)}, bf16[2,48,3072]{2,1,0:T(8,128)(2,1)S(1)}, u32[]{:S(2)}, u32[]{:S(2)}) collective-permute-start(bf16[2,48,3072]{2,1,0:T(8,128)(2,1)S(1)} %collective-permute-done.1.refs_2_), channel_id=1, source_target_pairs={{0,8},{8,0},{1,9},{9,1},{2,10},{10,2},{3,11},{11,3},{4,12},{12,4},... | collective-permute-start | bytes 1769480 | tf_op jit(solution)/shard_map/ppermute | solution.py:35
  146.4 16.1 %collective-permute-start.6 = (bf16[2,48,3072]{2,1,0:T(8,128)(2,1)S(1)}, bf16[2,48,3072]{2,1,0:T(8,128)(2,1)}, u32[]{:S(2)}, u32[]{:S(2)}) collective-permute-start(bf16[2,48,3072]{2,1,0:T(8,128)(2,1)S(1)} %collective-permute-done.2.refs_3_), channel_id=1, source_target_pairs={{0,8},{8,0},{1,9},{9,1},{2,10},{10,2},{3,11},{11,3},{4,12},{12,4},... | collective-permute-start | bytes 1769480 | tf_op jit(solution)/shard_map/ppermute | solution.py:35
  152.0 23.2 %collective-permute-start.7 = (bf16[2,1,1,8,1536]{4,0,3,2,1:T(2,128)(2,1)}, bf16[2,1,1,8,1536]{4,0,3,2,1:T(2,128)(2,1)}, u32[]{:S(2)}, u32[]{:S(2)}) collective-permute-start(bf16[2,1,1,8,1536]{4,0,3,2,1:T(2,128)(2,1)} %bitcast.12), channel_id=1, source_target_pairs={{0,16},{16,0},{32,48},{48,32},{1,17},{17,1},{33,49},{49,33},{2,18}... | collective-permute-start | bytes 147464 | tf_op jit(solution)/shard_map/ppermute | solution.py:35
  155.4 21.3 %collective-permute-start.8 = (bf16[2,1,1,8,1536]{4,0,3,2,1:T(2,128)(2,1)}, bf16[2,1,1,8,1536]{4,0,3,2,1:T(2,128)(2,1)}, u32[]{:S(2)}, u32[]{:S(2)}) collective-permute-start(bf16[2,1,1,8,1536]{4,0,3,2,1:T(2,128)(2,1)} %bitcast.12), channel_id=1, source_target_pairs={{0,32},{16,48},{32,0},{48,16},{1,33},{17,49},{33,1},{49,17},{2,34}... | collective-permute-start | bytes 147464 | tf_op jit(solution)/shard_map/ppermute | solution.py:35
  160.0 25.2 %collective-permute-start.9 = (bf16[2,1,1,8,1536]{4,0,3,2,1:T(2,128)(2,1)}, bf16[2,1,1,8,1536]{4,0,3,2,1:T(2,128)(2,1)}, u32[]{:S(2)}, u32[]{:S(2)}) collective-permute-start(bf16[2,1,1,8,1536]{4,0,3,2,1:T(2,128)(2,1)} %bitcast.12), channel_id=1, source_target_pairs={{0,48},{16,32},{32,16},{48,0},{1,49},{17,33},{33,17},{49,1},{2,50}... | collective-permute-start | bytes 147464 | tf_op jit(solution)/shard_map/ppermute | solution.py:35
  168.1 22.9 %copy-start.1 = (bf16[2,48,3072]{2,1,0:T(8,128)(2,1)S(1)}, bf16[2,48,3072]{2,1,0:T(8,128)(2,1)}, u32[]{:S(2)}) copy-start(bf16[2,48,3072]{2,1,0:T(8,128)(2,1)} %get-tuple-element.13.refs_0_) | copy-start | bytes 1769476
  168.1 10.8 %all-to-all-start.2 = ((f32[4,2,2,48,128]{4,3,2,1,0:T(8,128)}), f32[4,2,2,48,128]{4,3,2,1,0:T(8,128)}, u32[]{:S(2)}, u32[]{:S(2)}) async-start(f32[4,2,2,48,128]{4,3,2,1,0:T(8,128)} %copy-done.4), calls=%async_computation.2 | async-start | bytes 786432 | tf_op jit(solution)/shard_map/all_to_all | solution.py:27
  180.6 10.4 %all-to-all-start.3 = ((bf16[4,2,2,48,128]{4,3,2,1,0:T(8,128)(2,1)}), bf16[4,2,2,48,128]{4,3,2,1,0:T(8,128)(2,1)}, u32[]{:S(2)}, u32[]{:S(2)}) async-start(bf16[4,2,2,48,128]{4,3,2,1,0:T(8,128)(2,1)} %get-tuple-element.17), calls=%async_computation.3 | async-start | bytes 393216 | tf_op jit(solution)/shard_map/all_to_all | solution.py:27
  187.3 3.1 %collective-permute-start.14 = (bf16[2,48,128]{2,1,0:T(8,128)(2,1)S(1)}, bf16[2,48,128]{2,1,0:T(8,128)(2,1)S(1)}, u32[]{:S(2)}, u32[]{:S(2)}) collective-permute-start(bf16[2,48,128]{2,1,0:T(8,128)(2,1)S(1)} %slice_bitcast_fusion.1), channel_id=1, source_target_pairs={{0,8},{8,0},{1,9},{9,1},{2,10},{10,2},{3,11},{11,3},{4,12},{12,4},... | collective-permute-start | bytes 73736 | tf_op jit(solution)/shard_map/ppermute | solution.py:35
  195.5 36.5 %all-to-all-start.4 = ((bf16[16,2,8,3072]{3,2,1,0:T(8,128)(2,1)}), bf16[16,2,8,3072]{3,2,1,0:T(8,128)(2,1)S(1)}, u32[]{:S(2)}, u32[]{:S(2)}) async-start(bf16[16,2,8,3072]{3,2,1,0:T(8,128)(2,1)} %output_parts.1), calls=%async_computation.4 | async-start | bytes 3145728 | tf_op jit(solution)/shard_map/all_to_all | solution.py:27
  202.2 24.4 %collective-permute-start.10 = (bf16[2,1,4,8,1536]{4,3,2,1,0:T(8,128)(2,1)}, bf16[2,1,4,8,1536]{4,3,2,1,0:T(8,128)(2,1)S(1)}, u32[]{:S(2)}, u32[]{:S(2)}) collective-permute-start(bf16[2,1,4,8,1536]{4,3,2,1,0:T(8,128)(2,1)} %copy_dynamic-update-slice_fusion), channel_id=1, source_target_pairs={{0,128},{128,0},{256,384},{384,256},{1,129},{129,1},{257,385},{385... | collective-permute-start | bytes 589832 | tf_op jit(solution)/shard_map/ppermute | solution.py:35
  205.0 24.7 %collective-permute-start.11 = (bf16[2,1,4,8,1536]{4,3,2,1,0:T(8,128)(2,1)}, bf16[2,1,4,8,1536]{4,3,2,1,0:T(8,128)(2,1)S(1)}, u32[]{:S(2)}, u32[]{:S(2)}) collective-permute-start(bf16[2,1,4,8,1536]{4,3,2,1,0:T(8,128)(2,1)} %copy_dynamic-update-slice_fusion), channel_id=1, source_target_pairs={{0,256},{128,384},{256,0},{384,128},{1,257},{129,385},{257,1},{385... | collective-permute-start | bytes 589832 | tf_op jit(solution)/shard_map/ppermute | solution.py:35
  207.6 22.1 %collective-permute-start.12 = (bf16[2,1,4,8,1536]{4,3,2,1,0:T(8,128)(2,1)}, bf16[2,1,4,8,1536]{4,3,2,1,0:T(8,128)(2,1)S(1)}, u32[]{:S(2)}, u32[]{:S(2)}) collective-permute-start(bf16[2,1,4,8,1536]{4,3,2,1,0:T(8,128)(2,1)} %copy_dynamic-update-slice_fusion), channel_id=1, source_target_pairs={{0,384},{128,256},{256,128},{384,0},{1,385},{129,257},{257,129},{3... | collective-permute-start | bytes 589832 | tf_op jit(solution)/shard_map/ppermute | solution.py:35
  212.7 11.5 %collective-permute-start.15 = (bf16[2,1,48,256]{3,2,0,1:T(8,128)(2,1)S(1)}, bf16[2,1,48,256]{3,2,0,1:T(8,128)(2,1)S(1)}, u32[]{:S(2)}, u32[]{:S(2)}) collective-permute-start(bf16[2,1,48,256]{3,2,0,1:T(8,128)(2,1)S(1)} %bitcast.55), channel_id=1, source_target_pairs={{0,4},{4,0},{1,5},{5,1},{2,6},{6,2},{3,7},{7,3},{8,12},{12,8},{9,1... | collective-permute-start | bytes 147464 | tf_op jit(solution)/shard_map/ppermute | solution.py:35
  224.1 7.8 %collective-permute-start.16 = (bf16[2,2,1,48,256]{4,3,2,1,0:T(8,128)(2,1)S(1)}, bf16[2,2,1,48,256]{4,3,2,1,0:T(8,128)(2,1)S(1)}, u32[]{:S(2)}, u32[]{:S(2)}) collective-permute-start(bf16[2,2,1,48,256]{4,3,2,1,0:T(8,128)(2,1)S(1)} %bitcast_dynamic-update-slice_fusion), channel_id=1, source_target_pairs={{0,2},{2,0},{1,3},{3,1},{4,6},{6,4},{5,7},{7,5},{8,10},{10,8},{9,1... | collective-permute-start | bytes 294920 | tf_op jit(solution)/shard_map/ppermute | solution.py:35
  229.7 25.6 %collective-permute-start.13 = (bf16[2,128,1536]{2,1,0:T(8,128)(2,1)S(1)}, bf16[2,128,1536]{2,1,0:T(8,128)(2,1)}, u32[]{:S(2)}, u32[]{:S(2)}) collective-permute-start(bf16[2,128,1536]{2,1,0:T(8,128)(2,1)S(1)} %bitcast.46), channel_id=1, source_target_pairs={{0,8},{8,0},{1,9},{9,1},{2,10},{10,2},{3,11},{11,3},{4,12},{12,4},... | collective-permute-start | bytes 2359304 | tf_op jit(solution)/shard_map/ppermute | solution.py:35
  233.1 27.4 %all-to-all-start.5 = ((bf16[8,2,4,1536]{3,2,1,0:T(4,128)(2,1)}), bf16[8,2,4,1536]{3,2,1,0:T(4,128)(2,1)S(1)}, u32[]{:S(2)}, u32[]{:S(2)}) async-start(bf16[8,2,4,1536]{3,2,1,0:T(4,128)(2,1)} %bitcast.7), calls=%async_computation.5 | async-start | bytes 393216 | tf_op jit(solution)/shard_map/all_to_all | solution.py:27
  240.1 15.1 %collective-permute-start.17 = (bf16[2,2,2,1,48,256]{5,4,3,2,1,0:T(8,128)(2,1)S(1)}, bf16[2,2,2,1,48,256]{5,4,3,2,1,0:T(8,128)(2,1)S(1)}, u32[]{:S(2)}, u32[]{:S(2)}) collective-permute-start(bf16[2,2,2,1,48,256]{5,4,3,2,1,0:T(8,128)(2,1)S(1)} %bitcast.52), channel_id=1, source_target_pairs={{0,1},{1,0},{2,3},{3,2},{4,5},{5,4},{6,7},{7,6},{8,9},{9,8},{10,11... | collective-permute-start | bytes 589832 | tf_op jit(solution)/shard_map/ppermute | solution.py:35
  (6 other events, 22.5 us)

commit v3 on v2

--- a/solution.py
+++ b/solution.py
@@ -45,8 +45,8 @@
     shape[dim] = count
     start = [0] * len(shape)
     whole = jnp.zeros(shape, value.dtype)
-    for step in range(count):
-        block = partner(value, axes, count, step) if step else value
+    blocks = [value] + [partner(value, axes, count, step) for step in range(1, count)]
+    for step, block in enumerate(lax.optimization_barrier(blocks)):
         start[dim] = here ^ step
         whole = lax.dynamic_update_slice(whole, block, tuple(start))
     return whole
@@ -62,24 +62,13 @@
     )
 
 
-def cut_kernel(member_ref, up_ref, down_ref, *refs):
-    pieces, sems = refs[:4], refs[4]
+def cut_kernel(member_ref, up_ref, down_ref, *pieces):
     width = pieces[0].shape[2] // 2
-    copies = []
     for step in range(4):
         for kind, source in enumerate((up_ref, down_ref)):
             for far in range(2):
                 column = pl.multiple_of((far * 4 + (member_ref[0] ^ step)) * width, width)
-                copies.append(
-                    pltpu.make_async_copy(
-                        source.at[:, pl.ds(column, width)],
-                        pieces[step].at[kind, :, pl.ds(far * width, width)],
-                        sems.at[len(copies)],
-                    )
-                )
-                copies[-1].start()
-    for copy in copies:
-        copy.wait()
+                pieces[step][kind, :, far * width : (far + 1) * width] = source[:, pl.ds(column, width)]
 
 
 def cut(member, up_rows, down_rows):
@@ -88,10 +77,10 @@
     return pl.pallas_call(
         cut_kernel,
         out_shape=[piece] * 4,
-        in_specs=[pl.BlockSpec(memory_space=pltpu.SMEM)] + [pl.BlockSpec(memory_space=pl.ANY)] * 2,
-        out_specs=[pl.BlockSpec(memory_space=pl.ANY)] * 4,
-        scratch_shapes=[pltpu.SemaphoreType.DMA((16,))],
-        cost_estimate=pl.CostEstimate(flops=0, bytes_accessed=16 * units * features, transcendentals=0),
+        in_specs=[pl.BlockSpec(memory_space=pltpu.SMEM)] + [pl.BlockSpec(memory_space=pltpu.VMEM)] * 2,
+        out_specs=[pl.BlockSpec(memory_space=pltpu.VMEM)] * 4,
+        compiler_params=pltpu.CompilerParams(vmem_limit_bytes=VMEM_BYTES),
+        cost_estimate=pl.CostEstimate(flops=0, bytes_accessed=8 * units * features, transcendentals=0),
         name="cut_weights",
     )(member, up_rows, down_rows)
 
@@ -188,17 +177,24 @@
     units = down_proj.shape[0]
     member = lax.axis_index(GROUP).reshape(1).astype(jnp.int32)
 
+    pieces = cut(member, up_proj.T, down_proj)
+    own = [pieces[0]] + [partner(pieces[step], GROUP, 4, step) for step in range(1, 4)]
+    beside = [other_core(piece) for piece in own]
+
     both = jnp.concatenate([tokens, out_grad], axis=0)
     column = spread(both, COLUMN, 8).reshape(2, 2, 2, 2, 4, width)
     sent = column.transpose(2, 1, 3, 0, 4, 5).reshape(1, 2, 1, 2, 2, 8, width)
     sent = jnp.broadcast_to(sent, (2, 2, 4, 2, 2, 8, width)).reshape(16, 2, 2, 8, width)
-    plane = exchange(sent, PLANE)
-
-    pieces = cut(member, up_proj.T, down_proj)
-    own = [pieces[0]] + [partner(pieces[step], GROUP, 4, step) for step in range(1, 4)]
-    beside = [other_core(piece) for piece in own]
-
-    parts = hidden_parts(member, plane, own, beside)
+    plane = exchange(after(sent, *own), PLANE)
+
+    mine = lax.dynamic_index_in_dim(
+        column.reshape(2, 4, 2, 4, width), lax.axis_index(("z2", "z1")), 1, keepdims=False
+    )
+    mine = mine.transpose(1, 0, 2, 3).reshape(2, 1, 1, 8, width)
+    flat = gather_ring(mine, "y", 4, 2)
+    flat = gather_ring(flat, ("xh", "xp"), 4, 1).reshape(2, 128, width)
+
+    parts = hidden_parts(after(member, flat), plane, own, beside)
     hidden, shared = gelu_both(exchange(parts, GROUP))
     shared = exchange(shared, GROUP)
 
@@ -209,18 +205,12 @@
     summed = summed.transpose(2, 4, 0, 1, 3, 5).reshape(8, 2, 4, width)
     ends = jnp.sum(exchange(summed, COLUMN).astype(F32), axis=0).astype(BF16)
 
-    mine = lax.dynamic_index_in_dim(
-        column.reshape(2, 4, 2, 4, width), lax.axis_index(("z2", "z1")), 1, keepdims=False
-    )
-    mine = mine.transpose(1, 0, 2, 3).reshape(2, 1, 1, 8, width)
-    flat = gather_ring(mine, "y", 4, 2)
-    flat = gather_ring(after(flat, partials), ("xh", "xp"), 4, 1).reshape(2, 128, width)
     flat = jnp.concatenate([flat, other_core(flat)], axis=1)
-    units_all = jnp.concatenate([hidden[:, 0], other_core(hidden[:, 1])], axis=2)
-    units_all = gather_ring(after(units_all, partials)[:, None], "z2", 2, 1)
-    units_all = gather_ring(units_all[:, :, None], "z1", 2, 2)
-    units_all = gather_ring(after(units_all, arrived)[:, :, :, None], "zp", 2, 3)
-    units_all = units_all.reshape(2, 8 * units, 256)
+    lines = lax.dynamic_slice_in_dim(shared, member[0] // 2 * 2, 2, 0)[None, None]
+    lines = gather_ring(after(lines, partials), "z2", 2, 0)
+    lines = gather_ring(lines, "z1", 2, 1)
+    lines = after(lines, arrived).transpose(4, 3, 0, 1, 2, 5, 6).reshape(2, 2, 8 * units, 128)
+    units_all = jnp.concatenate([lines[0], other_core(lines[1])], axis=2)
     down_grad = dot(units_all[0], flat[1], 1, 0).astype(BF16)
     up_grad = dot(flat[0], units_all[1], 0, 1).astype(BF16)
     return (ends[0], ends[1], up_grad, down_grad)

time: 265 us -> 194 us (0.73)
  Pallas kernels: 80.8 us -> 7.68 us
  blocking collectives: 33.6 us -> 20.6 us
  local copies, waits for them, and re-layouts: 19 us -> 30.7 us
  starting transfers between devices: 81.9 us -> 91.3 us
  waiting for transfers between devices: 38 us -> 34.4 us
    pallas_call x1, Pallas kernels: 72.7 us -> 0.97 us  [cut(): pl.pallas_call(cut_kernel, out_shape=[piece] * 4, in_specs=[pl.BlockSpec(...]
    ppermute x18 -> x17, waiting for transfers between devices: 37.1 us -> 20.1 us  [partner(): return lax.ppermute(value, axes, [(at, at ^ step) for at in range(count)])]
    all_to_all x5 -> x4, waiting for transfers between devices: 0.82 us -> 14.3 us  [exchange(): return lax.all_to_all(value, axes, split_axis=0, concat_axis=0, tiled=True)]
    all_to_all x1 -> x2, blocking collectives: 33.6 us -> 20.6 us  [exchange(): return lax.all_to_all(value, axes, split_axis=0, concat_axis=0, tiled=True)]
    all_to_all x5 -> x4, starting transfers between devices: 30.8 us -> 41.4 us  [exchange(): return lax.all_to_all(value, axes, split_axis=0, concat_axis=0, tiled=True)]
    unnamed x15 -> x22, local copies, waits for them, and re-layouts: 4.36 us -> 9.95 us
    dynamic_update_slice x14 -> x12, local copies, waits for them, and re-layouts: 6.8 us -> 9.59 us  [gather_ring(): whole = lax.dynamic_update_slice(whole, block, tuple(start))]
    ppermute x18 -> x17, starting transfers between devices: 51.2 us -> 49.9 us  [partner(): return lax.ppermute(value, axes, [(at, at ^ step) for at in range(count)])]
  transfers between devices with their start and end apart: 23 -> 21, of which waited for: 8 -> 8; matrix products, arithmetic and copies ran while one was open for 7% -> 13% of each run, Pallas kernels for 30% -> 1%
where the time goes in v3:
time: 194 us; the launch traced here: 192 us
  starting transfers between devices  91.3 us (47%)
  waiting for transfers between devices  34.4 us (18%)
  local copies, waits for them, and re-layouts  30.7 us (16%)
  blocking collectives  20.6 us (11%)
  Pallas kernels  7.68 us (4%)
  matrix products  5.11 us (3%)
    ppermute x17, starting transfers between devices, partner(): return lax.ppermute(value, axes, [(at, at ^ step) for at in range(count)])  49.9 us
    all_to_all x4, starting transfers between devices, exchange(): return lax.all_to_all(value, axes, split_axis=0, concat_axis=0, tiled=True)  41.4 us
    all_to_all x2, blocking collectives, exchange(): return lax.all_to_all(value, axes, split_axis=0, concat_axis=0, tiled=True)  20.6 us
    ppermute x17, waiting for transfers between devices, partner(): return lax.ppermute(value, axes, [(at, at ^ step) for at in range(count)])  20.1 us
    all_to_all x4, waiting for transfers between devices, exchange(): return lax.all_to_all(value, axes, split_axis=0, concat_axis=0, tiled=True)  14.3 us
    unnamed x22, local copies, waits for them, and re-layouts  9.95 us
    dynamic_update_slice x12, local copies, waits for them, and re-layouts, gather_ring(): whole = lax.dynamic_update_slice(whole, block, tuple(start))  9.59 us
    dot_general x2, matrix products, dot(): lax.dot_general(left, right, (((left_dim,), (right_dim,)), ((), ())), pre...  5.11 us
  transfers between devices with their start and end apart: 21, of which 8 were waited for; matrix products, arithmetic and copies ran while one was open for 13% of the time, Pallas kernels for 1%

profile of v3, /device:TPU:6, one launch (start us, length us, event | category | flops | bytes accessed | tf_op | source)
XLA Modules:
  0.0 192.0 jit_solution(4348973239698260866)
XLA Ops:
  2.1 15.1 %all-to-all-start = ((bf16[8,8,1536]{2,1,0:T(8,128)(2,1)}), bf16[8,8,1536]{2,1,0:T(8,128)(2,1)}, u32[]{:S(2)}, u32[]{:S(2)}) async-start(bf16[8,8,1536]{2,1,0:T(8,128)(2,1)} %broadcast_in_dim.30), calls=%async_computation | async-start | bytes 393216 | tf_op jit(solution)/shard_map/all_to_all | solution.py:27
  20.7 2.9 %collective-permute-start.6 = (bf16[2,48,3072]{2,1,0:T(8,128)(2,1)}, bf16[2,48,3072]{2,1,0:T(8,128)(2,1)S(1)}, u32[]{:S(2)}, u32[]{:S(2)}) collective-permute-start(bf16[2,48,3072]{2,1,0:T(8,128)(2,1)} %get-tuple-element.35), channel_id=1, source_target_pairs={{0,1},{1,0},{128,129},{129,128},{2,3},{3,2},{130,131},{131,130},{4... | collective-permute-start | bytes 1769480 | tf_op jit(solution)/shard_map/ppermute | solution.py:35
  23.6 2.7 %collective-permute-start.7 = (bf16[2,48,3072]{2,1,0:T(8,128)(2,1)S(1)}, bf16[2,48,3072]{2,1,0:T(8,128)(2,1)S(1)}, u32[]{:S(2)}, u32[]{:S(2)}) collective-permute-start(bf16[2,48,3072]{2,1,0:T(8,128)(2,1)S(1)} %get-tuple-element.36), channel_id=1, source_target_pairs={{0,128},{1,129},{128,0},{129,1},{2,130},{3,131},{130,2},{131,3},{4... | collective-permute-start | bytes 1769480 | tf_op jit(solution)/shard_map/ppermute | solution.py:35
  26.3 3.5 %collective-permute-start.8 = (bf16[2,48,3072]{2,1,0:T(8,128)(2,1)S(1)}, bf16[2,48,3072]{2,1,0:T(8,128)(2,1)S(1)}, u32[]{:S(2)}, u32[]{:S(2)}) collective-permute-start(bf16[2,48,3072]{2,1,0:T(8,128)(2,1)S(1)} %get-tuple-element.37), channel_id=1, source_target_pairs={{0,129},{1,128},{128,1},{129,0},{2,131},{3,130},{130,3},{131,2},{4... | collective-permute-start | bytes 1769480 | tf_op jit(solution)/shard_map/ppermute | solution.py:35
  29.9 6.4 %all-to-all-done = bf16[8,8,1536]{2,1,0:T(8,128)(2,1)} async-done(((bf16[8,8,1536]{2,1,0:T(8,128)(2,1)}), bf16[8,8,1536]{2,1,0:T(8,128)(2,1)}, u32[]{:S(2)}, u32[]{:S(2)}) %all-to-all-start) | async-done | bytes 196640 | tf_op jit(solution)/shard_map/all_to_all | solution.py:27
  39.4 3.5 %collective-permute-start = (bf16[2,1,1,8,1536]{4,0,3,2,1:T(2,128)(2,1)}, bf16[2,1,1,8,1536]{4,0,3,2,1:T(2,128)(2,1)}, u32[]{:S(2)}, u32[]{:S(2)}) collective-permute-start(bf16[2,1,1,8,1536]{4,0,3,2,1:T(2,128)(2,1)} %bitcast.3), channel_id=1, source_target_pairs={{0,16},{16,0},{32,48},{48,32},{1,17},{17,1},{33,49},{49,33},{2,18}... | collective-permute-start | bytes 147464 | tf_op jit(solution)/shard_map/ppermute | solution.py:35
  42.9 4.8 %collective-permute-start.1 = (bf16[2,1,1,8,1536]{4,0,3,2,1:T(2,128)(2,1)}, bf16[2,1,1,8,1536]{4,0,3,2,1:T(2,128)(2,1)}, u32[]{:S(2)}, u32[]{:S(2)}) collective-permute-start(bf16[2,1,1,8,1536]{4,0,3,2,1:T(2,128)(2,1)} %bitcast.3), channel_id=1, source_target_pairs={{0,32},{16,48},{32,0},{48,16},{1,33},{17,49},{33,1},{49,17},{2,34}... | collective-permute-start | bytes 147464 | tf_op jit(solution)/shard_map/ppermute | solution.py:35
  54.4 7.8 %all-to-all-start.1 = ((bf16[16,2,2,8,1536]{4,3,2,1,0:T(8,128)(2,1)}), bf16[16,2,2,8,1536]{4,3,2,1,0:T(8,128)(2,1)}, u32[]{:S(2)}, u32[]{:S(2)}) async-start(bf16[16,2,2,8,1536]{4,3,2,1,0:T(8,128)(2,1)} %bitcast.38), calls=%async_computation.1 | async-start | bytes 3145728 | tf_op jit(solution)/shard_map/all_to_all | solution.py:27
  68.6 2.8 %collective-permute-start.3 = (bf16[2,1,4,8,1536]{4,3,2,1,0:T(8,128)(2,1)}, bf16[2,1,4,8,1536]{4,3,2,1,0:T(8,128)(2,1)}, u32[]{:S(2)}, u32[]{:S(2)}) collective-permute-start(bf16[2,1,4,8,1536]{4,3,2,1,0:T(8,128)(2,1)} %copy_dynamic-update-slice_fusion.2), channel_id=1, source_target_pairs={{0,128},{128,0},{256,384},{384,256},{1,129},{129,1},{257,385},{385... | collective-permute-start | bytes 589832 | tf_op jit(solution)/shard_map/ppermute | solution.py:35
  71.4 2.7 %collective-permute-start.4 = (bf16[2,1,4,8,1536]{4,3,2,1,0:T(8,128)(2,1)}, bf16[2,1,4,8,1536]{4,3,2,1,0:T(8,128)(2,1)}, u32[]{:S(2)}, u32[]{:S(2)}) collective-permute-start(bf16[2,1,4,8,1536]{4,3,2,1,0:T(8,128)(2,1)} %copy_dynamic-update-slice_fusion.2), channel_id=1, source_target_pairs={{0,256},{128,384},{256,0},{384,128},{1,257},{129,385},{257,1},{385... | collective-permute-start | bytes 589832 | tf_op jit(solution)/shard_map/ppermute | solution.py:35
  74.0 5.0 %collective-permute-start.5 = (bf16[2,1,4,8,1536]{4,3,2,1,0:T(8,128)(2,1)}, bf16[2,1,4,8,1536]{4,3,2,1,0:T(8,128)(2,1)}, u32[]{:S(2)}, u32[]{:S(2)}) collective-permute-start(bf16[2,1,4,8,1536]{4,3,2,1,0:T(8,128)(2,1)} %copy_dynamic-update-slice_fusion.2), channel_id=1, source_target_pairs={{0,384},{128,256},{256,128},{384,0},{1,385},{129,257},{257,129},{3... | collective-permute-start | bytes 589832 | tf_op jit(solution)/shard_map/ppermute | solution.py:35
  81.0 2.4 %collective-permute-start.10 = (bf16[2,48,3072]{2,1,0:T(8,128)(2,1)S(1)}, bf16[2,48,3072]{2,1,0:T(8,128)(2,1)S(1)}, u32[]{:S(2)}, u32[]{:S(2)}) collective-permute-start(bf16[2,48,3072]{2,1,0:T(8,128)(2,1)S(1)} %collective-permute-done.6.refs_1_), channel_id=1, source_target_pairs={{0,8},{8,0},{1,9},{9,1},{2,10},{10,2},{3,11},{11,3},{4,12},{12,4},... | collective-permute-start | bytes 1769480 | tf_op jit(solution)/shard_map/ppermute | solution.py:35
  83.4 2.6 %collective-permute-done.3 = bf16[2,1,4,8,1536]{4,3,2,1,0:T(8,128)(2,1)} collective-permute-done((bf16[2,1,4,8,1536]{4,3,2,1,0:T(8,128)(2,1)}, bf16[2,1,4,8,1536]{4,3,2,1,0:T(8,128)(2,1)}, u32[]{:S(2)}, u32[]{:S(2)}) %collective-permute-start.3) | collective-permute-done | bytes 196640 | tf_op jit(solution)/shard_map/ppermute | solution.py:35
  99.2 2.8 %hidden_parts.1 = f32[4,2,2,48,128]{4,3,2,1,0:T(8,128)S(1)} custom-call(s32[1]{0:T(128)} %bitcast.member_ref, bf16[16,2,2,8,1536]{4,3,2,1,0:T(8,128)(2,1)} %all-to-all-done.1.rows_ref, bf16[2,48,3072]{2,1,0:T(8,128)(2,1)S(1)} %get-tuple-element.34.refs_0_, bf16[2,48,3072]{2,1,0:T(8,128)(2,1)S(1)} %collective-permute-done.6.refs_1_, ...), custom_call_target="tpu_custom_call" | custom-call | flops 604000000 | bytes 6700000 | tf_op jit(solution)/shard_map/hidden_parts/pallas_call | solution.py:109
  102.0 11.9 %all_to_all.30.parts_ref = f32[4,2,2,48,128]{4,3,2,1,0:T(8,128)} all-to-all(f32[4,2,2,48,128]{4,3,2,1,0:T(8,128)S(1)} %hidden_parts.1), channel_id=1, replica_groups=mesh['xh'=2,'xp'=2,'zh'=2,'y'=4,'c'=2,'z2'=2,'z1'=2,'zp'=2] {'xp','zp'}, dimensions={0} | all-to-all | bytes 786432 | tf_op jit(solution)/shard_map/all_to_all | solution.py:27
  115.6 8.7 %all_to_all.31.shared_ref = bf16[4,2,2,48,128]{4,3,2,1,0:T(8,128)(2,1)S(1)} all-to-all(bf16[4,2,2,48,128]{4,3,2,1,0:T(8,128)(2,1)} %get-tuple-element.39), channel_id=1, replica_groups=mesh['xh'=2,'xp'=2,'zh'=2,'y'=4,'c'=2,'z2'=2,'z1'=2,'zp'=2] {'xp','zp'}, dimensions={0} | all-to-all | bytes 393216 | tf_op jit(solution)/shard_map/all_to_all | solution.py:27
  129.3 7.8 %all-to-all-start.4 = ((bf16[16,2,8,3072]{3,2,1,0:T(8,128)(2,1)}), bf16[16,2,8,3072]{3,2,1,0:T(8,128)(2,1)S(1)}, u32[]{:S(2)}, u32[]{:S(2)}) async-start(bf16[16,2,8,3072]{3,2,1,0:T(8,128)(2,1)} %output_parts.1), calls=%async_computation.4 | async-start | bytes 3145728 | tf_op jit(solution)/shard_map/all_to_all | solution.py:27
  138.1 6.0 %collective-permute-start.14 = (bf16[1,1,2,2,2,48,128]{6,5,4,3,2,1,0:T(8,128)(2,1)S(1)}, bf16[1,1,2,2,2,48,128]{6,5,4,3,2,1,0:T(8,128)(2,1)S(1)}, u32[]{:S(2)}, u32[]{:S(2)}) collective-permute-start(bf16[1,1,2,2,2,48,128]{6,5,4,3,2,1,0:T(8,128)(2,1)S(1)} %dynamic-slice_bitcast_fusion), channel_id=1, source_target_pairs={{0,4},{4,0},{1,5},{5,1},{2,6},{6,2},{3,7},{7,3},{8,12},{12,8},{9,1... | collective-permute-start | bytes 294920 | tf_op jit(solution)/shard_map/ppermute | solution.py:35
  144.1 8.2 %collective-permute-done.14 = bf16[1,1,2,2,2,48,128]{6,5,4,3,2,1,0:T(8,128)(2,1)S(1)} collective-permute-done((bf16[1,1,2,2,2,48,128]{6,5,4,3,2,1,0:T(8,128)(2,1)S(1)}, bf16[1,1,2,2,2,48,128]{6,5,4,3,2,1,0:T(8,128)(2,1)S(1)}, u32[]{:S(2)}, u32[]{:S(2)}) %collective-permute-start.14) | collective-permute-done | bytes 98336 | tf_op jit(solution)/shard_map/ppermute | solution.py:35
  156.2 6.7 %collective-permute-done.15 = bf16[2,1,2,2,2,48,128]{6,5,2,1,0,3,4:T(8,128)(2,1)S(1)} collective-permute-done((bf16[2,1,2,2,2,48,128]{6,5,2,1,0,3,4:T(8,128)(2,1)S(1)}, bf16[2,1,2,2,2,48,128]{6,5,2,1,0,3,4:T(8,128)(2,1)S(1)}, u32[]{:S(2)}, u32[]{:S(2)}) %collective-permute-start.15) | collective-permute-done | bytes 196640 | tf_op jit(solution)/shard_map/ppermute | solution.py:35
  164.2 10.7 %all-to-all-start.5 = ((bf16[8,2,4,1536]{3,2,1,0:T(4,128)(2,1)}), bf16[8,2,4,1536]{3,2,1,0:T(4,128)(2,1)S(1)}, u32[]{:S(2)}, u32[]{:S(2)}) async-start(bf16[8,2,4,1536]{3,2,1,0:T(4,128)(2,1)} %bitcast.11), calls=%async_computation.5 | async-start | bytes 393216 | tf_op jit(solution)/shard_map/all_to_all | solution.py:27
  178.3 2.5 %convolution_convert_fusion = bf16[384,1536]{1,0:T(8,128)(2,1)} fusion(bf16[2,128,1536]{2,1,0:T(8,128)(2,1)} %collective-permute-done.13, bf16[2,128,1536]{2,1,0:T(8,128)(2,1)S(1)} %bitcast.41, bf16[2,384,128]{2,1,0:T(8,128)(2,1)S(1)} %collective-permute-done.16, bf16[2,384,128]{2,1,0:T(8,128)(2,1)S(1)} %bitcast.44), kind=kOutput, calls=%fused_computation | convolution fusion | flops 304545792 | bytes 3145728 | tf_op jit(solution)/shard_map/dot_general | solution.py:60
  180.8 2.6 %convolution_convert_fusion.1 = bf16[1536,384]{1,0:T(8,128)(2,1)} fusion(bf16[2,128,1536]{2,1,0:T(8,128)(2,1)S(1)} %bitcast.42, bf16[2,128,1536]{2,1,0:T(8,128)(2,1)} %collective-permute-done.13, bf16[2,384,128]{2,1,0:T(8,128)(2,1)S(1)} %bitcast.45, bf16[2,384,128]{2,1,0:T(8,128)(2,1)S(1)} %collective-permute-done.16), kind=kOutput, calls=%fused_computation.1 | convolution fusion | flops 304545792 | bytes 3145728 | tf_op jit(solution)/shard_map/dot_general | solution.py:60
  183.4 7.9 %all-to-all-done.5 = bf16[8,2,4,1536]{3,2,1,0:T(4,128)(2,1)S(1)} async-done(((bf16[8,2,4,1536]{3,2,1,0:T(4,128)(2,1)}), bf16[8,2,4,1536]{3,2,1,0:T(4,128)(2,1)S(1)}, u32[]{:S(2)}, u32[]{:S(2)}) %all-to-all-start.5) | async-done | bytes 196640 | tf_op jit(solution)/shard_map/all_to_all | solution.py:27
  (80 shorter events, 53.0 us)
Async XLA Ops:
  2.1 34.2 %all-to-all-start = ((bf16[8,8,1536]{2,1,0:T(8,128)(2,1)}), bf16[8,8,1536]{2,1,0:T(8,128)(2,1)}, u32[]{:S(2)}, u32[]{:S(2)}) async-start(bf16[8,8,1536]{2,1,0:T(8,128)(2,1)} %broadcast_in_dim.30), calls=%async_computation | async-start | bytes 393216 | tf_op jit(solution)/shard_map/all_to_all | solution.py:27
  17.2 1.3 copy-start.7
  18.4 1.3 copy-start.8
  20.7 27.1 %collective-permute-start.6 = (bf16[2,48,3072]{2,1,0:T(8,128)(2,1)}, bf16[2,48,3072]{2,1,0:T(8,128)(2,1)S(1)}, u32[]{:S(2)}, u32[]{:S(2)}) collective-permute-start(bf16[2,48,3072]{2,1,0:T(8,128)(2,1)} %get-tuple-element.35), channel_id=1, source_target_pairs={{0,1},{1,0},{128,129},{129,128},{2,3},{3,2},{130,131},{131,130},{4... | collective-permute-start | bytes 1769480 | tf_op jit(solution)/shard_map/ppermute | solution.py:35
  23.6 29.1 %collective-permute-start.7 = (bf16[2,48,3072]{2,1,0:T(8,128)(2,1)S(1)}, bf16[2,48,3072]{2,1,0:T(8,128)(2,1)S(1)}, u32[]{:S(2)}, u32[]{:S(2)}) collective-permute-start(bf16[2,48,3072]{2,1,0:T(8,128)(2,1)S(1)} %get-tuple-element.36), channel_id=1, source_target_pairs={{0,128},{1,129},{128,0},{129,1},{2,130},{3,131},{130,2},{131,3},{4... | collective-permute-start | bytes 1769480 | tf_op jit(solution)/shard_map/ppermute | solution.py:35
  26.3 26.7 %collective-permute-start.8 = (bf16[2,48,3072]{2,1,0:T(8,128)(2,1)S(1)}, bf16[2,48,3072]{2,1,0:T(8,128)(2,1)S(1)}, u32[]{:S(2)}, u32[]{:S(2)}) collective-permute-start(bf16[2,48,3072]{2,1,0:T(8,128)(2,1)S(1)} %get-tuple-element.37), channel_id=1, source_target_pairs={{0,129},{1,128},{128,1},{129,0},{2,131},{3,130},{130,3},{131,2},{4... | collective-permute-start | bytes 1769480 | tf_op jit(solution)/shard_map/ppermute | solution.py:35
  39.4 22.8 %collective-permute-start = (bf16[2,1,1,8,1536]{4,0,3,2,1:T(2,128)(2,1)}, bf16[2,1,1,8,1536]{4,0,3,2,1:T(2,128)(2,1)}, u32[]{:S(2)}, u32[]{:S(2)}) collective-permute-start(bf16[2,1,1,8,1536]{4,0,3,2,1:T(2,128)(2,1)} %bitcast.3), channel_id=1, source_target_pairs={{0,16},{16,0},{32,48},{48,32},{1,17},{17,1},{33,49},{49,33},{2,18}... | collective-permute-start | bytes 147464 | tf_op jit(solution)/shard_map/ppermute | solution.py:35
  42.9 19.3 %collective-permute-start.1 = (bf16[2,1,1,8,1536]{4,0,3,2,1:T(2,128)(2,1)}, bf16[2,1,1,8,1536]{4,0,3,2,1:T(2,128)(2,1)}, u32[]{:S(2)}, u32[]{:S(2)}) collective-permute-start(bf16[2,1,1,8,1536]{4,0,3,2,1:T(2,128)(2,1)} %bitcast.3), channel_id=1, source_target_pairs={{0,32},{16,48},{32,0},{48,16},{1,33},{17,49},{33,1},{49,17},{2,34}... | collective-permute-start | bytes 147464 | tf_op jit(solution)/shard_map/ppermute | solution.py:35
  47.7 14.5 %collective-permute-start.2 = (bf16[2,1,1,8,1536]{4,0,3,2,1:T(2,128)(2,1)}, bf16[2,1,1,8,1536]{4,0,3,2,1:T(2,128)(2,1)}, u32[]{:S(2)}, u32[]{:S(2)}) collective-permute-start(bf16[2,1,1,8,1536]{4,0,3,2,1:T(2,128)(2,1)} %bitcast.3), channel_id=1, source_target_pairs={{0,48},{16,32},{32,16},{48,0},{1,49},{17,33},{33,17},{49,1},{2,50}... | collective-permute-start | bytes 147464 | tf_op jit(solution)/shard_map/ppermute | solution.py:35
  54.4 42.7 %all-to-all-start.1 = ((bf16[16,2,2,8,1536]{4,3,2,1,0:T(8,128)(2,1)}), bf16[16,2,2,8,1536]{4,3,2,1,0:T(8,128)(2,1)}, u32[]{:S(2)}, u32[]{:S(2)}) async-start(bf16[16,2,2,8,1536]{4,3,2,1,0:T(8,128)(2,1)} %bitcast.38), calls=%async_computation.1 | async-start | bytes 3145728 | tf_op jit(solution)/shard_map/all_to_all | solution.py:27
  68.6 17.4 %collective-permute-start.3 = (bf16[2,1,4,8,1536]{4,3,2,1,0:T(8,128)(2,1)}, bf16[2,1,4,8,1536]{4,3,2,1,0:T(8,128)(2,1)}, u32[]{:S(2)}, u32[]{:S(2)}) collective-permute-start(bf16[2,1,4,8,1536]{4,3,2,1,0:T(8,128)(2,1)} %copy_dynamic-update-slice_fusion.2), channel_id=1, source_target_pairs={{0,128},{128,0},{256,384},{384,256},{1,129},{129,1},{257,385},{385... | collective-permute-start | bytes 589832 | tf_op jit(solution)/shard_map/ppermute | solution.py:35
  71.4 17.4 %collective-permute-start.4 = (bf16[2,1,4,8,1536]{4,3,2,1,0:T(8,128)(2,1)}, bf16[2,1,4,8,1536]{4,3,2,1,0:T(8,128)(2,1)}, u32[]{:S(2)}, u32[]{:S(2)}) collective-permute-start(bf16[2,1,4,8,1536]{4,3,2,1,0:T(8,128)(2,1)} %copy_dynamic-update-slice_fusion.2), channel_id=1, source_target_pairs={{0,256},{128,384},{256,0},{384,128},{1,257},{129,385},{257,1},{385... | collective-permute-start | bytes 589832 | tf_op jit(solution)/shard_map/ppermute | solution.py:35
  74.0 16.6 %collective-permute-start.5 = (bf16[2,1,4,8,1536]{4,3,2,1,0:T(8,128)(2,1)}, bf16[2,1,4,8,1536]{4,3,2,1,0:T(8,128)(2,1)}, u32[]{:S(2)}, u32[]{:S(2)}) collective-permute-start(bf16[2,1,4,8,1536]{4,3,2,1,0:T(8,128)(2,1)} %copy_dynamic-update-slice_fusion.2), channel_id=1, source_target_pairs={{0,384},{128,256},{256,128},{384,0},{1,385},{129,257},{257,129},{3... | collective-permute-start | bytes 589832 | tf_op jit(solution)/shard_map/ppermute | solution.py:35
  79.0 15.5 %collective-permute-start.9 = (bf16[2,48,3072]{2,1,0:T(8,128)(2,1)S(1)}, bf16[2,48,3072]{2,1,0:T(8,128)(2,1)S(1)}, u32[]{:S(2)}, u32[]{:S(2)}) collective-permute-start(bf16[2,48,3072]{2,1,0:T(8,128)(2,1)S(1)} %get-tuple-element.34.refs_0_), channel_id=1, source_target_pairs={{0,8},{8,0},{1,9},{9,1},{2,10},{10,2},{3,11},{11,3},{4,12},{12,4},... | collective-permute-start | bytes 1769480 | tf_op jit(solution)/shard_map/ppermute | solution.py:35
  81.0 13.6 %collective-permute-start.10 = (bf16[2,48,3072]{2,1,0:T(8,128)(2,1)S(1)}, bf16[2,48,3072]{2,1,0:T(8,128)(2,1)S(1)}, u32[]{:S(2)}, u32[]{:S(2)}) collective-permute-start(bf16[2,48,3072]{2,1,0:T(8,128)(2,1)S(1)} %collective-permute-done.6.refs_1_), channel_id=1, source_target_pairs={{0,8},{8,0},{1,9},{9,1},{2,10},{10,2},{3,11},{11,3},{4,12},{12,4},... | collective-permute-start | bytes 1769480 | tf_op jit(solution)/shard_map/ppermute | solution.py:35
  86.0 8.6 %collective-permute-start.11 = (bf16[2,48,3072]{2,1,0:T(8,128)(2,1)S(1)}, bf16[2,48,3072]{2,1,0:T(8,128)(2,1)S(1)}, u32[]{:S(2)}, u32[]{:S(2)}) collective-permute-start(bf16[2,48,3072]{2,1,0:T(8,128)(2,1)S(1)} %collective-permute-done.7.refs_2_), channel_id=1, source_target_pairs={{0,8},{8,0},{1,9},{9,1},{2,10},{10,2},{3,11},{11,3},{4,12},{12,4},... | collective-permute-start | bytes 1769480 | tf_op jit(solution)/shard_map/ppermute | solution.py:35
  88.7 7.5 %collective-permute-start.12 = (bf16[2,48,3072]{2,1,0:T(8,128)(2,1)S(1)}, bf16[2,48,3072]{2,1,0:T(8,128)(2,1)S(1)}, u32[]{:S(2)}, u32[]{:S(2)}) collective-permute-start(bf16[2,48,3072]{2,1,0:T(8,128)(2,1)S(1)} %collective-permute-done.8.refs_3_), channel_id=1, source_target_pairs={{0,8},{8,0},{1,9},{9,1},{2,10},{10,2},{3,11},{11,3},{4,12},{12,4},... | collective-permute-start | bytes 1769480 | tf_op jit(solution)/shard_map/ppermute | solution.py:35
  129.3 24.9 %copy-start.10 = (bf16[2,4,4,8,1536]{4,3,2,1,0:T(8,128)(2,1)S(1)}, bf16[2,4,4,8,1536]{4,3,2,1,0:T(8,128)(2,1)}, u32[]{:S(2)}) copy-start(bf16[2,4,4,8,1536]{4,3,2,1,0:T(8,128)(2,1)} %copy-done.9) | copy-start | bytes 2359300
  129.3 33.8 %all-to-all-start.4 = ((bf16[16,2,8,3072]{3,2,1,0:T(8,128)(2,1)}), bf16[16,2,8,3072]{3,2,1,0:T(8,128)(2,1)S(1)}, u32[]{:S(2)}, u32[]{:S(2)}) async-start(bf16[16,2,8,3072]{3,2,1,0:T(8,128)(2,1)} %output_parts.1), calls=%async_computation.4 | async-start | bytes 3145728 | tf_op jit(solution)/shard_map/all_to_all | solution.py:27
  138.1 14.2 %collective-permute-start.14 = (bf16[1,1,2,2,2,48,128]{6,5,4,3,2,1,0:T(8,128)(2,1)S(1)}, bf16[1,1,2,2,2,48,128]{6,5,4,3,2,1,0:T(8,128)(2,1)S(1)}, u32[]{:S(2)}, u32[]{:S(2)}) collective-permute-start(bf16[1,1,2,2,2,48,128]{6,5,4,3,2,1,0:T(8,128)(2,1)S(1)} %dynamic-slice_bitcast_fusion), channel_id=1, source_target_pairs={{0,4},{4,0},{1,5},{5,1},{2,6},{6,2},{3,7},{7,3},{8,12},{12,8},{9,1... | collective-permute-start | bytes 294920 | tf_op jit(solution)/shard_map/ppermute | solution.py:35
  152.3 10.6 %collective-permute-start.15 = (bf16[2,1,2,2,2,48,128]{6,5,2,1,0,3,4:T(8,128)(2,1)S(1)}, bf16[2,1,2,2,2,48,128]{6,5,2,1,0,3,4:T(8,128)(2,1)S(1)}, u32[]{:S(2)}, u32[]{:S(2)}) collective-permute-start(bf16[2,1,2,2,2,48,128]{6,5,2,1,0,3,4:T(8,128)(2,1)S(1)} %copy_dynamic-update-slice_fusion), channel_id=1, source_target_pairs={{0,2},{2,0},{1,3},{3,1},{4,6},{6,4},{5,7},{7,5},{8,10},{10,8},{9,1... | collective-permute-start | bytes 589832 | tf_op jit(solution)/shard_map/ppermute | solution.py:35
  154.3 22.6 %collective-permute-start.13 = (bf16[2,128,1536]{2,1,0:T(8,128)(2,1)S(1)}, bf16[2,128,1536]{2,1,0:T(8,128)(2,1)}, u32[]{:S(2)}, u32[]{:S(2)}) collective-permute-start(bf16[2,128,1536]{2,1,0:T(8,128)(2,1)S(1)} %bitcast.40), channel_id=1, source_target_pairs={{0,8},{8,0},{1,9},{9,1},{2,10},{10,2},{3,11},{11,3},{4,12},{12,4},... | collective-permute-start | bytes 2359304 | tf_op jit(solution)/shard_map/ppermute | solution.py:35
  164.2 27.0 %all-to-all-start.5 = ((bf16[8,2,4,1536]{3,2,1,0:T(4,128)(2,1)}), bf16[8,2,4,1536]{3,2,1,0:T(4,128)(2,1)S(1)}, u32[]{:S(2)}, u32[]{:S(2)}) async-start(bf16[8,2,4,1536]{3,2,1,0:T(4,128)(2,1)} %bitcast.11), calls=%async_computation.5 | async-start | bytes 393216 | tf_op jit(solution)/shard_map/all_to_all | solution.py:27
  175.0 3.3 %collective-permute-start.16 = (bf16[2,384,128]{2,1,0:T(8,128)(2,1)S(1)}, bf16[2,384,128]{2,1,0:T(8,128)(2,1)S(1)}, u32[]{:S(2)}, u32[]{:S(2)}) collective-permute-start(bf16[2,384,128]{2,1,0:T(8,128)(2,1)S(1)} %bitcast.49), channel_id=1, source_target_pairs={{0,8},{8,0},{1,9},{9,1},{2,10},{10,2},{3,11},{11,3},{4,12},{12,4},... | collective-permute-start | bytes 589832 | tf_op jit(solution)/shard_map/ppermute | solution.py:35
  (8 other events, 7.4 us)

commit v4 on v3

--- a/solution.py
+++ b/solution.py
@@ -7,7 +7,7 @@
 
 BF16 = jnp.bfloat16
 F32 = jnp.float32
-VMEM_BYTES = 48 * 1024 * 1024
+VMEM_BYTES = 20 * 1024 * 1024
 
 PLANE = ("xh", "xp", "y")
 COLUMN = ("zh", "z2", "z1")
@@ -83,6 +83,37 @@
         cost_estimate=pl.CostEstimate(flops=0, bytes_accessed=8 * units * features, transcendentals=0),
         name="cut_weights",
     )(member, up_rows, down_rows)
+
+
+def lay_out_kernel(block_ref, column_ref, sent_ref, mine_ref):
+    for far in range(2):
+        for near in range(2):
+            ends = [column_ref[end * 4 + far * 2 + near].astype(F32) for end in range(2)]
+            for array in range(2):
+                rows = jnp.concatenate([end[array * 4 : array * 4 + 4] for end in ends], axis=0).astype(BF16)
+                for half in range(2):
+                    for line in range(4):
+                        sent_ref[half * 8 + near * 4 + line, far, array] = rows
+    ends = [column_ref[end * 4 + block_ref[0]].astype(F32) for end in range(2)]
+    for array in range(2):
+        rows = jnp.concatenate([end[array * 4 : array * 4 + 4] for end in ends], axis=0)
+        mine_ref[array, 0, 0] = rows.astype(BF16)
+
+
+def lay_out(block, column):
+    unused, rows, width = column.shape
+    return pl.pallas_call(
+        lay_out_kernel,
+        out_shape=[
+            jax.ShapeDtypeStruct((16, 2, 2, rows, width), BF16),
+            jax.ShapeDtypeStruct((2, 1, 1, rows, width), BF16),
+        ],
+        in_specs=[pl.BlockSpec(memory_space=pltpu.SMEM), pl.BlockSpec(memory_space=pltpu.VMEM)],
+        out_specs=[pl.BlockSpec(memory_space=pltpu.VMEM)] * 2,
+        compiler_params=pltpu.CompilerParams(vmem_limit_bytes=VMEM_BYTES),
+        cost_estimate=pl.CostEstimate(flops=0, bytes_accessed=2_000_000, transcendentals=0),
+        name="lay_out_rows",
+    )(block, column)
 
 
 def hidden_kernel(member_ref, rows_ref, *refs):
@@ -99,8 +130,10 @@
                 )
                 term = dot(weight, rows[far], 1, 1)
                 total = term if total is None else total + term
+            total = total.astype(BF16)
             for step in range(4):
-                out_ref[member_ref[0] ^ step, kind, core] = total[step * units : (step + 1) * units]
+                for at in range(4):
+                    out_ref[at, member_ref[0] ^ step, kind, core] = total[step * units : (step + 1) * units]
 
 
 def hidden_parts(member, rows, own, beside):
@@ -108,7 +141,7 @@
     tokens = rows.shape[0] * rows.shape[3]
     return pl.pallas_call(
         hidden_kernel,
-        out_shape=jax.ShapeDtypeStruct((4, 2, 2, units, tokens), F32),
+        out_shape=jax.ShapeDtypeStruct((4, 4, 2, 2, units, tokens), BF16),
         in_specs=[pl.BlockSpec(memory_space=pltpu.SMEM)] + [pl.BlockSpec(memory_space=pltpu.VMEM)] * 9,
         out_specs=pl.BlockSpec(memory_space=pltpu.VMEM),
         compiler_params=pltpu.CompilerParams(vmem_limit_bytes=VMEM_BYTES),
@@ -117,59 +150,49 @@
     )(member, rows, *own, *beside)
 
 
-def gelu_kernel(parts_ref, own_ref, spread_ref):
-    pre_act = parts_ref[0, 0] + parts_ref[1, 0] + parts_ref[2, 0] + parts_ref[3, 0]
-    act_grad = parts_ref[0, 1] + parts_ref[1, 1] + parts_ref[2, 1] + parts_ref[3, 1]
-    for kind, value in enumerate((activate(pre_act), gelu_slope(pre_act, act_grad))):
-        value = value.astype(BF16)
-        own_ref[kind] = value
-        for at in range(4):
-            spread_ref[at, kind] = value
-
-
-def gelu_both(parts):
-    shape = parts.shape
-    return pl.pallas_call(
-        gelu_kernel,
-        out_shape=[jax.ShapeDtypeStruct(shape[1:], BF16), jax.ShapeDtypeStruct(shape, BF16)],
-        in_specs=[pl.BlockSpec(memory_space=pltpu.VMEM)],
-        out_specs=[pl.BlockSpec(memory_space=pltpu.VMEM)] * 2,
-        cost_estimate=pl.CostEstimate(flops=1_000_000, bytes_accessed=700_000, transcendentals=12_288),
-        name="gelu_both",
-    )(parts)
-
-
-def output_kernel(member_ref, shared_ref, *refs):
-    own, beside, out_ref = refs[:4], refs[4:8], refs[8]
+def output_kernel(member_ref, parts_ref, *refs):
+    own, beside, out_ref, pair_ref = refs[:4], refs[4:8], refs[8], refs[9]
     features = own[0].shape[2]
     count, unused, rows, unused = out_ref.shape
     step_of = features // 4
+    units = [[], []]
+    for core in range(2):
+        for step in range(4):
+            slot = member_ref[0] ^ step
+            pre_act, act_grad = (
+                sum(parts_ref[source, slot, kind, core].astype(F32) for source in range(4)) for kind in range(2)
+            )
+            values = (activate(pre_act).astype(BF16), gelu_slope(pre_act, act_grad).astype(BF16))
+            for kind in range(2):
+                units[kind].append(values[kind])
+                if step < 2:
+                    pair_ref[core, kind, 0, slot % 2] = values[kind]
     for result in range(2):
-        units = jnp.concatenate(
-            [shared_ref[member_ref[0] ^ step, result, core] for core in range(2) for step in range(4)],
-            axis=0,
-        )
+        left = jnp.concatenate(units[result], axis=0)
         for at in range(4):
             columns = slice(at * step_of, (at + 1) * step_of)
             weight = jnp.concatenate(
                 [piece[1 - result, :, columns] for piece in (*own, *beside)], axis=0
             )
-            total = dot(units, weight, 0, 0)
+            total = dot(left, weight, 0, 0)
             out_ref[:, result, :, columns] = total.astype(BF16).reshape(count, rows, step_of)
 
 
-def output_parts(member, shared, own, beside, count):
+def output_parts(member, parts, own, beside, count):
     features = own[0].shape[2]
-    rows = shared.shape[4] // count
+    units, tokens = parts.shape[4:]
     return pl.pallas_call(
         output_kernel,
-        out_shape=jax.ShapeDtypeStruct((count, 2, rows, features), BF16),
+        out_shape=[
+            jax.ShapeDtypeStruct((count, 2, tokens // count, features), BF16),
+            jax.ShapeDtypeStruct((2, 2, 1, 2, units, tokens), BF16),
+        ],
         in_specs=[pl.BlockSpec(memory_space=pltpu.SMEM)] + [pl.BlockSpec(memory_space=pltpu.VMEM)] * 9,
-        out_specs=pl.BlockSpec(memory_space=pltpu.VMEM),
-        compiler_params=pltpu.CompilerParams(vmem_limit_bytes=VMEM_BYTES),
-        cost_estimate=pl.CostEstimate(flops=604_000_000, bytes_accessed=6_700_000, transcendentals=0),
+        out_specs=[pl.BlockSpec(memory_space=pltpu.VMEM)] * 2,
+        compiler_params=pltpu.CompilerParams(vmem_limit_bytes=VMEM_BYTES),
+        cost_estimate=pl.CostEstimate(flops=604_000_000, bytes_accessed=6_700_000, transcendentals=49_152),
         name="output_parts",
-    )(member, shared, *own, *beside)
+    )(member, parts, *own, *beside)
 
 
 def local(tokens, up_proj, down_proj, out_grad):
@@ -179,26 +202,20 @@
 
     pieces = cut(member, up_proj.T, down_proj)
     own = [pieces[0]] + [partner(pieces[step], GROUP, 4, step) for step in range(1, 4)]
-    beside = [other_core(piece) for piece in own]
-
-    both = jnp.concatenate([tokens, out_grad], axis=0)
-    column = spread(both, COLUMN, 8).reshape(2, 2, 2, 2, 4, width)
-    sent = column.transpose(2, 1, 3, 0, 4, 5).reshape(1, 2, 1, 2, 2, 8, width)
-    sent = jnp.broadcast_to(sent, (2, 2, 4, 2, 2, 8, width)).reshape(16, 2, 2, 8, width)
+    first = other_core(after(pieces[0], *own[1:]))
+    beside = [first] + [other_core(piece) for piece in own[1:]]
+
+    both = after(jnp.concatenate([tokens, out_grad], axis=0), *pieces)
+    column = spread(both, COLUMN, 8)
+    sent, mine = lay_out(lax.axis_index(("z2", "z1")).reshape(1).astype(jnp.int32), column)
     plane = exchange(after(sent, *own), PLANE)
 
-    mine = lax.dynamic_index_in_dim(
-        column.reshape(2, 4, 2, 4, width), lax.axis_index(("z2", "z1")), 1, keepdims=False
-    )
-    mine = mine.transpose(1, 0, 2, 3).reshape(2, 1, 1, 8, width)
-    flat = gather_ring(mine, "y", 4, 2)
-    flat = gather_ring(flat, ("xh", "xp"), 4, 1).reshape(2, 128, width)
-
-    parts = hidden_parts(after(member, flat), plane, own, beside)
-    hidden, shared = gelu_both(exchange(parts, GROUP))
-    shared = exchange(shared, GROUP)
-
-    partials = output_parts(member, shared, own, beside, 16)
+    lines = gather_ring(after(mine, first), "y", 4, 2)
+    parts = hidden_parts(after(member, lines), plane, own, beside)
+    arrived = exchange(parts, GROUP)
+    flat = gather_ring(after(lines, parts), ("xh", "xp"), 4, 1).reshape(2, 128, width)
+
+    partials, pair = output_parts(member, arrived, own, beside, 16)
     arrived = exchange(partials, PLANE)
     summed = jnp.sum(arrived.reshape(2, 2, 4, 2, 8, 2 * width).astype(F32), axis=(0, 2))
     summed = summed.astype(BF16).reshape(2, 2, 2, 4, 2, width)
@@ -206,10 +223,8 @@
     ends = jnp.sum(exchange(summed, COLUMN).astype(F32), axis=0).astype(BF16)
 
     flat = jnp.concatenate([flat, other_core(flat)], axis=1)
-    lines = lax.dynamic_slice_in_dim(shared, member[0] // 2 * 2, 2, 0)[None, None]
-    lines = gather_ring(after(lines, partials), "z2", 2, 0)
-    lines = gather_ring(lines, "z1", 2, 1)
-    lines = after(lines, arrived).transpose(4, 3, 0, 1, 2, 5, 6).reshape(2, 2, 8 * units, 128)
+    lines = gather_ring(pair, ("z2", "z1"), 4, 2)
+    lines = after(lines, arrived).reshape(2, 2, 8 * units, 128)
     units_all = jnp.concatenate([lines[0], other_core(lines[1])], axis=2)
     down_grad = dot(units_all[0], flat[1], 1, 0).astype(BF16)
     up_grad = dot(flat[0], units_all[1], 0, 1).astype(BF16)

time: 194 us -> 184 us (0.948)
  blocking collectives: 20.6 us -> 0 us
  waiting for transfers between devices: 34.4 us -> 50.4 us
  local copies, waits for them, and re-layouts: 30.7 us -> 18 us
  starting transfers between devices: 91.3 us -> 99.4 us
    ppermute x17 -> x18, waiting for transfers between devices: 20.1 us -> 43.1 us  [partner(): return lax.ppermute(value, axes, [(at, at ^ step) for at in range(count)])]
    all_to_all x2 -> x0, blocking collectives: 20.6 us -> none  [exchange(): return lax.all_to_all(value, axes, split_axis=0, concat_axis=0, tiled=True)]
    all_to_all x4 -> x5, waiting for transfers between devices: 14.3 us -> 7.33 us  [exchange(): return lax.all_to_all(value, axes, split_axis=0, concat_axis=0, tiled=True)]
    dynamic_update_slice x12, local copies, waits for them, and re-layouts: 9.59 us -> 2.99 us  [gather_ring(): whole = lax.dynamic_update_slice(whole, block, tuple(start))]
    ppermute x17 -> x18, starting transfers between devices: 49.9 us -> 56.2 us  [partner(): return lax.ppermute(value, axes, [(at, at ^ step) for at in range(count)])]
    unnamed x22 -> x30, local copies, waits for them, and re-layouts: 9.95 us -> 12.7 us
    transpose x3 -> x0, local copies, waits for them, and re-layouts: 2.55 us -> none  [the longest x2 1.48 us: local(): mine = mine.transpose(1, 0, 2, 3).reshape(2, 1, 1, 8, width)]
    broadcast_in_dim x3 -> x0, local copies, waits for them, and re-layouts: 2.26 us -> none  [the longest x2 1.36 us: local(): jnp.broadcast_to(sent, (2, 2, 4, 2, 2, 8, width))]
  transfers between devices with their start and end apart: 21 -> 23, of which waited for: 8 -> 8; matrix products, arithmetic and copies ran while one was open for 13% -> 5% of each run, Pallas kernels for 1% -> 1%
where the time goes in v4:
time: 184 us; the launch traced here: 182 us
  starting transfers between devices  99.4 us (54%)
  waiting for transfers between devices  50.4 us (27%)
  local copies, waits for them, and re-layouts  18 us (10%)
  Pallas kernels  6.96 us (4%)
  matrix products  5.11 us (3%)
    ppermute x18, starting transfers between devices, partner(): return lax.ppermute(value, axes, [(at, at ^ step) for at in range(count)])  56.2 us
    all_to_all x5, starting transfers between devices, exchange(): return lax.all_to_all(value, axes, split_axis=0, concat_axis=0, tiled=True)  43.3 us
    ppermute x18, waiting for transfers between devices, partner(): return lax.ppermute(value, axes, [(at, at ^ step) for at in range(count)])  43.1 us
    unnamed x30, local copies, waits for them, and re-layouts  12.7 us
    all_to_all x5, waiting for transfers between devices, exchange(): return lax.all_to_all(value, axes, split_axis=0, concat_axis=0, tiled=True)  7.33 us
    dot_general x2, matrix products, dot(): lax.dot_general(left, right, (((left_dim,), (right_dim,)), ((), ())), pre...  5.11 us
  transfers between devices with their start and end apart: 23, of which 8 were waited for; matrix products, arithmetic and copies ran while one was open for 5% of the time, Pallas kernels for 1%

profile of v4, /device:TPU:6, one launch (start us, length us, event | category | flops | bytes accessed | tf_op | source)
XLA Modules:
  0.0 182.1 jit_solution(16399958908606058588)
XLA Ops:
  5.6 15.1 %all-to-all-start = ((bf16[8,8,1536]{2,1,0:T(8,128)(2,1)}), bf16[8,8,1536]{2,1,0:T(8,128)(2,1)S(1)}, u32[]{:S(2)}, u32[]{:S(2)}) async-start(bf16[8,8,1536]{2,1,0:T(8,128)(2,1)} %broadcast_in_dim.16), calls=%async_computation | async-start | bytes 393216 | tf_op jit(solution)/shard_map/all_to_all | solution.py:27
  20.7 2.9 %collective-permute-start = (bf16[2,48,3072]{2,1,0:T(8,128)(2,1)}, bf16[2,48,3072]{2,1,0:T(8,128)(2,1)S(1)}, u32[]{:S(2)}, u32[]{:S(2)}) collective-permute-start(bf16[2,48,3072]{2,1,0:T(8,128)(2,1)} %get-tuple-element.32), channel_id=1, source_target_pairs={{0,1},{1,0},{128,129},{129,128},{2,3},{3,2},{130,131},{131,130},{4... | collective-permute-start | bytes 1769480 | tf_op jit(solution)/shard_map/ppermute | solution.py:35
  23.6 2.7 %collective-permute-start.1 = (bf16[2,48,3072]{2,1,0:T(8,128)(2,1)S(1)}, bf16[2,48,3072]{2,1,0:T(8,128)(2,1)S(1)}, u32[]{:S(2)}, u32[]{:S(2)}) collective-permute-start(bf16[2,48,3072]{2,1,0:T(8,128)(2,1)S(1)} %get-tuple-element.33), channel_id=1, source_target_pairs={{0,128},{1,129},{128,0},{129,1},{2,130},{3,131},{130,2},{131,3},{4... | collective-permute-start | bytes 1769480 | tf_op jit(solution)/shard_map/ppermute | solution.py:35
  26.3 3.6 %collective-permute-start.2 = (bf16[2,48,3072]{2,1,0:T(8,128)(2,1)S(1)}, bf16[2,48,3072]{2,1,0:T(8,128)(2,1)}, u32[]{:S(2)}, u32[]{:S(2)}) collective-permute-start(bf16[2,48,3072]{2,1,0:T(8,128)(2,1)S(1)} %get-tuple-element.34), channel_id=1, source_target_pairs={{0,129},{1,128},{128,1},{129,0},{2,131},{3,130},{130,3},{131,2},{4... | collective-permute-start | bytes 1769480 | tf_op jit(solution)/shard_map/ppermute | solution.py:35
  29.9 13.8 %collective-permute-done.refs_1_ = bf16[2,48,3072]{2,1,0:T(8,128)(2,1)S(1)} collective-permute-done((bf16[2,48,3072]{2,1,0:T(8,128)(2,1)}, bf16[2,48,3072]{2,1,0:T(8,128)(2,1)S(1)}, u32[]{:S(2)}, u32[]{:S(2)}) %collective-permute-start) | collective-permute-done | bytes 589856 | tf_op jit(solution)/shard_map/ppermute | solution.py:35
  43.7 12.8 %collective-permute-done.2.refs_3_ = bf16[2,48,3072]{2,1,0:T(8,128)(2,1)} collective-permute-done((bf16[2,48,3072]{2,1,0:T(8,128)(2,1)S(1)}, bf16[2,48,3072]{2,1,0:T(8,128)(2,1)}, u32[]{:S(2)}, u32[]{:S(2)}) %collective-permute-start.2) | collective-permute-done | bytes 589856 | tf_op jit(solution)/shard_map/ppermute | solution.py:35
  59.7 7.8 %all-to-all-start.1 = ((bf16[16,2,2,8,1536]{4,3,2,1,0:T(8,128)(2,1)}), bf16[16,2,2,8,1536]{4,3,2,1,0:T(8,128)(2,1)S(1)}, u32[]{:S(2)}, u32[]{:S(2)}) async-start(bf16[16,2,2,8,1536]{4,3,2,1,0:T(8,128)(2,1)} %copy-done.10), calls=%async_computation.1 | async-start | bytes 3145728 | tf_op jit(solution)/shard_map/all_to_all | solution.py:27
  67.5 3.4 %collective-permute-start.4 = (bf16[2,1,1,8,1536]{4,3,2,1,0:T(8,128)(2,1)S(1)}, bf16[2,1,1,8,1536]{4,3,2,1,0:T(8,128)(2,1)S(1)}, u32[]{:S(2)}, u32[]{:S(2)}) collective-permute-start(bf16[2,1,1,8,1536]{4,3,2,1,0:T(8,128)(2,1)S(1)} %get-tuple-element.39), channel_id=1, source_target_pairs={{0,16},{16,0},{32,48},{48,32},{1,17},{17,1},{33,49},{49,33},{2,18}... | collective-permute-start | bytes 147464 | tf_op jit(solution)/shard_map/ppermute | solution.py:35
  70.9 4.6 %collective-permute-start.5 = (bf16[2,1,1,8,1536]{4,3,2,1,0:T(8,128)(2,1)S(1)}, bf16[2,1,1,8,1536]{4,3,2,1,0:T(8,128)(2,1)S(1)}, u32[]{:S(2)}, u32[]{:S(2)}) collective-permute-start(bf16[2,1,1,8,1536]{4,3,2,1,0:T(8,128)(2,1)S(1)} %get-tuple-element.39), channel_id=1, source_target_pairs={{0,32},{16,48},{32,0},{48,16},{1,33},{17,49},{33,1},{49,17},{2,34}... | collective-permute-start | bytes 147464 | tf_op jit(solution)/shard_map/ppermute | solution.py:35
  75.5 2.5 %collective-permute-start.6 = (bf16[2,1,1,8,1536]{4,3,2,1,0:T(8,128)(2,1)S(1)}, bf16[2,1,1,8,1536]{4,3,2,1,0:T(8,128)(2,1)S(1)}, u32[]{:S(2)}, u32[]{:S(2)}) collective-permute-start(bf16[2,1,1,8,1536]{4,3,2,1,0:T(8,128)(2,1)S(1)} %get-tuple-element.39), channel_id=1, source_target_pairs={{0,48},{16,32},{32,16},{48,0},{1,49},{17,33},{33,17},{49,1},{2,50}... | collective-permute-start | bytes 147464 | tf_op jit(solution)/shard_map/ppermute | solution.py:35
  79.9 2.4 %collective-permute-start.8 = (bf16[2,48,3072]{2,1,0:T(8,128)(2,1)S(1)}, bf16[2,48,3072]{2,1,0:T(8,128)(2,1)S(1)}, u32[]{:S(2)}, u32[]{:S(2)}) collective-permute-start(bf16[2,48,3072]{2,1,0:T(8,128)(2,1)S(1)} %collective-permute-done.1.refs_2_), channel_id=1, source_target_pairs={{0,8},{8,0},{1,9},{9,1},{2,10},{10,2},{3,11},{11,3},{4,12},{12,4},... | collective-permute-start | bytes 1769480 | tf_op jit(solution)/shard_map/ppermute | solution.py:35
  82.3 6.6 %collective-permute-done.4 = bf16[2,1,1,8,1536]{4,3,2,1,0:T(8,128)(2,1)S(1)} collective-permute-done((bf16[2,1,1,8,1536]{4,3,2,1,0:T(8,128)(2,1)S(1)}, bf16[2,1,1,8,1536]{4,3,2,1,0:T(8,128)(2,1)S(1)}, u32[]{:S(2)}, u32[]{:S(2)}) %collective-permute-start.4) | collective-permute-done | bytes 49184 | tf_op jit(solution)/shard_map/ppermute | solution.py:35
  97.0 3.5 %hidden_parts.1 = bf16[4,4,2,2,48,128]{5,4,3,2,1,0:T(8,128)(2,1)} custom-call(s32[1]{0:T(128)} %bitcast.member_ref, bf16[16,2,2,8,1536]{4,3,2,1,0:T(8,128)(2,1)S(1)} %all-to-all-done.1.rows_ref, bf16[2,48,3072]{2,1,0:T(8,128)(2,1)S(1)} %get-tuple-element.37.refs_0_, bf16[2,48,3072]{2,1,0:T(8,128)(2,1)S(1)} %collective-permute-done.refs_1_, ...), custom_call_target="tpu_custom_call" | custom-call | flops 604000000 | bytes 6700000 | tf_op jit(solution)/shard_map/hidden_parts/pallas_call | solution.py:142
  100.5 4.3 %all-to-all-start.2 = ((bf16[4,4,2,2,48,128]{5,4,3,2,1,0:T(8,128)(2,1)}), bf16[4,4,2,2,48,128]{5,4,3,2,1,0:T(8,128)(2,1)S(1)}, u32[]{:S(2)}, u32[]{:S(2)}) async-start(bf16[4,4,2,2,48,128]{5,4,3,2,1,0:T(8,128)(2,1)} %hidden_parts.1), calls=%async_computation.2 | async-start | bytes 1572864 | tf_op jit(solution)/shard_map/all_to_all | solution.py:27
  106.8 2.8 %collective-permute-start.11 = (bf16[2,1,4,8,1536]{4,3,2,1,0:T(8,128)(2,1)S(1)}, bf16[2,1,4,8,1536]{4,3,2,1,0:T(8,128)(2,1)}, u32[]{:S(2)}, u32[]{:S(2)}) collective-permute-start(bf16[2,1,4,8,1536]{4,3,2,1,0:T(8,128)(2,1)S(1)} %copy-done.14), channel_id=1, source_target_pairs={{0,256},{128,384},{256,0},{384,128},{1,257},{129,385},{257,1},{385... | collective-permute-start | bytes 589832 | tf_op jit(solution)/shard_map/ppermute | solution.py:35
  109.6 5.7 %collective-permute-start.12 = (bf16[2,1,4,8,1536]{4,3,2,1,0:T(8,128)(2,1)S(1)}, bf16[2,1,4,8,1536]{4,3,2,1,0:T(8,128)(2,1)}, u32[]{:S(2)}, u32[]{:S(2)}) collective-permute-start(bf16[2,1,4,8,1536]{4,3,2,1,0:T(8,128)(2,1)S(1)} %copy-done.14), channel_id=1, source_target_pairs={{0,384},{128,256},{256,128},{384,0},{1,385},{129,257},{257,129},{3... | collective-permute-start | bytes 589832 | tf_op jit(solution)/shard_map/ppermute | solution.py:35
  121.1 6.1 %all-to-all-start.3 = ((bf16[16,2,8,3072]{3,2,1,0:T(8,128)(2,1)}), bf16[16,2,8,3072]{3,2,1,0:T(8,128)(2,1)S(1)}, u32[]{:S(2)}, u32[]{:S(2)}) async-start(bf16[16,2,8,3072]{3,2,1,0:T(8,128)(2,1)} %copy-done.9), calls=%async_computation.3 | async-start | bytes 3145728 | tf_op jit(solution)/shard_map/all_to_all | solution.py:27
  129.2 4.9 %collective-permute-start.14 = (bf16[2,2,1,2,48,128]{5,4,3,2,1,0:T(8,128)(2,1)S(1)}, bf16[2,2,1,2,48,128]{5,4,3,2,1,0:T(8,128)(2,1)S(1)}, u32[]{:S(2)}, u32[]{:S(2)}) collective-permute-start(bf16[2,2,1,2,48,128]{5,4,3,2,1,0:T(8,128)(2,1)S(1)} %get-tuple-element.53), channel_id=1, source_target_pairs={{0,2},{2,0},{4,6},{6,4},{1,3},{3,1},{5,7},{7,5},{8,10},{10,8},{12,... | collective-permute-start | bytes 294920 | tf_op jit(solution)/shard_map/ppermute | solution.py:35
  134.2 7.3 %collective-permute-start.15 = (bf16[2,2,1,2,48,128]{5,4,3,2,1,0:T(8,128)(2,1)S(1)}, bf16[2,2,1,2,48,128]{5,4,3,2,1,0:T(8,128)(2,1)S(1)}, u32[]{:S(2)}, u32[]{:S(2)}) collective-permute-start(bf16[2,2,1,2,48,128]{5,4,3,2,1,0:T(8,128)(2,1)S(1)} %get-tuple-element.53), channel_id=1, source_target_pairs={{0,4},{2,6},{4,0},{6,2},{1,5},{3,7},{5,1},{7,3},{8,12},{10,14},{12... | collective-permute-start | bytes 294920 | tf_op jit(solution)/shard_map/ppermute | solution.py:35
  146.3 8.1 %collective-permute-done.15 = bf16[2,2,1,2,48,128]{5,4,3,2,1,0:T(8,128)(2,1)S(1)} collective-permute-done((bf16[2,2,1,2,48,128]{5,4,3,2,1,0:T(8,128)(2,1)S(1)}, bf16[2,2,1,2,48,128]{5,4,3,2,1,0:T(8,128)(2,1)S(1)}, u32[]{:S(2)}, u32[]{:S(2)}) %collective-permute-start.15) | collective-permute-done | bytes 98336 | tf_op jit(solution)/shard_map/ppermute | solution.py:35
  155.7 10.0 %all-to-all-start.4 = ((bf16[8,2,4,1536]{3,2,1,0:T(4,128)(2,1)}), bf16[8,2,4,1536]{3,2,1,0:T(4,128)(2,1)S(1)}, u32[]{:S(2)}, u32[]{:S(2)}) async-start(bf16[8,2,4,1536]{3,2,1,0:T(4,128)(2,1)} %bitcast.5), calls=%async_computation.4 | async-start | bytes 393216 | tf_op jit(solution)/shard_map/all_to_all | solution.py:27
  169.1 2.5 %convolution_convert_fusion = bf16[384,1536]{1,0:T(8,128)(2,1)} fusion(bf16[2,128,1536]{2,1,0:T(8,128)(2,1)} %collective-permute-done.13, bf16[2,128,1536]{2,1,0:T(8,128)(2,1)S(1)} %bitcast.30, bf16[2,384,128]{2,1,0:T(8,128)(2,1)S(1)} %collective-permute-done.17, bf16[2,384,128]{2,1,0:T(8,128)(2,1)S(1)} %bitcast.32), kind=kOutput, calls=%fused_computation | convolution fusion | flops 304545792 | bytes 3145728 | tf_op jit(solution)/shard_map/dot_general | solution.py:60
  171.5 2.6 %convolution_convert_fusion.1 = bf16[1536,384]{1,0:T(8,128)(2,1)} fusion(bf16[2,128,1536]{2,1,0:T(8,128)(2,1)S(1)} %bitcast.31, bf16[2,128,1536]{2,1,0:T(8,128)(2,1)} %collective-permute-done.13, bf16[2,384,128]{2,1,0:T(8,128)(2,1)S(1)} %bitcast.33, bf16[2,384,128]{2,1,0:T(8,128)(2,1)S(1)} %collective-permute-done.17), kind=kOutput, calls=%fused_computation.1 | convolution fusion | flops 304545792 | bytes 3145728 | tf_op jit(solution)/shard_map/dot_general | solution.py:60
  174.2 7.2 %all-to-all-done.4 = bf16[8,2,4,1536]{3,2,1,0:T(4,128)(2,1)S(1)} async-done(((bf16[8,2,4,1536]{3,2,1,0:T(4,128)(2,1)}), bf16[8,2,4,1536]{3,2,1,0:T(4,128)(2,1)S(1)}, u32[]{:S(2)}, u32[]{:S(2)}) %all-to-all-start.4) | async-done | bytes 196640 | tf_op jit(solution)/shard_map/all_to_all | solution.py:27
  (81 shorter events, 37.9 us)
Async XLA Ops:
  5.6 52.8 %all-to-all-start = ((bf16[8,8,1536]{2,1,0:T(8,128)(2,1)}), bf16[8,8,1536]{2,1,0:T(8,128)(2,1)S(1)}, u32[]{:S(2)}, u32[]{:S(2)}) async-start(bf16[8,8,1536]{2,1,0:T(8,128)(2,1)} %broadcast_in_dim.16), calls=%async_computation | async-start | bytes 393216 | tf_op jit(solution)/shard_map/all_to_all | solution.py:27
  20.7 23.0 %collective-permute-start = (bf16[2,48,3072]{2,1,0:T(8,128)(2,1)}, bf16[2,48,3072]{2,1,0:T(8,128)(2,1)S(1)}, u32[]{:S(2)}, u32[]{:S(2)}) collective-permute-start(bf16[2,48,3072]{2,1,0:T(8,128)(2,1)} %get-tuple-element.32), channel_id=1, source_target_pairs={{0,1},{1,0},{128,129},{129,128},{2,3},{3,2},{130,131},{131,130},{4... | collective-permute-start | bytes 1769480 | tf_op jit(solution)/shard_map/ppermute | solution.py:35
  23.6 20.1 %collective-permute-start.1 = (bf16[2,48,3072]{2,1,0:T(8,128)(2,1)S(1)}, bf16[2,48,3072]{2,1,0:T(8,128)(2,1)S(1)}, u32[]{:S(2)}, u32[]{:S(2)}) collective-permute-start(bf16[2,48,3072]{2,1,0:T(8,128)(2,1)S(1)} %get-tuple-element.33), channel_id=1, source_target_pairs={{0,128},{1,129},{128,0},{129,1},{2,130},{3,131},{130,2},{131,3},{4... | collective-permute-start | bytes 1769480 | tf_op jit(solution)/shard_map/ppermute | solution.py:35
  26.3 30.1 %collective-permute-start.2 = (bf16[2,48,3072]{2,1,0:T(8,128)(2,1)S(1)}, bf16[2,48,3072]{2,1,0:T(8,128)(2,1)}, u32[]{:S(2)}, u32[]{:S(2)}) collective-permute-start(bf16[2,48,3072]{2,1,0:T(8,128)(2,1)S(1)} %get-tuple-element.34), channel_id=1, source_target_pairs={{0,129},{1,128},{128,1},{129,0},{2,131},{3,130},{130,3},{131,2},{4... | collective-permute-start | bytes 1769480 | tf_op jit(solution)/shard_map/ppermute | solution.py:35
  56.5 11.0 %collective-permute-start.3 = (bf16[2,48,3072]{2,1,0:T(8,128)(2,1)S(1)}, bf16[2,48,3072]{2,1,0:T(8,128)(2,1)}, u32[]{:S(2)}, u32[]{:S(2)}) collective-permute-start(bf16[2,48,3072]{2,1,0:T(8,128)(2,1)S(1)} %get-tuple-element.37.refs_0_), channel_id=1, source_target_pairs={{0,8},{8,0},{1,9},{9,1},{2,10},{10,2},{3,11},{11,3},{4,12},{12,4},... | collective-permute-start | bytes 1769480 | tf_op jit(solution)/shard_map/ppermute | solution.py:35
  59.7 34.1 %all-to-all-start.1 = ((bf16[16,2,2,8,1536]{4,3,2,1,0:T(8,128)(2,1)}), bf16[16,2,2,8,1536]{4,3,2,1,0:T(8,128)(2,1)S(1)}, u32[]{:S(2)}, u32[]{:S(2)}) async-start(bf16[16,2,2,8,1536]{4,3,2,1,0:T(8,128)(2,1)} %copy-done.10), calls=%async_computation.1 | async-start | bytes 3145728 | tf_op jit(solution)/shard_map/all_to_all | solution.py:27
  67.5 21.4 %collective-permute-start.4 = (bf16[2,1,1,8,1536]{4,3,2,1,0:T(8,128)(2,1)S(1)}, bf16[2,1,1,8,1536]{4,3,2,1,0:T(8,128)(2,1)S(1)}, u32[]{:S(2)}, u32[]{:S(2)}) collective-permute-start(bf16[2,1,1,8,1536]{4,3,2,1,0:T(8,128)(2,1)S(1)} %get-tuple-element.39), channel_id=1, source_target_pairs={{0,16},{16,0},{32,48},{48,32},{1,17},{17,1},{33,49},{49,33},{2,18}... | collective-permute-start | bytes 147464 | tf_op jit(solution)/shard_map/ppermute | solution.py:35
  70.9 20.0 %collective-permute-start.5 = (bf16[2,1,1,8,1536]{4,3,2,1,0:T(8,128)(2,1)S(1)}, bf16[2,1,1,8,1536]{4,3,2,1,0:T(8,128)(2,1)S(1)}, u32[]{:S(2)}, u32[]{:S(2)}) collective-permute-start(bf16[2,1,1,8,1536]{4,3,2,1,0:T(8,128)(2,1)S(1)} %get-tuple-element.39), channel_id=1, source_target_pairs={{0,32},{16,48},{32,0},{48,16},{1,33},{17,49},{33,1},{49,17},{2,34}... | collective-permute-start | bytes 147464 | tf_op jit(solution)/shard_map/ppermute | solution.py:35
  75.5 15.4 %collective-permute-start.6 = (bf16[2,1,1,8,1536]{4,3,2,1,0:T(8,128)(2,1)S(1)}, bf16[2,1,1,8,1536]{4,3,2,1,0:T(8,128)(2,1)S(1)}, u32[]{:S(2)}, u32[]{:S(2)}) collective-permute-start(bf16[2,1,1,8,1536]{4,3,2,1,0:T(8,128)(2,1)S(1)} %get-tuple-element.39), channel_id=1, source_target_pairs={{0,48},{16,32},{32,16},{48,0},{1,49},{17,33},{33,17},{49,1},{2,50}... | collective-permute-start | bytes 147464 | tf_op jit(solution)/shard_map/ppermute | solution.py:35
  78.0 13.0 %collective-permute-start.7 = (bf16[2,48,3072]{2,1,0:T(8,128)(2,1)S(1)}, bf16[2,48,3072]{2,1,0:T(8,128)(2,1)S(1)}, u32[]{:S(2)}, u32[]{:S(2)}) collective-permute-start(bf16[2,48,3072]{2,1,0:T(8,128)(2,1)S(1)} %collective-permute-done.refs_1_), channel_id=1, source_target_pairs={{0,8},{8,0},{1,9},{9,1},{2,10},{10,2},{3,11},{11,3},{4,12},{12,4},... | collective-permute-start | bytes 1769480 | tf_op jit(solution)/shard_map/ppermute | solution.py:35
  79.9 11.9 %collective-permute-start.8 = (bf16[2,48,3072]{2,1,0:T(8,128)(2,1)S(1)}, bf16[2,48,3072]{2,1,0:T(8,128)(2,1)S(1)}, u32[]{:S(2)}, u32[]{:S(2)}) collective-permute-start(bf16[2,48,3072]{2,1,0:T(8,128)(2,1)S(1)} %collective-permute-done.1.refs_2_), channel_id=1, source_target_pairs={{0,8},{8,0},{1,9},{9,1},{2,10},{10,2},{3,11},{11,3},{4,12},{12,4},... | collective-permute-start | bytes 1769480 | tf_op jit(solution)/shard_map/ppermute | solution.py:35
  88.9 4.1 %collective-permute-start.9 = (bf16[2,48,3072]{2,1,0:T(8,128)(2,1)}, bf16[2,48,3072]{2,1,0:T(8,128)(2,1)S(1)}, u32[]{:S(2)}, u32[]{:S(2)}) collective-permute-start(bf16[2,48,3072]{2,1,0:T(8,128)(2,1)} %collective-permute-done.2.refs_3_), channel_id=1, source_target_pairs={{0,8},{8,0},{1,9},{9,1},{2,10},{10,2},{3,11},{11,3},{4,12},{12,4},... | collective-permute-start | bytes 1769480 | tf_op jit(solution)/shard_map/ppermute | solution.py:35
  100.5 14.9 %copy-start.2 = (bf16[2,48,3072]{2,1,0:T(8,128)(2,1)S(1)}, bf16[2,48,3072]{2,1,0:T(8,128)(2,1)}, u32[]{:S(2)}) copy-start(bf16[2,48,3072]{2,1,0:T(8,128)(2,1)} %copy-done) | copy-start | bytes 1769476
  100.5 14.9 %all-to-all-start.2 = ((bf16[4,4,2,2,48,128]{5,4,3,2,1,0:T(8,128)(2,1)}), bf16[4,4,2,2,48,128]{5,4,3,2,1,0:T(8,128)(2,1)S(1)}, u32[]{:S(2)}, u32[]{:S(2)}) async-start(bf16[4,4,2,2,48,128]{5,4,3,2,1,0:T(8,128)(2,1)} %hidden_parts.1), calls=%async_computation.2 | async-start | bytes 1572864 | tf_op jit(solution)/shard_map/all_to_all | solution.py:27
  104.9 22.4 %collective-permute-start.10 = (bf16[2,1,4,8,1536]{4,3,2,1,0:T(8,128)(2,1)S(1)}, bf16[2,1,4,8,1536]{4,3,2,1,0:T(8,128)(2,1)}, u32[]{:S(2)}, u32[]{:S(2)}) collective-permute-start(bf16[2,1,4,8,1536]{4,3,2,1,0:T(8,128)(2,1)S(1)} %copy-done.14), channel_id=1, source_target_pairs={{0,128},{128,0},{256,384},{384,256},{1,129},{129,1},{257,385},{385... | collective-permute-start | bytes 589832 | tf_op jit(solution)/shard_map/ppermute | solution.py:35
  106.8 20.4 %collective-permute-start.11 = (bf16[2,1,4,8,1536]{4,3,2,1,0:T(8,128)(2,1)S(1)}, bf16[2,1,4,8,1536]{4,3,2,1,0:T(8,128)(2,1)}, u32[]{:S(2)}, u32[]{:S(2)}) collective-permute-start(bf16[2,1,4,8,1536]{4,3,2,1,0:T(8,128)(2,1)S(1)} %copy-done.14), channel_id=1, source_target_pairs={{0,256},{128,384},{256,0},{384,128},{1,257},{129,385},{257,1},{385... | collective-permute-start | bytes 589832 | tf_op jit(solution)/shard_map/ppermute | solution.py:35
  109.6 17.6 %collective-permute-start.12 = (bf16[2,1,4,8,1536]{4,3,2,1,0:T(8,128)(2,1)S(1)}, bf16[2,1,4,8,1536]{4,3,2,1,0:T(8,128)(2,1)}, u32[]{:S(2)}, u32[]{:S(2)}) collective-permute-start(bf16[2,1,4,8,1536]{4,3,2,1,0:T(8,128)(2,1)S(1)} %copy-done.14), channel_id=1, source_target_pairs={{0,384},{128,256},{256,128},{384,0},{1,385},{129,257},{257,129},{3... | collective-permute-start | bytes 589832 | tf_op jit(solution)/shard_map/ppermute | solution.py:35
  121.1 33.5 %all-to-all-start.3 = ((bf16[16,2,8,3072]{3,2,1,0:T(8,128)(2,1)}), bf16[16,2,8,3072]{3,2,1,0:T(8,128)(2,1)S(1)}, u32[]{:S(2)}, u32[]{:S(2)}) async-start(bf16[16,2,8,3072]{3,2,1,0:T(8,128)(2,1)} %copy-done.9), calls=%async_computation.3 | async-start | bytes 3145728 | tf_op jit(solution)/shard_map/all_to_all | solution.py:27
  129.2 17.0 %collective-permute-start.14 = (bf16[2,2,1,2,48,128]{5,4,3,2,1,0:T(8,128)(2,1)S(1)}, bf16[2,2,1,2,48,128]{5,4,3,2,1,0:T(8,128)(2,1)S(1)}, u32[]{:S(2)}, u32[]{:S(2)}) collective-permute-start(bf16[2,2,1,2,48,128]{5,4,3,2,1,0:T(8,128)(2,1)S(1)} %get-tuple-element.53), channel_id=1, source_target_pairs={{0,2},{2,0},{4,6},{6,4},{1,3},{3,1},{5,7},{7,5},{8,10},{10,8},{12,... | collective-permute-start | bytes 294920 | tf_op jit(solution)/shard_map/ppermute | solution.py:35
  134.2 20.2 %collective-permute-start.15 = (bf16[2,2,1,2,48,128]{5,4,3,2,1,0:T(8,128)(2,1)S(1)}, bf16[2,2,1,2,48,128]{5,4,3,2,1,0:T(8,128)(2,1)S(1)}, u32[]{:S(2)}, u32[]{:S(2)}) collective-permute-start(bf16[2,2,1,2,48,128]{5,4,3,2,1,0:T(8,128)(2,1)S(1)} %get-tuple-element.53), channel_id=1, source_target_pairs={{0,4},{2,6},{4,0},{6,2},{1,5},{3,7},{5,1},{7,3},{8,12},{10,14},{12... | collective-permute-start | bytes 294920 | tf_op jit(solution)/shard_map/ppermute | solution.py:35
  141.4 13.0 %collective-permute-start.16 = (bf16[2,2,1,2,48,128]{5,4,3,2,1,0:T(8,128)(2,1)S(1)}, bf16[2,2,1,2,48,128]{5,4,3,2,1,0:T(8,128)(2,1)S(1)}, u32[]{:S(2)}, u32[]{:S(2)}) collective-permute-start(bf16[2,2,1,2,48,128]{5,4,3,2,1,0:T(8,128)(2,1)S(1)} %get-tuple-element.53), channel_id=1, source_target_pairs={{0,6},{2,4},{4,2},{6,0},{1,7},{3,5},{5,3},{7,1},{8,14},{10,12},{12... | collective-permute-start | bytes 294920 | tf_op jit(solution)/shard_map/ppermute | solution.py:35
  144.3 23.3 %collective-permute-start.13 = (bf16[2,128,1536]{2,1,0:T(8,128)(2,1)S(1)}, bf16[2,128,1536]{2,1,0:T(8,128)(2,1)}, u32[]{:S(2)}, u32[]{:S(2)}) collective-permute-start(bf16[2,128,1536]{2,1,0:T(8,128)(2,1)S(1)} %bitcast.29), channel_id=1, source_target_pairs={{0,8},{8,0},{1,9},{9,1},{2,10},{10,2},{3,11},{11,3},{4,12},{12,4},... | collective-permute-start | bytes 2359304 | tf_op jit(solution)/shard_map/ppermute | solution.py:35
  155.7 25.6 %all-to-all-start.4 = ((bf16[8,2,4,1536]{3,2,1,0:T(4,128)(2,1)}), bf16[8,2,4,1536]{3,2,1,0:T(4,128)(2,1)S(1)}, u32[]{:S(2)}, u32[]{:S(2)}) async-start(bf16[8,2,4,1536]{3,2,1,0:T(4,128)(2,1)} %bitcast.5), calls=%async_computation.4 | async-start | bytes 393216 | tf_op jit(solution)/shard_map/all_to_all | solution.py:27
  165.7 3.3 %collective-permute-start.17 = (bf16[2,384,128]{2,1,0:T(8,128)(2,1)S(1)}, bf16[2,384,128]{2,1,0:T(8,128)(2,1)S(1)}, u32[]{:S(2)}, u32[]{:S(2)}) collective-permute-start(bf16[2,384,128]{2,1,0:T(8,128)(2,1)S(1)} %bitcast.35), channel_id=1, source_target_pairs={{0,8},{8,0},{1,9},{9,1},{2,10},{10,2},{3,11},{11,3},{4,12},{12,4},... | collective-permute-start | bytes 589832 | tf_op jit(solution)/shard_map/ppermute | solution.py:35
  (14 other events, 17.9 us)

commit v5 on v4

v5 whole, which is shorter than its diff:
```python
import jax
import jax.numpy as jnp
from jax import lax
from jax.experimental import pallas as pl
from jax.experimental.pallas import tpu as pltpu
from jax.sharding import Mesh, PartitionSpec as P

BF16 = jnp.bfloat16
F32 = jnp.float32
VMEM_BYTES = 60 * 1024 * 1024

PLANE = ("x", "y")
COLUMN = ("zh", "z2")
GROUP = ("m",)


def activate(values):
    return jax.nn.gelu(values, approximate=True)


def gelu_slope(pre_act, cotangent):
    unused, pullback = jax.vjp(activate, pre_act)
    return pullback(cotangent)[0]


def exchange(value, axes):
    return lax.all_to_all(value, axes, split_axis=0, concat_axis=0, tiled=True)


def spread(value, axes, count):
    return exchange(jnp.broadcast_to(value[None], (count,) + value.shape), axes)


def partner(value, axes, count, step):
    return lax.ppermute(value, axes, [(at, at ^ step) for at in range(count)])


def other_core(value):
    return partner(value, "c", 2, 1)


def gather_ring(value, axes, count, dim):
    here = lax.axis_index(axes)
    shape = list(value.shape)
    shape[dim] = count
    start = [0] * len(shape)
    whole = jnp.zeros(shape, value.dtype)
    blocks = [value] + [partner(value, axes, count, step) for step in range(1, count)]
    for step, block in enumerate(lax.optimization_barrier(blocks)):
        start[dim] = here ^ step
        whole = lax.dynamic_update_slice(whole, block, tuple(start))
    return whole


def after(value, *others):
    return lax.optimization_barrier((value,) + others)[0]


def dot(left, right, left_dim, right_dim):
    return lax.dot_general(
        left, right, (((left_dim,), (right_dim,)), ((), ())), preferred_element_type=F32
    )


def cut_kernel(place_ref, up_ref, down_ref, *refs):
    pieces, held_ref, in_sems, out_sems = refs[:7], refs[7], refs[8], refs[9]
    width = held_ref.shape[3] // 2
    arriving = {}
    for kind, source in enumerate((up_ref, down_ref)):
        for step in range(4):
            for far in range(2):
                column = pl.multiple_of((far * 4 + (place_ref[0] ^ step)) * width, width)
                arriving[kind, step, far] = pltpu.make_async_copy(
                    source.at[:, pl.ds(column, width)],
                    held_ref.at[step, kind, :, pl.ds(far * width, width)],
                    in_sems.at[kind * 8 + step * 2 + far],
                )
                arriving[kind, step, far].start()
    leaving = []
    for kind in range(2):
        for step in range(1, 4):
            for far in range(2):
                arriving[kind, step, far].wait()
            at = kind * 3 + step
            leaving.append(pltpu.make_async_copy(held_ref.at[step, kind], pieces[at], out_sems.at[at]))
            leaving[-1].start()
    for kind in range(2):
        for far in range(2):
            arriving[kind, 0, far].wait()
    leaving.append(pltpu.make_async_copy(held_ref.at[0], pieces[0], out_sems.at[0]))
    leaving[-1].start()
    for copy in leaving:
        copy.wait()


def cut(place, up_rows, down_rows):
    units, features = up_rows.shape
    pair = (2, units, features // 4)
    return pl.pallas_call(
        cut_kernel,
        out_shape=[jax.ShapeDtypeStruct(pair, BF16)] + [jax.ShapeDtypeStruct(pair[1:], BF16)] * 6,
        in_specs=[pl.BlockSpec(memory_space=pltpu.SMEM)] + [pl.BlockSpec(memory_space=pltpu.HBM)] * 2,
        out_specs=[pl.BlockSpec(memory_space=pltpu.HBM)] * 7,
        scratch_shapes=[
            pltpu.VMEM((4,) + pair, BF16),
            pltpu.SemaphoreType.DMA((16,)),
            pltpu.SemaphoreType.DMA((7,)),
        ],
        compiler_params=pltpu.CompilerParams(vmem_limit_bytes=VMEM_BYTES),
        cost_estimate=pl.CostEstimate(flops=0, bytes_accessed=16 * units * features, transcendentals=0),
        name="cut_weights",
    )(place, up_rows, down_rows)


def lay_out_kernel(column_ref, sent_ref):
    for far in range(2):
        ends = [column_ref[end * 2 + far].astype(F32) for end in range(2)]
        for array in range(2):
            rows = jnp.concatenate([end[array * 4 : array * 4 + 4] for end in ends], axis=0).astype(BF16)
            for at in range(sent_ref.shape[0]):
                sent_ref[at, far, array] = rows


def lay_out(column, count):
    unused, rows, width = column.shape
    return pl.pallas_call(
        lay_out_kernel,
        out_shape=jax.ShapeDtypeStruct((count, 2, 2, rows, width), BF16),
        in_specs=[pl.BlockSpec(memory_space=pltpu.VMEM)],
        out_specs=pl.BlockSpec(memory_space=pltpu.VMEM),
        compiler_params=pltpu.CompilerParams(vmem_limit_bytes=VMEM_BYTES),
        cost_estimate=pl.CostEstimate(flops=0, bytes_accessed=2_000_000, transcendentals=0),
        name="lay_out_rows",
    )(column)


def fetch(pieces, held_ref, sems):
    units = pieces[0].shape[1]
    copies = [[], []]
    for core in range(2):
        for at, piece in enumerate(pieces[core * 7 : core * 7 + 7]):
            if at == 0:
                target = held_ref.at[:, pl.ds(core * 4 * units, units), :]
            else:
                kind, step = (at - 1) // 3, (at - 1) % 3 + 1
                target = held_ref.at[kind, pl.ds((core * 4 + step) * units, units), :]
            copies[core].append(pltpu.make_async_copy(piece, target, sems.at[core * 7 + at]))
            copies[core][-1].start()
    return copies


def hidden_kernel(place_ref, rows_ref, *refs):
    pieces, (out_ref, mine_ref, held_ref, sems) = refs[:14], refs[14:]
    units = pieces[0].shape[1]
    width = rows_ref.shape[4]
    copies = fetch(pieces, held_ref, sems)
    for kind in range(2):
        mine_ref[kind] = rows_ref[:, place_ref[1], kind].reshape(-1, width)
    for core in range(2):
        for copy in copies[core]:
            copy.wait()
        for kind in range(2):
            total = None
            for far in range(2):
                weight = held_ref[kind, core * 4 * units : (core + 1) * 4 * units, far * width : (far + 1) * width]
                term = dot(weight, rows_ref[:, far, kind].reshape(-1, width), 1, 1)
                total = term if total is None else total + term
            total = total.astype(BF16)
            for step in range(4):
                for at in range(4):
                    out_ref[at, place_ref[0] ^ step, kind, core] = total[step * units : (step + 1) * units]


def hidden_parts(place, rows, own, beside):
    units, features = own[0].shape[1:]
    tokens = rows.shape[0] * rows.shape[3]
    return pl.pallas_call(
        hidden_kernel,
        out_shape=[
            jax.ShapeDtypeStruct((4, 4, 2, 2, units, tokens), BF16),
            jax.ShapeDtypeStruct((2, tokens, features // 2), BF16),
        ],
        in_specs=[pl.BlockSpec(memory_space=pltpu.SMEM), pl.BlockSpec(memory_space=pltpu.VMEM)]
        + [pl.BlockSpec(memory_space=pltpu.HBM)] * 14,
        out_specs=[pl.BlockSpec(memory_space=pltpu.VMEM)] * 2,
        scratch_shapes=[pltpu.VMEM((2, 8 * units, features), BF16), pltpu.SemaphoreType.DMA((14,))],
        compiler_params=pltpu.CompilerParams(vmem_limit_bytes=VMEM_BYTES),
        cost_estimate=pl.CostEstimate(flops=604_000_000, bytes_accessed=6_700_000, transcendentals=0),
        name="hidden_parts",
    )(place, rows, *own, *beside)


def output_kernel(place_ref, parts_ref, *refs):
    pieces, (out_ref, quad_ref, held_ref, sems) = refs[:14], refs[14:]
    features = pieces[0].shape[2]
    count, unused, rows, unused = out_ref.shape
    step_of = features // 4
    copies = fetch(pieces, held_ref, sems)
    units = [[], []]
    for core in range(2):
        for step in range(4):
            slot = place_ref[0] ^ step
            pre_act, act_grad = (
                sum(parts_ref[source, slot, kind, core].astype(F32) for source in range(4)) for kind in range(2)
            )
            values = (activate(pre_act).astype(BF16), gelu_slope(pre_act, act_grad).astype(BF16))
            for kind in range(2):
                units[kind].append(values[kind])
                quad_ref[core, kind, 0, slot] = values[kind]
    for copy in copies[0] + copies[1]:
        copy.wait()
    for result in range(2):
        left = jnp.concatenate(units[result], axis=0)
        for at in range(4):
            columns = slice(at * step_of, (at + 1) * step_of)
            total = dot(left, held_ref[1 - result, :, columns], 0, 0)
            out_ref[:, result, :, columns] = total.astype(BF16).reshape(count, rows, step_of)


def output_parts(place, parts, own, beside, count):
    features = own[0].shape[2]
    units, tokens = parts.shape[4:]
    return pl.pallas_call(
        output_kernel,
        out_shape=[
            jax.ShapeDtypeStruct((count, 2, tokens // count, features), BF16),
            jax.ShapeDtypeStruct((2, 2, 1, 4, units, tokens), BF16),
        ],
        in_specs=[pl.BlockSpec(memory_space=pltpu.SMEM), pl.BlockSpec(memory_space=pltpu.VMEM)]
        + [pl.BlockSpec(memory_space=pltpu.HBM)] * 14,
        out_specs=[pl.BlockSpec(memory_space=pltpu.VMEM)] * 2,
        scratch_shapes=[pltpu.VMEM((2, 8 * units, features), BF16), pltpu.SemaphoreType.DMA((14,))],
        compiler_params=pltpu.CompilerParams(vmem_limit_bytes=VMEM_BYTES),
        cost_estimate=pl.CostEstimate(flops=604_000_000, bytes_accessed=6_700_000, transcendentals=49_152),
        name="output_parts",
    )(place, parts, *own, *beside)


def local(tokens, up_proj, down_proj, out_grad):
    width = tokens.shape[1]
    units = down_proj.shape[0]
    place = jnp.stack([lax.axis_index("m"), lax.axis_index("z2")]).astype(jnp.int32)

    pieces = cut(place, up_proj.T, down_proj)
    first = other_core(pieces[0])
    own = [pieces[0]] + [partner(pieces[at], GROUP, 4, (at - 1) % 3 + 1) for at in range(1, 7)]
    beside = [first] + [other_core(piece) for piece in own[1:]]

    both = after(jnp.concatenate([tokens, out_grad], axis=0), first)
    column = spread(both, COLUMN, 4)
    sent = lay_out(column, 16)
    plane = exchange(after(sent, *own[1:4]), PLANE)

    parts, mine = hidden_parts(place, plane, own, beside)
    arrived = exchange(parts, GROUP)

    partials, quad = output_parts(place, arrived, own, beside, 16)
    arrived = exchange(partials, PLANE)
    summed = jnp.sum(arrived.reshape(16, 2, 2, 4, 2, width).astype(F32), axis=0)
    summed = summed.transpose(1, 3, 0, 2, 4).reshape(4, 2, 4, width)
    ends = jnp.sum(exchange(summed, COLUMN), axis=0).astype(BF16)

    flat = jnp.concatenate([mine, other_core(mine)], axis=1)
    lines = gather_ring(quad, "z2", 2, 2)
    lines = after(lines, arrived).reshape(2, 2, 8 * units, 128)
    units_all = jnp.concatenate([lines[0], other_core(lines[1])], axis=2)
    down_grad = dot(units_all[0], flat[1], 1, 0).astype(BF16)
    up_grad = dot(flat[0], units_all[1], 0, 1).astype(BF16)
    return (ends[0], ends[1], up_grad, down_grad)


def solution(mesh):
    fine = Mesh(mesh.devices.reshape(4, 2, 4, 2, 2, 4), ("x", "zh", "y", "c", "z2", "m"))
    owners = ("x", "zh", "y", "c")
    features = ("z2", "m")
    return jax.shard_map(
        local,
        mesh=fine,
        in_specs=(
            P(owners, features),
            P(None, owners + features),
            P(owners + features, None),
            P(owners, features),
        ),
        out_specs=(
            P(owners, features),
            P(owners, features),
            P(features, owners),
            P(owners, features),
        ),
        check_vma=False,
    )
```

time: 184 us -> 211 us (1.15)
  blocking collectives: 0 us -> 25.7 us
  starting transfers between devices: 99.4 us -> 89.1 us
  Pallas kernels: 6.96 us -> 17.1 us
  waiting for transfers between devices: 50.4 us -> 58.5 us
  local copies, waits for them, and re-layouts: 18 us -> 13.5 us
    all_to_all x0 -> x1, blocking collectives: none -> 25.7 us  [exchange(): return lax.all_to_all(value, axes, split_axis=0, concat_axis=0, tiled=True)]
    all_to_all x5 -> x4, waiting for transfers between devices: 7.33 us -> 17.6 us  [exchange(): return lax.all_to_all(value, axes, split_axis=0, concat_axis=0, tiled=True)]
    unnamed x30 -> x37, local copies, waits for them, and re-layouts: 12.7 us -> 5.27 us
    pallas_call x3, Pallas kernels: 4.6 us -> 11.3 us  [the longest x1 5.58 us: hidden_parts(): pl.pallas_call(hidden_kernel, out_shape=[jax.ShapeDtypeStruct((4, 4, 2, 2...]
    ppermute x18 -> x16, starting transfers between devices: 56.2 us -> 50.2 us  [partner(): return lax.ppermute(value, axes, [(at, at ^ step) for at in range(count)])]
    all_to_all x5 -> x4, starting transfers between devices: 43.3 us -> 39 us  [exchange(): return lax.all_to_all(value, axes, split_axis=0, concat_axis=0, tiled=True)]
    pallas_call x1, Pallas kernels: 2.36 us -> 5.76 us  [output_parts(): pl.pallas_call(output_kernel, out_shape=[jax.ShapeDtypeStruct((count, 2,...]
    ppermute x18 -> x16, waiting for transfers between devices: 43.1 us -> 40.9 us  [partner(): return lax.ppermute(value, axes, [(at, at ^ step) for at in range(count)])]
  transfers between devices with their start and end apart: 23 -> 20, of which waited for: 8 -> 5; matrix products, arithmetic and copies ran while one was open for 5% -> 6% of each run, Pallas kernels for 1% -> 1%
where the time goes in v5:
time: 211 us; the launch traced here: 210 us
  starting transfers between devices  89.1 us (42%)
  waiting for transfers between devices  58.5 us (28%)
  blocking collectives  25.7 us (12%)
  Pallas kernels  17.1 us (8%)
  local copies, waits for them, and re-layouts  13.5 us (6%)
  matrix products  3.12 us (1%)
    ppermute x16, starting transfers between devices, partner(): return lax.ppermute(value, axes, [(at, at ^ step) for at in range(count)])  50.2 us
    ppermute x16, waiting for transfers between devices, partner(): return lax.ppermute(value, axes, [(at, at ^ step) for at in range(count)])  40.9 us
    all_to_all x4, starting transfers between devices, exchange(): return lax.all_to_all(value, axes, split_axis=0, concat_axis=0, tiled=True)  39 us
    all_to_all x1, blocking collectives, exchange(): return lax.all_to_all(value, axes, split_axis=0, concat_axis=0, tiled=True)  25.7 us
    all_to_all x4, waiting for transfers between devices, exchange(): return lax.all_to_all(value, axes, split_axis=0, concat_axis=0, tiled=True)  17.6 us
    pallas_call x1, Pallas kernels, output_parts(): pl.pallas_call(output_kernel, out_shape=[jax.ShapeDtypeStruct((count, 2,...  5.76 us
    pallas_call x1, Pallas kernels, hidden_parts(): pl.pallas_call(hidden_kernel, out_shape=[jax.ShapeDtypeStruct((4, 4, 2, 2...  5.58 us
    unnamed x37, local copies, waits for them, and re-layouts  5.27 us
  transfers between devices with their start and end apart: 20, of which 5 were waited for; matrix products, arithmetic and copies ran while one was open for 6% of the time, Pallas kernels for 1%

profile of v5, /device:TPU:6, one launch (start us, length us, event | category | flops | bytes accessed | tf_op | source)
XLA Modules:
  0.0 209.6 jit_solution(2157173485648038872)
XLA Ops:
  1.3 3.5 %cut_weights.1 = (bf16[2,48,3072]{2,1,0:T(8,128)(2,1)}, bf16[48,3072]{1,0:T(8,128)(2,1)}, bf16[48,3072]{1,0:T(8,128)(2,1)}, bf16[48,3072]{1,0:T(8,128)(2,1)}, bf...) custom-call(s32[2]{0:T(128)} %pad_add_fusion.place_ref, bf16[48,12288]{1,0:T(8,128)(2,1)} %bitcast.25, ...), custom_call_target="tpu_custom_call" | custom-call | bytes 9437184 | tf_op jit(solution)/shard_map/cut_weights/pallas_call | solution.py:99
  6.7 3.8 %collective-permute-start.1 = (bf16[48,3072]{1,0:T(8,128)(2,1)}, bf16[48,3072]{1,0:T(8,128)(2,1)S(1)}, u32[]{:S(2)}, u32[]{:S(2)}) collective-permute-start(bf16[48,3072]{1,0:T(8,128)(2,1)} %get-tuple-element.22), channel_id=1, source_target_pairs={{0,1},{1,0},{2,3},{3,2},{4,5},{5,4},{6,7},{7,6},{8,9},{9,8},{10,11... | collective-permute-start | bytes 884744 | tf_op jit(solution)/shard_map/ppermute | solution.py:35
  11.3 14.2 %all-to-all-start = ((bf16[4,8,1536]{2,1,0:T(8,128)(2,1)}), bf16[4,8,1536]{2,1,0:T(8,128)(2,1)S(1)}, u32[]{:S(2)}, u32[]{:S(2)}) async-start(bf16[4,8,1536]{2,1,0:T(8,128)(2,1)} %broadcast_in_dim.4), calls=%async_computation | async-start | bytes 196608 | tf_op jit(solution)/shard_map/all_to_all | solution.py:27
  25.5 3.4 %collective-permute-start.2 = (bf16[48,3072]{1,0:T(8,128)(2,1)}, bf16[48,3072]{1,0:T(8,128)(2,1)S(1)}, u32[]{:S(2)}, u32[]{:S(2)}) collective-permute-start(bf16[48,3072]{1,0:T(8,128)(2,1)} %get-tuple-element.23), channel_id=1, source_target_pairs={{0,2},{1,3},{2,0},{3,1},{4,6},{5,7},{6,4},{7,5},{8,10},{9,11},{10,... | collective-permute-start | bytes 884744 | tf_op jit(solution)/shard_map/ppermute | solution.py:35
  28.8 3.8 %collective-permute-start.3 = (bf16[48,3072]{1,0:T(8,128)(2,1)}, bf16[48,3072]{1,0:T(8,128)(2,1)S(1)}, u32[]{:S(2)}, u32[]{:S(2)}) collective-permute-start(bf16[48,3072]{1,0:T(8,128)(2,1)} %get-tuple-element.24), channel_id=1, source_target_pairs={{0,3},{1,2},{2,1},{3,0},{4,7},{5,6},{6,5},{7,4},{8,11},{9,10},{10,... | collective-permute-start | bytes 884744 | tf_op jit(solution)/shard_map/ppermute | solution.py:35
  32.6 7.1 %all-to-all-done.column_ref = bf16[4,8,1536]{2,1,0:T(8,128)(2,1)S(1)} async-done(((bf16[4,8,1536]{2,1,0:T(8,128)(2,1)}), bf16[4,8,1536]{2,1,0:T(8,128)(2,1)S(1)}, u32[]{:S(2)}, u32[]{:S(2)}) %all-to-all-start) | async-done | bytes 98336 | tf_op jit(solution)/shard_map/all_to_all | solution.py:27
  40.3 2.2 %lay_out_rows.1 = bf16[16,2,2,8,1536]{4,3,2,1,0:T(8,128)(2,1)} custom-call(bf16[4,8,1536]{2,1,0:T(8,128)(2,1)} %copy-done.14), custom_call_target="tpu_custom_call" | custom-call | bytes 2000000 | tf_op jit(solution)/shard_map/lay_out_rows/pallas_call | solution.py:126
  42.6 10.5 %collective-permute-done.2.refs_2_ = bf16[48,3072]{1,0:T(8,128)(2,1)S(1)} collective-permute-done((bf16[48,3072]{1,0:T(8,128)(2,1)}, bf16[48,3072]{1,0:T(8,128)(2,1)S(1)}, u32[]{:S(2)}, u32[]{:S(2)}) %collective-permute-start.2) | collective-permute-done | bytes 294944 | tf_op jit(solution)/shard_map/ppermute | solution.py:35
  53.1 7.4 %all-to-all-start.1 = ((bf16[16,2,2,8,1536]{4,3,2,1,0:T(8,128)(2,1)}), bf16[16,2,2,8,1536]{4,3,2,1,0:T(8,128)(2,1)S(1)}, u32[]{:S(2)}, u32[]{:S(2)}) async-start(bf16[16,2,2,8,1536]{4,3,2,1,0:T(8,128)(2,1)} %lay_out_rows.1), calls=%async_computation.1 | async-start | bytes 3145728 | tf_op jit(solution)/shard_map/all_to_all | solution.py:27
  60.6 8.2 %collective-permute-start.4 = (bf16[48,3072]{1,0:T(8,128)(2,1)}, bf16[48,3072]{1,0:T(8,128)(2,1)S(1)}, u32[]{:S(2)}, u32[]{:S(2)}) collective-permute-start(bf16[48,3072]{1,0:T(8,128)(2,1)} %get-tuple-element.26), channel_id=1, source_target_pairs={{0,1},{1,0},{2,3},{3,2},{4,5},{5,4},{6,7},{7,6},{8,9},{9,8},{10,11... | collective-permute-start | bytes 884744 | tf_op jit(solution)/shard_map/ppermute | solution.py:35
  68.8 2.4 %collective-permute-start.5 = (bf16[48,3072]{1,0:T(8,128)(2,1)}, bf16[48,3072]{1,0:T(8,128)(2,1)S(1)}, u32[]{:S(2)}, u32[]{:S(2)}) collective-permute-start(bf16[48,3072]{1,0:T(8,128)(2,1)} %get-tuple-element.27), channel_id=1, source_target_pairs={{0,2},{1,3},{2,0},{3,1},{4,6},{5,7},{6,4},{7,5},{8,10},{9,11},{10,... | collective-permute-start | bytes 884744 | tf_op jit(solution)/shard_map/ppermute | solution.py:35
  71.2 3.8 %collective-permute-start.6 = (bf16[48,3072]{1,0:T(8,128)(2,1)}, bf16[48,3072]{1,0:T(8,128)(2,1)S(1)}, u32[]{:S(2)}, u32[]{:S(2)}) collective-permute-start(bf16[48,3072]{1,0:T(8,128)(2,1)} %get-tuple-element.28), channel_id=1, source_target_pairs={{0,3},{1,2},{2,1},{3,0},{4,7},{5,6},{6,5},{7,4},{8,11},{9,10},{10,... | collective-permute-start | bytes 884744 | tf_op jit(solution)/shard_map/ppermute | solution.py:35
  76.9 2.4 %collective-permute-start.8 = (bf16[48,3072]{1,0:T(8,128)(2,1)S(1)}, bf16[48,3072]{1,0:T(8,128)(2,1)S(1)}, u32[]{:S(2)}, u32[]{:S(2)}) collective-permute-start(bf16[48,3072]{1,0:T(8,128)(2,1)S(1)} %collective-permute-done.2.refs_2_), channel_id=1, source_target_pairs={{0,8},{8,0},{1,9},{9,1},{2,10},{10,2},{3,11},{11,3},{4,12},{12,4},... | collective-permute-start | bytes 884744 | tf_op jit(solution)/shard_map/ppermute | solution.py:35
  81.3 12.8 %collective-permute-done.5.refs_5_ = bf16[48,3072]{1,0:T(8,128)(2,1)S(1)} collective-permute-done((bf16[48,3072]{1,0:T(8,128)(2,1)}, bf16[48,3072]{1,0:T(8,128)(2,1)S(1)}, u32[]{:S(2)}, u32[]{:S(2)}) %collective-permute-start.5) | collective-permute-done | bytes 294944 | tf_op jit(solution)/shard_map/ppermute | solution.py:35
  96.0 2.4 %collective-permute-start.11 = (bf16[48,3072]{1,0:T(8,128)(2,1)S(1)}, bf16[48,3072]{1,0:T(8,128)(2,1)S(1)}, u32[]{:S(2)}, u32[]{:S(2)}) collective-permute-start(bf16[48,3072]{1,0:T(8,128)(2,1)S(1)} %collective-permute-done.5.refs_5_), channel_id=1, source_target_pairs={{0,8},{8,0},{1,9},{9,1},{2,10},{10,2},{3,11},{11,3},{4,12},{12,4},... | collective-permute-start | bytes 884744 | tf_op jit(solution)/shard_map/ppermute | solution.py:35
  103.9 5.6 %hidden_parts.1 = (bf16[4,4,2,2,48,128]{5,4,3,2,1,0:T(8,128)(2,1)}, bf16[2,128,1536]{2,1,0:T(8,128)(2,1)}) custom-call(s32[2]{0:T(128)} %pad_add_fusion.place_ref, bf16[16,2,2,8,1536]{4,3,2,1,0:T(8,128)(2,1)} %copy-done, bf16[2,48,3072]{2,1,0:T(8,128)(2,1)} %get-tuple-element.20.refs_0_, bf16[48,3072]{1,0:T(8,128)(2,1)} %copy-done.2, ...), custom_call_target="tpu_custom_call" | custom-call | flops 604000000 | bytes 6700000 | tf_op jit(solution)/shard_map/hidden_parts/pallas_call | solution.py:177
  109.5 25.7 %all_to_all.25.parts_ref = bf16[4,4,2,2,48,128]{5,4,3,2,1,0:T(8,128)(2,1)} all-to-all(bf16[4,4,2,2,48,128]{5,4,3,2,1,0:T(8,128)(2,1)} %get-tuple-element.29), channel_id=1, replica_groups=mesh['x'=4,'zh'=2,'y'=4,'c'=2,'z2'=2,'m'=4] {'m'}, dimensions={0} | all-to-all | bytes 1572864 | tf_op jit(solution)/shard_map/all_to_all | solution.py:27
  135.2 5.8 %output_parts.1 = (bf16[16,2,8,3072]{3,2,1,0:T(8,128)(2,1)}, bf16[2,2,1,4,48,128]{5,4,3,2,1,0:T(8,128)(2,1)}) custom-call(s32[2]{0:T(128)} %pad_add_fusion.place_ref, bf16[4,4,2,2,48,128]{5,4,3,2,1,0:T(8,128)(2,1)} %all_to_all.25.parts_ref, bf16[2,48,3072]{2,1,0:T(8,128)(2,1)} %get-tuple-element.20.refs_0_, bf16[48,3072]{1,0:T(8,128)(2,1)} %copy-done.2, ...), custom_call_target="tpu_custom_call" | custom-call | flops 604000000 | bytes 6700000 | tf_op jit(solution)/shard_map/output_parts/pallas_call | solution.py:223
  141.0 7.4 %all-to-all-start.3 = ((bf16[16,2,8,3072]{3,2,1,0:T(8,128)(2,1)}), bf16[16,2,8,3072]{3,2,1,0:T(8,128)(2,1)S(1)}, u32[]{:S(2)}, u32[]{:S(2)}) async-start(bf16[16,2,8,3072]{3,2,1,0:T(8,128)(2,1)} %get-tuple-element.30), calls=%async_computation.3 | async-start | bytes 3145728 | tf_op jit(solution)/shard_map/all_to_all | solution.py:27
  150.3 6.5 %collective-permute-start.14 = (bf16[2,2,1,4,48,128]{5,4,3,2,1,0:T(8,128)(2,1)S(1)}, bf16[2,2,1,4,48,128]{5,4,3,2,1,0:T(8,128)(2,1)S(1)}, u32[]{:S(2)}, u32[]{:S(2)}) collective-permute-start(bf16[2,2,1,4,48,128]{5,4,3,2,1,0:T(8,128)(2,1)S(1)} %copy-done.15), channel_id=1, source_target_pairs={{0,4},{4,0},{1,5},{5,1},{2,6},{6,2},{3,7},{7,3},{8,12},{12,8},{9,1... | collective-permute-start | bytes 589832 | tf_op jit(solution)/shard_map/ppermute | solution.py:35
  157.9 17.6 %collective-permute-done.14 = bf16[2,2,1,4,48,128]{5,4,3,2,1,0:T(8,128)(2,1)S(1)} collective-permute-done((bf16[2,2,1,4,48,128]{5,4,3,2,1,0:T(8,128)(2,1)S(1)}, bf16[2,2,1,4,48,128]{5,4,3,2,1,0:T(8,128)(2,1)S(1)}, u32[]{:S(2)}, u32[]{:S(2)}) %collective-permute-start.14) | collective-permute-done | bytes 196640 | tf_op jit(solution)/shard_map/ppermute | solution.py:35
  179.5 2.0 collective-permute-start.15
  184.2 10.0 %all-to-all-start.4 = ((f32[4,2,4,1536]{3,2,1,0:T(4,128)}), f32[4,2,4,1536]{3,2,1,0:T(4,128)S(1)}, u32[]{:S(2)}, u32[]{:S(2)}) async-start(f32[4,2,4,1536]{3,2,1,0:T(4,128)} %bitcast.4), calls=%async_computation.4 | async-start | bytes 393216 | tf_op jit(solution)/shard_map/all_to_all | solution.py:27
  198.5 10.5 %all-to-all-done.4 = f32[4,2,4,1536]{3,2,1,0:T(4,128)S(1)} async-done(((f32[4,2,4,1536]{3,2,1,0:T(4,128)}), f32[4,2,4,1536]{3,2,1,0:T(4,128)S(1)}, u32[]{:S(2)}, u32[]{:S(2)}) %all-to-all-start.4) | async-done | bytes 196640 | tf_op jit(solution)/shard_map/all_to_all | solution.py:27
  (73 shorter events, 29.7 us)
Async XLA Ops:
  4.8 5.8 %collective-permute-start = (bf16[2,48,3072]{2,1,0:T(8,128)(2,1)}, bf16[2,48,3072]{2,1,0:T(8,128)(2,1)S(1)}, u32[]{:S(2)}, u32[]{:S(2)}) collective-permute-start(bf16[2,48,3072]{2,1,0:T(8,128)(2,1)} %get-tuple-element.20.refs_0_), channel_id=1, source_target_pairs={{0,8},{8,0},{1,9},{9,1},{2,10},{10,2},{3,11},{11,3},{4,12},{12,4},... | collective-permute-start | bytes 1769480 | tf_op jit(solution)/shard_map/ppermute | solution.py:35
  6.7 35.9 %collective-permute-start.1 = (bf16[48,3072]{1,0:T(8,128)(2,1)}, bf16[48,3072]{1,0:T(8,128)(2,1)S(1)}, u32[]{:S(2)}, u32[]{:S(2)}) collective-permute-start(bf16[48,3072]{1,0:T(8,128)(2,1)} %get-tuple-element.22), channel_id=1, source_target_pairs={{0,1},{1,0},{2,3},{3,2},{4,5},{5,4},{6,7},{7,6},{8,9},{9,8},{10,11... | collective-permute-start | bytes 884744 | tf_op jit(solution)/shard_map/ppermute | solution.py:35
  10.6 42.5 %copy-start.1 = (bf16[2,48,3072]{2,1,0:T(8,128)(2,1)}, bf16[2,48,3072]{2,1,0:T(8,128)(2,1)S(1)}, u32[]{:S(2)}) copy-start(bf16[2,48,3072]{2,1,0:T(8,128)(2,1)S(1)} %collective-permute-done.refs_7_) | copy-start | bytes 1769476
  11.3 28.4 %all-to-all-start = ((bf16[4,8,1536]{2,1,0:T(8,128)(2,1)}), bf16[4,8,1536]{2,1,0:T(8,128)(2,1)S(1)}, u32[]{:S(2)}, u32[]{:S(2)}) async-start(bf16[4,8,1536]{2,1,0:T(8,128)(2,1)} %broadcast_in_dim.4), calls=%async_computation | async-start | bytes 196608 | tf_op jit(solution)/shard_map/all_to_all | solution.py:27
  25.5 27.7 %collective-permute-start.2 = (bf16[48,3072]{1,0:T(8,128)(2,1)}, bf16[48,3072]{1,0:T(8,128)(2,1)S(1)}, u32[]{:S(2)}, u32[]{:S(2)}) collective-permute-start(bf16[48,3072]{1,0:T(8,128)(2,1)} %get-tuple-element.23), channel_id=1, source_target_pairs={{0,2},{1,3},{2,0},{3,1},{4,6},{5,7},{6,4},{7,5},{8,10},{9,11},{10,... | collective-permute-start | bytes 884744 | tf_op jit(solution)/shard_map/ppermute | solution.py:35
  28.8 24.3 %collective-permute-start.3 = (bf16[48,3072]{1,0:T(8,128)(2,1)}, bf16[48,3072]{1,0:T(8,128)(2,1)S(1)}, u32[]{:S(2)}, u32[]{:S(2)}) collective-permute-start(bf16[48,3072]{1,0:T(8,128)(2,1)} %get-tuple-element.24), channel_id=1, source_target_pairs={{0,3},{1,2},{2,1},{3,0},{4,7},{5,6},{6,5},{7,4},{8,11},{9,10},{10,... | collective-permute-start | bytes 884744 | tf_op jit(solution)/shard_map/ppermute | solution.py:35
  42.6 32.4 %copy-start.2 = (bf16[48,3072]{1,0:T(8,128)(2,1)}, bf16[48,3072]{1,0:T(8,128)(2,1)S(1)}, u32[]{:S(2)}) copy-start(bf16[48,3072]{1,0:T(8,128)(2,1)S(1)} %collective-permute-done.1.refs_1_) | copy-start | bytes 884740
  53.1 23.8 %copy-start.3 = (bf16[48,3072]{1,0:T(8,128)(2,1)}, bf16[48,3072]{1,0:T(8,128)(2,1)S(1)}, u32[]{:S(2)}) copy-start(bf16[48,3072]{1,0:T(8,128)(2,1)S(1)} %collective-permute-done.2.refs_2_) | copy-start | bytes 884740
  53.1 26.3 %copy-start.4 = (bf16[48,3072]{1,0:T(8,128)(2,1)}, bf16[48,3072]{1,0:T(8,128)(2,1)S(1)}, u32[]{:S(2)}) copy-start(bf16[48,3072]{1,0:T(8,128)(2,1)S(1)} %collective-permute-done.3.refs_3_) | copy-start | bytes 884740
  53.1 48.9 %all-to-all-start.1 = ((bf16[16,2,2,8,1536]{4,3,2,1,0:T(8,128)(2,1)}), bf16[16,2,2,8,1536]{4,3,2,1,0:T(8,128)(2,1)S(1)}, u32[]{:S(2)}, u32[]{:S(2)}) async-start(bf16[16,2,2,8,1536]{4,3,2,1,0:T(8,128)(2,1)} %lay_out_rows.1), calls=%async_computation.1 | async-start | bytes 3145728 | tf_op jit(solution)/shard_map/all_to_all | solution.py:27
  60.6 18.8 %collective-permute-start.4 = (bf16[48,3072]{1,0:T(8,128)(2,1)}, bf16[48,3072]{1,0:T(8,128)(2,1)S(1)}, u32[]{:S(2)}, u32[]{:S(2)}) collective-permute-start(bf16[48,3072]{1,0:T(8,128)(2,1)} %get-tuple-element.26), channel_id=1, source_target_pairs={{0,1},{1,0},{2,3},{3,2},{4,5},{5,4},{6,7},{7,6},{8,9},{9,8},{10,11... | collective-permute-start | bytes 884744 | tf_op jit(solution)/shard_map/ppermute | solution.py:35
  68.8 25.3 %collective-permute-start.5 = (bf16[48,3072]{1,0:T(8,128)(2,1)}, bf16[48,3072]{1,0:T(8,128)(2,1)S(1)}, u32[]{:S(2)}, u32[]{:S(2)}) collective-permute-start(bf16[48,3072]{1,0:T(8,128)(2,1)} %get-tuple-element.27), channel_id=1, source_target_pairs={{0,2},{1,3},{2,0},{3,1},{4,6},{5,7},{6,4},{7,5},{8,10},{9,11},{10,... | collective-permute-start | bytes 884744 | tf_op jit(solution)/shard_map/ppermute | solution.py:35
  71.2 24.8 %collective-permute-start.6 = (bf16[48,3072]{1,0:T(8,128)(2,1)}, bf16[48,3072]{1,0:T(8,128)(2,1)S(1)}, u32[]{:S(2)}, u32[]{:S(2)}) collective-permute-start(bf16[48,3072]{1,0:T(8,128)(2,1)} %get-tuple-element.28), channel_id=1, source_target_pairs={{0,3},{1,2},{2,1},{3,0},{4,7},{5,6},{6,5},{7,4},{8,11},{9,10},{10,... | collective-permute-start | bytes 884744 | tf_op jit(solution)/shard_map/ppermute | solution.py:35
  75.0 23.4 %collective-permute-start.7 = (bf16[48,3072]{1,0:T(8,128)(2,1)S(1)}, bf16[48,3072]{1,0:T(8,128)(2,1)S(1)}, u32[]{:S(2)}, u32[]{:S(2)}) collective-permute-start(bf16[48,3072]{1,0:T(8,128)(2,1)S(1)} %collective-permute-done.1.refs_1_), channel_id=1, source_target_pairs={{0,8},{8,0},{1,9},{9,1},{2,10},{10,2},{3,11},{11,3},{4,12},{12,4},... | collective-permute-start | bytes 884744 | tf_op jit(solution)/shard_map/ppermute | solution.py:35
  76.9 23.4 %collective-permute-start.8 = (bf16[48,3072]{1,0:T(8,128)(2,1)S(1)}, bf16[48,3072]{1,0:T(8,128)(2,1)S(1)}, u32[]{:S(2)}, u32[]{:S(2)}) collective-permute-start(bf16[48,3072]{1,0:T(8,128)(2,1)S(1)} %collective-permute-done.2.refs_2_), channel_id=1, source_target_pairs={{0,8},{8,0},{1,9},{9,1},{2,10},{10,2},{3,11},{11,3},{4,12},{12,4},... | collective-permute-start | bytes 884744 | tf_op jit(solution)/shard_map/ppermute | solution.py:35
  79.4 21.0 %collective-permute-start.9 = (bf16[48,3072]{1,0:T(8,128)(2,1)S(1)}, bf16[48,3072]{1,0:T(8,128)(2,1)S(1)}, u32[]{:S(2)}, u32[]{:S(2)}) collective-permute-start(bf16[48,3072]{1,0:T(8,128)(2,1)S(1)} %collective-permute-done.3.refs_3_), channel_id=1, source_target_pairs={{0,8},{8,0},{1,9},{9,1},{2,10},{10,2},{3,11},{11,3},{4,12},{12,4},... | collective-permute-start | bytes 884744 | tf_op jit(solution)/shard_map/ppermute | solution.py:35
  94.1 6.3 %collective-permute-start.10 = (bf16[48,3072]{1,0:T(8,128)(2,1)S(1)}, bf16[48,3072]{1,0:T(8,128)(2,1)S(1)}, u32[]{:S(2)}, u32[]{:S(2)}) collective-permute-start(bf16[48,3072]{1,0:T(8,128)(2,1)S(1)} %collective-permute-done.4.refs_4_), channel_id=1, source_target_pairs={{0,8},{8,0},{1,9},{9,1},{2,10},{10,2},{3,11},{11,3},{4,12},{12,4},... | collective-permute-start | bytes 884744 | tf_op jit(solution)/shard_map/ppermute | solution.py:35
  96.0 4.4 %collective-permute-start.11 = (bf16[48,3072]{1,0:T(8,128)(2,1)S(1)}, bf16[48,3072]{1,0:T(8,128)(2,1)S(1)}, u32[]{:S(2)}, u32[]{:S(2)}) collective-permute-start(bf16[48,3072]{1,0:T(8,128)(2,1)S(1)} %collective-permute-done.5.refs_5_), channel_id=1, source_target_pairs={{0,8},{8,0},{1,9},{9,1},{2,10},{10,2},{3,11},{11,3},{4,12},{12,4},... | collective-permute-start | bytes 884744 | tf_op jit(solution)/shard_map/ppermute | solution.py:35
  98.5 3.6 %collective-permute-start.12 = (bf16[48,3072]{1,0:T(8,128)(2,1)S(1)}, bf16[48,3072]{1,0:T(8,128)(2,1)S(1)}, u32[]{:S(2)}, u32[]{:S(2)}) collective-permute-start(bf16[48,3072]{1,0:T(8,128)(2,1)S(1)} %collective-permute-done.6.refs_6_), channel_id=1, source_target_pairs={{0,8},{8,0},{1,9},{9,1},{2,10},{10,2},{3,11},{11,3},{4,12},{12,4},... | collective-permute-start | bytes 884744 | tf_op jit(solution)/shard_map/ppermute | solution.py:35
  141.0 36.8 %all-to-all-start.3 = ((bf16[16,2,8,3072]{3,2,1,0:T(8,128)(2,1)}), bf16[16,2,8,3072]{3,2,1,0:T(8,128)(2,1)S(1)}, u32[]{:S(2)}, u32[]{:S(2)}) async-start(bf16[16,2,8,3072]{3,2,1,0:T(8,128)(2,1)} %get-tuple-element.30), calls=%async_computation.3 | async-start | bytes 3145728 | tf_op jit(solution)/shard_map/all_to_all | solution.py:27
  148.3 45.8 %collective-permute-start.13 = (bf16[2,128,1536]{2,1,0:T(8,128)(2,1)}, bf16[2,128,1536]{2,1,0:T(8,128)(2,1)}, u32[]{:S(2)}, u32[]{:S(2)}) collective-permute-start(bf16[2,128,1536]{2,1,0:T(8,128)(2,1)} %get-tuple-element.31), channel_id=1, source_target_pairs={{0,8},{8,0},{1,9},{9,1},{2,10},{10,2},{3,11},{11,3},{4,12},{12,4},... | collective-permute-start | bytes 2359304 | tf_op jit(solution)/shard_map/ppermute | solution.py:35
  150.3 25.3 %collective-permute-start.14 = (bf16[2,2,1,4,48,128]{5,4,3,2,1,0:T(8,128)(2,1)S(1)}, bf16[2,2,1,4,48,128]{5,4,3,2,1,0:T(8,128)(2,1)S(1)}, u32[]{:S(2)}, u32[]{:S(2)}) collective-permute-start(bf16[2,2,1,4,48,128]{5,4,3,2,1,0:T(8,128)(2,1)S(1)} %copy-done.15), channel_id=1, source_target_pairs={{0,4},{4,0},{1,5},{5,1},{2,6},{6,2},{3,7},{7,3},{8,12},{12,8},{9,1... | collective-permute-start | bytes 589832 | tf_op jit(solution)/shard_map/ppermute | solution.py:35
  179.5 15.9 %collective-permute-start.15 = (bf16[2,384,128]{2,1,0:T(8,128)(2,1)}, bf16[2,384,128]{2,1,0:T(8,128)(2,1)S(1)}, u32[]{:S(2)}, u32[]{:S(2)}) collective-permute-start(bf16[2,384,128]{2,1,0:T(8,128)(2,1)} %bitcast.9), channel_id=1, source_target_pairs={{0,8},{8,0},{1,9},{9,1},{2,10},{10,2},{3,11},{11,3},{4,12},{12,4},... | collective-permute-start | bytes 589832 | tf_op jit(solution)/shard_map/ppermute | solution.py:35
  184.2 24.8 %all-to-all-start.4 = ((f32[4,2,4,1536]{3,2,1,0:T(4,128)}), f32[4,2,4,1536]{3,2,1,0:T(4,128)S(1)}, u32[]{:S(2)}, u32[]{:S(2)}) async-start(f32[4,2,4,1536]{3,2,1,0:T(4,128)} %bitcast.4), calls=%async_computation.4 | async-start | bytes 393216 | tf_op jit(solution)/shard_map/all_to_all | solution.py:27
  (14 other events, 73.4 us)

commit v6 on v4

--- a/solution.py
+++ b/solution.py
@@ -39,14 +39,14 @@
     return partner(value, "c", 2, 1)
 
 
-def gather_ring(value, axes, count, dim):
+def gather_ring(value, axes, count, dim, *others):
     here = lax.axis_index(axes)
     shape = list(value.shape)
     shape[dim] = count
     start = [0] * len(shape)
     whole = jnp.zeros(shape, value.dtype)
     blocks = [value] + [partner(value, axes, count, step) for step in range(1, count)]
-    for step, block in enumerate(lax.optimization_barrier(blocks)):
+    for step, block in enumerate(lax.optimization_barrier(blocks + list(others))[:count]):
         start[dim] = here ^ step
         whole = lax.dynamic_update_slice(whole, block, tuple(start))
     return whole
@@ -130,10 +130,13 @@
                 )
                 term = dot(weight, rows[far], 1, 1)
                 total = term if total is None else total + term
-            total = total.astype(BF16)
-            for step in range(4):
-                for at in range(4):
-                    out_ref[at, member_ref[0] ^ step, kind, core] = total[step * units : (step + 1) * units]
+            sends = [(kind, total.astype(BF16))]
+            if kind == 0:
+                sends.append((2, (total - sends[0][1].astype(F32)).astype(BF16)))
+            for row, value in sends:
+                for step in range(4):
+                    for at in range(4):
+                        out_ref[at, member_ref[0] ^ step, row, core] = value[step * units : (step + 1) * units]
 
 
 def hidden_parts(member, rows, own, beside):
@@ -141,7 +144,7 @@
     tokens = rows.shape[0] * rows.shape[3]
     return pl.pallas_call(
         hidden_kernel,
-        out_shape=jax.ShapeDtypeStruct((4, 4, 2, 2, units, tokens), BF16),
+        out_shape=jax.ShapeDtypeStruct((4, 4, 3, 2, units, tokens), BF16),
         in_specs=[pl.BlockSpec(memory_space=pltpu.SMEM)] + [pl.BlockSpec(memory_space=pltpu.VMEM)] * 9,
         out_specs=pl.BlockSpec(memory_space=pltpu.VMEM),
         compiler_params=pltpu.CompilerParams(vmem_limit_bytes=VMEM_BYTES),
@@ -159,9 +162,10 @@
     for core in range(2):
         for step in range(4):
             slot = member_ref[0] ^ step
-            pre_act, act_grad = (
-                sum(parts_ref[source, slot, kind, core].astype(F32) for source in range(4)) for kind in range(2)
+            value, act_grad, rest = (
+                sum(parts_ref[source, slot, row, core].astype(F32) for source in range(4)) for row in range(3)
             )
+            pre_act = value + rest
             values = (activate(pre_act).astype(BF16), gelu_slope(pre_act, act_grad).astype(BF16))
             for kind in range(2):
                 units[kind].append(values[kind])
@@ -202,20 +206,19 @@
 
     pieces = cut(member, up_proj.T, down_proj)
     own = [pieces[0]] + [partner(pieces[step], GROUP, 4, step) for step in range(1, 4)]
-    first = other_core(after(pieces[0], *own[1:]))
-    beside = [first] + [other_core(piece) for piece in own[1:]]
-
-    both = after(jnp.concatenate([tokens, out_grad], axis=0), *pieces)
+    beside = [other_core(piece) for piece in own]
+
+    both = after(jnp.concatenate([tokens, out_grad], axis=0), beside[0])
     column = spread(both, COLUMN, 8)
-    sent, mine = lay_out(lax.axis_index(("z2", "z1")).reshape(1).astype(jnp.int32), column)
-    plane = exchange(after(sent, *own), PLANE)
-
-    lines = gather_ring(after(mine, first), "y", 4, 2)
+    sent, mine = lay_out(lax.axis_index(("z2", "z1")).reshape(1).astype(jnp.int32), after(column, *beside))
+    plane = exchange(sent, PLANE)
+
+    lines = gather_ring(after(mine, sent), "y", 4, 2)
     parts = hidden_parts(after(member, lines), plane, own, beside)
     arrived = exchange(parts, GROUP)
     flat = gather_ring(after(lines, parts), ("xh", "xp"), 4, 1).reshape(2, 128, width)
 
-    partials, pair = output_parts(member, arrived, own, beside, 16)
+    partials, pair = output_parts(after(member, flat), arrived, own, beside, 16)
     arrived = exchange(partials, PLANE)
     summed = jnp.sum(arrived.reshape(2, 2, 4, 2, 8, 2 * width).astype(F32), axis=(0, 2))
     summed = summed.astype(BF16).reshape(2, 2, 2, 4, 2, width)
@@ -223,8 +226,9 @@
     ends = jnp.sum(exchange(summed, COLUMN).astype(F32), axis=0).astype(BF16)
 
     flat = jnp.concatenate([flat, other_core(flat)], axis=1)
-    lines = gather_ring(pair, ("z2", "z1"), 4, 2)
-    lines = after(lines, arrived).reshape(2, 2, 8 * units, 128)
+    lines = gather_ring(pair, "z2", 2, 2)[:, :, :, None]
+    lines = gather_ring(lines, "z1", 2, 3, arrived)
+    lines = lines.reshape(2, 2, 8 * units, 128)
     units_all = jnp.concatenate([lines[0], other_core(lines[1])], axis=2)
     down_grad = dot(units_all[0], flat[1], 1, 0).astype(BF16)
     up_grad = dot(flat[0], units_all[1], 0, 1).astype(BF16)

time: 184 us -> 191 us (1.038)
  waiting for transfers between devices: 50.4 us -> 74 us
  starting transfers between devices: 99.4 us -> 84.2 us
  matrix products: 5.11 us -> 3.12 us
    all_to_all x5, waiting for transfers between devices: 7.33 us -> 21.8 us  [exchange(): return lax.all_to_all(value, axes, split_axis=0, concat_axis=0, tiled=True)]
    ppermute x18 -> x17, starting transfers between devices: 56.2 us -> 46 us  [partner(): return lax.ppermute(value, axes, [(at, at ^ step) for at in range(count)])]
    ppermute x18 -> x17, waiting for transfers between devices: 43.1 us -> 52.2 us  [partner(): return lax.ppermute(value, axes, [(at, at ^ step) for at in range(count)])]
    all_to_all x5, starting transfers between devices: 43.3 us -> 38.2 us  [exchange(): return lax.all_to_all(value, axes, split_axis=0, concat_axis=0, tiled=True)]
    dot_general x2, matrix products: 5.11 us -> 3.12 us  [dot(): lax.dot_general(left, right, (((left_dim,), (right_dim,)), ((), ())), pre...]
    unnamed x30 -> x32, local copies, waits for them, and re-layouts: 12.7 us -> 12.3 us
  transfers between devices with their start and end apart: 23 -> 22, of which waited for: 8 -> 11; matrix products, arithmetic and copies ran while one was open for 5% -> 5% of each run, Pallas kernels for 1% -> 0%
where the time goes in v6:
time: 191 us; the launch traced here: 190 us
  starting transfers between devices  84.2 us (44%)
  waiting for transfers between devices  74 us (39%)
  local copies, waits for them, and re-layouts  19 us (10%)
  Pallas kernels  7.91 us (4%)
  matrix products  3.12 us (2%)
    ppermute x17, waiting for transfers between devices, partner(): return lax.ppermute(value, axes, [(at, at ^ step) for at in range(count)])  52.2 us
    ppermute x17, starting transfers between devices, partner(): return lax.ppermute(value, axes, [(at, at ^ step) for at in range(count)])  46 us
    all_to_all x5, starting transfers between devices, exchange(): return lax.all_to_all(value, axes, split_axis=0, concat_axis=0, tiled=True)  38.2 us
    all_to_all x5, waiting for transfers between devices, exchange(): return lax.all_to_all(value, axes, split_axis=0, concat_axis=0, tiled=True)  21.8 us
    unnamed x32, local copies, waits for them, and re-layouts  12.3 us
    pallas_call x1, Pallas kernels, hidden_parts(): pl.pallas_call(hidden_kernel, out_shape=jax.ShapeDtypeStruct((4, 4, 3, 2,...  3.85 us
  transfers between devices with their start and end apart: 22, of which 11 were waited for; matrix products, arithmetic and copies ran while one was open for 5% of the time, Pallas kernels for 0%

profile of v6, /device:TPU:6, one launch (start us, length us, event | category | flops | bytes accessed | tf_op | source)
XLA Modules:
  0.0 189.7 jit_solution(3245656386215126162)
XLA Ops:
  6.4 3.8 %collective-permute-start.1 = (bf16[2,48,3072]{2,1,0:T(8,128)(2,1)}, bf16[2,48,3072]{2,1,0:T(8,128)(2,1)S(1)}, u32[]{:S(2)}, u32[]{:S(2)}) collective-permute-start(bf16[2,48,3072]{2,1,0:T(8,128)(2,1)} %get-tuple-element.32), channel_id=1, source_target_pairs={{0,1},{1,0},{128,129},{129,128},{2,3},{3,2},{130,131},{131,130},{4... | collective-permute-start | bytes 1769480 | tf_op jit(solution)/shard_map/ppermute | solution.py:35
  10.3 2.7 %collective-permute-start.3 = (bf16[2,48,3072]{2,1,0:T(8,128)(2,1)}, bf16[2,48,3072]{2,1,0:T(8,128)(2,1)S(1)}, u32[]{:S(2)}, u32[]{:S(2)}) collective-permute-start(bf16[2,48,3072]{2,1,0:T(8,128)(2,1)} %get-tuple-element.33), channel_id=1, source_target_pairs={{0,128},{1,129},{128,0},{129,1},{2,130},{3,131},{130,2},{131,3},{4... | collective-permute-start | bytes 1769480 | tf_op jit(solution)/shard_map/ppermute | solution.py:35
  13.0 2.7 %collective-permute-start.5 = (bf16[2,48,3072]{2,1,0:T(8,128)(2,1)}, bf16[2,48,3072]{2,1,0:T(8,128)(2,1)S(1)}, u32[]{:S(2)}, u32[]{:S(2)}) collective-permute-start(bf16[2,48,3072]{2,1,0:T(8,128)(2,1)} %get-tuple-element.34), channel_id=1, source_target_pairs={{0,129},{1,128},{128,1},{129,0},{2,131},{3,130},{130,3},{131,2},{4... | collective-permute-start | bytes 1769480 | tf_op jit(solution)/shard_map/ppermute | solution.py:35
  16.4 15.1 %all-to-all-start = ((bf16[8,8,1536]{2,1,0:T(8,128)(2,1)}), bf16[8,8,1536]{2,1,0:T(8,128)(2,1)S(1)}, u32[]{:S(2)}, u32[]{:S(2)}) async-start(bf16[8,8,1536]{2,1,0:T(8,128)(2,1)} %broadcast_in_dim.25), calls=%async_computation | async-start | bytes 393216 | tf_op jit(solution)/shard_map/all_to_all | solution.py:27
  33.4 7.0 %collective-permute-done.3.refs_2_ = bf16[2,48,3072]{2,1,0:T(8,128)(2,1)S(1)} collective-permute-done((bf16[2,48,3072]{2,1,0:T(8,128)(2,1)}, bf16[2,48,3072]{2,1,0:T(8,128)(2,1)S(1)}, u32[]{:S(2)}, u32[]{:S(2)}) %collective-permute-start.3) | collective-permute-done | bytes 589856 | tf_op jit(solution)/shard_map/ppermute | solution.py:35
  43.2 2.4 %collective-permute-start.6 = (bf16[2,48,3072]{2,1,0:T(8,128)(2,1)S(1)}, bf16[2,48,3072]{2,1,0:T(8,128)(2,1)}, u32[]{:S(2)}, u32[]{:S(2)}) collective-permute-start(bf16[2,48,3072]{2,1,0:T(8,128)(2,1)S(1)} %collective-permute-done.5.refs_3_), channel_id=1, source_target_pairs={{0,8},{8,0},{1,9},{9,1},{2,10},{10,2},{3,11},{11,3},{4,12},{12,4},... | collective-permute-start | bytes 1769480 | tf_op jit(solution)/shard_map/ppermute | solution.py:35
  47.3 10.9 %all-to-all-done.column_ref = bf16[8,8,1536]{2,1,0:T(8,128)(2,1)S(1)} async-done(((bf16[8,8,1536]{2,1,0:T(8,128)(2,1)}), bf16[8,8,1536]{2,1,0:T(8,128)(2,1)S(1)}, u32[]{:S(2)}, u32[]{:S(2)}) %all-to-all-start) | async-done | bytes 196640 | tf_op jit(solution)/shard_map/all_to_all | solution.py:27
  59.5 7.4 %all-to-all-start.1 = ((bf16[16,2,2,8,1536]{4,3,2,1,0:T(8,128)(2,1)}), bf16[16,2,2,8,1536]{4,3,2,1,0:T(8,128)(2,1)S(1)}, u32[]{:S(2)}, u32[]{:S(2)}) async-start(bf16[16,2,2,8,1536]{4,3,2,1,0:T(8,128)(2,1)} %copy-done.6), calls=%async_computation.1 | async-start | bytes 3145728 | tf_op jit(solution)/shard_map/all_to_all | solution.py:27
  66.9 3.4 %collective-permute-start.7 = (bf16[2,1,1,8,1536]{4,3,2,1,0:T(8,128)(2,1)S(1)}, bf16[2,1,1,8,1536]{4,3,2,1,0:T(8,128)(2,1)S(1)}, u32[]{:S(2)}, u32[]{:S(2)}) collective-permute-start(bf16[2,1,1,8,1536]{4,3,2,1,0:T(8,128)(2,1)S(1)} %get-tuple-element.39), channel_id=1, source_target_pairs={{0,16},{16,0},{32,48},{48,32},{1,17},{17,1},{33,49},{49,33},{2,18}... | collective-permute-start | bytes 147464 | tf_op jit(solution)/shard_map/ppermute | solution.py:35
  70.3 4.6 %collective-permute-start.8 = (bf16[2,1,1,8,1536]{4,3,2,1,0:T(8,128)(2,1)S(1)}, bf16[2,1,1,8,1536]{4,3,2,1,0:T(8,128)(2,1)S(1)}, u32[]{:S(2)}, u32[]{:S(2)}) collective-permute-start(bf16[2,1,1,8,1536]{4,3,2,1,0:T(8,128)(2,1)S(1)} %get-tuple-element.39), channel_id=1, source_target_pairs={{0,32},{16,48},{32,0},{48,16},{1,33},{17,49},{33,1},{49,17},{2,34}... | collective-permute-start | bytes 147464 | tf_op jit(solution)/shard_map/ppermute | solution.py:35
  74.9 2.5 %collective-permute-start.9 = (bf16[2,1,1,8,1536]{4,3,2,1,0:T(8,128)(2,1)S(1)}, bf16[2,1,1,8,1536]{4,3,2,1,0:T(8,128)(2,1)S(1)}, u32[]{:S(2)}, u32[]{:S(2)}) collective-permute-start(bf16[2,1,1,8,1536]{4,3,2,1,0:T(8,128)(2,1)S(1)} %get-tuple-element.39), channel_id=1, source_target_pairs={{0,48},{16,32},{32,16},{48,0},{1,49},{17,33},{33,17},{49,1},{2,50}... | collective-permute-start | bytes 147464 | tf_op jit(solution)/shard_map/ppermute | solution.py:35
  77.4 8.7 %collective-permute-done.7 = bf16[2,1,1,8,1536]{4,3,2,1,0:T(8,128)(2,1)S(1)} collective-permute-done((bf16[2,1,1,8,1536]{4,3,2,1,0:T(8,128)(2,1)S(1)}, bf16[2,1,1,8,1536]{4,3,2,1,0:T(8,128)(2,1)S(1)}, u32[]{:S(2)}, u32[]{:S(2)}) %collective-permute-start.7) | collective-permute-done | bytes 49184 | tf_op jit(solution)/shard_map/ppermute | solution.py:35
  93.7 3.9 %hidden_parts.1 = bf16[4,4,3,2,48,128]{5,4,3,2,1,0:T(8,128)(2,1)} custom-call(s32[1]{0:T(128)} %bitcast.member_ref, bf16[16,2,2,8,1536]{4,3,2,1,0:T(8,128)(2,1)S(1)} %all-to-all-done.1.rows_ref, bf16[2,48,3072]{2,1,0:T(8,128)(2,1)S(1)} %get-tuple-element.30.refs_0_, bf16[2,48,3072]{2,1,0:T(8,128)(2,1)S(1)} %collective-permute-done.1.refs_1_, ...), custom_call_target="tpu_custom_call" | custom-call | flops 604000000 | bytes 6700000 | tf_op jit(solution)/shard_map/hidden_parts/pallas_call | solution.py:145
  97.6 4.0 %all-to-all-start.2 = ((bf16[4,4,3,2,48,128]{5,4,3,2,1,0:T(8,128)(2,1)}), bf16[4,4,3,2,48,128]{5,4,3,2,1,0:T(8,128)(2,1)S(1)}, u32[]{:S(2)}, u32[]{:S(2)}) async-start(bf16[4,4,3,2,48,128]{5,4,3,2,1,0:T(8,128)(2,1)} %hidden_parts.1), calls=%async_computation.2 | async-start | bytes 2359296 | tf_op jit(solution)/shard_map/all_to_all | solution.py:27
  103.5 2.8 %collective-permute-start.11 = (bf16[2,1,4,8,1536]{4,3,2,1,0:T(8,128)(2,1)}, bf16[2,1,4,8,1536]{4,3,2,1,0:T(8,128)(2,1)S(1)}, u32[]{:S(2)}, u32[]{:S(2)}) collective-permute-start(bf16[2,1,4,8,1536]{4,3,2,1,0:T(8,128)(2,1)} %constant_dynamic-update-slice_fusion.6), channel_id=1, source_target_pairs={{0,256},{128,384},{256,0},{384,128},{1,257},{129,385},{257,1},{385... | collective-permute-start | bytes 589832 | tf_op jit(solution)/shard_map/ppermute | solution.py:35
  106.3 5.7 %collective-permute-start.12 = (bf16[2,1,4,8,1536]{4,3,2,1,0:T(8,128)(2,1)}, bf16[2,1,4,8,1536]{4,3,2,1,0:T(8,128)(2,1)S(1)}, u32[]{:S(2)}, u32[]{:S(2)}) collective-permute-start(bf16[2,1,4,8,1536]{4,3,2,1,0:T(8,128)(2,1)} %constant_dynamic-update-slice_fusion.6), channel_id=1, source_target_pairs={{0,384},{128,256},{256,128},{384,0},{1,385},{129,257},{257,129},{3... | collective-permute-start | bytes 589832 | tf_op jit(solution)/shard_map/ppermute | solution.py:35
  112.0 7.6 %collective-permute-done.10 = bf16[2,1,4,8,1536]{4,3,2,1,0:T(8,128)(2,1)S(1)} collective-permute-done((bf16[2,1,4,8,1536]{4,3,2,1,0:T(8,128)(2,1)}, bf16[2,1,4,8,1536]{4,3,2,1,0:T(8,128)(2,1)S(1)}, u32[]{:S(2)}, u32[]{:S(2)}) %collective-permute-start.10) | collective-permute-done | bytes 196640 | tf_op jit(solution)/shard_map/ppermute | solution.py:35
  119.6 3.3 %collective-permute-done.11 = bf16[2,1,4,8,1536]{4,3,2,1,0:T(8,128)(2,1)S(1)} collective-permute-done((bf16[2,1,4,8,1536]{4,3,2,1,0:T(8,128)(2,1)}, bf16[2,1,4,8,1536]{4,3,2,1,0:T(8,128)(2,1)S(1)}, u32[]{:S(2)}, u32[]{:S(2)}) %collective-permute-start.11) | collective-permute-done | bytes 196640 | tf_op jit(solution)/shard_map/ppermute | solution.py:35
  126.9 2.6 %output_parts.1 = (bf16[16,2,8,3072]{3,2,1,0:T(8,128)(2,1)S(1)}, bf16[2,2,1,2,48,128]{5,4,3,2,1,0:T(8,128)(2,1)S(1)}) custom-call(s32[1]{0:T(128)} %bitcast.member_ref, bf16[4,4,3,2,48,128]{5,4,3,2,1,0:T(8,128)(2,1)S(1)} %all-to-all-done.2.parts_ref, bf16[2,48,3072]{2,1,0:T(8,128)(2,1)S(1)} %get-tuple-element.30.refs_0_, ...), custom_call_target="tpu_custom_call" | custom-call | flops 604000000 | bytes 6700000 | tf_op jit(solution)/shard_map/output_parts/pallas_call | solution.py:188
  130.8 8.4 %all-to-all-start.3 = ((bf16[16,2,8,3072]{3,2,1,0:T(8,128)(2,1)}), bf16[16,2,8,3072]{3,2,1,0:T(8,128)(2,1)S(1)}, u32[]{:S(2)}, u32[]{:S(2)}) async-start(bf16[16,2,8,3072]{3,2,1,0:T(8,128)(2,1)} %copy-done.7), calls=%async_computation.3 | async-start | bytes 3145728 | tf_op jit(solution)/shard_map/all_to_all | solution.py:27
  141.2 13.1 %collective-permute-done.14 = bf16[2,2,1,2,48,128]{5,4,3,2,1,0:T(8,128)(2,1)S(1)} collective-permute-done((bf16[2,2,1,2,48,128]{5,4,3,2,1,0:T(8,128)(2,1)S(1)}, bf16[2,2,1,2,48,128]{5,4,3,2,1,0:T(8,128)(2,1)S(1)}, u32[]{:S(2)}, u32[]{:S(2)}) %collective-permute-start.14) | collective-permute-done | bytes 98336 | tf_op jit(solution)/shard_map/ppermute | solution.py:35
  158.3 7.9 %collective-permute-done.15 = bf16[2,2,2,1,2,48,128]{6,5,4,3,2,1,0:T(8,128)(2,1)S(1)} collective-permute-done((bf16[2,2,2,1,2,48,128]{6,5,4,3,2,1,0:T(8,128)(2,1)S(1)}, bf16[2,2,2,1,2,48,128]{6,5,4,3,2,1,0:T(8,128)(2,1)S(1)}, u32[]{:S(2)}, u32[]{:S(2)}) %collective-permute-start.15) | collective-permute-done | bytes 196640 | tf_op jit(solution)/shard_map/ppermute | solution.py:35
  168.0 3.4 %all-to-all-start.4 = ((bf16[8,2,4,1536]{3,2,1,0:T(4,128)(2,1)}), bf16[8,2,4,1536]{3,2,1,0:T(4,128)(2,1)S(1)}, u32[]{:S(2)}, u32[]{:S(2)}) async-start(bf16[8,2,4,1536]{3,2,1,0:T(4,128)(2,1)} %bitcast.6), calls=%async_computation.4 | async-start | bytes 393216 | tf_op jit(solution)/shard_map/all_to_all | solution.py:27
  178.0 11.0 %all-to-all-done.4 = bf16[8,2,4,1536]{3,2,1,0:T(4,128)(2,1)S(1)} async-done(((bf16[8,2,4,1536]{3,2,1,0:T(4,128)(2,1)}), bf16[8,2,4,1536]{3,2,1,0:T(4,128)(2,1)S(1)}, u32[]{:S(2)}, u32[]{:S(2)}) %all-to-all-start.4) | async-done | bytes 196640 | tf_op jit(solution)/shard_map/all_to_all | solution.py:27
  (82 shorter events, 44.1 us)
Async XLA Ops:
  0.6 15.0 %copy-start.14 = (bf16[4,1536]{1,0:T(4,128)(2,1)S(1)}, bf16[4,1536]{1,0:T(4,128)(2,1)}, u32[]{:S(2)}) copy-start(bf16[4,1536]{1,0:T(4,128)(2,1)} %param.7) | copy-start | bytes 36868
  4.5 11.2 %collective-permute-start = (bf16[2,48,3072]{2,1,0:T(8,128)(2,1)S(1)}, bf16[2,48,3072]{2,1,0:T(8,128)(2,1)S(1)}, u32[]{:S(2)}, u32[]{:S(2)}) collective-permute-start(bf16[2,48,3072]{2,1,0:T(8,128)(2,1)S(1)} %get-tuple-element.30.refs_0_), channel_id=1, source_target_pairs={{0,8},{8,0},{1,9},{9,1},{2,10},{10,2},{3,11},{11,3},{4,12},{12,4},... | collective-permute-start | bytes 1769480 | tf_op jit(solution)/shard_map/ppermute | solution.py:35
  6.4 25.1 %collective-permute-start.1 = (bf16[2,48,3072]{2,1,0:T(8,128)(2,1)}, bf16[2,48,3072]{2,1,0:T(8,128)(2,1)S(1)}, u32[]{:S(2)}, u32[]{:S(2)}) collective-permute-start(bf16[2,48,3072]{2,1,0:T(8,128)(2,1)} %get-tuple-element.32), channel_id=1, source_target_pairs={{0,1},{1,0},{128,129},{129,128},{2,3},{3,2},{130,131},{131,130},{4... | collective-permute-start | bytes 1769480 | tf_op jit(solution)/shard_map/ppermute | solution.py:35
  10.3 30.2 %collective-permute-start.3 = (bf16[2,48,3072]{2,1,0:T(8,128)(2,1)}, bf16[2,48,3072]{2,1,0:T(8,128)(2,1)S(1)}, u32[]{:S(2)}, u32[]{:S(2)}) collective-permute-start(bf16[2,48,3072]{2,1,0:T(8,128)(2,1)} %get-tuple-element.33), channel_id=1, source_target_pairs={{0,128},{1,129},{128,0},{129,1},{2,130},{3,131},{130,2},{131,3},{4... | collective-permute-start | bytes 1769480 | tf_op jit(solution)/shard_map/ppermute | solution.py:35
  13.0 30.2 %collective-permute-start.5 = (bf16[2,48,3072]{2,1,0:T(8,128)(2,1)}, bf16[2,48,3072]{2,1,0:T(8,128)(2,1)S(1)}, u32[]{:S(2)}, u32[]{:S(2)}) collective-permute-start(bf16[2,48,3072]{2,1,0:T(8,128)(2,1)} %get-tuple-element.34), channel_id=1, source_target_pairs={{0,129},{1,128},{128,1},{129,0},{2,131},{3,130},{130,3},{131,2},{4... | collective-permute-start | bytes 1769480 | tf_op jit(solution)/shard_map/ppermute | solution.py:35
  16.4 41.8 %all-to-all-start = ((bf16[8,8,1536]{2,1,0:T(8,128)(2,1)}), bf16[8,8,1536]{2,1,0:T(8,128)(2,1)S(1)}, u32[]{:S(2)}, u32[]{:S(2)}) async-start(bf16[8,8,1536]{2,1,0:T(8,128)(2,1)} %broadcast_in_dim.25), calls=%async_computation | async-start | bytes 393216 | tf_op jit(solution)/shard_map/all_to_all | solution.py:27
  31.5 14.9 %collective-permute-start.2 = (bf16[2,48,3072]{2,1,0:T(8,128)(2,1)S(1)}, bf16[2,48,3072]{2,1,0:T(8,128)(2,1)}, u32[]{:S(2)}, u32[]{:S(2)}) collective-permute-start(bf16[2,48,3072]{2,1,0:T(8,128)(2,1)S(1)} %collective-permute-done.1.refs_1_), channel_id=1, source_target_pairs={{0,8},{8,0},{1,9},{9,1},{2,10},{10,2},{3,11},{11,3},{4,12},{12,4},... | collective-permute-start | bytes 1769480 | tf_op jit(solution)/shard_map/ppermute | solution.py:35
  40.5 6.0 %collective-permute-start.4 = (bf16[2,48,3072]{2,1,0:T(8,128)(2,1)S(1)}, bf16[2,48,3072]{2,1,0:T(8,128)(2,1)}, u32[]{:S(2)}, u32[]{:S(2)}) collective-permute-start(bf16[2,48,3072]{2,1,0:T(8,128)(2,1)S(1)} %collective-permute-done.3.refs_2_), channel_id=1, source_target_pairs={{0,8},{8,0},{1,9},{9,1},{2,10},{10,2},{3,11},{11,3},{4,12},{12,4},... | collective-permute-start | bytes 1769480 | tf_op jit(solution)/shard_map/ppermute | solution.py:35
  43.2 4.1 %collective-permute-start.6 = (bf16[2,48,3072]{2,1,0:T(8,128)(2,1)S(1)}, bf16[2,48,3072]{2,1,0:T(8,128)(2,1)}, u32[]{:S(2)}, u32[]{:S(2)}) collective-permute-start(bf16[2,48,3072]{2,1,0:T(8,128)(2,1)S(1)} %collective-permute-done.5.refs_3_), channel_id=1, source_target_pairs={{0,8},{8,0},{1,9},{9,1},{2,10},{10,2},{3,11},{11,3},{4,12},{12,4},... | collective-permute-start | bytes 1769480 | tf_op jit(solution)/shard_map/ppermute | solution.py:35
  59.5 32.1 %all-to-all-start.1 = ((bf16[16,2,2,8,1536]{4,3,2,1,0:T(8,128)(2,1)}), bf16[16,2,2,8,1536]{4,3,2,1,0:T(8,128)(2,1)S(1)}, u32[]{:S(2)}, u32[]{:S(2)}) async-start(bf16[16,2,2,8,1536]{4,3,2,1,0:T(8,128)(2,1)} %copy-done.6), calls=%async_computation.1 | async-start | bytes 3145728 | tf_op jit(solution)/shard_map/all_to_all | solution.py:27
  66.9 19.1 %collective-permute-start.7 = (bf16[2,1,1,8,1536]{4,3,2,1,0:T(8,128)(2,1)S(1)}, bf16[2,1,1,8,1536]{4,3,2,1,0:T(8,128)(2,1)S(1)}, u32[]{:S(2)}, u32[]{:S(2)}) collective-permute-start(bf16[2,1,1,8,1536]{4,3,2,1,0:T(8,128)(2,1)S(1)} %get-tuple-element.39), channel_id=1, source_target_pairs={{0,16},{16,0},{32,48},{48,32},{1,17},{17,1},{33,49},{49,33},{2,18}... | collective-permute-start | bytes 147464 | tf_op jit(solution)/shard_map/ppermute | solution.py:35
  70.3 18.1 %collective-permute-start.8 = (bf16[2,1,1,8,1536]{4,3,2,1,0:T(8,128)(2,1)S(1)}, bf16[2,1,1,8,1536]{4,3,2,1,0:T(8,128)(2,1)S(1)}, u32[]{:S(2)}, u32[]{:S(2)}) collective-permute-start(bf16[2,1,1,8,1536]{4,3,2,1,0:T(8,128)(2,1)S(1)} %get-tuple-element.39), channel_id=1, source_target_pairs={{0,32},{16,48},{32,0},{48,16},{1,33},{17,49},{33,1},{49,17},{2,34}... | collective-permute-start | bytes 147464 | tf_op jit(solution)/shard_map/ppermute | solution.py:35
  74.9 13.5 %collective-permute-start.9 = (bf16[2,1,1,8,1536]{4,3,2,1,0:T(8,128)(2,1)S(1)}, bf16[2,1,1,8,1536]{4,3,2,1,0:T(8,128)(2,1)S(1)}, u32[]{:S(2)}, u32[]{:S(2)}) collective-permute-start(bf16[2,1,1,8,1536]{4,3,2,1,0:T(8,128)(2,1)S(1)} %get-tuple-element.39), channel_id=1, source_target_pairs={{0,48},{16,32},{32,16},{48,0},{1,49},{17,33},{33,17},{49,1},{2,50}... | collective-permute-start | bytes 147464 | tf_op jit(solution)/shard_map/ppermute | solution.py:35
  97.6 27.2 %all-to-all-start.2 = ((bf16[4,4,3,2,48,128]{5,4,3,2,1,0:T(8,128)(2,1)}), bf16[4,4,3,2,48,128]{5,4,3,2,1,0:T(8,128)(2,1)S(1)}, u32[]{:S(2)}, u32[]{:S(2)}) async-start(bf16[4,4,3,2,48,128]{5,4,3,2,1,0:T(8,128)(2,1)} %hidden_parts.1), calls=%async_computation.2 | async-start | bytes 2359296 | tf_op jit(solution)/shard_map/all_to_all | solution.py:27
  101.5 18.0 %collective-permute-start.10 = (bf16[2,1,4,8,1536]{4,3,2,1,0:T(8,128)(2,1)}, bf16[2,1,4,8,1536]{4,3,2,1,0:T(8,128)(2,1)S(1)}, u32[]{:S(2)}, u32[]{:S(2)}) collective-permute-start(bf16[2,1,4,8,1536]{4,3,2,1,0:T(8,128)(2,1)} %constant_dynamic-update-slice_fusion.6), channel_id=1, source_target_pairs={{0,128},{128,0},{256,384},{384,256},{1,129},{129,1},{257,385},{385... | collective-permute-start | bytes 589832 | tf_op jit(solution)/shard_map/ppermute | solution.py:35
  103.5 19.3 %collective-permute-start.11 = (bf16[2,1,4,8,1536]{4,3,2,1,0:T(8,128)(2,1)}, bf16[2,1,4,8,1536]{4,3,2,1,0:T(8,128)(2,1)S(1)}, u32[]{:S(2)}, u32[]{:S(2)}) collective-permute-start(bf16[2,1,4,8,1536]{4,3,2,1,0:T(8,128)(2,1)} %constant_dynamic-update-slice_fusion.6), channel_id=1, source_target_pairs={{0,256},{128,384},{256,0},{384,128},{1,257},{129,385},{257,1},{385... | collective-permute-start | bytes 589832 | tf_op jit(solution)/shard_map/ppermute | solution.py:35
  106.3 16.6 %collective-permute-start.12 = (bf16[2,1,4,8,1536]{4,3,2,1,0:T(8,128)(2,1)}, bf16[2,1,4,8,1536]{4,3,2,1,0:T(8,128)(2,1)S(1)}, u32[]{:S(2)}, u32[]{:S(2)}) collective-permute-start(bf16[2,1,4,8,1536]{4,3,2,1,0:T(8,128)(2,1)} %constant_dynamic-update-slice_fusion.6), channel_id=1, source_target_pairs={{0,384},{128,256},{256,128},{384,0},{1,385},{129,257},{257,129},{3... | collective-permute-start | bytes 589832 | tf_op jit(solution)/shard_map/ppermute | solution.py:35
  130.8 25.6 %copy-start.11 = (bf16[2,4,4,8,1536]{4,3,2,1,0:T(8,128)(2,1)S(1)}, bf16[2,4,4,8,1536]{4,3,2,1,0:T(8,128)(2,1)}, u32[]{:S(2)}) copy-start(bf16[2,4,4,8,1536]{4,3,2,1,0:T(8,128)(2,1)} %copy-done.10) | copy-start | bytes 2359300
  130.8 35.4 %all-to-all-start.3 = ((bf16[16,2,8,3072]{3,2,1,0:T(8,128)(2,1)}), bf16[16,2,8,3072]{3,2,1,0:T(8,128)(2,1)S(1)}, u32[]{:S(2)}, u32[]{:S(2)}) async-start(bf16[16,2,8,3072]{3,2,1,0:T(8,128)(2,1)} %copy-done.7), calls=%async_computation.3 | async-start | bytes 3145728 | tf_op jit(solution)/shard_map/all_to_all | solution.py:27
  139.1 15.2 %collective-permute-start.14 = (bf16[2,2,1,2,48,128]{5,4,3,2,1,0:T(8,128)(2,1)S(1)}, bf16[2,2,1,2,48,128]{5,4,3,2,1,0:T(8,128)(2,1)S(1)}, u32[]{:S(2)}, u32[]{:S(2)}) collective-permute-start(bf16[2,2,1,2,48,128]{5,4,3,2,1,0:T(8,128)(2,1)S(1)} %get-tuple-element.52), channel_id=1, source_target_pairs={{0,4},{4,0},{1,5},{5,1},{2,6},{6,2},{3,7},{7,3},{8,12},{12,8},{9,1... | collective-permute-start | bytes 294920 | tf_op jit(solution)/shard_map/ppermute | solution.py:35
  154.4 11.8 %collective-permute-start.15 = (bf16[2,2,2,1,2,48,128]{6,5,4,3,2,1,0:T(8,128)(2,1)S(1)}, bf16[2,2,2,1,2,48,128]{6,5,4,3,2,1,0:T(8,128)(2,1)S(1)}, u32[]{:S(2)}, u32[]{:S(2)}) collective-permute-start(bf16[2,2,2,1,2,48,128]{6,5,4,3,2,1,0:T(8,128)(2,1)S(1)} %bitcast_dynamic-update-slice_fusion), channel_id=1, source_target_pairs={{0,2},{2,0},{1,3},{3,1},{4,6},{6,4},{5,7},{7,5},{8,10},{10,8},{9,1... | collective-permute-start | bytes 589832 | tf_op jit(solution)/shard_map/ppermute | solution.py:35
  156.3 17.2 %collective-permute-start.13 = (bf16[2,128,1536]{2,1,0:T(8,128)(2,1)S(1)}, bf16[2,128,1536]{2,1,0:T(8,128)(2,1)S(1)}, u32[]{:S(2)}, u32[]{:S(2)}) collective-permute-start(bf16[2,128,1536]{2,1,0:T(8,128)(2,1)S(1)} %bitcast.37), channel_id=1, source_target_pairs={{0,8},{8,0},{1,9},{9,1},{2,10},{10,2},{3,11},{11,3},{4,12},{12,4},... | collective-permute-start | bytes 2359304 | tf_op jit(solution)/shard_map/ppermute | solution.py:35
  168.0 21.0 %all-to-all-start.4 = ((bf16[8,2,4,1536]{3,2,1,0:T(4,128)(2,1)}), bf16[8,2,4,1536]{3,2,1,0:T(4,128)(2,1)S(1)}, u32[]{:S(2)}, u32[]{:S(2)}) async-start(bf16[8,2,4,1536]{3,2,1,0:T(4,128)(2,1)} %bitcast.6), calls=%async_computation.4 | async-start | bytes 393216 | tf_op jit(solution)/shard_map/all_to_all | solution.py:27
  171.6 3.3 %collective-permute-start.16 = (bf16[2,384,128]{2,1,0:T(8,128)(2,1)S(1)}, bf16[2,384,128]{2,1,0:T(8,128)(2,1)S(1)}, u32[]{:S(2)}, u32[]{:S(2)}) collective-permute-start(bf16[2,384,128]{2,1,0:T(8,128)(2,1)S(1)} %bitcast.43), channel_id=1, source_target_pairs={{0,8},{8,0},{1,9},{9,1},{2,10},{10,2},{3,11},{11,3},{4,12},{12,4},... | collective-permute-start | bytes 589832 | tf_op jit(solution)/shard_map/ppermute | solution.py:35
  (14 other events, 29.2 us)

commit v7 on v6

--- a/solution.py
+++ b/solution.py
@@ -85,43 +85,41 @@
     )(member, up_rows, down_rows)
 
 
-def lay_out_kernel(block_ref, column_ref, sent_ref, mine_ref):
-    for far in range(2):
+def lay_out_kernel(block_ref, column_ref, sent_ref):
+    def rows_of(at, array):
+        ends = [column_ref[end * 4 + at, array * 4 : array * 4 + 4].astype(F32) for end in range(2)]
+        return jnp.concatenate(ends, axis=0).astype(BF16)
+
+    for array in range(2):
+        own = rows_of(block_ref[0], array)
         for near in range(2):
-            ends = [column_ref[end * 4 + far * 2 + near].astype(F32) for end in range(2)]
-            for array in range(2):
-                rows = jnp.concatenate([end[array * 4 : array * 4 + 4] for end in ends], axis=0).astype(BF16)
-                for half in range(2):
-                    for line in range(4):
-                        sent_ref[half * 8 + near * 4 + line, far, array] = rows
-    ends = [column_ref[end * 4 + block_ref[0]].astype(F32) for end in range(2)]
-    for array in range(2):
-        rows = jnp.concatenate([end[array * 4 : array * 4 + 4] for end in ends], axis=0)
-        mine_ref[array, 0, 0] = rows.astype(BF16)
+            blocks = [rows_of(far * 2 + near, array) for far in range(2)] + [own]
+            for half in range(2):
+                for line in range(4):
+                    for far in range(3):
+                        sent_ref[half * 8 + near * 4 + line, far, array] = blocks[far]
 
 
 def lay_out(block, column):
     unused, rows, width = column.shape
     return pl.pallas_call(
         lay_out_kernel,
-        out_shape=[
-            jax.ShapeDtypeStruct((16, 2, 2, rows, width), BF16),
-            jax.ShapeDtypeStruct((2, 1, 1, rows, width), BF16),
-        ],
+        out_shape=jax.ShapeDtypeStruct((16, 3, 2, rows, width), BF16),
         in_specs=[pl.BlockSpec(memory_space=pltpu.SMEM), pl.BlockSpec(memory_space=pltpu.VMEM)],
-        out_specs=[pl.BlockSpec(memory_space=pltpu.VMEM)] * 2,
-        compiler_params=pltpu.CompilerParams(vmem_limit_bytes=VMEM_BYTES),
-        cost_estimate=pl.CostEstimate(flops=0, bytes_accessed=2_000_000, transcendentals=0),
+        out_specs=pl.BlockSpec(memory_space=pltpu.VMEM),
+        compiler_params=pltpu.CompilerParams(vmem_limit_bytes=VMEM_BYTES),
+        cost_estimate=pl.CostEstimate(flops=0, bytes_accessed=2_800_000, transcendentals=0),
         name="lay_out_rows",
     )(block, column)
 
 
 def hidden_kernel(member_ref, rows_ref, *refs):
-    own, beside, out_ref = refs[:4], refs[4:8], refs[8]
+    own, beside, out_ref, mine_ref = refs[:4], refs[4:8], refs[8], refs[9]
     units = own[0].shape[1]
     width = rows_ref.shape[4]
     for kind in range(2):
-        rows = [rows_ref[:, far, kind].reshape(-1, width) for far in range(2)]
+        rows = [rows_ref[:, far, kind].reshape(-1, width) for far in range(3)]
+        mine_ref[kind] = rows[2]
         for core, pieces in enumerate((own, beside)):
             total = None
             for far in range(2):
@@ -144,9 +142,12 @@
     tokens = rows.shape[0] * rows.shape[3]
     return pl.pallas_call(
         hidden_kernel,
-        out_shape=jax.ShapeDtypeStruct((4, 4, 3, 2, units, tokens), BF16),
+        out_shape=[
+            jax.ShapeDtypeStruct((4, 4, 3, 2, units, tokens), BF16),
+            jax.ShapeDtypeStruct((2, tokens, rows.shape[4]), BF16),
+        ],
         in_specs=[pl.BlockSpec(memory_space=pltpu.SMEM)] + [pl.BlockSpec(memory_space=pltpu.VMEM)] * 9,
-        out_specs=pl.BlockSpec(memory_space=pltpu.VMEM),
+        out_specs=[pl.BlockSpec(memory_space=pltpu.VMEM)] * 2,
         compiler_params=pltpu.CompilerParams(vmem_limit_bytes=VMEM_BYTES),
         cost_estimate=pl.CostEstimate(flops=604_000_000, bytes_accessed=6_700_000, transcendentals=0),
         name="hidden_parts",
@@ -206,28 +207,30 @@
 
     pieces = cut(member, up_proj.T, down_proj)
     own = [pieces[0]] + [partner(pieces[step], GROUP, 4, step) for step in range(1, 4)]
-    beside = [other_core(piece) for piece in own]
-
-    both = after(jnp.concatenate([tokens, out_grad], axis=0), beside[0])
+    beside = [other_core(pieces[0])]
+    waits = own[1:]
+    for piece in own[1:]:
+        beside.append(other_core(after(piece, *waits)))
+        waits = beside[-1:]
+
+    both = jnp.concatenate([tokens, out_grad], axis=0)
     column = spread(both, COLUMN, 8)
-    sent, mine = lay_out(lax.axis_index(("z2", "z1")).reshape(1).astype(jnp.int32), after(column, *beside))
+    block = lax.axis_index(("z2", "z1")).reshape(1).astype(jnp.int32)
+    sent = lay_out(block, after(column, beside[0]))
     plane = exchange(sent, PLANE)
 
-    lines = gather_ring(after(mine, sent), "y", 4, 2)
-    parts = hidden_parts(after(member, lines), plane, own, beside)
+    parts, mine = hidden_parts(member, plane, own, beside)
     arrived = exchange(parts, GROUP)
-    flat = gather_ring(after(lines, parts), ("xh", "xp"), 4, 1).reshape(2, 128, width)
-
-    partials, pair = output_parts(after(member, flat), arrived, own, beside, 16)
+
+    partials, pair = output_parts(member, arrived, own, beside, 16)
     arrived = exchange(partials, PLANE)
     summed = jnp.sum(arrived.reshape(2, 2, 4, 2, 8, 2 * width).astype(F32), axis=(0, 2))
     summed = summed.astype(BF16).reshape(2, 2, 2, 4, 2, width)
     summed = summed.transpose(2, 4, 0, 1, 3, 5).reshape(8, 2, 4, width)
     ends = jnp.sum(exchange(summed, COLUMN).astype(F32), axis=0).astype(BF16)
 
-    flat = jnp.concatenate([flat, other_core(flat)], axis=1)
-    lines = gather_ring(pair, "z2", 2, 2)[:, :, :, None]
-    lines = gather_ring(lines, "z1", 2, 3, arrived)
+    flat = jnp.concatenate([mine, other_core(mine)], axis=1)
+    lines = gather_ring(pair, ("z2", "z1"), 4, 2, arrived)
     lines = lines.reshape(2, 2, 8 * units, 128)
     units_all = jnp.concatenate([lines[0], other_core(lines[1])], axis=2)
     down_grad = dot(units_all[0], flat[1], 1, 0).astype(BF16)

time: 191 us -> 175 us (0.916)
  waiting for transfers between devices: 74 us -> 46.1 us
  blocking collectives: 0 us -> 17.7 us
  starting transfers between devices: 84.2 us -> 78.8 us
  local copies, waits for them, and re-layouts: 19 us -> 16.7 us
    ppermute x17 -> x12, waiting for transfers between devices: 52.2 us -> 19.6 us  [partner(): return lax.ppermute(value, axes, [(at, at ^ step) for at in range(count)])]
    all_to_all x0 -> x1, blocking collectives: none -> 17.7 us  [exchange(): return lax.all_to_all(value, axes, split_axis=0, concat_axis=0, tiled=True)]
    ppermute x17 -> x12, starting transfers between devices: 46 us -> 35 us  [partner(): return lax.ppermute(value, axes, [(at, at ^ step) for at in range(count)])]
    all_to_all x5 -> x4, starting transfers between devices: 38.2 us -> 43.8 us  [exchange(): return lax.all_to_all(value, axes, split_axis=0, concat_axis=0, tiled=True)]
    all_to_all x5 -> x4, waiting for transfers between devices: 21.8 us -> 26.5 us  [exchange(): return lax.all_to_all(value, axes, split_axis=0, concat_axis=0, tiled=True)]
    unnamed x32 -> x31, local copies, waits for them, and re-layouts: 12.3 us -> 11.5 us
  transfers between devices with their start and end apart: 22 -> 16, of which waited for: 11 -> 9; matrix products, arithmetic and copies ran while one was open for 5% -> 5% of each run, Pallas kernels for 0% -> 1%
where the time goes in v7:
time: 175 us; the launch traced here: 173 us
  starting transfers between devices  78.8 us (45%)
  waiting for transfers between devices  46.1 us (26%)
  blocking collectives  17.7 us (10%)
  local copies, waits for them, and re-layouts  16.7 us (10%)
  Pallas kernels  8.25 us (5%)
  matrix products  3.12 us (2%)
  other arithmetic  1.75 us (1%)
    all_to_all x4, starting transfers between devices, exchange(): return lax.all_to_all(value, axes, split_axis=0, concat_axis=0, tiled=True)  43.8 us
    ppermute x12, starting transfers between devices, partner(): return lax.ppermute(value, axes, [(at, at ^ step) for at in range(count)])  35 us
    all_to_all x4, waiting for transfers between devices, exchange(): return lax.all_to_all(value, axes, split_axis=0, concat_axis=0, tiled=True)  26.5 us
    ppermute x12, waiting for transfers between devices, partner(): return lax.ppermute(value, axes, [(at, at ^ step) for at in range(count)])  19.6 us
    all_to_all x1, blocking collectives, exchange(): return lax.all_to_all(value, axes, split_axis=0, concat_axis=0, tiled=True)  17.7 us
    unnamed x31, local copies, waits for them, and re-layouts  11.5 us
    pallas_call x1, Pallas kernels, output_parts(): pl.pallas_call(output_kernel, out_shape=[jax.ShapeDtypeStruct((count, 2,...  3.81 us
  transfers between devices with their start and end apart: 16, of which 9 were waited for; matrix products, arithmetic and copies ran while one was open for 5% of the time, Pallas kernels for 1%

profile of v7, /device:TPU:6, one launch (start us, length us, event | category | flops | bytes accessed | tf_op | source)
XLA Modules:
  0.0 173.4 jit_solution(11005441942595143227)
XLA Ops:
  2.1 15.1 %all-to-all-start = ((bf16[8,8,1536]{2,1,0:T(8,128)(2,1)}), bf16[8,8,1536]{2,1,0:T(8,128)(2,1)S(1)}, u32[]{:S(2)}, u32[]{:S(2)}) async-start(bf16[8,8,1536]{2,1,0:T(8,128)(2,1)} %broadcast_in_dim.4), calls=%async_computation | async-start | bytes 393216 | tf_op jit(solution)/shard_map/all_to_all | solution.py:27
  23.0 2.9 %collective-permute-start.1 = (bf16[2,48,3072]{2,1,0:T(8,128)(2,1)}, bf16[2,48,3072]{2,1,0:T(8,128)(2,1)}, u32[]{:S(2)}, u32[]{:S(2)}) collective-permute-start(bf16[2,48,3072]{2,1,0:T(8,128)(2,1)} %get-tuple-element.22), channel_id=1, source_target_pairs={{0,1},{1,0},{128,129},{129,128},{2,3},{3,2},{130,131},{131,130},{4... | collective-permute-start | bytes 1769480 | tf_op jit(solution)/shard_map/ppermute | solution.py:35
  25.9 2.7 %collective-permute-start.2 = (bf16[2,48,3072]{2,1,0:T(8,128)(2,1)}, bf16[2,48,3072]{2,1,0:T(8,128)(2,1)}, u32[]{:S(2)}, u32[]{:S(2)}) collective-permute-start(bf16[2,48,3072]{2,1,0:T(8,128)(2,1)} %get-tuple-element.23), channel_id=1, source_target_pairs={{0,128},{1,129},{128,0},{129,1},{2,130},{3,131},{130,2},{131,3},{4... | collective-permute-start | bytes 1769480 | tf_op jit(solution)/shard_map/ppermute | solution.py:35
  28.6 3.6 %collective-permute-start.3 = (bf16[2,48,3072]{2,1,0:T(8,128)(2,1)}, bf16[2,48,3072]{2,1,0:T(8,128)(2,1)}, u32[]{:S(2)}, u32[]{:S(2)}) collective-permute-start(bf16[2,48,3072]{2,1,0:T(8,128)(2,1)} %get-tuple-element.24), channel_id=1, source_target_pairs={{0,129},{1,128},{128,1},{129,0},{2,131},{3,130},{130,3},{131,2},{4... | collective-permute-start | bytes 1769480 | tf_op jit(solution)/shard_map/ppermute | solution.py:35
  32.2 3.6 %all-to-all-done.column_ref = bf16[8,8,1536]{2,1,0:T(8,128)(2,1)S(1)} async-done(((bf16[8,8,1536]{2,1,0:T(8,128)(2,1)}), bf16[8,8,1536]{2,1,0:T(8,128)(2,1)S(1)}, u32[]{:S(2)}, u32[]{:S(2)}) %all-to-all-start) | async-done | bytes 196640 | tf_op jit(solution)/shard_map/all_to_all | solution.py:27
  37.5 7.4 %all-to-all-start.1 = ((bf16[16,3,2,8,1536]{4,3,2,1,0:T(8,128)(2,1)}), bf16[16,3,2,8,1536]{4,3,2,1,0:T(8,128)(2,1)S(1)}, u32[]{:S(2)}, u32[]{:S(2)}) async-start(bf16[16,3,2,8,1536]{4,3,2,1,0:T(8,128)(2,1)} %copy-done), calls=%async_computation.1 | async-start | bytes 4718592 | tf_op jit(solution)/shard_map/all_to_all | solution.py:27
  44.9 12.0 %collective-permute-done.2.refs_2_ = bf16[2,48,3072]{2,1,0:T(8,128)(2,1)} collective-permute-done((bf16[2,48,3072]{2,1,0:T(8,128)(2,1)}, bf16[2,48,3072]{2,1,0:T(8,128)(2,1)}, u32[]{:S(2)}, u32[]{:S(2)}) %collective-permute-start.2) | collective-permute-done | bytes 589856 | tf_op jit(solution)/shard_map/ppermute | solution.py:35
  58.8 2.2 %collective-permute-done.4.refs_5_ = bf16[2,48,3072]{2,1,0:T(8,128)(2,1)S(1)} collective-permute-done((bf16[2,48,3072]{2,1,0:T(8,128)(2,1)}, bf16[2,48,3072]{2,1,0:T(8,128)(2,1)S(1)}, u32[]{:S(2)}, u32[]{:S(2)}) %collective-permute-start.4) | collective-permute-done | bytes 589856 | tf_op jit(solution)/shard_map/ppermute | solution.py:35
  61.8 2.0 %collective-permute-start.5 = (bf16[2,48,3072]{2,1,0:T(8,128)(2,1)}, bf16[2,48,3072]{2,1,0:T(8,128)(2,1)S(1)}, u32[]{:S(2)}, u32[]{:S(2)}) collective-permute-start(bf16[2,48,3072]{2,1,0:T(8,128)(2,1)} %collective-permute-done.2.refs_2_), channel_id=1, source_target_pairs={{0,8},{8,0},{1,9},{9,1},{2,10},{10,2},{3,11},{11,3},{4,12},{12,4},... | collective-permute-start | bytes 1769480 | tf_op jit(solution)/shard_map/ppermute | solution.py:35
  63.9 2.1 %collective-permute-done.5.refs_6_ = bf16[2,48,3072]{2,1,0:T(8,128)(2,1)S(1)} collective-permute-done((bf16[2,48,3072]{2,1,0:T(8,128)(2,1)}, bf16[2,48,3072]{2,1,0:T(8,128)(2,1)S(1)}, u32[]{:S(2)}, u32[]{:S(2)}) %collective-permute-start.5) | collective-permute-done | bytes 589856 | tf_op jit(solution)/shard_map/ppermute | solution.py:35
  66.8 2.0 %collective-permute-start.6 = (bf16[2,48,3072]{2,1,0:T(8,128)(2,1)}, bf16[2,48,3072]{2,1,0:T(8,128)(2,1)S(1)}, u32[]{:S(2)}, u32[]{:S(2)}) collective-permute-start(bf16[2,48,3072]{2,1,0:T(8,128)(2,1)} %collective-permute-done.3.refs_3_), channel_id=1, source_target_pairs={{0,8},{8,0},{1,9},{9,1},{2,10},{10,2},{3,11},{11,3},{4,12},{12,4},... | collective-permute-start | bytes 1769480 | tf_op jit(solution)/shard_map/ppermute | solution.py:35
  68.8 2.1 %collective-permute-done.6.refs_7_ = bf16[2,48,3072]{2,1,0:T(8,128)(2,1)S(1)} collective-permute-done((bf16[2,48,3072]{2,1,0:T(8,128)(2,1)}, bf16[2,48,3072]{2,1,0:T(8,128)(2,1)S(1)}, u32[]{:S(2)}, u32[]{:S(2)}) %collective-permute-start.6) | collective-permute-done | bytes 589856 | tf_op jit(solution)/shard_map/ppermute | solution.py:35
  71.7 12.4 %all-to-all-done.1.rows_ref = bf16[16,3,2,8,1536]{4,3,2,1,0:T(8,128)(2,1)S(1)} async-done(((bf16[16,3,2,8,1536]{4,3,2,1,0:T(8,128)(2,1)}), bf16[16,3,2,8,1536]{4,3,2,1,0:T(8,128)(2,1)S(1)}, u32[]{:S(2)}, u32[]{:S(2)}) %all-to-all-start.1) | async-done | bytes 2359328 | tf_op jit(solution)/shard_map/all_to_all | solution.py:27
  87.3 2.9 %hidden_parts.1 = (bf16[4,4,3,2,48,128]{5,4,3,2,1,0:T(8,128)(2,1)S(1)}, bf16[2,128,1536]{2,1,0:T(8,128)(2,1)S(1)}) custom-call(s32[1]{0:T(128)} %bitcast.member_ref, bf16[16,3,2,8,1536]{4,3,2,1,0:T(8,128)(2,1)S(1)} %all-to-all-done.1.rows_ref, bf16[2,48,3072]{2,1,0:T(8,128)(2,1)S(1)} %get-tuple-element.20.refs_0_, ...), custom_call_target="tpu_custom_call" | custom-call | flops 604000000 | bytes 6700000 | tf_op jit(solution)/shard_map/hidden_parts/pallas_call | solution.py:143
  91.1 17.7 %all_to_all.25.parts_ref = bf16[4,4,3,2,48,128]{5,4,3,2,1,0:T(8,128)(2,1)S(1)} all-to-all(bf16[4,4,3,2,48,128]{5,4,3,2,1,0:T(8,128)(2,1)S(1)} %get-tuple-element.28), channel_id=1, replica_groups=mesh['xh'=2,'xp'=2,'zh'=2,'y'=4,'c'=2,'z2'=2,'z1'=2,'zp'=2] {'xp','zp'}, dimensions={0} | all-to-all | bytes 2359296 | tf_op jit(solution)/shard_map/all_to_all | solution.py:27
  108.8 3.8 %output_parts.1 = (bf16[16,2,8,3072]{3,2,1,0:T(8,128)(2,1)}, bf16[2,2,1,2,48,128]{5,4,3,2,1,0:T(8,128)(2,1)S(1)}) custom-call(s32[1]{0:T(128)} %bitcast.member_ref, bf16[4,4,3,2,48,128]{5,4,3,2,1,0:T(8,128)(2,1)S(1)} %all_to_all.25.parts_ref, bf16[2,48,3072]{2,1,0:T(8,128)(2,1)S(1)} %get-tuple-element.20.refs_0_, ...), custom_call_target="tpu_custom_call" | custom-call | flops 604000000 | bytes 6700000 | tf_op jit(solution)/shard_map/output_parts/pallas_call | solution.py:189
  112.6 9.3 %all-to-all-start.3 = ((bf16[16,2,8,3072]{3,2,1,0:T(8,128)(2,1)}), bf16[16,2,8,3072]{3,2,1,0:T(8,128)(2,1)S(1)}, u32[]{:S(2)}, u32[]{:S(2)}) async-start(bf16[16,2,8,3072]{3,2,1,0:T(8,128)(2,1)} %get-tuple-element.29), calls=%async_computation.3 | async-start | bytes 3145728 | tf_op jit(solution)/shard_map/all_to_all | solution.py:27
  121.9 1.9 %collective-permute-start.7 = (bf16[2,128,1536]{2,1,0:T(8,128)(2,1)S(1)}, bf16[2,128,1536]{2,1,0:T(8,128)(2,1)S(1)}, u32[]{:S(2)}, u32[]{:S(2)}) collective-permute-start(bf16[2,128,1536]{2,1,0:T(8,128)(2,1)S(1)} %copy-done.13), channel_id=1, source_target_pairs={{0,8},{8,0},{1,9},{9,1},{2,10},{10,2},{3,11},{11,3},{4,12},{12,4},... | collective-permute-start | bytes 2359304 | tf_op jit(solution)/shard_map/ppermute | solution.py:35
  123.8 4.8 %collective-permute-start.8 = (bf16[2,2,1,2,48,128]{5,4,3,2,1,0:T(8,128)(2,1)S(1)}, bf16[2,2,1,2,48,128]{5,4,3,2,1,0:T(8,128)(2,1)S(1)}, u32[]{:S(2)}, u32[]{:S(2)}) collective-permute-start(bf16[2,2,1,2,48,128]{5,4,3,2,1,0:T(8,128)(2,1)S(1)} %get-tuple-element.32), channel_id=1, source_target_pairs={{0,2},{2,0},{4,6},{6,4},{1,3},{3,1},{5,7},{7,5},{8,10},{10,8},{12,... | collective-permute-start | bytes 294920 | tf_op jit(solution)/shard_map/ppermute | solution.py:35
  128.6 7.3 %collective-permute-start.9 = (bf16[2,2,1,2,48,128]{5,4,3,2,1,0:T(8,128)(2,1)S(1)}, bf16[2,2,1,2,48,128]{5,4,3,2,1,0:T(8,128)(2,1)}, u32[]{:S(2)}, u32[]{:S(2)}) collective-permute-start(bf16[2,2,1,2,48,128]{5,4,3,2,1,0:T(8,128)(2,1)S(1)} %get-tuple-element.32), channel_id=1, source_target_pairs={{0,4},{2,6},{4,0},{6,2},{1,5},{3,7},{5,1},{7,3},{8,12},{10,14},{12... | collective-permute-start | bytes 294920 | tf_op jit(solution)/shard_map/ppermute | solution.py:35
  135.9 1.9 %collective-permute-start.10 = (bf16[2,2,1,2,48,128]{5,4,3,2,1,0:T(8,128)(2,1)S(1)}, bf16[2,2,1,2,48,128]{5,4,3,2,1,0:T(8,128)(2,1)}, u32[]{:S(2)}, u32[]{:S(2)}) collective-permute-start(bf16[2,2,1,2,48,128]{5,4,3,2,1,0:T(8,128)(2,1)S(1)} %get-tuple-element.32), channel_id=1, source_target_pairs={{0,6},{2,4},{4,2},{6,0},{1,7},{3,5},{5,3},{7,1},{8,14},{10,12},{12... | collective-permute-start | bytes 294920 | tf_op jit(solution)/shard_map/ppermute | solution.py:35
  138.8 2.6 %all-to-all-done.3 = bf16[16,2,8,3072]{3,2,1,0:T(8,128)(2,1)S(1)} async-done(((bf16[16,2,8,3072]{3,2,1,0:T(8,128)(2,1)}), bf16[16,2,8,3072]{3,2,1,0:T(8,128)(2,1)S(1)}, u32[]{:S(2)}, u32[]{:S(2)}) %all-to-all-start.3) | async-done | bytes 1572896 | tf_op jit(solution)/shard_map/all_to_all | solution.py:27
  144.2 12.1 %all-to-all-start.4 = ((bf16[8,2,4,1536]{3,2,1,0:T(4,128)(2,1)}), bf16[8,2,4,1536]{3,2,1,0:T(4,128)(2,1)S(1)}, u32[]{:S(2)}, u32[]{:S(2)}) async-start(bf16[8,2,4,1536]{3,2,1,0:T(4,128)(2,1)} %bitcast.30), calls=%async_computation.4 | async-start | bytes 393216 | tf_op jit(solution)/shard_map/all_to_all | solution.py:27
  164.8 7.9 %all-to-all-done.4 = bf16[8,2,4,1536]{3,2,1,0:T(4,128)(2,1)S(1)} async-done(((bf16[8,2,4,1536]{3,2,1,0:T(4,128)(2,1)}), bf16[8,2,4,1536]{3,2,1,0:T(4,128)(2,1)S(1)}, u32[]{:S(2)}, u32[]{:S(2)}) %all-to-all-start.4) | async-done | bytes 196640 | tf_op jit(solution)/shard_map/all_to_all | solution.py:27
  (60 shorter events, 30.2 us)
Async XLA Ops:
  2.1 33.8 %all-to-all-start = ((bf16[8,8,1536]{2,1,0:T(8,128)(2,1)}), bf16[8,8,1536]{2,1,0:T(8,128)(2,1)S(1)}, u32[]{:S(2)}, u32[]{:S(2)}) async-start(bf16[8,8,1536]{2,1,0:T(8,128)(2,1)} %broadcast_in_dim.4), calls=%async_computation | async-start | bytes 393216 | tf_op jit(solution)/shard_map/all_to_all | solution.py:27
  17.2 1.3 copy-start.10
  18.4 1.3 copy-start.11
  21.0 11.2 %collective-permute-start = (bf16[2,48,3072]{2,1,0:T(8,128)(2,1)S(1)}, bf16[2,48,3072]{2,1,0:T(8,128)(2,1)S(1)}, u32[]{:S(2)}, u32[]{:S(2)}) collective-permute-start(bf16[2,48,3072]{2,1,0:T(8,128)(2,1)S(1)} %get-tuple-element.20.refs_0_), channel_id=1, source_target_pairs={{0,8},{8,0},{1,9},{9,1},{2,10},{10,2},{3,11},{11,3},{4,12},{12,4},... | collective-permute-start | bytes 1769480 | tf_op jit(solution)/shard_map/ppermute | solution.py:35
  23.0 21.9 %collective-permute-start.1 = (bf16[2,48,3072]{2,1,0:T(8,128)(2,1)}, bf16[2,48,3072]{2,1,0:T(8,128)(2,1)}, u32[]{:S(2)}, u32[]{:S(2)}) collective-permute-start(bf16[2,48,3072]{2,1,0:T(8,128)(2,1)} %get-tuple-element.22), channel_id=1, source_target_pairs={{0,1},{1,0},{128,129},{129,128},{2,3},{3,2},{130,131},{131,130},{4... | collective-permute-start | bytes 1769480 | tf_op jit(solution)/shard_map/ppermute | solution.py:35
  25.9 31.0 %collective-permute-start.2 = (bf16[2,48,3072]{2,1,0:T(8,128)(2,1)}, bf16[2,48,3072]{2,1,0:T(8,128)(2,1)}, u32[]{:S(2)}, u32[]{:S(2)}) collective-permute-start(bf16[2,48,3072]{2,1,0:T(8,128)(2,1)} %get-tuple-element.23), channel_id=1, source_target_pairs={{0,128},{1,129},{128,0},{129,1},{2,130},{3,131},{130,2},{131,3},{4... | collective-permute-start | bytes 1769480 | tf_op jit(solution)/shard_map/ppermute | solution.py:35
  28.6 28.3 %collective-permute-start.3 = (bf16[2,48,3072]{2,1,0:T(8,128)(2,1)}, bf16[2,48,3072]{2,1,0:T(8,128)(2,1)}, u32[]{:S(2)}, u32[]{:S(2)}) collective-permute-start(bf16[2,48,3072]{2,1,0:T(8,128)(2,1)} %get-tuple-element.24), channel_id=1, source_target_pairs={{0,129},{1,128},{128,1},{129,0},{2,131},{3,130},{130,3},{131,2},{4... | collective-permute-start | bytes 1769480 | tf_op jit(solution)/shard_map/ppermute | solution.py:35
  36.0 1.4 copy-start
  37.5 46.7 %all-to-all-start.1 = ((bf16[16,3,2,8,1536]{4,3,2,1,0:T(8,128)(2,1)}), bf16[16,3,2,8,1536]{4,3,2,1,0:T(8,128)(2,1)S(1)}, u32[]{:S(2)}, u32[]{:S(2)}) async-start(bf16[16,3,2,8,1536]{4,3,2,1,0:T(8,128)(2,1)} %copy-done), calls=%async_computation.1 | async-start | bytes 4718592 | tf_op jit(solution)/shard_map/all_to_all | solution.py:27
  56.9 4.1 %collective-permute-start.4 = (bf16[2,48,3072]{2,1,0:T(8,128)(2,1)}, bf16[2,48,3072]{2,1,0:T(8,128)(2,1)S(1)}, u32[]{:S(2)}, u32[]{:S(2)}) collective-permute-start(bf16[2,48,3072]{2,1,0:T(8,128)(2,1)} %collective-permute-done.1.refs_1_), channel_id=1, source_target_pairs={{0,8},{8,0},{1,9},{9,1},{2,10},{10,2},{3,11},{11,3},{4,12},{12,4},... | collective-permute-start | bytes 1769480 | tf_op jit(solution)/shard_map/ppermute | solution.py:35
  61.8 4.1 %collective-permute-start.5 = (bf16[2,48,3072]{2,1,0:T(8,128)(2,1)}, bf16[2,48,3072]{2,1,0:T(8,128)(2,1)S(1)}, u32[]{:S(2)}, u32[]{:S(2)}) collective-permute-start(bf16[2,48,3072]{2,1,0:T(8,128)(2,1)} %collective-permute-done.2.refs_2_), channel_id=1, source_target_pairs={{0,8},{8,0},{1,9},{9,1},{2,10},{10,2},{3,11},{11,3},{4,12},{12,4},... | collective-permute-start | bytes 1769480 | tf_op jit(solution)/shard_map/ppermute | solution.py:35
  66.8 4.1 %collective-permute-start.6 = (bf16[2,48,3072]{2,1,0:T(8,128)(2,1)}, bf16[2,48,3072]{2,1,0:T(8,128)(2,1)S(1)}, u32[]{:S(2)}, u32[]{:S(2)}) collective-permute-start(bf16[2,48,3072]{2,1,0:T(8,128)(2,1)} %collective-permute-done.3.refs_3_), channel_id=1, source_target_pairs={{0,8},{8,0},{1,9},{9,1},{2,10},{10,2},{3,11},{11,3},{4,12},{12,4},... | collective-permute-start | bytes 1769480 | tf_op jit(solution)/shard_map/ppermute | solution.py:35
  91.1 17.7 %copy-start.3 = (bf16[2,48,3072]{2,1,0:T(8,128)(2,1)S(1)}, bf16[2,48,3072]{2,1,0:T(8,128)(2,1)}, u32[]{:S(2)}) copy-start(bf16[2,48,3072]{2,1,0:T(8,128)(2,1)} %copy-done.1) | copy-start | bytes 1769476
  91.1 17.7 %copy-start.6 = (bf16[2,48,3072]{2,1,0:T(8,128)(2,1)S(1)}, bf16[2,48,3072]{2,1,0:T(8,128)(2,1)}, u32[]{:S(2)}) copy-start(bf16[2,48,3072]{2,1,0:T(8,128)(2,1)} %copy-done.4) | copy-start | bytes 1769476
  91.1 17.7 %copy-start.9 = (bf16[2,48,3072]{2,1,0:T(8,128)(2,1)S(1)}, bf16[2,48,3072]{2,1,0:T(8,128)(2,1)}, u32[]{:S(2)}) copy-start(bf16[2,48,3072]{2,1,0:T(8,128)(2,1)} %copy-done.7) | copy-start | bytes 1769476
  112.6 9.3 %copy-start.13 = (bf16[2,128,1536]{2,1,0:T(8,128)(2,1)S(1)}, bf16[2,128,1536]{2,1,0:T(8,128)(2,1)}, u32[]{:S(2)}) copy-start(bf16[2,128,1536]{2,1,0:T(8,128)(2,1)} %copy-done.12) | copy-start | bytes 2359300
  112.6 28.8 %all-to-all-start.3 = ((bf16[16,2,8,3072]{3,2,1,0:T(8,128)(2,1)}), bf16[16,2,8,3072]{3,2,1,0:T(8,128)(2,1)S(1)}, u32[]{:S(2)}, u32[]{:S(2)}) async-start(bf16[16,2,8,3072]{3,2,1,0:T(8,128)(2,1)} %get-tuple-element.29), calls=%async_computation.3 | async-start | bytes 3145728 | tf_op jit(solution)/shard_map/all_to_all | solution.py:27
  121.9 38.4 %collective-permute-start.7 = (bf16[2,128,1536]{2,1,0:T(8,128)(2,1)S(1)}, bf16[2,128,1536]{2,1,0:T(8,128)(2,1)S(1)}, u32[]{:S(2)}, u32[]{:S(2)}) collective-permute-start(bf16[2,128,1536]{2,1,0:T(8,128)(2,1)S(1)} %copy-done.13), channel_id=1, source_target_pairs={{0,8},{8,0},{1,9},{9,1},{2,10},{10,2},{3,11},{11,3},{4,12},{12,4},... | collective-permute-start | bytes 2359304 | tf_op jit(solution)/shard_map/ppermute | solution.py:35
  123.8 32.5 %collective-permute-start.8 = (bf16[2,2,1,2,48,128]{5,4,3,2,1,0:T(8,128)(2,1)S(1)}, bf16[2,2,1,2,48,128]{5,4,3,2,1,0:T(8,128)(2,1)S(1)}, u32[]{:S(2)}, u32[]{:S(2)}) collective-permute-start(bf16[2,2,1,2,48,128]{5,4,3,2,1,0:T(8,128)(2,1)S(1)} %get-tuple-element.32), channel_id=1, source_target_pairs={{0,2},{2,0},{4,6},{6,4},{1,3},{3,1},{5,7},{7,5},{8,10},{10,8},{12,... | collective-permute-start | bytes 294920 | tf_op jit(solution)/shard_map/ppermute | solution.py:35
  128.6 27.7 %collective-permute-start.9 = (bf16[2,2,1,2,48,128]{5,4,3,2,1,0:T(8,128)(2,1)S(1)}, bf16[2,2,1,2,48,128]{5,4,3,2,1,0:T(8,128)(2,1)}, u32[]{:S(2)}, u32[]{:S(2)}) collective-permute-start(bf16[2,2,1,2,48,128]{5,4,3,2,1,0:T(8,128)(2,1)S(1)} %get-tuple-element.32), channel_id=1, source_target_pairs={{0,4},{2,6},{4,0},{6,2},{1,5},{3,7},{5,1},{7,3},{8,12},{10,14},{12... | collective-permute-start | bytes 294920 | tf_op jit(solution)/shard_map/ppermute | solution.py:35
  135.9 20.4 %collective-permute-start.10 = (bf16[2,2,1,2,48,128]{5,4,3,2,1,0:T(8,128)(2,1)S(1)}, bf16[2,2,1,2,48,128]{5,4,3,2,1,0:T(8,128)(2,1)}, u32[]{:S(2)}, u32[]{:S(2)}) collective-permute-start(bf16[2,2,1,2,48,128]{5,4,3,2,1,0:T(8,128)(2,1)S(1)} %get-tuple-element.32), channel_id=1, source_target_pairs={{0,6},{2,4},{4,2},{6,0},{1,7},{3,5},{5,3},{7,1},{8,14},{10,12},{12... | collective-permute-start | bytes 294920 | tf_op jit(solution)/shard_map/ppermute | solution.py:35
  142.3 18.0 %copy-start.14 = (bf16[2,256,1536]{2,1,0:T(8,128)(2,1)S(1)}, bf16[2,256,1536]{2,1,0:T(8,128)(2,1)}, u32[]{:S(2)}) copy-start(bf16[2,256,1536]{2,1,0:T(8,128)(2,1)} %constant_dynamic-update-slice_fusion.1) | copy-start | bytes 4718596
  144.2 28.4 %all-to-all-start.4 = ((bf16[8,2,4,1536]{3,2,1,0:T(4,128)(2,1)}), bf16[8,2,4,1536]{3,2,1,0:T(4,128)(2,1)S(1)}, u32[]{:S(2)}, u32[]{:S(2)}) async-start(bf16[8,2,4,1536]{3,2,1,0:T(4,128)(2,1)} %bitcast.30), calls=%async_computation.4 | async-start | bytes 393216 | tf_op jit(solution)/shard_map/all_to_all | solution.py:27
  158.3 3.3 %collective-permute-start.11 = (bf16[2,384,128]{2,1,0:T(8,128)(2,1)S(1)}, bf16[2,384,128]{2,1,0:T(8,128)(2,1)S(1)}, u32[]{:S(2)}, u32[]{:S(2)}) collective-permute-start(bf16[2,384,128]{2,1,0:T(8,128)(2,1)S(1)} %bitcast.32), channel_id=1, source_target_pairs={{0,8},{8,0},{1,9},{9,1},{2,10},{10,2},{3,11},{11,3},{4,12},{12,4},... | collective-permute-start | bytes 589832 | tf_op jit(solution)/shard_map/ppermute | solution.py:35
  (7 other events, 6.6 us)

commit v8 on v6

--- a/solution.py
+++ b/solution.py
@@ -39,14 +39,17 @@
     return partner(value, "c", 2, 1)
 
 
-def gather_ring(value, axes, count, dim, *others):
-    here = lax.axis_index(axes)
-    shape = list(value.shape)
+def blocks_of(value, axes, count):
+    return [value] + [partner(value, axes, count, step) for step in range(1, count)]
+
+
+def in_order(blocks, axes, dim, *others):
+    count, here = len(blocks), lax.axis_index(axes)
+    shape = list(blocks[0].shape)
     shape[dim] = count
     start = [0] * len(shape)
-    whole = jnp.zeros(shape, value.dtype)
-    blocks = [value] + [partner(value, axes, count, step) for step in range(1, count)]
-    for step, block in enumerate(lax.optimization_barrier(blocks + list(others))[:count]):
+    whole = jnp.zeros(shape, blocks[0].dtype)
+    for step, block in enumerate(lax.optimization_barrier(list(blocks) + list(others))[:count]):
         start[dim] = here ^ step
         whole = lax.dynamic_update_slice(whole, block, tuple(start))
     return whole
@@ -199,35 +202,70 @@
     )(member, parts, *own, *beside)
 
 
+def sum_kernel(arrived_ref, out_ref):
+    width = out_ref.shape[3]
+    for near in range(2):
+        for array in range(2):
+            total = None
+            for half in range(2):
+                for line in range(4):
+                    term = arrived_ref[half * 8 + near * 4 + line, array].astype(F32)
+                    total = term if total is None else total + term
+            for end in range(2):
+                for far in range(2):
+                    rows = total[end * 4 : end * 4 + 4, far * width : (far + 1) * width]
+                    out_ref[end * 4 + far * 2 + near, array] = rows.astype(BF16)
+
+
+def plane_sums(arrived):
+    width = arrived.shape[3] // 2
+    return pl.pallas_call(
+        sum_kernel,
+        out_shape=jax.ShapeDtypeStruct((8, 2, 4, width), BF16),
+        in_specs=[pl.BlockSpec(memory_space=pltpu.VMEM)],
+        out_specs=pl.BlockSpec(memory_space=pltpu.VMEM),
+        compiler_params=pltpu.CompilerParams(vmem_limit_bytes=VMEM_BYTES),
+        cost_estimate=pl.CostEstimate(flops=800_000, bytes_accessed=1_800_000, transcendentals=0),
+        name="plane_sums",
+    )(arrived)
+
+
 def local(tokens, up_proj, down_proj, out_grad):
     width = tokens.shape[1]
     units = down_proj.shape[0]
     member = lax.axis_index(GROUP).reshape(1).astype(jnp.int32)
 
     pieces = cut(member, up_proj.T, down_proj)
-    own = [pieces[0]] + [partner(pieces[step], GROUP, 4, step) for step in range(1, 4)]
-    beside = [other_core(piece) for piece in own]
-
+    beside = [other_core(pieces[0])]
+
+    sideways = partner(pieces[2], GROUP, 4, 2)
     both = after(jnp.concatenate([tokens, out_grad], axis=0), beside[0])
     column = spread(both, COLUMN, 8)
-    sent, mine = lay_out(lax.axis_index(("z2", "z1")).reshape(1).astype(jnp.int32), after(column, *beside))
+    block = lax.axis_index(("z2", "z1")).reshape(1).astype(jnp.int32)
+    sent, mine = lay_out(block, column)
     plane = exchange(sent, PLANE)
 
-    lines = gather_ring(after(mine, sent), "y", 4, 2)
-    parts = hidden_parts(after(member, lines), plane, own, beside)
+    own = [pieces[0], partner(after(pieces[1], column), GROUP, 4, 1), sideways]
+    own.append(partner(after(pieces[3], column), GROUP, 4, 3))
+    rows = blocks_of(mine, ("xh", "xp"), 4)
+    waits = own[1:] + rows
+    for piece in own[1:]:
+        beside.append(other_core(after(piece, *waits)))
+        waits = beside[1:2]
+
+    flat = in_order(rows, ("xh", "xp"), 1)
+    parts = hidden_parts(after(member, flat), plane, own, beside)
     arrived = exchange(parts, GROUP)
-    flat = gather_ring(after(lines, parts), ("xh", "xp"), 4, 1).reshape(2, 128, width)
-
-    partials, pair = output_parts(after(member, flat), arrived, own, beside, 16)
+    flats = blocks_of(after(flat, parts), "y", 4)
+
+    partials, pair = output_parts(after(member, *flats), arrived, own, beside, 16)
     arrived = exchange(partials, PLANE)
-    summed = jnp.sum(arrived.reshape(2, 2, 4, 2, 8, 2 * width).astype(F32), axis=(0, 2))
-    summed = summed.astype(BF16).reshape(2, 2, 2, 4, 2, width)
-    summed = summed.transpose(2, 4, 0, 1, 3, 5).reshape(8, 2, 4, width)
+    summed = plane_sums(arrived)
     ends = jnp.sum(exchange(summed, COLUMN).astype(F32), axis=0).astype(BF16)
 
+    flat = in_order(flats, "y", 2, partials).reshape(2, 128, width)
     flat = jnp.concatenate([flat, other_core(flat)], axis=1)
-    lines = gather_ring(pair, "z2", 2, 2)[:, :, :, None]
-    lines = gather_ring(lines, "z1", 2, 3, arrived)
+    lines = in_order(blocks_of(pair, ("z2", "z1"), 4), ("z2", "z1"), 2, arrived)
     lines = lines.reshape(2, 2, 8 * units, 128)
     units_all = jnp.concatenate([lines[0], other_core(lines[1])], axis=2)
     down_grad = dot(units_all[0], flat[1], 1, 0).astype(BF16)

time: 191 us -> 180 us (0.942)
  waiting for transfers between devices: 74 us -> 57 us
  starting transfers between devices: 84.2 us -> 94.4 us
  local copies, waits for them, and re-layouts: 19 us -> 11.5 us
  matrix products: 3.12 us -> 5.11 us
    ppermute x17 -> x18, waiting for transfers between devices: 52.2 us -> 32.4 us  [partner(): return lax.ppermute(value, axes, [(at, at ^ step) for at in range(count)])]
    ppermute x17 -> x18, starting transfers between devices: 46 us -> 55.6 us  [partner(): return lax.ppermute(value, axes, [(at, at ^ step) for at in range(count)])]
    unnamed x32 -> x12, local copies, waits for them, and re-layouts: 12.3 us -> 4.86 us
    all_to_all x5, waiting for transfers between devices: 21.8 us -> 24.6 us  [exchange(): return lax.all_to_all(value, axes, split_axis=0, concat_axis=0, tiled=True)]
    dot_general x2, matrix products: 3.12 us -> 5.11 us  [dot(): lax.dot_general(left, right, (((left_dim,), (right_dim,)), ((), ())), pre...]
  transfers between devices with their start and end apart: 22 -> 23, of which waited for: 11 -> 10; matrix products, arithmetic and copies ran while one was open for 5% -> 6% of each run, Pallas kernels for 0% -> 1%
where the time goes in v8:
time: 180 us; the launch traced here: 179 us
  starting transfers between devices  94.4 us (52%)
  waiting for transfers between devices  57 us (32%)
  local copies, waits for them, and re-layouts  11.5 us (6%)
  Pallas kernels  9.56 us (5%)
  matrix products  5.11 us (3%)
    ppermute x18, starting transfers between devices, partner(): return lax.ppermute(value, axes, [(at, at ^ step) for at in range(count)])  55.6 us
    all_to_all x5, starting transfers between devices, exchange(): return lax.all_to_all(value, axes, split_axis=0, concat_axis=0, tiled=True)  38.8 us
    ppermute x18, waiting for transfers between devices, partner(): return lax.ppermute(value, axes, [(at, at ^ step) for at in range(count)])  32.4 us
    all_to_all x5, waiting for transfers between devices, exchange(): return lax.all_to_all(value, axes, split_axis=0, concat_axis=0, tiled=True)  24.6 us
    dot_general x2, matrix products, dot(): lax.dot_general(left, right, (((left_dim,), (right_dim,)), ((), ())), pre...  5.11 us
    unnamed x12, local copies, waits for them, and re-layouts  4.86 us
    dynamic_update_slice x12, local copies, waits for them, and re-layouts, in_order(): whole = lax.dynamic_update_slice(whole, block, tuple(start))  4.51 us
    pallas_call x1, Pallas kernels, hidden_parts(): pl.pallas_call(hidden_kernel, out_shape=jax.ShapeDtypeStruct((4, 4, 3, 2,...  4.23 us
  transfers between devices with their start and end apart: 23, of which 10 were waited for; matrix products, arithmetic and copies ran while one was open for 6% of the time, Pallas kernels for 1%

profile of v8, /device:TPU:6, one launch (start us, length us, event | category | flops | bytes accessed | tf_op | source)
XLA Modules:
  0.0 178.7 jit_solution(12081886942148430767)
XLA Ops:
  9.1 15.1 %all-to-all-start = ((bf16[8,8,1536]{2,1,0:T(8,128)(2,1)}), bf16[8,8,1536]{2,1,0:T(8,128)(2,1)S(1)}, u32[]{:S(2)}, u32[]{:S(2)}) async-start(bf16[8,8,1536]{2,1,0:T(8,128)(2,1)} %broadcast_in_dim.16), calls=%async_computation | async-start | bytes 393216 | tf_op jit(solution)/shard_map/all_to_all | solution.py:27
  24.2 2.7 %collective-permute-start.5 = (bf16[2,48,3072]{2,1,0:T(8,128)(2,1)}, bf16[2,48,3072]{2,1,0:T(8,128)(2,1)S(1)}, u32[]{:S(2)}, u32[]{:S(2)}) collective-permute-start(bf16[2,48,3072]{2,1,0:T(8,128)(2,1)} %get-tuple-element.44), channel_id=1, source_target_pairs={{0,128},{1,129},{128,0},{129,1},{2,130},{3,131},{130,2},{131,3},{4... | collective-permute-start | bytes 1769480 | tf_op jit(solution)/shard_map/ppermute | solution.py:35
  26.9 16.2 %all-to-all-done.column_ref = bf16[8,8,1536]{2,1,0:T(8,128)(2,1)S(1)} async-done(((bf16[8,8,1536]{2,1,0:T(8,128)(2,1)}), bf16[8,8,1536]{2,1,0:T(8,128)(2,1)S(1)}, u32[]{:S(2)}, u32[]{:S(2)}) %all-to-all-start) | async-done | bytes 196640 | tf_op jit(solution)/shard_map/all_to_all | solution.py:27
  45.7 3.5 %collective-permute-start.4 = (bf16[2,48,3072]{2,1,0:T(8,128)(2,1)}, bf16[2,48,3072]{2,1,0:T(8,128)(2,1)}, u32[]{:S(2)}, u32[]{:S(2)}) collective-permute-start(bf16[2,48,3072]{2,1,0:T(8,128)(2,1)} %get-tuple-element.43), channel_id=1, source_target_pairs={{0,1},{1,0},{128,129},{129,128},{2,3},{3,2},{130,131},{131,130},{4... | collective-permute-start | bytes 1769480 | tf_op jit(solution)/shard_map/ppermute | solution.py:35
  50.6 7.8 %all-to-all-start.1 = ((bf16[16,2,2,8,1536]{4,3,2,1,0:T(8,128)(2,1)}), bf16[16,2,2,8,1536]{4,3,2,1,0:T(8,128)(2,1)S(1)}, u32[]{:S(2)}, u32[]{:S(2)}) async-start(bf16[16,2,2,8,1536]{4,3,2,1,0:T(8,128)(2,1)} %copy-done.1), calls=%async_computation.1 | async-start | bytes 3145728 | tf_op jit(solution)/shard_map/all_to_all | solution.py:27
  58.4 2.8 %collective-permute-start.1 = (bf16[2,1,1,8,1536]{4,3,2,1,0:T(8,128)(2,1)S(1)}, bf16[2,1,1,8,1536]{4,3,2,1,0:T(8,128)(2,1)S(1)}, u32[]{:S(2)}, u32[]{:S(2)}) collective-permute-start(bf16[2,1,1,8,1536]{4,3,2,1,0:T(8,128)(2,1)S(1)} %get-tuple-element.36), channel_id=1, source_target_pairs={{0,128},{128,0},{256,384},{384,256},{1,129},{129,1},{257,385},{385... | collective-permute-start | bytes 147464 | tf_op jit(solution)/shard_map/ppermute | solution.py:35
  61.1 2.6 %collective-permute-start.2 = (bf16[2,1,1,8,1536]{4,3,2,1,0:T(8,128)(2,1)S(1)}, bf16[2,1,1,8,1536]{4,3,2,1,0:T(8,128)(2,1)S(1)}, u32[]{:S(2)}, u32[]{:S(2)}) collective-permute-start(bf16[2,1,1,8,1536]{4,3,2,1,0:T(8,128)(2,1)S(1)} %get-tuple-element.36), channel_id=1, source_target_pairs={{0,256},{128,384},{256,0},{384,128},{1,257},{129,385},{257,1},{385... | collective-permute-start | bytes 147464 | tf_op jit(solution)/shard_map/ppermute | solution.py:35
  63.8 5.0 %collective-permute-start.3 = (bf16[2,1,1,8,1536]{4,3,2,1,0:T(8,128)(2,1)S(1)}, bf16[2,1,1,8,1536]{4,3,2,1,0:T(8,128)(2,1)S(1)}, u32[]{:S(2)}, u32[]{:S(2)}) collective-permute-start(bf16[2,1,1,8,1536]{4,3,2,1,0:T(8,128)(2,1)S(1)} %get-tuple-element.36), channel_id=1, source_target_pairs={{0,384},{128,256},{256,128},{384,0},{1,385},{129,257},{257,129},{3... | collective-permute-start | bytes 147464 | tf_op jit(solution)/shard_map/ppermute | solution.py:35
  68.8 9.5 %collective-permute-done.1 = bf16[2,1,1,8,1536]{4,3,2,1,0:T(8,128)(2,1)S(1)} collective-permute-done((bf16[2,1,1,8,1536]{4,3,2,1,0:T(8,128)(2,1)S(1)}, bf16[2,1,1,8,1536]{4,3,2,1,0:T(8,128)(2,1)S(1)}, u32[]{:S(2)}, u32[]{:S(2)}) %collective-permute-start.1) | collective-permute-done | bytes 49184 | tf_op jit(solution)/shard_map/ppermute | solution.py:35
  88.9 4.2 %hidden_parts.1 = bf16[4,4,3,2,48,128]{5,4,3,2,1,0:T(8,128)(2,1)} custom-call(s32[1]{0:T(128)} %bitcast.member_ref, bf16[16,2,2,8,1536]{4,3,2,1,0:T(8,128)(2,1)S(1)} %all-to-all-done.1.rows_ref, bf16[2,48,3072]{2,1,0:T(8,128)(2,1)S(1)} %get-tuple-element.33.refs_0_, bf16[2,48,3072]{2,1,0:T(8,128)(2,1)} %collective-permute-done.4.refs_1_, ...), custom_call_target="tpu_custom_call" | custom-call | flops 604000000 | bytes 6700000 | tf_op jit(solution)/shard_map/hidden_parts/pallas_call | solution.py:148
  93.1 3.9 %all-to-all-start.2 = ((bf16[4,4,3,2,48,128]{5,4,3,2,1,0:T(8,128)(2,1)}), bf16[4,4,3,2,48,128]{5,4,3,2,1,0:T(8,128)(2,1)S(1)}, u32[]{:S(2)}, u32[]{:S(2)}) async-start(bf16[4,4,3,2,48,128]{5,4,3,2,1,0:T(8,128)(2,1)} %hidden_parts.1), calls=%async_computation.2 | async-start | bytes 2359296 | tf_op jit(solution)/shard_map/all_to_all | solution.py:27
  97.0 3.5 %collective-permute-start.10 = (bf16[2,4,1,8,1536]{4,3,2,1,0:T(8,128)(2,1)}, bf16[2,4,1,8,1536]{4,3,2,1,0:T(8,128)(2,1)S(1)}, u32[]{:S(2)}, u32[]{:S(2)}) collective-permute-start(bf16[2,4,1,8,1536]{4,3,2,1,0:T(8,128)(2,1)} %constant_dynamic-update-slice_fusion.8), channel_id=1, source_target_pairs={{0,16},{16,0},{32,48},{48,32},{1,17},{17,1},{33,49},{49,33},{2,18}... | collective-permute-start | bytes 589832 | tf_op jit(solution)/shard_map/ppermute | solution.py:35
  100.4 4.9 %collective-permute-start.11 = (bf16[2,4,1,8,1536]{4,3,2,1,0:T(8,128)(2,1)}, bf16[2,4,1,8,1536]{4,3,2,1,0:T(8,128)(2,1)S(1)}, u32[]{:S(2)}, u32[]{:S(2)}) collective-permute-start(bf16[2,4,1,8,1536]{4,3,2,1,0:T(8,128)(2,1)} %constant_dynamic-update-slice_fusion.8), channel_id=1, source_target_pairs={{0,32},{16,48},{32,0},{48,16},{1,33},{17,49},{33,1},{49,17},{2,34}... | collective-permute-start | bytes 589832 | tf_op jit(solution)/shard_map/ppermute | solution.py:35
  107.4 5.3 %collective-permute-done.11 = bf16[2,4,1,8,1536]{4,3,2,1,0:T(8,128)(2,1)S(1)} collective-permute-done((bf16[2,4,1,8,1536]{4,3,2,1,0:T(8,128)(2,1)}, bf16[2,4,1,8,1536]{4,3,2,1,0:T(8,128)(2,1)S(1)}, u32[]{:S(2)}, u32[]{:S(2)}) %collective-permute-start.11) | collective-permute-done | bytes 196640 | tf_op jit(solution)/shard_map/ppermute | solution.py:35
  112.7 4.2 %collective-permute-done.12 = bf16[2,4,1,8,1536]{4,3,2,1,0:T(8,128)(2,1)} collective-permute-done((bf16[2,4,1,8,1536]{4,3,2,1,0:T(8,128)(2,1)}, bf16[2,4,1,8,1536]{4,3,2,1,0:T(8,128)(2,1)}, u32[]{:S(2)}, u32[]{:S(2)}) %collective-permute-start.12) | collective-permute-done | bytes 196640 | tf_op jit(solution)/shard_map/ppermute | solution.py:35
  116.9 3.0 %output_parts.1 = (bf16[16,2,8,3072]{3,2,1,0:T(8,128)(2,1)S(1)}, bf16[2,2,1,2,48,128]{5,4,3,2,1,0:T(8,128)(2,1)S(1)}) custom-call(s32[1]{0:T(128)} %bitcast.member_ref, bf16[4,4,3,2,48,128]{5,4,3,2,1,0:T(8,128)(2,1)S(1)} %all-to-all-done.2.parts_ref, bf16[2,48,3072]{2,1,0:T(8,128)(2,1)S(1)} %get-tuple-element.33.refs_0_, ...), custom_call_target="tpu_custom_call" | custom-call | flops 604000000 | bytes 6700000 | tf_op jit(solution)/shard_map/output_parts/pallas_call | solution.py:191
  121.1 5.7 %all-to-all-start.3 = ((bf16[16,2,8,3072]{3,2,1,0:T(8,128)(2,1)}), bf16[16,2,8,3072]{3,2,1,0:T(8,128)(2,1)S(1)}, u32[]{:S(2)}, u32[]{:S(2)}) async-start(bf16[16,2,8,3072]{3,2,1,0:T(8,128)(2,1)} %copy-done), calls=%async_computation.3 | async-start | bytes 3145728 | tf_op jit(solution)/shard_map/all_to_all | solution.py:27
  126.8 3.8 %collective-permute-start.14 = (bf16[2,2,1,2,48,128]{5,4,3,2,1,0:T(8,128)(2,1)S(1)}, bf16[2,2,1,2,48,128]{5,4,3,2,1,0:T(8,128)(2,1)S(1)}, u32[]{:S(2)}, u32[]{:S(2)}) collective-permute-start(bf16[2,2,1,2,48,128]{5,4,3,2,1,0:T(8,128)(2,1)S(1)} %get-tuple-element.58), channel_id=1, source_target_pairs={{0,2},{2,0},{4,6},{6,4},{1,3},{3,1},{5,7},{7,5},{8,10},{10,8},{12,... | collective-permute-start | bytes 294920 | tf_op jit(solution)/shard_map/ppermute | solution.py:35
  130.6 3.0 %collective-permute-start.15 = (bf16[2,2,1,2,48,128]{5,4,3,2,1,0:T(8,128)(2,1)S(1)}, bf16[2,2,1,2,48,128]{5,4,3,2,1,0:T(8,128)(2,1)S(1)}, u32[]{:S(2)}, u32[]{:S(2)}) collective-permute-start(bf16[2,2,1,2,48,128]{5,4,3,2,1,0:T(8,128)(2,1)S(1)} %get-tuple-element.58), channel_id=1, source_target_pairs={{0,4},{2,6},{4,0},{6,2},{1,5},{3,7},{5,1},{7,3},{8,12},{10,14},{12... | collective-permute-start | bytes 294920 | tf_op jit(solution)/shard_map/ppermute | solution.py:35
  133.6 7.2 %collective-permute-start.16 = (bf16[2,2,1,2,48,128]{5,4,3,2,1,0:T(8,128)(2,1)S(1)}, bf16[2,2,1,2,48,128]{5,4,3,2,1,0:T(8,128)(2,1)S(1)}, u32[]{:S(2)}, u32[]{:S(2)}) collective-permute-start(bf16[2,2,1,2,48,128]{5,4,3,2,1,0:T(8,128)(2,1)S(1)} %get-tuple-element.58), channel_id=1, source_target_pairs={{0,6},{2,4},{4,2},{6,0},{1,7},{3,5},{5,3},{7,1},{8,14},{10,12},{12... | collective-permute-start | bytes 294920 | tf_op jit(solution)/shard_map/ppermute | solution.py:35
  144.7 9.0 %collective-permute-done.15 = bf16[2,2,1,2,48,128]{5,4,3,2,1,0:T(8,128)(2,1)S(1)} collective-permute-done((bf16[2,2,1,2,48,128]{5,4,3,2,1,0:T(8,128)(2,1)S(1)}, bf16[2,2,1,2,48,128]{5,4,3,2,1,0:T(8,128)(2,1)S(1)}, u32[]{:S(2)}, u32[]{:S(2)}) %collective-permute-start.15) | collective-permute-done | bytes 98336 | tf_op jit(solution)/shard_map/ppermute | solution.py:35
  154.7 6.3 %all-to-all-start.4 = ((bf16[8,2,4,1536]{3,2,1,0:T(4,128)(2,1)}), bf16[8,2,4,1536]{3,2,1,0:T(4,128)(2,1)S(1)}, u32[]{:S(2)}, u32[]{:S(2)}) async-start(bf16[8,2,4,1536]{3,2,1,0:T(4,128)(2,1)} %plane_sums.1), calls=%async_computation.4 | async-start | bytes 393216 | tf_op jit(solution)/shard_map/all_to_all | solution.py:27
  167.0 2.6 %convolution_convert_fusion.1 = bf16[1536,384]{1,0:T(8,128)(2,1)} fusion(bf16[2,128,1536]{2,1,0:T(8,128)(2,1)S(1)} %bitcast.25, bf16[2,128,1536]{2,1,0:T(8,128)(2,1)} %collective-permute-done.13, bf16[2,384,128]{2,1,0:T(8,128)(2,1)S(1)} %bitcast.27, bf16[2,384,128]{2,1,0:T(8,128)(2,1)S(1)} %collective-permute-done.17), kind=kOutput, calls=%fused_computation.1 | convolution fusion | flops 304545792 | bytes 3145728 | tf_op jit(solution)/shard_map/dot_general | solution.py:63
  169.6 8.4 %all-to-all-done.4 = bf16[8,2,4,1536]{3,2,1,0:T(4,128)(2,1)S(1)} async-done(((bf16[8,2,4,1536]{3,2,1,0:T(4,128)(2,1)}), bf16[8,2,4,1536]{3,2,1,0:T(4,128)(2,1)S(1)}, u32[]{:S(2)}, u32[]{:S(2)}) %all-to-all-start.4) | async-done | bytes 196640 | tf_op jit(solution)/shard_map/all_to_all | solution.py:27
  (61 shorter events, 37.4 us)
Async XLA Ops:
  0.6 5.8 %copy-start.4 = (bf16[4,1536]{1,0:T(4,128)(2,1)S(1)}, bf16[4,1536]{1,0:T(4,128)(2,1)}, u32[]{:S(2)}) copy-start(bf16[4,1536]{1,0:T(4,128)(2,1)} %param.7) | copy-start | bytes 36868
  4.5 3.9 %collective-permute-start = (bf16[2,48,3072]{2,1,0:T(8,128)(2,1)S(1)}, bf16[2,48,3072]{2,1,0:T(8,128)(2,1)S(1)}, u32[]{:S(2)}, u32[]{:S(2)}) collective-permute-start(bf16[2,48,3072]{2,1,0:T(8,128)(2,1)S(1)} %get-tuple-element.33.refs_0_), channel_id=1, source_target_pairs={{0,8},{8,0},{1,9},{9,1},{2,10},{10,2},{3,11},{11,3},{4,12},{12,4},... | collective-permute-start | bytes 1769480 | tf_op jit(solution)/shard_map/ppermute | solution.py:35
  9.1 34.1 %all-to-all-start = ((bf16[8,8,1536]{2,1,0:T(8,128)(2,1)}), bf16[8,8,1536]{2,1,0:T(8,128)(2,1)S(1)}, u32[]{:S(2)}, u32[]{:S(2)}) async-start(bf16[8,8,1536]{2,1,0:T(8,128)(2,1)} %broadcast_in_dim.16), calls=%async_computation | async-start | bytes 393216 | tf_op jit(solution)/shard_map/all_to_all | solution.py:27
  24.2 39.6 %collective-permute-start.5 = (bf16[2,48,3072]{2,1,0:T(8,128)(2,1)}, bf16[2,48,3072]{2,1,0:T(8,128)(2,1)S(1)}, u32[]{:S(2)}, u32[]{:S(2)}) collective-permute-start(bf16[2,48,3072]{2,1,0:T(8,128)(2,1)} %get-tuple-element.44), channel_id=1, source_target_pairs={{0,128},{1,129},{128,0},{129,1},{2,130},{3,131},{130,2},{131,3},{4... | collective-permute-start | bytes 1769480 | tf_op jit(solution)/shard_map/ppermute | solution.py:35
  43.2 35.3 %collective-permute-start.6 = (bf16[2,48,3072]{2,1,0:T(8,128)(2,1)}, bf16[2,48,3072]{2,1,0:T(8,128)(2,1)}, u32[]{:S(2)}, u32[]{:S(2)}) collective-permute-start(bf16[2,48,3072]{2,1,0:T(8,128)(2,1)} %get-tuple-element.46), channel_id=1, source_target_pairs={{0,129},{1,128},{128,1},{129,0},{2,131},{3,130},{130,3},{131,2},{4... | collective-permute-start | bytes 1769480 | tf_op jit(solution)/shard_map/ppermute | solution.py:35
  45.7 32.7 %collective-permute-start.4 = (bf16[2,48,3072]{2,1,0:T(8,128)(2,1)}, bf16[2,48,3072]{2,1,0:T(8,128)(2,1)}, u32[]{:S(2)}, u32[]{:S(2)}) collective-permute-start(bf16[2,48,3072]{2,1,0:T(8,128)(2,1)} %get-tuple-element.43), channel_id=1, source_target_pairs={{0,1},{1,0},{128,129},{129,128},{2,3},{3,2},{130,131},{131,130},{4... | collective-permute-start | bytes 1769480 | tf_op jit(solution)/shard_map/ppermute | solution.py:35
  50.6 38.3 %all-to-all-start.1 = ((bf16[16,2,2,8,1536]{4,3,2,1,0:T(8,128)(2,1)}), bf16[16,2,2,8,1536]{4,3,2,1,0:T(8,128)(2,1)S(1)}, u32[]{:S(2)}, u32[]{:S(2)}) async-start(bf16[16,2,2,8,1536]{4,3,2,1,0:T(8,128)(2,1)} %copy-done.1), calls=%async_computation.1 | async-start | bytes 3145728 | tf_op jit(solution)/shard_map/all_to_all | solution.py:27
  58.4 20.0 %collective-permute-start.1 = (bf16[2,1,1,8,1536]{4,3,2,1,0:T(8,128)(2,1)S(1)}, bf16[2,1,1,8,1536]{4,3,2,1,0:T(8,128)(2,1)S(1)}, u32[]{:S(2)}, u32[]{:S(2)}) collective-permute-start(bf16[2,1,1,8,1536]{4,3,2,1,0:T(8,128)(2,1)S(1)} %get-tuple-element.36), channel_id=1, source_target_pairs={{0,128},{128,0},{256,384},{384,256},{1,129},{129,1},{257,385},{385... | collective-permute-start | bytes 147464 | tf_op jit(solution)/shard_map/ppermute | solution.py:35
  61.1 17.3 %collective-permute-start.2 = (bf16[2,1,1,8,1536]{4,3,2,1,0:T(8,128)(2,1)S(1)}, bf16[2,1,1,8,1536]{4,3,2,1,0:T(8,128)(2,1)S(1)}, u32[]{:S(2)}, u32[]{:S(2)}) collective-permute-start(bf16[2,1,1,8,1536]{4,3,2,1,0:T(8,128)(2,1)S(1)} %get-tuple-element.36), channel_id=1, source_target_pairs={{0,256},{128,384},{256,0},{384,128},{1,257},{129,385},{257,1},{385... | collective-permute-start | bytes 147464 | tf_op jit(solution)/shard_map/ppermute | solution.py:35
  63.8 14.6 %collective-permute-start.3 = (bf16[2,1,1,8,1536]{4,3,2,1,0:T(8,128)(2,1)S(1)}, bf16[2,1,1,8,1536]{4,3,2,1,0:T(8,128)(2,1)S(1)}, u32[]{:S(2)}, u32[]{:S(2)}) collective-permute-start(bf16[2,1,1,8,1536]{4,3,2,1,0:T(8,128)(2,1)S(1)} %get-tuple-element.36), channel_id=1, source_target_pairs={{0,384},{128,256},{256,128},{384,0},{1,385},{129,257},{257,129},{3... | collective-permute-start | bytes 147464 | tf_op jit(solution)/shard_map/ppermute | solution.py:35
  78.4 4.2 %collective-permute-start.7 = (bf16[2,48,3072]{2,1,0:T(8,128)(2,1)}, bf16[2,48,3072]{2,1,0:T(8,128)(2,1)}, u32[]{:S(2)}, u32[]{:S(2)}) collective-permute-start(bf16[2,48,3072]{2,1,0:T(8,128)(2,1)} %collective-permute-done.4.refs_1_), channel_id=1, source_target_pairs={{0,8},{8,0},{1,9},{9,1},{2,10},{10,2},{3,11},{11,3},{4,12},{12,4},... | collective-permute-start | bytes 1769480 | tf_op jit(solution)/shard_map/ppermute | solution.py:35
  82.7 6.2 %collective-permute-start.9 = (bf16[2,48,3072]{2,1,0:T(8,128)(2,1)}, bf16[2,48,3072]{2,1,0:T(8,128)(2,1)}, u32[]{:S(2)}, u32[]{:S(2)}) collective-permute-start(bf16[2,48,3072]{2,1,0:T(8,128)(2,1)} %collective-permute-done.6.refs_3_), channel_id=1, source_target_pairs={{0,8},{8,0},{1,9},{9,1},{2,10},{10,2},{3,11},{11,3},{4,12},{12,4},... | collective-permute-start | bytes 1769480 | tf_op jit(solution)/shard_map/ppermute | solution.py:35
  84.7 4.2 %collective-permute-start.8 = (bf16[2,48,3072]{2,1,0:T(8,128)(2,1)S(1)}, bf16[2,48,3072]{2,1,0:T(8,128)(2,1)}, u32[]{:S(2)}, u32[]{:S(2)}) collective-permute-start(bf16[2,48,3072]{2,1,0:T(8,128)(2,1)S(1)} %collective-permute-done.5.refs_2_), channel_id=1, source_target_pairs={{0,8},{8,0},{1,9},{9,1},{2,10},{10,2},{3,11},{11,3},{4,12},{12,4},... | collective-permute-start | bytes 1769480 | tf_op jit(solution)/shard_map/ppermute | solution.py:35
  93.1 23.8 %all-to-all-start.2 = ((bf16[4,4,3,2,48,128]{5,4,3,2,1,0:T(8,128)(2,1)}), bf16[4,4,3,2,48,128]{5,4,3,2,1,0:T(8,128)(2,1)S(1)}, u32[]{:S(2)}, u32[]{:S(2)}) async-start(bf16[4,4,3,2,48,128]{5,4,3,2,1,0:T(8,128)(2,1)} %hidden_parts.1), calls=%async_computation.2 | async-start | bytes 2359296 | tf_op jit(solution)/shard_map/all_to_all | solution.py:27
  97.0 10.4 %collective-permute-start.10 = (bf16[2,4,1,8,1536]{4,3,2,1,0:T(8,128)(2,1)}, bf16[2,4,1,8,1536]{4,3,2,1,0:T(8,128)(2,1)S(1)}, u32[]{:S(2)}, u32[]{:S(2)}) collective-permute-start(bf16[2,4,1,8,1536]{4,3,2,1,0:T(8,128)(2,1)} %constant_dynamic-update-slice_fusion.8), channel_id=1, source_target_pairs={{0,16},{16,0},{32,48},{48,32},{1,17},{17,1},{33,49},{49,33},{2,18}... | collective-permute-start | bytes 589832 | tf_op jit(solution)/shard_map/ppermute | solution.py:35
  100.4 12.2 %collective-permute-start.11 = (bf16[2,4,1,8,1536]{4,3,2,1,0:T(8,128)(2,1)}, bf16[2,4,1,8,1536]{4,3,2,1,0:T(8,128)(2,1)S(1)}, u32[]{:S(2)}, u32[]{:S(2)}) collective-permute-start(bf16[2,4,1,8,1536]{4,3,2,1,0:T(8,128)(2,1)} %constant_dynamic-update-slice_fusion.8), channel_id=1, source_target_pairs={{0,32},{16,48},{32,0},{48,16},{1,33},{17,49},{33,1},{49,17},{2,34}... | collective-permute-start | bytes 589832 | tf_op jit(solution)/shard_map/ppermute | solution.py:35
  105.4 11.5 %collective-permute-start.12 = (bf16[2,4,1,8,1536]{4,3,2,1,0:T(8,128)(2,1)}, bf16[2,4,1,8,1536]{4,3,2,1,0:T(8,128)(2,1)}, u32[]{:S(2)}, u32[]{:S(2)}) collective-permute-start(bf16[2,4,1,8,1536]{4,3,2,1,0:T(8,128)(2,1)} %constant_dynamic-update-slice_fusion.8), channel_id=1, source_target_pairs={{0,48},{16,32},{32,16},{48,0},{1,49},{17,33},{33,17},{49,1},{2,50}... | collective-permute-start | bytes 589832 | tf_op jit(solution)/shard_map/ppermute | solution.py:35
  121.1 32.7 %all-to-all-start.3 = ((bf16[16,2,8,3072]{3,2,1,0:T(8,128)(2,1)}), bf16[16,2,8,3072]{3,2,1,0:T(8,128)(2,1)S(1)}, u32[]{:S(2)}, u32[]{:S(2)}) async-start(bf16[16,2,8,3072]{3,2,1,0:T(8,128)(2,1)} %copy-done), calls=%async_computation.3 | async-start | bytes 3145728 | tf_op jit(solution)/shard_map/all_to_all | solution.py:27
  126.8 18.0 %collective-permute-start.14 = (bf16[2,2,1,2,48,128]{5,4,3,2,1,0:T(8,128)(2,1)S(1)}, bf16[2,2,1,2,48,128]{5,4,3,2,1,0:T(8,128)(2,1)S(1)}, u32[]{:S(2)}, u32[]{:S(2)}) collective-permute-start(bf16[2,2,1,2,48,128]{5,4,3,2,1,0:T(8,128)(2,1)S(1)} %get-tuple-element.58), channel_id=1, source_target_pairs={{0,2},{2,0},{4,6},{6,4},{1,3},{3,1},{5,7},{7,5},{8,10},{10,8},{12,... | collective-permute-start | bytes 294920 | tf_op jit(solution)/shard_map/ppermute | solution.py:35
  130.6 23.2 %collective-permute-start.15 = (bf16[2,2,1,2,48,128]{5,4,3,2,1,0:T(8,128)(2,1)S(1)}, bf16[2,2,1,2,48,128]{5,4,3,2,1,0:T(8,128)(2,1)S(1)}, u32[]{:S(2)}, u32[]{:S(2)}) collective-permute-start(bf16[2,2,1,2,48,128]{5,4,3,2,1,0:T(8,128)(2,1)S(1)} %get-tuple-element.58), channel_id=1, source_target_pairs={{0,4},{2,6},{4,0},{6,2},{1,5},{3,7},{5,1},{7,3},{8,12},{10,14},{12... | collective-permute-start | bytes 294920 | tf_op jit(solution)/shard_map/ppermute | solution.py:35
  133.6 20.2 %collective-permute-start.16 = (bf16[2,2,1,2,48,128]{5,4,3,2,1,0:T(8,128)(2,1)S(1)}, bf16[2,2,1,2,48,128]{5,4,3,2,1,0:T(8,128)(2,1)S(1)}, u32[]{:S(2)}, u32[]{:S(2)}) collective-permute-start(bf16[2,2,1,2,48,128]{5,4,3,2,1,0:T(8,128)(2,1)S(1)} %get-tuple-element.58), channel_id=1, source_target_pairs={{0,6},{2,4},{4,2},{6,0},{1,7},{3,5},{5,3},{7,1},{8,14},{10,12},{12... | collective-permute-start | bytes 294920 | tf_op jit(solution)/shard_map/ppermute | solution.py:35
  142.8 20.3 %collective-permute-start.13 = (bf16[2,128,1536]{2,1,0:T(8,128)(2,1)S(1)}, bf16[2,128,1536]{2,1,0:T(8,128)(2,1)}, u32[]{:S(2)}, u32[]{:S(2)}) collective-permute-start(bf16[2,128,1536]{2,1,0:T(8,128)(2,1)S(1)} %bitcast.23), channel_id=1, source_target_pairs={{0,8},{8,0},{1,9},{9,1},{2,10},{10,2},{3,11},{11,3},{4,12},{12,4},... | collective-permute-start | bytes 2359304 | tf_op jit(solution)/shard_map/ppermute | solution.py:35
  154.7 23.3 %all-to-all-start.4 = ((bf16[8,2,4,1536]{3,2,1,0:T(4,128)(2,1)}), bf16[8,2,4,1536]{3,2,1,0:T(4,128)(2,1)S(1)}, u32[]{:S(2)}, u32[]{:S(2)}) async-start(bf16[8,2,4,1536]{3,2,1,0:T(4,128)(2,1)} %plane_sums.1), calls=%async_computation.4 | async-start | bytes 393216 | tf_op jit(solution)/shard_map/all_to_all | solution.py:27
  161.2 3.3 %collective-permute-start.17 = (bf16[2,384,128]{2,1,0:T(8,128)(2,1)S(1)}, bf16[2,384,128]{2,1,0:T(8,128)(2,1)S(1)}, u32[]{:S(2)}, u32[]{:S(2)}) collective-permute-start(bf16[2,384,128]{2,1,0:T(8,128)(2,1)S(1)} %bitcast.28), channel_id=1, source_target_pairs={{0,8},{8,0},{1,9},{9,1},{2,10},{10,2},{3,11},{11,3},{4,12},{12,4},... | collective-permute-start | bytes 589832 | tf_op jit(solution)/shard_map/ppermute | solution.py:35
  (5 other events, 8.2 us)

commit v9 on v7

--- a/solution.py
+++ b/solution.py
@@ -12,6 +12,7 @@
 PLANE = ("xh", "xp", "y")
 COLUMN = ("zh", "z2", "z1")
 GROUP = ("xp", "zp")
+STEPS = (0, 2, 3, 1)
 
 
 def activate(values):
@@ -64,11 +65,11 @@
 
 def cut_kernel(member_ref, up_ref, down_ref, *pieces):
     width = pieces[0].shape[2] // 2
-    for step in range(4):
+    for at, step in enumerate(STEPS):
         for kind, source in enumerate((up_ref, down_ref)):
             for far in range(2):
                 column = pl.multiple_of((far * 4 + (member_ref[0] ^ step)) * width, width)
-                pieces[step][kind, :, far * width : (far + 1) * width] = source[:, pl.ds(column, width)]
+                pieces[at][kind, :, far * width : (far + 1) * width] = source[:, pl.ds(column, width)]
 
 
 def cut(member, up_rows, down_rows):
@@ -132,9 +133,9 @@
             if kind == 0:
                 sends.append((2, (total - sends[0][1].astype(F32)).astype(BF16)))
             for row, value in sends:
-                for step in range(4):
+                for place, step in enumerate(STEPS):
                     for at in range(4):
-                        out_ref[at, member_ref[0] ^ step, row, core] = value[step * units : (step + 1) * units]
+                        out_ref[at, member_ref[0] ^ step, row, core] = value[place * units : (place + 1) * units]
 
 
 def hidden_parts(member, rows, own, beside):
@@ -161,7 +162,7 @@
     step_of = features // 4
     units = [[], []]
     for core in range(2):
-        for step in range(4):
+        for step in STEPS:
             slot = member_ref[0] ^ step
             value, act_grad, rest = (
                 sum(parts_ref[source, slot, row, core].astype(F32) for source in range(4)) for row in range(3)
@@ -200,13 +201,41 @@
     )(member, parts, *own, *beside)
 
 
+def sum_kernel(arrived_ref, out_ref):
+    width = out_ref.shape[3]
+    for near in range(2):
+        for array in range(2):
+            total = None
+            for half in range(2):
+                for line in range(4):
+                    term = arrived_ref[half * 8 + near * 4 + line, array].astype(F32)
+                    total = term if total is None else total + term
+            for end in range(2):
+                for far in range(2):
+                    rows = total[end * 4 : end * 4 + 4, far * width : (far + 1) * width]
+                    out_ref[end * 4 + far * 2 + near, array] = rows.astype(BF16)
+
+
+def plane_sums(arrived):
+    width = arrived.shape[3] // 2
+    return pl.pallas_call(
+        sum_kernel,
+        out_shape=jax.ShapeDtypeStruct((8, 2, 4, width), BF16),
+        in_specs=[pl.BlockSpec(memory_space=pltpu.VMEM)],
+        out_specs=pl.BlockSpec(memory_space=pltpu.VMEM),
+        compiler_params=pltpu.CompilerParams(vmem_limit_bytes=VMEM_BYTES),
+        cost_estimate=pl.CostEstimate(flops=800_000, bytes_accessed=1_800_000, transcendentals=0),
+        name="plane_sums",
+    )(arrived)
+
+
 def local(tokens, up_proj, down_proj, out_grad):
     width = tokens.shape[1]
     units = down_proj.shape[0]
     member = lax.axis_index(GROUP).reshape(1).astype(jnp.int32)
 
     pieces = cut(member, up_proj.T, down_proj)
-    own = [pieces[0]] + [partner(pieces[step], GROUP, 4, step) for step in range(1, 4)]
+    own = [pieces[0]] + [partner(pieces[at], GROUP, 4, STEPS[at]) for at in range(1, 4)]
     beside = [other_core(pieces[0])]
     waits = own[1:]
     for piece in own[1:]:
@@ -216,7 +245,7 @@
     both = jnp.concatenate([tokens, out_grad], axis=0)
     column = spread(both, COLUMN, 8)
     block = lax.axis_index(("z2", "z1")).reshape(1).astype(jnp.int32)
-    sent = lay_out(block, after(column, beside[0]))
+    sent = lay_out(block, column)
     plane = exchange(sent, PLANE)
 
     parts, mine = hidden_parts(member, plane, own, beside)
@@ -224,9 +253,7 @@
 
     partials, pair = output_parts(member, arrived, own, beside, 16)
     arrived = exchange(partials, PLANE)
-    summed = jnp.sum(arrived.reshape(2, 2, 4, 2, 8, 2 * width).astype(F32), axis=(0, 2))
-    summed = summed.astype(BF16).reshape(2, 2, 2, 4, 2, width)
-    summed = summed.transpose(2, 4, 0, 1, 3, 5).reshape(8, 2, 4, width)
+    summed = plane_sums(arrived)
     ends = jnp.sum(exchange(summed, COLUMN).astype(F32), axis=0).astype(BF16)
 
     flat = jnp.concatenate([mine, other_core(mine)], axis=1)

time: 175 us -> 163 us (0.931)
  waiting for transfers between devices: 46.1 us -> 39.3 us
  starting transfers between devices: 78.8 us -> 75.2 us
    ppermute x12, waiting for transfers between devices: 19.6 us -> 14.5 us  [partner(): return lax.ppermute(value, axes, [(at, at ^ step) for at in range(count)])]
    all_to_all x4, starting transfers between devices: 43.8 us -> 39.9 us  [exchange(): return lax.all_to_all(value, axes, split_axis=0, concat_axis=0, tiled=True)]
    unnamed x31 -> x37, local copies, waits for them, and re-layouts: 11.5 us -> 13.4 us
  transfers between devices with their start and end apart: 16 -> 16, of which waited for: 9 -> 9; matrix products, arithmetic and copies ran while one was open for 5% -> 4% of each run, Pallas kernels for 1% -> 1%
where the time goes in v9:
time: 163 us; the launch traced here: 162 us
  starting transfers between devices  75.2 us (46%)
  waiting for transfers between devices  39.3 us (24%)
  blocking collectives  16.9 us (10%)
  local copies, waits for them, and re-layouts  16.7 us (10%)
  Pallas kernels  8.79 us (5%)
  matrix products  3.12 us (2%)
    all_to_all x4, starting transfers between devices, exchange(): return lax.all_to_all(value, axes, split_axis=0, concat_axis=0, tiled=True)  39.9 us
    ppermute x12, starting transfers between devices, partner(): return lax.ppermute(value, axes, [(at, at ^ step) for at in range(count)])  35.3 us
    all_to_all x4, waiting for transfers between devices, exchange(): return lax.all_to_all(value, axes, split_axis=0, concat_axis=0, tiled=True)  24.8 us
    all_to_all x1, blocking collectives, exchange(): return lax.all_to_all(value, axes, split_axis=0, concat_axis=0, tiled=True)  16.9 us
    ppermute x12, waiting for transfers between devices, partner(): return lax.ppermute(value, axes, [(at, at ^ step) for at in range(count)])  14.5 us
    unnamed x37, local copies, waits for them, and re-layouts  13.4 us
    pallas_call x1, Pallas kernels, output_parts(): pl.pallas_call(output_kernel, out_shape=[jax.ShapeDtypeStruct((count, 2,...  3.65 us
  transfers between devices with their start and end apart: 16, of which 9 were waited for; matrix products, arithmetic and copies ran while one was open for 4% of the time, Pallas kernels for 1%

profile of v9, /device:TPU:6, one launch (start us, length us, event | category | flops | bytes accessed | tf_op | source)
XLA Modules:
  0.0 161.8 jit_solution(3425611354560099402)
XLA Ops:
  2.1 15.1 %all-to-all-start = ((bf16[8,8,1536]{2,1,0:T(8,128)(2,1)}), bf16[8,8,1536]{2,1,0:T(8,128)(2,1)S(1)}, u32[]{:S(2)}, u32[]{:S(2)}) async-start(bf16[8,8,1536]{2,1,0:T(8,128)(2,1)} %broadcast_in_dim.4), calls=%async_computation | async-start | bytes 393216 | tf_op jit(solution)/shard_map/all_to_all | solution.py:28
  21.0 2.7 %collective-permute-start = (bf16[2,48,3072]{2,1,0:T(8,128)(2,1)}, bf16[2,48,3072]{2,1,0:T(8,128)(2,1)S(1)}, u32[]{:S(2)}, u32[]{:S(2)}) collective-permute-start(bf16[2,48,3072]{2,1,0:T(8,128)(2,1)} %get-tuple-element.20), channel_id=1, source_target_pairs={{0,128},{1,129},{128,0},{129,1},{2,130},{3,131},{130,2},{131,3},{4... | collective-permute-start | bytes 1769480 | tf_op jit(solution)/shard_map/ppermute | solution.py:36
  23.8 3.6 %collective-permute-start.1 = (bf16[2,48,3072]{2,1,0:T(8,128)(2,1)}, bf16[2,48,3072]{2,1,0:T(8,128)(2,1)}, u32[]{:S(2)}, u32[]{:S(2)}) collective-permute-start(bf16[2,48,3072]{2,1,0:T(8,128)(2,1)} %get-tuple-element.21), channel_id=1, source_target_pairs={{0,129},{1,128},{128,1},{129,0},{2,131},{3,130},{130,3},{131,2},{4... | collective-permute-start | bytes 1769480 | tf_op jit(solution)/shard_map/ppermute | solution.py:36
  27.3 2.9 %collective-permute-start.2 = (bf16[2,48,3072]{2,1,0:T(8,128)(2,1)}, bf16[2,48,3072]{2,1,0:T(8,128)(2,1)}, u32[]{:S(2)}, u32[]{:S(2)}) collective-permute-start(bf16[2,48,3072]{2,1,0:T(8,128)(2,1)} %get-tuple-element.22), channel_id=1, source_target_pairs={{0,1},{1,0},{128,129},{129,128},{2,3},{3,2},{130,131},{131,130},{4... | collective-permute-start | bytes 1769480 | tf_op jit(solution)/shard_map/ppermute | solution.py:36
  30.3 5.6 %all-to-all-done.column_ref = bf16[8,8,1536]{2,1,0:T(8,128)(2,1)S(1)} async-done(((bf16[8,8,1536]{2,1,0:T(8,128)(2,1)}), bf16[8,8,1536]{2,1,0:T(8,128)(2,1)S(1)}, u32[]{:S(2)}, u32[]{:S(2)}) %all-to-all-start) | async-done | bytes 196640 | tf_op jit(solution)/shard_map/all_to_all | solution.py:28
  37.5 7.4 %all-to-all-start.1 = ((bf16[16,3,2,8,1536]{4,3,2,1,0:T(8,128)(2,1)}), bf16[16,3,2,8,1536]{4,3,2,1,0:T(8,128)(2,1)S(1)}, u32[]{:S(2)}, u32[]{:S(2)}) async-start(bf16[16,3,2,8,1536]{4,3,2,1,0:T(8,128)(2,1)} %copy-done), calls=%async_computation.1 | async-start | bytes 4718592 | tf_op jit(solution)/shard_map/all_to_all | solution.py:28
  44.9 7.1 %collective-permute-done.refs_1_ = bf16[2,48,3072]{2,1,0:T(8,128)(2,1)S(1)} collective-permute-done((bf16[2,48,3072]{2,1,0:T(8,128)(2,1)}, bf16[2,48,3072]{2,1,0:T(8,128)(2,1)S(1)}, u32[]{:S(2)}, u32[]{:S(2)}) %collective-permute-start) | collective-permute-done | bytes 589856 | tf_op jit(solution)/shard_map/ppermute | solution.py:36
  52.0 2.8 %collective-permute-done.2.refs_3_ = bf16[2,48,3072]{2,1,0:T(8,128)(2,1)} collective-permute-done((bf16[2,48,3072]{2,1,0:T(8,128)(2,1)}, bf16[2,48,3072]{2,1,0:T(8,128)(2,1)}, u32[]{:S(2)}, u32[]{:S(2)}) %collective-permute-start.2) | collective-permute-done | bytes 589856 | tf_op jit(solution)/shard_map/ppermute | solution.py:36
  56.8 2.0 %collective-permute-done.4.refs_5_ = bf16[2,48,3072]{2,1,0:T(8,128)(2,1)S(1)} collective-permute-done((bf16[2,48,3072]{2,1,0:T(8,128)(2,1)S(1)}, bf16[2,48,3072]{2,1,0:T(8,128)(2,1)S(1)}, u32[]{:S(2)}, u32[]{:S(2)}) %collective-permute-start.4) | collective-permute-done | bytes 589856 | tf_op jit(solution)/shard_map/ppermute | solution.py:36
  59.6 2.0 %collective-permute-start.5 = (bf16[2,48,3072]{2,1,0:T(8,128)(2,1)}, bf16[2,48,3072]{2,1,0:T(8,128)(2,1)S(1)}, u32[]{:S(2)}, u32[]{:S(2)}) collective-permute-start(bf16[2,48,3072]{2,1,0:T(8,128)(2,1)} %collective-permute-done.1.refs_2_), channel_id=1, source_target_pairs={{0,8},{8,0},{1,9},{9,1},{2,10},{10,2},{3,11},{11,3},{4,12},{12,4},... | collective-permute-start | bytes 1769480 | tf_op jit(solution)/shard_map/ppermute | solution.py:36
  61.6 2.3 %collective-permute-start.3 = (bf16[2,48,3072]{2,1,0:T(8,128)(2,1)S(1)}, bf16[2,48,3072]{2,1,0:T(8,128)(2,1)S(1)}, u32[]{:S(2)}, u32[]{:S(2)}) collective-permute-start(bf16[2,48,3072]{2,1,0:T(8,128)(2,1)S(1)} %get-tuple-element.19.refs_0_), channel_id=1, source_target_pairs={{0,8},{8,0},{1,9},{9,1},{2,10},{10,2},{3,11},{11,3},{4,12},{12,4},... | collective-permute-start | bytes 1769480 | tf_op jit(solution)/shard_map/ppermute | solution.py:36
  64.7 2.0 %collective-permute-start.6 = (bf16[2,48,3072]{2,1,0:T(8,128)(2,1)}, bf16[2,48,3072]{2,1,0:T(8,128)(2,1)S(1)}, u32[]{:S(2)}, u32[]{:S(2)}) collective-permute-start(bf16[2,48,3072]{2,1,0:T(8,128)(2,1)} %collective-permute-done.2.refs_3_), channel_id=1, source_target_pairs={{0,8},{8,0},{1,9},{9,1},{2,10},{10,2},{3,11},{11,3},{4,12},{12,4},... | collective-permute-start | bytes 1769480 | tf_op jit(solution)/shard_map/ppermute | solution.py:36
  69.7 8.8 %all-to-all-done.1.rows_ref = bf16[16,3,2,8,1536]{4,3,2,1,0:T(8,128)(2,1)S(1)} async-done(((bf16[16,3,2,8,1536]{4,3,2,1,0:T(8,128)(2,1)}), bf16[16,3,2,8,1536]{4,3,2,1,0:T(8,128)(2,1)S(1)}, u32[]{:S(2)}, u32[]{:S(2)}) %all-to-all-start.1) | async-done | bytes 2359328 | tf_op jit(solution)/shard_map/all_to_all | solution.py:28
  82.8 2.7 %hidden_parts.1 = (bf16[4,4,3,2,48,128]{5,4,3,2,1,0:T(8,128)(2,1)S(1)}, bf16[2,128,1536]{2,1,0:T(8,128)(2,1)S(1)}) custom-call(s32[1]{0:T(128)} %bitcast.member_ref, bf16[16,3,2,8,1536]{4,3,2,1,0:T(8,128)(2,1)S(1)} %all-to-all-done.1.rows_ref, bf16[2,48,3072]{2,1,0:T(8,128)(2,1)S(1)} %get-tuple-element.19.refs_0_, ...), custom_call_target="tpu_custom_call" | custom-call | flops 604000000 | bytes 6700000 | tf_op jit(solution)/shard_map/hidden_parts/pallas_call | solution.py:144
  86.4 16.9 %all_to_all.25.parts_ref = bf16[4,4,3,2,48,128]{5,4,3,2,1,0:T(8,128)(2,1)S(1)} all-to-all(bf16[4,4,3,2,48,128]{5,4,3,2,1,0:T(8,128)(2,1)S(1)} %get-tuple-element.26), channel_id=1, replica_groups=mesh['xh'=2,'xp'=2,'zh'=2,'y'=4,'c'=2,'z2'=2,'z1'=2,'zp'=2] {'xp','zp'}, dimensions={0} | all-to-all | bytes 2359296 | tf_op jit(solution)/shard_map/all_to_all | solution.py:28
  103.4 3.7 %output_parts.1 = (bf16[16,2,8,3072]{3,2,1,0:T(8,128)(2,1)}, bf16[2,2,1,2,48,128]{5,4,3,2,1,0:T(8,128)(2,1)S(1)}) custom-call(s32[1]{0:T(128)} %bitcast.member_ref, bf16[4,4,3,2,48,128]{5,4,3,2,1,0:T(8,128)(2,1)S(1)} %all_to_all.25.parts_ref, bf16[2,48,3072]{2,1,0:T(8,128)(2,1)S(1)} %get-tuple-element.19.refs_0_, ...), custom_call_target="tpu_custom_call" | custom-call | flops 604000000 | bytes 6700000 | tf_op jit(solution)/shard_map/output_parts/pallas_call | solution.py:190
  107.0 5.9 %all-to-all-start.3 = ((bf16[16,2,8,3072]{3,2,1,0:T(8,128)(2,1)}), bf16[16,2,8,3072]{3,2,1,0:T(8,128)(2,1)S(1)}, u32[]{:S(2)}, u32[]{:S(2)}) async-start(bf16[16,2,8,3072]{3,2,1,0:T(8,128)(2,1)} %get-tuple-element.27), calls=%async_computation.3 | async-start | bytes 3145728 | tf_op jit(solution)/shard_map/all_to_all | solution.py:28
  112.9 1.9 %collective-permute-start.7 = (bf16[2,128,1536]{2,1,0:T(8,128)(2,1)S(1)}, bf16[2,128,1536]{2,1,0:T(8,128)(2,1)S(1)}, u32[]{:S(2)}, u32[]{:S(2)}) collective-permute-start(bf16[2,128,1536]{2,1,0:T(8,128)(2,1)S(1)} %copy-done.16), channel_id=1, source_target_pairs={{0,8},{8,0},{1,9},{9,1},{2,10},{10,2},{3,11},{11,3},{4,12},{12,4},... | collective-permute-start | bytes 2359304 | tf_op jit(solution)/shard_map/ppermute | solution.py:36
  114.9 4.2 %collective-permute-start.8 = (bf16[2,2,1,2,48,128]{5,4,3,2,1,0:T(8,128)(2,1)S(1)}, bf16[2,2,1,2,48,128]{5,4,3,2,1,0:T(8,128)(2,1)S(1)}, u32[]{:S(2)}, u32[]{:S(2)}) collective-permute-start(bf16[2,2,1,2,48,128]{5,4,3,2,1,0:T(8,128)(2,1)S(1)} %get-tuple-element.30), channel_id=1, source_target_pairs={{0,2},{2,0},{4,6},{6,4},{1,3},{3,1},{5,7},{7,5},{8,10},{10,8},{12,... | collective-permute-start | bytes 294920 | tf_op jit(solution)/shard_map/ppermute | solution.py:36
  119.1 7.3 %collective-permute-start.9 = (bf16[2,2,1,2,48,128]{5,4,3,2,1,0:T(8,128)(2,1)S(1)}, bf16[2,2,1,2,48,128]{5,4,3,2,1,0:T(8,128)(2,1)}, u32[]{:S(2)}, u32[]{:S(2)}) collective-permute-start(bf16[2,2,1,2,48,128]{5,4,3,2,1,0:T(8,128)(2,1)S(1)} %get-tuple-element.30), channel_id=1, source_target_pairs={{0,4},{2,6},{4,0},{6,2},{1,5},{3,7},{5,1},{7,3},{8,12},{10,14},{12... | collective-permute-start | bytes 294920 | tf_op jit(solution)/shard_map/ppermute | solution.py:36
  126.4 2.5 %collective-permute-start.10 = (bf16[2,2,1,2,48,128]{5,4,3,2,1,0:T(8,128)(2,1)S(1)}, bf16[2,2,1,2,48,128]{5,4,3,2,1,0:T(8,128)(2,1)}, u32[]{:S(2)}, u32[]{:S(2)}) collective-permute-start(bf16[2,2,1,2,48,128]{5,4,3,2,1,0:T(8,128)(2,1)S(1)} %get-tuple-element.30), channel_id=1, source_target_pairs={{0,6},{2,4},{4,2},{6,0},{1,7},{3,5},{5,3},{7,1},{8,14},{10,12},{12... | collective-permute-start | bytes 294920 | tf_op jit(solution)/shard_map/ppermute | solution.py:36
  132.1 11.4 %all-to-all-start.4 = ((bf16[8,2,4,1536]{3,2,1,0:T(4,128)(2,1)}), bf16[8,2,4,1536]{3,2,1,0:T(4,128)(2,1)S(1)}, u32[]{:S(2)}, u32[]{:S(2)}) async-start(bf16[8,2,4,1536]{3,2,1,0:T(4,128)(2,1)} %plane_sums.1), calls=%async_computation.4 | async-start | bytes 393216 | tf_op jit(solution)/shard_map/all_to_all | solution.py:28
  145.6 1.9 %collective-permute-start.11 = (bf16[2,384,128]{2,1,0:T(8,128)(2,1)S(1)}, bf16[2,384,128]{2,1,0:T(8,128)(2,1)S(1)}, u32[]{:S(2)}, u32[]{:S(2)}) collective-permute-start(bf16[2,384,128]{2,1,0:T(8,128)(2,1)S(1)} %bitcast.24), channel_id=1, source_target_pairs={{0,8},{8,0},{1,9},{9,1},{2,10},{10,2},{3,11},{11,3},{4,12},{12,4},... | collective-permute-start | bytes 589832 | tf_op jit(solution)/shard_map/ppermute | solution.py:36
  152.0 9.1 %all-to-all-done.4 = bf16[8,2,4,1536]{3,2,1,0:T(4,128)(2,1)S(1)} async-done(((bf16[8,2,4,1536]{3,2,1,0:T(4,128)(2,1)}), bf16[8,2,4,1536]{3,2,1,0:T(4,128)(2,1)S(1)}, u32[]{:S(2)}, u32[]{:S(2)}) %all-to-all-start.4) | async-done | bytes 196640 | tf_op jit(solution)/shard_map/all_to_all | solution.py:28
  (64 shorter events, 28.9 us)
Async XLA Ops:
  2.1 33.8 %all-to-all-start = ((bf16[8,8,1536]{2,1,0:T(8,128)(2,1)}), bf16[8,8,1536]{2,1,0:T(8,128)(2,1)S(1)}, u32[]{:S(2)}, u32[]{:S(2)}) async-start(bf16[8,8,1536]{2,1,0:T(8,128)(2,1)} %broadcast_in_dim.4), calls=%async_computation | async-start | bytes 393216 | tf_op jit(solution)/shard_map/all_to_all | solution.py:28
  17.2 1.3 copy-start.13
  21.0 31.0 %collective-permute-start = (bf16[2,48,3072]{2,1,0:T(8,128)(2,1)}, bf16[2,48,3072]{2,1,0:T(8,128)(2,1)S(1)}, u32[]{:S(2)}, u32[]{:S(2)}) collective-permute-start(bf16[2,48,3072]{2,1,0:T(8,128)(2,1)} %get-tuple-element.20), channel_id=1, source_target_pairs={{0,128},{1,129},{128,0},{129,1},{2,130},{3,131},{130,2},{131,3},{4... | collective-permute-start | bytes 1769480 | tf_op jit(solution)/shard_map/ppermute | solution.py:36
  23.8 28.3 %collective-permute-start.1 = (bf16[2,48,3072]{2,1,0:T(8,128)(2,1)}, bf16[2,48,3072]{2,1,0:T(8,128)(2,1)}, u32[]{:S(2)}, u32[]{:S(2)}) collective-permute-start(bf16[2,48,3072]{2,1,0:T(8,128)(2,1)} %get-tuple-element.21), channel_id=1, source_target_pairs={{0,129},{1,128},{128,1},{129,0},{2,131},{3,130},{130,3},{131,2},{4... | collective-permute-start | bytes 1769480 | tf_op jit(solution)/shard_map/ppermute | solution.py:36
  27.3 27.5 %collective-permute-start.2 = (bf16[2,48,3072]{2,1,0:T(8,128)(2,1)}, bf16[2,48,3072]{2,1,0:T(8,128)(2,1)}, u32[]{:S(2)}, u32[]{:S(2)}) collective-permute-start(bf16[2,48,3072]{2,1,0:T(8,128)(2,1)} %get-tuple-element.22), channel_id=1, source_target_pairs={{0,1},{1,0},{128,129},{129,128},{2,3},{3,2},{130,131},{131,130},{4... | collective-permute-start | bytes 1769480 | tf_op jit(solution)/shard_map/ppermute | solution.py:36
  36.0 1.4 copy-start
  37.5 41.1 %all-to-all-start.1 = ((bf16[16,3,2,8,1536]{4,3,2,1,0:T(8,128)(2,1)}), bf16[16,3,2,8,1536]{4,3,2,1,0:T(8,128)(2,1)S(1)}, u32[]{:S(2)}, u32[]{:S(2)}) async-start(bf16[16,3,2,8,1536]{4,3,2,1,0:T(8,128)(2,1)} %copy-done), calls=%async_computation.1 | async-start | bytes 4718592 | tf_op jit(solution)/shard_map/all_to_all | solution.py:28
  54.9 3.9 %collective-permute-start.4 = (bf16[2,48,3072]{2,1,0:T(8,128)(2,1)S(1)}, bf16[2,48,3072]{2,1,0:T(8,128)(2,1)S(1)}, u32[]{:S(2)}, u32[]{:S(2)}) collective-permute-start(bf16[2,48,3072]{2,1,0:T(8,128)(2,1)S(1)} %collective-permute-done.refs_1_), channel_id=1, source_target_pairs={{0,8},{8,0},{1,9},{9,1},{2,10},{10,2},{3,11},{11,3},{4,12},{12,4},... | collective-permute-start | bytes 1769480 | tf_op jit(solution)/shard_map/ppermute | solution.py:36
  59.6 4.3 %collective-permute-start.5 = (bf16[2,48,3072]{2,1,0:T(8,128)(2,1)}, bf16[2,48,3072]{2,1,0:T(8,128)(2,1)S(1)}, u32[]{:S(2)}, u32[]{:S(2)}) collective-permute-start(bf16[2,48,3072]{2,1,0:T(8,128)(2,1)} %collective-permute-done.1.refs_2_), channel_id=1, source_target_pairs={{0,8},{8,0},{1,9},{9,1},{2,10},{10,2},{3,11},{11,3},{4,12},{12,4},... | collective-permute-start | bytes 1769480 | tf_op jit(solution)/shard_map/ppermute | solution.py:36
  61.6 5.2 %collective-permute-start.3 = (bf16[2,48,3072]{2,1,0:T(8,128)(2,1)S(1)}, bf16[2,48,3072]{2,1,0:T(8,128)(2,1)S(1)}, u32[]{:S(2)}, u32[]{:S(2)}) collective-permute-start(bf16[2,48,3072]{2,1,0:T(8,128)(2,1)S(1)} %get-tuple-element.19.refs_0_), channel_id=1, source_target_pairs={{0,8},{8,0},{1,9},{9,1},{2,10},{10,2},{3,11},{11,3},{4,12},{12,4},... | collective-permute-start | bytes 1769480 | tf_op jit(solution)/shard_map/ppermute | solution.py:36
  64.7 4.1 %collective-permute-start.6 = (bf16[2,48,3072]{2,1,0:T(8,128)(2,1)}, bf16[2,48,3072]{2,1,0:T(8,128)(2,1)S(1)}, u32[]{:S(2)}, u32[]{:S(2)}) collective-permute-start(bf16[2,48,3072]{2,1,0:T(8,128)(2,1)} %collective-permute-done.2.refs_3_), channel_id=1, source_target_pairs={{0,8},{8,0},{1,9},{9,1},{2,10},{10,2},{3,11},{11,3},{4,12},{12,4},... | collective-permute-start | bytes 1769480 | tf_op jit(solution)/shard_map/ppermute | solution.py:36
  86.4 16.9 %copy-start.3 = (bf16[2,48,3072]{2,1,0:T(8,128)(2,1)S(1)}, bf16[2,48,3072]{2,1,0:T(8,128)(2,1)}, u32[]{:S(2)}) copy-start(bf16[2,48,3072]{2,1,0:T(8,128)(2,1)} %copy-done.1) | copy-start | bytes 1769476
  86.4 16.9 %copy-start.6 = (bf16[2,48,3072]{2,1,0:T(8,128)(2,1)S(1)}, bf16[2,48,3072]{2,1,0:T(8,128)(2,1)}, u32[]{:S(2)}) copy-start(bf16[2,48,3072]{2,1,0:T(8,128)(2,1)} %copy-done.4) | copy-start | bytes 1769476
  86.4 16.9 %copy-start.9 = (bf16[2,48,3072]{2,1,0:T(8,128)(2,1)S(1)}, bf16[2,48,3072]{2,1,0:T(8,128)(2,1)}, u32[]{:S(2)}) copy-start(bf16[2,48,3072]{2,1,0:T(8,128)(2,1)} %copy-done.7) | copy-start | bytes 1769476
  86.4 16.9 %copy-start.12 = (bf16[2,48,3072]{2,1,0:T(8,128)(2,1)S(1)}, bf16[2,48,3072]{2,1,0:T(8,128)(2,1)}, u32[]{:S(2)}) copy-start(bf16[2,48,3072]{2,1,0:T(8,128)(2,1)} %copy-done.10) | copy-start | bytes 1769476
  107.0 5.9 %copy-start.16 = (bf16[2,128,1536]{2,1,0:T(8,128)(2,1)S(1)}, bf16[2,128,1536]{2,1,0:T(8,128)(2,1)}, u32[]{:S(2)}) copy-start(bf16[2,128,1536]{2,1,0:T(8,128)(2,1)} %copy-done.15) | copy-start | bytes 2359300
  107.0 24.2 %all-to-all-start.3 = ((bf16[16,2,8,3072]{3,2,1,0:T(8,128)(2,1)}), bf16[16,2,8,3072]{3,2,1,0:T(8,128)(2,1)S(1)}, u32[]{:S(2)}, u32[]{:S(2)}) async-start(bf16[16,2,8,3072]{3,2,1,0:T(8,128)(2,1)} %get-tuple-element.27), calls=%async_computation.3 | async-start | bytes 3145728 | tf_op jit(solution)/shard_map/all_to_all | solution.py:28
  112.9 34.6 %collective-permute-start.7 = (bf16[2,128,1536]{2,1,0:T(8,128)(2,1)S(1)}, bf16[2,128,1536]{2,1,0:T(8,128)(2,1)S(1)}, u32[]{:S(2)}, u32[]{:S(2)}) collective-permute-start(bf16[2,128,1536]{2,1,0:T(8,128)(2,1)S(1)} %copy-done.16), channel_id=1, source_target_pairs={{0,8},{8,0},{1,9},{9,1},{2,10},{10,2},{3,11},{11,3},{4,12},{12,4},... | collective-permute-start | bytes 2359304 | tf_op jit(solution)/shard_map/ppermute | solution.py:36
  114.9 28.7 %collective-permute-start.8 = (bf16[2,2,1,2,48,128]{5,4,3,2,1,0:T(8,128)(2,1)S(1)}, bf16[2,2,1,2,48,128]{5,4,3,2,1,0:T(8,128)(2,1)S(1)}, u32[]{:S(2)}, u32[]{:S(2)}) collective-permute-start(bf16[2,2,1,2,48,128]{5,4,3,2,1,0:T(8,128)(2,1)S(1)} %get-tuple-element.30), channel_id=1, source_target_pairs={{0,2},{2,0},{4,6},{6,4},{1,3},{3,1},{5,7},{7,5},{8,10},{10,8},{12,... | collective-permute-start | bytes 294920 | tf_op jit(solution)/shard_map/ppermute | solution.py:36
  119.1 24.5 %collective-permute-start.9 = (bf16[2,2,1,2,48,128]{5,4,3,2,1,0:T(8,128)(2,1)S(1)}, bf16[2,2,1,2,48,128]{5,4,3,2,1,0:T(8,128)(2,1)}, u32[]{:S(2)}, u32[]{:S(2)}) collective-permute-start(bf16[2,2,1,2,48,128]{5,4,3,2,1,0:T(8,128)(2,1)S(1)} %get-tuple-element.30), channel_id=1, source_target_pairs={{0,4},{2,6},{4,0},{6,2},{1,5},{3,7},{5,1},{7,3},{8,12},{10,14},{12... | collective-permute-start | bytes 294920 | tf_op jit(solution)/shard_map/ppermute | solution.py:36
  126.4 17.2 %collective-permute-start.10 = (bf16[2,2,1,2,48,128]{5,4,3,2,1,0:T(8,128)(2,1)S(1)}, bf16[2,2,1,2,48,128]{5,4,3,2,1,0:T(8,128)(2,1)}, u32[]{:S(2)}, u32[]{:S(2)}) collective-permute-start(bf16[2,2,1,2,48,128]{5,4,3,2,1,0:T(8,128)(2,1)S(1)} %get-tuple-element.30), channel_id=1, source_target_pairs={{0,6},{2,4},{4,2},{6,0},{1,7},{3,5},{5,3},{7,1},{8,14},{10,12},{12... | collective-permute-start | bytes 294920 | tf_op jit(solution)/shard_map/ppermute | solution.py:36
  132.1 15.4 %copy-start.17 = (bf16[2,256,1536]{2,1,0:T(8,128)(2,1)S(1)}, bf16[2,256,1536]{2,1,0:T(8,128)(2,1)}, u32[]{:S(2)}) copy-start(bf16[2,256,1536]{2,1,0:T(8,128)(2,1)} %constant_dynamic-update-slice_fusion.1) | copy-start | bytes 4718596
  132.1 29.0 %all-to-all-start.4 = ((bf16[8,2,4,1536]{3,2,1,0:T(4,128)(2,1)}), bf16[8,2,4,1536]{3,2,1,0:T(4,128)(2,1)S(1)}, u32[]{:S(2)}, u32[]{:S(2)}) async-start(bf16[8,2,4,1536]{3,2,1,0:T(4,128)(2,1)} %plane_sums.1), calls=%async_computation.4 | async-start | bytes 393216 | tf_op jit(solution)/shard_map/all_to_all | solution.py:28
  145.6 3.3 %collective-permute-start.11 = (bf16[2,384,128]{2,1,0:T(8,128)(2,1)S(1)}, bf16[2,384,128]{2,1,0:T(8,128)(2,1)S(1)}, u32[]{:S(2)}, u32[]{:S(2)}) collective-permute-start(bf16[2,384,128]{2,1,0:T(8,128)(2,1)S(1)} %bitcast.24), channel_id=1, source_target_pairs={{0,8},{8,0},{1,9},{9,1},{2,10},{10,2},{3,11},{11,3},{4,12},{12,4},... | collective-permute-start | bytes 589832 | tf_op jit(solution)/shard_map/ppermute | solution.py:36
  (10 other events, 9.7 us)

commit v10 on v9

--- a/solution.py
+++ b/solution.py
@@ -114,10 +114,17 @@
     )(block, column)
 
 
-def hidden_kernel(member_ref, rows_ref, *refs):
-    own, beside, out_ref, mine_ref = refs[:4], refs[4:8], refs[8], refs[9]
-    units = own[0].shape[1]
+def hidden_kernel(member_ref, source_ref, *refs):
+    pieces, (out_ref, mine_ref, rows_ref, held_ref, sems) = refs[:8], refs[8:]
+    units = pieces[0].shape[1]
     width = rows_ref.shape[4]
+    copies = [pltpu.make_async_copy(source_ref, rows_ref, sems.at[8])]
+    copies += [pltpu.make_async_copy(pieces[at], held_ref.at[at], sems.at[at]) for at in range(8)]
+    for copy in copies:
+        copy.start()
+    for copy in copies:
+        copy.wait()
+    own, beside = ([held_ref.at[core * 4 + at] for at in range(4)] for core in range(2))
     for kind in range(2):
         rows = [rows_ref[:, far, kind].reshape(-1, width) for far in range(3)]
         mine_ref[kind] = rows[2]
@@ -147,9 +154,14 @@
             jax.ShapeDtypeStruct((4, 4, 3, 2, units, tokens), BF16),
             jax.ShapeDtypeStruct((2, tokens, rows.shape[4]), BF16),
         ],
-        in_specs=[pl.BlockSpec(memory_space=pltpu.SMEM)] + [pl.BlockSpec(memory_space=pltpu.VMEM)] * 9,
+        in_specs=[pl.BlockSpec(memory_space=pltpu.SMEM)] + [pl.BlockSpec(memory_space=pltpu.HBM)] * 9,
         out_specs=[pl.BlockSpec(memory_space=pltpu.VMEM)] * 2,
-        compiler_params=pltpu.CompilerParams(vmem_limit_bytes=VMEM_BYTES),
+        scratch_shapes=[
+            pltpu.VMEM(rows.shape, BF16),
+            pltpu.VMEM((8,) + own[0].shape, BF16),
+            pltpu.SemaphoreType.DMA((9,)),
+        ],
+        compiler_params=pltpu.CompilerParams(vmem_limit_bytes=3 * VMEM_BYTES),
         cost_estimate=pl.CostEstimate(flops=604_000_000, bytes_accessed=6_700_000, transcendentals=0),
         name="hidden_parts",
     )(member, rows, *own, *beside)

time: 163 us -> 164 us (level)
  local copies, waits for them, and re-layouts: 16.7 us -> 9.34 us
  Pallas kernels: 8.79 us -> 13 us
  waiting for transfers between devices: 39.3 us -> 42.5 us
    unnamed x37 -> x33, local copies, waits for them, and re-layouts: 13.4 us -> 6.7 us
    all_to_all x4, waiting for transfers between devices: 24.8 us -> 29.3 us  [exchange(): return lax.all_to_all(value, axes, split_axis=0, concat_axis=0, tiled=True)]
    pallas_call x1, Pallas kernels: 2.72 us -> 5.8 us  [hidden_parts(): pl.pallas_call(hidden_kernel, out_shape=[jax.ShapeDtypeStruct((4, 4, 3, 2...]
    dynamic_update_slice x4, local copies, waits for them, and re-layouts: 1.87 us -> 0.08 us  [gather_ring(): whole = lax.dynamic_update_slice(whole, block, tuple(start))]
  transfers between devices with their start and end apart: 16 -> 16, of which waited for: 9 -> 9; matrix products, arithmetic and copies ran while one was open for 4% -> 3% of each run, Pallas kernels for 1% -> 2%
where the time goes in v10:
time: 164 us; the launch traced here: 163 us
  starting transfers between devices  75.8 us (46%)
  waiting for transfers between devices  42.5 us (26%)
  blocking collectives  17.1 us (10%)
  Pallas kernels  13 us (8%)
  local copies, waits for them, and re-layouts  9.34 us (6%)
  matrix products  3.12 us (2%)
    all_to_all x4, starting transfers between devices, exchange(): return lax.all_to_all(value, axes, split_axis=0, concat_axis=0, tiled=True)  40.5 us
    ppermute x12, starting transfers between devices, partner(): return lax.ppermute(value, axes, [(at, at ^ step) for at in range(count)])  35.3 us
    all_to_all x4, waiting for transfers between devices, exchange(): return lax.all_to_all(value, axes, split_axis=0, concat_axis=0, tiled=True)  29.3 us
    all_to_all x1, blocking collectives, exchange(): return lax.all_to_all(value, axes, split_axis=0, concat_axis=0, tiled=True)  17.1 us
    ppermute x12, waiting for transfers between devices, partner(): return lax.ppermute(value, axes, [(at, at ^ step) for at in range(count)])  13.2 us
    unnamed x33, local copies, waits for them, and re-layouts  6.7 us
    pallas_call x1, Pallas kernels, hidden_parts(): pl.pallas_call(hidden_kernel, out_shape=[jax.ShapeDtypeStruct((4, 4, 3, 2...  5.8 us
    pallas_call x1, Pallas kernels, output_parts(): pl.pallas_call(output_kernel, out_shape=[jax.ShapeDtypeStruct((count, 2,...  3.48 us
  transfers between devices with their start and end apart: 16, of which 9 were waited for; matrix products, arithmetic and copies ran while one was open for 3% of the time, Pallas kernels for 2%

profile of v10, /device:TPU:6, one launch (start us, length us, event | category | flops | bytes accessed | tf_op | source)
XLA Modules:
  0.0 162.7 jit_solution(5255247165665371818)
XLA Ops:
  2.1 15.1 %all-to-all-start = ((bf16[8,8,1536]{2,1,0:T(8,128)(2,1)}), bf16[8,8,1536]{2,1,0:T(8,128)(2,1)S(1)}, u32[]{:S(2)}, u32[]{:S(2)}) async-start(bf16[8,8,1536]{2,1,0:T(8,128)(2,1)} %broadcast_in_dim.4), calls=%async_computation | async-start | bytes 393216 | tf_op jit(solution)/shard_map/all_to_all | solution.py:28
  20.9 2.7 %collective-permute-start = (bf16[2,48,3072]{2,1,0:T(8,128)(2,1)}, bf16[2,48,3072]{2,1,0:T(8,128)(2,1)S(1)}, u32[]{:S(2)}, u32[]{:S(2)}) collective-permute-start(bf16[2,48,3072]{2,1,0:T(8,128)(2,1)} %get-tuple-element.20), channel_id=1, source_target_pairs={{0,128},{1,129},{128,0},{129,1},{2,130},{3,131},{130,2},{131,3},{4... | collective-permute-start | bytes 1769480 | tf_op jit(solution)/shard_map/ppermute | solution.py:36
  23.6 3.6 %collective-permute-start.1 = (bf16[2,48,3072]{2,1,0:T(8,128)(2,1)}, bf16[2,48,3072]{2,1,0:T(8,128)(2,1)S(1)}, u32[]{:S(2)}, u32[]{:S(2)}) collective-permute-start(bf16[2,48,3072]{2,1,0:T(8,128)(2,1)} %get-tuple-element.21), channel_id=1, source_target_pairs={{0,129},{1,128},{128,1},{129,0},{2,131},{3,130},{130,3},{131,2},{4... | collective-permute-start | bytes 1769480 | tf_op jit(solution)/shard_map/ppermute | solution.py:36
  27.2 2.9 %collective-permute-start.2 = (bf16[2,48,3072]{2,1,0:T(8,128)(2,1)S(1)}, bf16[2,48,3072]{2,1,0:T(8,128)(2,1)S(1)}, u32[]{:S(2)}, u32[]{:S(2)}) collective-permute-start(bf16[2,48,3072]{2,1,0:T(8,128)(2,1)S(1)} %get-tuple-element.22), channel_id=1, source_target_pairs={{0,1},{1,0},{128,129},{129,128},{2,3},{3,2},{130,131},{131,130},{4... | collective-permute-start | bytes 1769480 | tf_op jit(solution)/shard_map/ppermute | solution.py:36
  30.1 5.7 %all-to-all-done.column_ref = bf16[8,8,1536]{2,1,0:T(8,128)(2,1)S(1)} async-done(((bf16[8,8,1536]{2,1,0:T(8,128)(2,1)}), bf16[8,8,1536]{2,1,0:T(8,128)(2,1)S(1)}, u32[]{:S(2)}, u32[]{:S(2)}) %all-to-all-start) | async-done | bytes 196640 | tf_op jit(solution)/shard_map/all_to_all | solution.py:28
  37.5 7.4 %all-to-all-start.1 = ((bf16[16,3,2,8,1536]{4,3,2,1,0:T(8,128)(2,1)}), bf16[16,3,2,8,1536]{4,3,2,1,0:T(8,128)(2,1)}, u32[]{:S(2)}, u32[]{:S(2)}) async-start(bf16[16,3,2,8,1536]{4,3,2,1,0:T(8,128)(2,1)} %lay_out_rows.1), calls=%async_computation.1 | async-start | bytes 4718592 | tf_op jit(solution)/shard_map/all_to_all | solution.py:28
  44.9 6.9 %collective-permute-done.refs_1_ = bf16[2,48,3072]{2,1,0:T(8,128)(2,1)S(1)} collective-permute-done((bf16[2,48,3072]{2,1,0:T(8,128)(2,1)}, bf16[2,48,3072]{2,1,0:T(8,128)(2,1)S(1)}, u32[]{:S(2)}, u32[]{:S(2)}) %collective-permute-start) | collective-permute-done | bytes 589856 | tf_op jit(solution)/shard_map/ppermute | solution.py:36
  51.8 2.9 %collective-permute-done.2.refs_3_ = bf16[2,48,3072]{2,1,0:T(8,128)(2,1)S(1)} collective-permute-done((bf16[2,48,3072]{2,1,0:T(8,128)(2,1)S(1)}, bf16[2,48,3072]{2,1,0:T(8,128)(2,1)S(1)}, u32[]{:S(2)}, u32[]{:S(2)}) %collective-permute-start.2) | collective-permute-done | bytes 589856 | tf_op jit(solution)/shard_map/ppermute | solution.py:36
  56.7 2.0 %collective-permute-done.4.refs_5_ = bf16[2,48,3072]{2,1,0:T(8,128)(2,1)S(1)} collective-permute-done((bf16[2,48,3072]{2,1,0:T(8,128)(2,1)S(1)}, bf16[2,48,3072]{2,1,0:T(8,128)(2,1)S(1)}, u32[]{:S(2)}, u32[]{:S(2)}) %collective-permute-start.4) | collective-permute-done | bytes 589856 | tf_op jit(solution)/shard_map/ppermute | solution.py:36
  58.6 2.0 %collective-permute-start.5 = (bf16[2,48,3072]{2,1,0:T(8,128)(2,1)S(1)}, bf16[2,48,3072]{2,1,0:T(8,128)(2,1)S(1)}, u32[]{:S(2)}, u32[]{:S(2)}) collective-permute-start(bf16[2,48,3072]{2,1,0:T(8,128)(2,1)S(1)} %collective-permute-done.1.refs_2_), channel_id=1, source_target_pairs={{0,8},{8,0},{1,9},{9,1},{2,10},{10,2},{3,11},{11,3},{4,12},{12,4},... | collective-permute-start | bytes 1769480 | tf_op jit(solution)/shard_map/ppermute | solution.py:36
  60.7 2.3 %collective-permute-start.3 = (bf16[2,48,3072]{2,1,0:T(8,128)(2,1)S(1)}, bf16[2,48,3072]{2,1,0:T(8,128)(2,1)S(1)}, u32[]{:S(2)}, u32[]{:S(2)}) collective-permute-start(bf16[2,48,3072]{2,1,0:T(8,128)(2,1)S(1)} %get-tuple-element.19.refs_0_), channel_id=1, source_target_pairs={{0,8},{8,0},{1,9},{9,1},{2,10},{10,2},{3,11},{11,3},{4,12},{12,4},... | collective-permute-start | bytes 1769480 | tf_op jit(solution)/shard_map/ppermute | solution.py:36
  63.0 2.0 %collective-permute-start.6 = (bf16[2,48,3072]{2,1,0:T(8,128)(2,1)S(1)}, bf16[2,48,3072]{2,1,0:T(8,128)(2,1)}, u32[]{:S(2)}, u32[]{:S(2)}) collective-permute-start(bf16[2,48,3072]{2,1,0:T(8,128)(2,1)S(1)} %collective-permute-done.2.refs_3_), channel_id=1, source_target_pairs={{0,8},{8,0},{1,9},{9,1},{2,10},{10,2},{3,11},{11,3},{4,12},{12,4},... | collective-permute-start | bytes 1769480 | tf_op jit(solution)/shard_map/ppermute | solution.py:36
  67.0 11.4 %all-to-all-done.1.source_ref = bf16[16,3,2,8,1536]{4,3,2,1,0:T(8,128)(2,1)} async-done(((bf16[16,3,2,8,1536]{4,3,2,1,0:T(8,128)(2,1)}), bf16[16,3,2,8,1536]{4,3,2,1,0:T(8,128)(2,1)}, u32[]{:S(2)}, u32[]{:S(2)}) %all-to-all-start.1) | async-done | bytes 2359328 | tf_op jit(solution)/shard_map/all_to_all | solution.py:28
  78.5 5.8 %hidden_parts.1 = (bf16[4,4,3,2,48,128]{5,4,3,2,1,0:T(8,128)(2,1)}, bf16[2,128,1536]{2,1,0:T(8,128)(2,1)}) custom-call(s32[1]{0:T(128)} %bitcast.member_ref, bf16[16,3,2,8,1536]{4,3,2,1,0:T(8,128)(2,1)} %all-to-all-done.1.source_ref, bf16[2,48,3072]{2,1,0:T(8,128)(2,1)} %copy-done, bf16[2,48,3072]{2,1,0:T(8,128)(2,1)} %copy-done.2, ...), custom_call_target="tpu_custom_call" | custom-call | flops 604000000 | bytes 6700000 | tf_op jit(solution)/shard_map/hidden_parts/pallas_call | solution.py:151
  84.3 17.1 %all_to_all.25.parts_ref = bf16[4,4,3,2,48,128]{5,4,3,2,1,0:T(8,128)(2,1)S(1)} all-to-all(bf16[4,4,3,2,48,128]{5,4,3,2,1,0:T(8,128)(2,1)} %get-tuple-element.26), channel_id=1, replica_groups=mesh['xh'=2,'xp'=2,'zh'=2,'y'=4,'c'=2,'z2'=2,'z1'=2,'zp'=2] {'xp','zp'}, dimensions={0} | all-to-all | bytes 2359296 | tf_op jit(solution)/shard_map/all_to_all | solution.py:28
  103.6 3.5 %output_parts.1 = (bf16[16,2,8,3072]{3,2,1,0:T(8,128)(2,1)}, bf16[2,2,1,2,48,128]{5,4,3,2,1,0:T(8,128)(2,1)S(1)}) custom-call(s32[1]{0:T(128)} %bitcast.member_ref, bf16[4,4,3,2,48,128]{5,4,3,2,1,0:T(8,128)(2,1)S(1)} %all_to_all.25.parts_ref, bf16[2,48,3072]{2,1,0:T(8,128)(2,1)S(1)} %copy-done.1, bf16[2,48,3072]{2,1,0:T(8,128)(2,1)S(1)} %copy-done.3, ...), custom_call_target="tpu_custom_call" | custom-call | flops 604000000 | bytes 6700000 | tf_op jit(solution)/shard_map/output_parts/pallas_call | solution.py:202
  107.1 6.6 %all-to-all-start.3 = ((bf16[16,2,8,3072]{3,2,1,0:T(8,128)(2,1)}), bf16[16,2,8,3072]{3,2,1,0:T(8,128)(2,1)S(1)}, u32[]{:S(2)}, u32[]{:S(2)}) async-start(bf16[16,2,8,3072]{3,2,1,0:T(8,128)(2,1)} %get-tuple-element.27), calls=%async_computation.3 | async-start | bytes 3145728 | tf_op jit(solution)/shard_map/all_to_all | solution.py:28
  113.7 1.9 %collective-permute-start.7 = (bf16[2,128,1536]{2,1,0:T(8,128)(2,1)}, bf16[2,128,1536]{2,1,0:T(8,128)(2,1)}, u32[]{:S(2)}, u32[]{:S(2)}) collective-permute-start(bf16[2,128,1536]{2,1,0:T(8,128)(2,1)} %get-tuple-element.28), channel_id=1, source_target_pairs={{0,8},{8,0},{1,9},{9,1},{2,10},{10,2},{3,11},{11,3},{4,12},{12,4},... | collective-permute-start | bytes 2359304 | tf_op jit(solution)/shard_map/ppermute | solution.py:36
  115.7 4.3 %collective-permute-start.8 = (bf16[2,2,1,2,48,128]{5,4,3,2,1,0:T(8,128)(2,1)S(1)}, bf16[2,2,1,2,48,128]{5,4,3,2,1,0:T(8,128)(2,1)S(1)}, u32[]{:S(2)}, u32[]{:S(2)}) collective-permute-start(bf16[2,2,1,2,48,128]{5,4,3,2,1,0:T(8,128)(2,1)S(1)} %get-tuple-element.30), channel_id=1, source_target_pairs={{0,2},{2,0},{4,6},{6,4},{1,3},{3,1},{5,7},{7,5},{8,10},{10,8},{12,... | collective-permute-start | bytes 294920 | tf_op jit(solution)/shard_map/ppermute | solution.py:36
  119.9 7.3 %collective-permute-start.9 = (bf16[2,2,1,2,48,128]{5,4,3,2,1,0:T(8,128)(2,1)S(1)}, bf16[2,2,1,2,48,128]{5,4,3,2,1,0:T(8,128)(2,1)S(1)}, u32[]{:S(2)}, u32[]{:S(2)}) collective-permute-start(bf16[2,2,1,2,48,128]{5,4,3,2,1,0:T(8,128)(2,1)S(1)} %get-tuple-element.30), channel_id=1, source_target_pairs={{0,4},{2,6},{4,0},{6,2},{1,5},{3,7},{5,1},{7,3},{8,12},{10,14},{12... | collective-permute-start | bytes 294920 | tf_op jit(solution)/shard_map/ppermute | solution.py:36
  127.2 2.5 %collective-permute-start.10 = (bf16[2,2,1,2,48,128]{5,4,3,2,1,0:T(8,128)(2,1)S(1)}, bf16[2,2,1,2,48,128]{5,4,3,2,1,0:T(8,128)(2,1)S(1)}, u32[]{:S(2)}, u32[]{:S(2)}) collective-permute-start(bf16[2,2,1,2,48,128]{5,4,3,2,1,0:T(8,128)(2,1)S(1)} %get-tuple-element.30), channel_id=1, source_target_pairs={{0,6},{2,4},{4,2},{6,0},{1,7},{3,5},{5,3},{7,1},{8,14},{10,12},{12... | collective-permute-start | bytes 294920 | tf_op jit(solution)/shard_map/ppermute | solution.py:36
  132.9 11.3 %all-to-all-start.4 = ((bf16[8,2,4,1536]{3,2,1,0:T(4,128)(2,1)}), bf16[8,2,4,1536]{3,2,1,0:T(4,128)(2,1)S(1)}, u32[]{:S(2)}, u32[]{:S(2)}) async-start(bf16[8,2,4,1536]{3,2,1,0:T(4,128)(2,1)} %plane_sums.1), calls=%async_computation.4 | async-start | bytes 393216 | tf_op jit(solution)/shard_map/all_to_all | solution.py:28
  144.5 1.9 %collective-permute-start.11 = (bf16[2,384,128]{2,1,0:T(8,128)(2,1)S(1)}, bf16[2,384,128]{2,1,0:T(8,128)(2,1)S(1)}, u32[]{:S(2)}, u32[]{:S(2)}) collective-permute-start(bf16[2,384,128]{2,1,0:T(8,128)(2,1)S(1)} %bitcast.24), channel_id=1, source_target_pairs={{0,8},{8,0},{1,9},{9,1},{2,10},{10,2},{3,11},{11,3},{4,12},{12,4},... | collective-permute-start | bytes 589832 | tf_op jit(solution)/shard_map/ppermute | solution.py:36
  151.0 11.0 %all-to-all-done.4 = bf16[8,2,4,1536]{3,2,1,0:T(4,128)(2,1)S(1)} async-done(((bf16[8,2,4,1536]{3,2,1,0:T(4,128)(2,1)}), bf16[8,2,4,1536]{3,2,1,0:T(4,128)(2,1)S(1)}, u32[]{:S(2)}, u32[]{:S(2)}) %all-to-all-start.4) | async-done | bytes 196640 | tf_op jit(solution)/shard_map/all_to_all | solution.py:28
  (60 shorter events, 21.4 us)
Async XLA Ops:
  2.1 33.8 %all-to-all-start = ((bf16[8,8,1536]{2,1,0:T(8,128)(2,1)}), bf16[8,8,1536]{2,1,0:T(8,128)(2,1)S(1)}, u32[]{:S(2)}, u32[]{:S(2)}) async-start(bf16[8,8,1536]{2,1,0:T(8,128)(2,1)} %broadcast_in_dim.4), calls=%async_computation | async-start | bytes 393216 | tf_op jit(solution)/shard_map/all_to_all | solution.py:28
  20.9 39.8 %copy-start = (bf16[2,48,3072]{2,1,0:T(8,128)(2,1)}, bf16[2,48,3072]{2,1,0:T(8,128)(2,1)S(1)}, u32[]{:S(2)}) copy-start(bf16[2,48,3072]{2,1,0:T(8,128)(2,1)S(1)} %get-tuple-element.19.refs_0_) | copy-start | bytes 1769476
  20.9 31.0 %collective-permute-start = (bf16[2,48,3072]{2,1,0:T(8,128)(2,1)}, bf16[2,48,3072]{2,1,0:T(8,128)(2,1)S(1)}, u32[]{:S(2)}, u32[]{:S(2)}) collective-permute-start(bf16[2,48,3072]{2,1,0:T(8,128)(2,1)} %get-tuple-element.20), channel_id=1, source_target_pairs={{0,128},{1,129},{128,0},{129,1},{2,130},{3,131},{130,2},{131,3},{4... | collective-permute-start | bytes 1769480 | tf_op jit(solution)/shard_map/ppermute | solution.py:36
  23.6 28.3 %collective-permute-start.1 = (bf16[2,48,3072]{2,1,0:T(8,128)(2,1)}, bf16[2,48,3072]{2,1,0:T(8,128)(2,1)S(1)}, u32[]{:S(2)}, u32[]{:S(2)}) collective-permute-start(bf16[2,48,3072]{2,1,0:T(8,128)(2,1)} %get-tuple-element.21), channel_id=1, source_target_pairs={{0,129},{1,128},{128,1},{129,0},{2,131},{3,130},{130,3},{131,2},{4... | collective-permute-start | bytes 1769480 | tf_op jit(solution)/shard_map/ppermute | solution.py:36
  27.2 27.6 %collective-permute-start.2 = (bf16[2,48,3072]{2,1,0:T(8,128)(2,1)S(1)}, bf16[2,48,3072]{2,1,0:T(8,128)(2,1)S(1)}, u32[]{:S(2)}, u32[]{:S(2)}) collective-permute-start(bf16[2,48,3072]{2,1,0:T(8,128)(2,1)S(1)} %get-tuple-element.22), channel_id=1, source_target_pairs={{0,1},{1,0},{128,129},{129,128},{2,3},{3,2},{130,131},{131,130},{4... | collective-permute-start | bytes 1769480 | tf_op jit(solution)/shard_map/ppermute | solution.py:36
  37.5 41.0 %all-to-all-start.1 = ((bf16[16,3,2,8,1536]{4,3,2,1,0:T(8,128)(2,1)}), bf16[16,3,2,8,1536]{4,3,2,1,0:T(8,128)(2,1)}, u32[]{:S(2)}, u32[]{:S(2)}) async-start(bf16[16,3,2,8,1536]{4,3,2,1,0:T(8,128)(2,1)} %lay_out_rows.1), calls=%async_computation.1 | async-start | bytes 4718592 | tf_op jit(solution)/shard_map/all_to_all | solution.py:28
  51.8 26.6 %copy-start.2 = (bf16[2,48,3072]{2,1,0:T(8,128)(2,1)}, bf16[2,48,3072]{2,1,0:T(8,128)(2,1)S(1)}, u32[]{:S(2)}) copy-start(bf16[2,48,3072]{2,1,0:T(8,128)(2,1)S(1)} %collective-permute-done.refs_1_) | copy-start | bytes 1769476
  51.8 26.6 %copy-start.4 = (bf16[2,48,3072]{2,1,0:T(8,128)(2,1)}, bf16[2,48,3072]{2,1,0:T(8,128)(2,1)S(1)}, u32[]{:S(2)}) copy-start(bf16[2,48,3072]{2,1,0:T(8,128)(2,1)S(1)} %collective-permute-done.1.refs_2_) | copy-start | bytes 1769476
  54.7 23.7 %copy-start.6 = (bf16[2,48,3072]{2,1,0:T(8,128)(2,1)}, bf16[2,48,3072]{2,1,0:T(8,128)(2,1)S(1)}, u32[]{:S(2)}) copy-start(bf16[2,48,3072]{2,1,0:T(8,128)(2,1)S(1)} %collective-permute-done.2.refs_3_) | copy-start | bytes 1769476
  54.7 3.9 %collective-permute-start.4 = (bf16[2,48,3072]{2,1,0:T(8,128)(2,1)S(1)}, bf16[2,48,3072]{2,1,0:T(8,128)(2,1)S(1)}, u32[]{:S(2)}, u32[]{:S(2)}) collective-permute-start(bf16[2,48,3072]{2,1,0:T(8,128)(2,1)S(1)} %collective-permute-done.refs_1_), channel_id=1, source_target_pairs={{0,8},{8,0},{1,9},{9,1},{2,10},{10,2},{3,11},{11,3},{4,12},{12,4},... | collective-permute-start | bytes 1769480 | tf_op jit(solution)/shard_map/ppermute | solution.py:36
  58.6 19.8 %copy-start.8 = (bf16[2,48,3072]{2,1,0:T(8,128)(2,1)}, bf16[2,48,3072]{2,1,0:T(8,128)(2,1)S(1)}, u32[]{:S(2)}) copy-start(bf16[2,48,3072]{2,1,0:T(8,128)(2,1)S(1)} %collective-permute-done.4.refs_5_) | copy-start | bytes 1769476
  58.6 4.3 %collective-permute-start.5 = (bf16[2,48,3072]{2,1,0:T(8,128)(2,1)S(1)}, bf16[2,48,3072]{2,1,0:T(8,128)(2,1)S(1)}, u32[]{:S(2)}, u32[]{:S(2)}) collective-permute-start(bf16[2,48,3072]{2,1,0:T(8,128)(2,1)S(1)} %collective-permute-done.1.refs_2_), channel_id=1, source_target_pairs={{0,8},{8,0},{1,9},{9,1},{2,10},{10,2},{3,11},{11,3},{4,12},{12,4},... | collective-permute-start | bytes 1769480 | tf_op jit(solution)/shard_map/ppermute | solution.py:36
  60.7 4.4 %collective-permute-start.3 = (bf16[2,48,3072]{2,1,0:T(8,128)(2,1)S(1)}, bf16[2,48,3072]{2,1,0:T(8,128)(2,1)S(1)}, u32[]{:S(2)}, u32[]{:S(2)}) collective-permute-start(bf16[2,48,3072]{2,1,0:T(8,128)(2,1)S(1)} %get-tuple-element.19.refs_0_), channel_id=1, source_target_pairs={{0,8},{8,0},{1,9},{9,1},{2,10},{10,2},{3,11},{11,3},{4,12},{12,4},... | collective-permute-start | bytes 1769480 | tf_op jit(solution)/shard_map/ppermute | solution.py:36
  63.0 4.0 %collective-permute-start.6 = (bf16[2,48,3072]{2,1,0:T(8,128)(2,1)S(1)}, bf16[2,48,3072]{2,1,0:T(8,128)(2,1)}, u32[]{:S(2)}, u32[]{:S(2)}) collective-permute-start(bf16[2,48,3072]{2,1,0:T(8,128)(2,1)S(1)} %collective-permute-done.2.refs_3_), channel_id=1, source_target_pairs={{0,8},{8,0},{1,9},{9,1},{2,10},{10,2},{3,11},{11,3},{4,12},{12,4},... | collective-permute-start | bytes 1769480 | tf_op jit(solution)/shard_map/ppermute | solution.py:36
  78.5 23.0 %copy-start.13 = (bf16[2,48,3072]{2,1,0:T(8,128)(2,1)S(1)}, bf16[2,48,3072]{2,1,0:T(8,128)(2,1)}, u32[]{:S(2)}) copy-start(bf16[2,48,3072]{2,1,0:T(8,128)(2,1)} %copy-done.12) | copy-start | bytes 1769476
  84.3 17.2 %copy-start.1 = (bf16[2,48,3072]{2,1,0:T(8,128)(2,1)S(1)}, bf16[2,48,3072]{2,1,0:T(8,128)(2,1)}, u32[]{:S(2)}) copy-start(bf16[2,48,3072]{2,1,0:T(8,128)(2,1)} %copy-done) | copy-start | bytes 1769476
  84.3 17.2 %copy-start.3 = (bf16[2,48,3072]{2,1,0:T(8,128)(2,1)S(1)}, bf16[2,48,3072]{2,1,0:T(8,128)(2,1)}, u32[]{:S(2)}) copy-start(bf16[2,48,3072]{2,1,0:T(8,128)(2,1)} %copy-done.2) | copy-start | bytes 1769476
  107.1 24.9 %all-to-all-start.3 = ((bf16[16,2,8,3072]{3,2,1,0:T(8,128)(2,1)}), bf16[16,2,8,3072]{3,2,1,0:T(8,128)(2,1)S(1)}, u32[]{:S(2)}, u32[]{:S(2)}) async-start(bf16[16,2,8,3072]{3,2,1,0:T(8,128)(2,1)} %get-tuple-element.27), calls=%async_computation.3 | async-start | bytes 3145728 | tf_op jit(solution)/shard_map/all_to_all | solution.py:28
  113.7 32.7 %collective-permute-start.7 = (bf16[2,128,1536]{2,1,0:T(8,128)(2,1)}, bf16[2,128,1536]{2,1,0:T(8,128)(2,1)}, u32[]{:S(2)}, u32[]{:S(2)}) collective-permute-start(bf16[2,128,1536]{2,1,0:T(8,128)(2,1)} %get-tuple-element.28), channel_id=1, source_target_pairs={{0,8},{8,0},{1,9},{9,1},{2,10},{10,2},{3,11},{11,3},{4,12},{12,4},... | collective-permute-start | bytes 2359304 | tf_op jit(solution)/shard_map/ppermute | solution.py:36
  115.7 28.6 %collective-permute-start.8 = (bf16[2,2,1,2,48,128]{5,4,3,2,1,0:T(8,128)(2,1)S(1)}, bf16[2,2,1,2,48,128]{5,4,3,2,1,0:T(8,128)(2,1)S(1)}, u32[]{:S(2)}, u32[]{:S(2)}) collective-permute-start(bf16[2,2,1,2,48,128]{5,4,3,2,1,0:T(8,128)(2,1)S(1)} %get-tuple-element.30), channel_id=1, source_target_pairs={{0,2},{2,0},{4,6},{6,4},{1,3},{3,1},{5,7},{7,5},{8,10},{10,8},{12,... | collective-permute-start | bytes 294920 | tf_op jit(solution)/shard_map/ppermute | solution.py:36
  119.9 24.3 %collective-permute-start.9 = (bf16[2,2,1,2,48,128]{5,4,3,2,1,0:T(8,128)(2,1)S(1)}, bf16[2,2,1,2,48,128]{5,4,3,2,1,0:T(8,128)(2,1)S(1)}, u32[]{:S(2)}, u32[]{:S(2)}) collective-permute-start(bf16[2,2,1,2,48,128]{5,4,3,2,1,0:T(8,128)(2,1)S(1)} %get-tuple-element.30), channel_id=1, source_target_pairs={{0,4},{2,6},{4,0},{6,2},{1,5},{3,7},{5,1},{7,3},{8,12},{10,14},{12... | collective-permute-start | bytes 294920 | tf_op jit(solution)/shard_map/ppermute | solution.py:36
  127.2 17.1 %collective-permute-start.10 = (bf16[2,2,1,2,48,128]{5,4,3,2,1,0:T(8,128)(2,1)S(1)}, bf16[2,2,1,2,48,128]{5,4,3,2,1,0:T(8,128)(2,1)S(1)}, u32[]{:S(2)}, u32[]{:S(2)}) collective-permute-start(bf16[2,2,1,2,48,128]{5,4,3,2,1,0:T(8,128)(2,1)S(1)} %get-tuple-element.30), channel_id=1, source_target_pairs={{0,6},{2,4},{4,2},{6,0},{1,7},{3,5},{5,3},{7,1},{8,14},{10,12},{12... | collective-permute-start | bytes 294920 | tf_op jit(solution)/shard_map/ppermute | solution.py:36
  132.9 29.0 %all-to-all-start.4 = ((bf16[8,2,4,1536]{3,2,1,0:T(4,128)(2,1)}), bf16[8,2,4,1536]{3,2,1,0:T(4,128)(2,1)S(1)}, u32[]{:S(2)}, u32[]{:S(2)}) async-start(bf16[8,2,4,1536]{3,2,1,0:T(4,128)(2,1)} %plane_sums.1), calls=%async_computation.4 | async-start | bytes 393216 | tf_op jit(solution)/shard_map/all_to_all | solution.py:28
  144.5 3.3 %collective-permute-start.11 = (bf16[2,384,128]{2,1,0:T(8,128)(2,1)S(1)}, bf16[2,384,128]{2,1,0:T(8,128)(2,1)S(1)}, u32[]{:S(2)}, u32[]{:S(2)}) collective-permute-start(bf16[2,384,128]{2,1,0:T(8,128)(2,1)S(1)} %bitcast.24), channel_id=1, source_target_pairs={{0,8},{8,0},{1,9},{9,1},{2,10},{10,2},{3,11},{11,3},{4,12},{12,4},... | collective-permute-start | bytes 589832 | tf_op jit(solution)/shard_map/ppermute | solution.py:36
  (8 other events, 55.3 us)

commit v11 on v10

--- a/solution.py
+++ b/solution.py
@@ -122,17 +122,19 @@
     copies += [pltpu.make_async_copy(pieces[at], held_ref.at[at], sems.at[at]) for at in range(8)]
     for copy in copies:
         copy.start()
-    for copy in copies:
-        copy.wait()
-    own, beside = ([held_ref.at[core * 4 + at] for at in range(4)] for core in range(2))
-    for kind in range(2):
-        rows = [rows_ref[:, far, kind].reshape(-1, width) for far in range(3)]
-        mine_ref[kind] = rows[2]
-        for core, pieces in enumerate((own, beside)):
+    copies[0].wait()
+    for core in range(2):
+        held = [held_ref.at[core * 4 + at] for at in range(4)]
+        for copy in copies[1 + core * 4 : 5 + core * 4]:
+            copy.wait()
+        for kind in range(2):
+            rows = [rows_ref[:, far, kind].reshape(-1, width) for far in range(2)]
+            if core == 0:
+                mine_ref[kind] = rows_ref[:, 2, kind].reshape(-1, width)
             total = None
             for far in range(2):
                 weight = jnp.concatenate(
-                    [piece[kind, :, far * width : (far + 1) * width] for piece in pieces], axis=0
+                    [piece[kind, :, far * width : (far + 1) * width] for piece in held], axis=0
                 )
                 term = dot(weight, rows[far], 1, 1)
                 total = term if total is None else total + term
@@ -168,8 +170,11 @@
 
 
 def output_kernel(member_ref, parts_ref, *refs):
-    own, beside, out_ref, pair_ref = refs[:4], refs[4:8], refs[8], refs[9]
-    features = own[0].shape[2]
+    pieces, (out_ref, pair_ref, held_ref, sems) = refs[:8], refs[8:]
+    copies = [pltpu.make_async_copy(pieces[at], held_ref.at[at], sems.at[at]) for at in range(8)]
+    for copy in copies:
+        copy.start()
+    features = pieces[0].shape[2]
     count, unused, rows, unused = out_ref.shape
     step_of = features // 4
     units = [[], []]
@@ -185,12 +190,14 @@
                 units[kind].append(values[kind])
                 if step < 2:
                     pair_ref[core, kind, 0, slot % 2] = values[kind]
+    for copy in copies:
+        copy.wait()
     for result in range(2):
         left = jnp.concatenate(units[result], axis=0)
-        for at in range(4):
-            columns = slice(at * step_of, (at + 1) * step_of)
+        for cut_at in range(4):
+            columns = slice(cut_at * step_of, (cut_at + 1) * step_of)
             weight = jnp.concatenate(
-                [piece[1 - result, :, columns] for piece in (*own, *beside)], axis=0
+                [held_ref[at, 1 - result, :, columns] for at in range(8)], axis=0
             )
             total = dot(left, weight, 0, 0)
             out_ref[:, result, :, columns] = total.astype(BF16).reshape(count, rows, step_of)
@@ -205,9 +212,11 @@
             jax.ShapeDtypeStruct((count, 2, tokens // count, features), BF16),
             jax.ShapeDtypeStruct((2, 2, 1, 2, units, tokens), BF16),
         ],
-        in_specs=[pl.BlockSpec(memory_space=pltpu.SMEM)] + [pl.BlockSpec(memory_space=pltpu.VMEM)] * 9,
+        in_specs=[pl.BlockSpec(memory_space=pltpu.SMEM), pl.BlockSpec(memory_space=pltpu.VMEM)]
+        + [pl.BlockSpec(memory_space=pltpu.HBM)] * 8,
         out_specs=[pl.BlockSpec(memory_space=pltpu.VMEM)] * 2,
-        compiler_params=pltpu.CompilerParams(vmem_limit_bytes=VMEM_BYTES),
+        scratch_shapes=[pltpu.VMEM((8,) + own[0].shape, BF16), pltpu.SemaphoreType.DMA((8,))],
+        compiler_params=pltpu.CompilerParams(vmem_limit_bytes=3 * VMEM_BYTES),
         cost_estimate=pl.CostEstimate(flops=604_000_000, bytes_accessed=6_700_000, transcendentals=49_152),
         name="output_parts",
     )(member, parts, *own, *beside)

time: 164 us -> 163 us (level)
  local copies, waits for them, and re-layouts: 9.34 us -> 6.4 us
    unnamed x33 -> x17, local copies, waits for them, and re-layouts: 6.7 us -> 3.75 us
    pallas_call x1, Pallas kernels: 3.48 us -> 5.89 us  [output_parts(): pl.pallas_call(output_kernel, out_shape=[jax.ShapeDtypeStruct((count, 2,...]
where the time goes in v11:
time: 163 us; the launch traced here: 162 us
  starting transfers between devices  76.1 us (47%)
  waiting for transfers between devices  43.1 us (26%)
  blocking collectives  17.7 us (11%)
  Pallas kernels  13.7 us (8%)
  local copies, waits for them, and re-layouts  6.4 us (4%)
  matrix products  3.12 us (2%)
    all_to_all x4, starting transfers between devices, exchange(): return lax.all_to_all(value, axes, split_axis=0, concat_axis=0, tiled=True)  40.7 us
    ppermute x12, starting transfers between devices, partner(): return lax.ppermute(value, axes, [(at, at ^ step) for at in range(count)])  35.3 us
    all_to_all x4, waiting for transfers between devices, exchange(): return lax.all_to_all(value, axes, split_axis=0, concat_axis=0, tiled=True)  29.6 us
    all_to_all x1, blocking collectives, exchange(): return lax.all_to_all(value, axes, split_axis=0, concat_axis=0, tiled=True)  17.7 us
    ppermute x12, waiting for transfers between devices, partner(): return lax.ppermute(value, axes, [(at, at ^ step) for at in range(count)])  13.5 us
    pallas_call x1, Pallas kernels, output_parts(): pl.pallas_call(output_kernel, out_shape=[jax.ShapeDtypeStruct((count, 2,...  5.89 us
    pallas_call x1, Pallas kernels, hidden_parts(): pl.pallas_call(hidden_kernel, out_shape=[jax.ShapeDtypeStruct((4, 4, 3, 2...  5.05 us
    unnamed x17, local copies, waits for them, and re-layouts  3.75 us
  transfers between devices with their start and end apart: 16, of which 9 were waited for; matrix products, arithmetic and copies ran while one was open for 3% of the time, Pallas kernels for 2%

profile of v11, /device:TPU:6, one launch (start us, length us, event | category | flops | bytes accessed | tf_op | source)
XLA Modules:
  0.0 161.9 jit_solution(10132531082770276189)
XLA Ops:
  2.1 15.1 %all-to-all-start = ((bf16[8,8,1536]{2,1,0:T(8,128)(2,1)}), bf16[8,8,1536]{2,1,0:T(8,128)(2,1)S(1)}, u32[]{:S(2)}, u32[]{:S(2)}) async-start(bf16[8,8,1536]{2,1,0:T(8,128)(2,1)} %broadcast_in_dim.4), calls=%async_computation | async-start | bytes 393216 | tf_op jit(solution)/shard_map/all_to_all | solution.py:28
  19.9 2.7 %collective-permute-start = (bf16[2,48,3072]{2,1,0:T(8,128)(2,1)S(1)}, bf16[2,48,3072]{2,1,0:T(8,128)(2,1)S(1)}, u32[]{:S(2)}, u32[]{:S(2)}) collective-permute-start(bf16[2,48,3072]{2,1,0:T(8,128)(2,1)S(1)} %get-tuple-element.20), channel_id=1, source_target_pairs={{0,128},{1,129},{128,0},{129,1},{2,130},{3,131},{130,2},{131,3},{4... | collective-permute-start | bytes 1769480 | tf_op jit(solution)/shard_map/ppermute | solution.py:36
  22.6 3.6 %collective-permute-start.1 = (bf16[2,48,3072]{2,1,0:T(8,128)(2,1)S(1)}, bf16[2,48,3072]{2,1,0:T(8,128)(2,1)}, u32[]{:S(2)}, u32[]{:S(2)}) collective-permute-start(bf16[2,48,3072]{2,1,0:T(8,128)(2,1)S(1)} %get-tuple-element.21), channel_id=1, source_target_pairs={{0,129},{1,128},{128,1},{129,0},{2,131},{3,130},{130,3},{131,2},{4... | collective-permute-start | bytes 1769480 | tf_op jit(solution)/shard_map/ppermute | solution.py:36
  26.2 2.9 %collective-permute-start.2 = (bf16[2,48,3072]{2,1,0:T(8,128)(2,1)S(1)}, bf16[2,48,3072]{2,1,0:T(8,128)(2,1)}, u32[]{:S(2)}, u32[]{:S(2)}) collective-permute-start(bf16[2,48,3072]{2,1,0:T(8,128)(2,1)S(1)} %get-tuple-element.22), channel_id=1, source_target_pairs={{0,1},{1,0},{128,129},{129,128},{2,3},{3,2},{130,131},{131,130},{4... | collective-permute-start | bytes 1769480 | tf_op jit(solution)/shard_map/ppermute | solution.py:36
  29.1 6.7 %all-to-all-done.column_ref = bf16[8,8,1536]{2,1,0:T(8,128)(2,1)S(1)} async-done(((bf16[8,8,1536]{2,1,0:T(8,128)(2,1)}), bf16[8,8,1536]{2,1,0:T(8,128)(2,1)S(1)}, u32[]{:S(2)}, u32[]{:S(2)}) %all-to-all-start) | async-done | bytes 196640 | tf_op jit(solution)/shard_map/all_to_all | solution.py:28
  37.5 7.4 %all-to-all-start.1 = ((bf16[16,3,2,8,1536]{4,3,2,1,0:T(8,128)(2,1)}), bf16[16,3,2,8,1536]{4,3,2,1,0:T(8,128)(2,1)}, u32[]{:S(2)}, u32[]{:S(2)}) async-start(bf16[16,3,2,8,1536]{4,3,2,1,0:T(8,128)(2,1)} %lay_out_rows.1), calls=%async_computation.1 | async-start | bytes 4718592 | tf_op jit(solution)/shard_map/all_to_all | solution.py:28
  44.9 5.7 %collective-permute-done.refs_1_ = bf16[2,48,3072]{2,1,0:T(8,128)(2,1)S(1)} collective-permute-done((bf16[2,48,3072]{2,1,0:T(8,128)(2,1)S(1)}, bf16[2,48,3072]{2,1,0:T(8,128)(2,1)S(1)}, u32[]{:S(2)}, u32[]{:S(2)}) %collective-permute-start) | collective-permute-done | bytes 589856 | tf_op jit(solution)/shard_map/ppermute | solution.py:36
  50.7 3.4 %collective-permute-done.2.refs_3_ = bf16[2,48,3072]{2,1,0:T(8,128)(2,1)} collective-permute-done((bf16[2,48,3072]{2,1,0:T(8,128)(2,1)S(1)}, bf16[2,48,3072]{2,1,0:T(8,128)(2,1)}, u32[]{:S(2)}, u32[]{:S(2)}) %collective-permute-start.2) | collective-permute-done | bytes 589856 | tf_op jit(solution)/shard_map/ppermute | solution.py:36
  56.0 2.0 %collective-permute-done.4.refs_5_ = bf16[2,48,3072]{2,1,0:T(8,128)(2,1)S(1)} collective-permute-done((bf16[2,48,3072]{2,1,0:T(8,128)(2,1)S(1)}, bf16[2,48,3072]{2,1,0:T(8,128)(2,1)S(1)}, u32[]{:S(2)}, u32[]{:S(2)}) %collective-permute-start.4) | collective-permute-done | bytes 589856 | tf_op jit(solution)/shard_map/ppermute | solution.py:36
  58.0 2.0 %collective-permute-start.5 = (bf16[2,48,3072]{2,1,0:T(8,128)(2,1)}, bf16[2,48,3072]{2,1,0:T(8,128)(2,1)S(1)}, u32[]{:S(2)}, u32[]{:S(2)}) collective-permute-start(bf16[2,48,3072]{2,1,0:T(8,128)(2,1)} %collective-permute-done.1.refs_2_), channel_id=1, source_target_pairs={{0,8},{8,0},{1,9},{9,1},{2,10},{10,2},{3,11},{11,3},{4,12},{12,4},... | collective-permute-start | bytes 1769480 | tf_op jit(solution)/shard_map/ppermute | solution.py:36
  60.0 2.3 %collective-permute-start.3 = (bf16[2,48,3072]{2,1,0:T(8,128)(2,1)S(1)}, bf16[2,48,3072]{2,1,0:T(8,128)(2,1)S(1)}, u32[]{:S(2)}, u32[]{:S(2)}) collective-permute-start(bf16[2,48,3072]{2,1,0:T(8,128)(2,1)S(1)} %get-tuple-element.19.refs_0_), channel_id=1, source_target_pairs={{0,8},{8,0},{1,9},{9,1},{2,10},{10,2},{3,11},{11,3},{4,12},{12,4},... | collective-permute-start | bytes 1769480 | tf_op jit(solution)/shard_map/ppermute | solution.py:36
  62.3 2.0 %collective-permute-start.6 = (bf16[2,48,3072]{2,1,0:T(8,128)(2,1)}, bf16[2,48,3072]{2,1,0:T(8,128)(2,1)}, u32[]{:S(2)}, u32[]{:S(2)}) collective-permute-start(bf16[2,48,3072]{2,1,0:T(8,128)(2,1)} %collective-permute-done.2.refs_3_), channel_id=1, source_target_pairs={{0,8},{8,0},{1,9},{9,1},{2,10},{10,2},{3,11},{11,3},{4,12},{12,4},... | collective-permute-start | bytes 1769480 | tf_op jit(solution)/shard_map/ppermute | solution.py:36
  64.4 2.2 %collective-permute-done.6.refs_7_ = bf16[2,48,3072]{2,1,0:T(8,128)(2,1)} collective-permute-done((bf16[2,48,3072]{2,1,0:T(8,128)(2,1)}, bf16[2,48,3072]{2,1,0:T(8,128)(2,1)}, u32[]{:S(2)}, u32[]{:S(2)}) %collective-permute-start.6) | collective-permute-done | bytes 589856 | tf_op jit(solution)/shard_map/ppermute | solution.py:36
  66.6 10.7 %all-to-all-done.1.source_ref = bf16[16,3,2,8,1536]{4,3,2,1,0:T(8,128)(2,1)} async-done(((bf16[16,3,2,8,1536]{4,3,2,1,0:T(8,128)(2,1)}), bf16[16,3,2,8,1536]{4,3,2,1,0:T(8,128)(2,1)}, u32[]{:S(2)}, u32[]{:S(2)}) %all-to-all-start.1) | async-done | bytes 2359328 | tf_op jit(solution)/shard_map/all_to_all | solution.py:28
  77.3 5.1 %hidden_parts.1 = (bf16[4,4,3,2,48,128]{5,4,3,2,1,0:T(8,128)(2,1)}, bf16[2,128,1536]{2,1,0:T(8,128)(2,1)}) custom-call(s32[1]{0:T(128)} %bitcast.member_ref, bf16[16,3,2,8,1536]{4,3,2,1,0:T(8,128)(2,1)} %all-to-all-done.1.source_ref, bf16[2,48,3072]{2,1,0:T(8,128)(2,1)} %copy-done, bf16[2,48,3072]{2,1,0:T(8,128)(2,1)} %copy-done.3, ...), custom_call_target="tpu_custom_call" | custom-call | flops 604000000 | bytes 6700000 | tf_op jit(solution)/shard_map/hidden_parts/pallas_call | solution.py:153
  82.3 17.7 %all_to_all.25.parts_ref = bf16[4,4,3,2,48,128]{5,4,3,2,1,0:T(8,128)(2,1)} all-to-all(bf16[4,4,3,2,48,128]{5,4,3,2,1,0:T(8,128)(2,1)} %get-tuple-element.26), channel_id=1, replica_groups=mesh['xh'=2,'xp'=2,'zh'=2,'y'=4,'c'=2,'z2'=2,'z1'=2,'zp'=2] {'xp','zp'}, dimensions={0} | all-to-all | bytes 2359296 | tf_op jit(solution)/shard_map/all_to_all | solution.py:28
  100.1 5.9 %output_parts.1 = (bf16[16,2,8,3072]{3,2,1,0:T(8,128)(2,1)}, bf16[2,2,1,2,48,128]{5,4,3,2,1,0:T(8,128)(2,1)}) custom-call(s32[1]{0:T(128)} %bitcast.member_ref, bf16[4,4,3,2,48,128]{5,4,3,2,1,0:T(8,128)(2,1)} %all_to_all.25.parts_ref, bf16[2,48,3072]{2,1,0:T(8,128)(2,1)} %copy-done, bf16[2,48,3072]{2,1,0:T(8,128)(2,1)} %copy-done.3, ...), custom_call_target="tpu_custom_call" | custom-call | flops 604000000 | bytes 6700000 | tf_op jit(solution)/shard_map/output_parts/pallas_call | solution.py:209
  106.0 6.9 %all-to-all-start.3 = ((bf16[16,2,8,3072]{3,2,1,0:T(8,128)(2,1)}), bf16[16,2,8,3072]{3,2,1,0:T(8,128)(2,1)S(1)}, u32[]{:S(2)}, u32[]{:S(2)}) async-start(bf16[16,2,8,3072]{3,2,1,0:T(8,128)(2,1)} %get-tuple-element.27), calls=%async_computation.3 | async-start | bytes 3145728 | tf_op jit(solution)/shard_map/all_to_all | solution.py:28
  114.8 4.3 %collective-permute-start.8 = (bf16[2,2,1,2,48,128]{5,4,3,2,1,0:T(8,128)(2,1)S(1)}, bf16[2,2,1,2,48,128]{5,4,3,2,1,0:T(8,128)(2,1)S(1)}, u32[]{:S(2)}, u32[]{:S(2)}) collective-permute-start(bf16[2,2,1,2,48,128]{5,4,3,2,1,0:T(8,128)(2,1)S(1)} %copy-done.7), channel_id=1, source_target_pairs={{0,2},{2,0},{4,6},{6,4},{1,3},{3,1},{5,7},{7,5},{8,10},{10,8},{12,... | collective-permute-start | bytes 294920 | tf_op jit(solution)/shard_map/ppermute | solution.py:36
  119.1 7.3 %collective-permute-start.9 = (bf16[2,2,1,2,48,128]{5,4,3,2,1,0:T(8,128)(2,1)S(1)}, bf16[2,2,1,2,48,128]{5,4,3,2,1,0:T(8,128)(2,1)S(1)}, u32[]{:S(2)}, u32[]{:S(2)}) collective-permute-start(bf16[2,2,1,2,48,128]{5,4,3,2,1,0:T(8,128)(2,1)S(1)} %copy-done.7), channel_id=1, source_target_pairs={{0,4},{2,6},{4,0},{6,2},{1,5},{3,7},{5,1},{7,3},{8,12},{10,14},{12... | collective-permute-start | bytes 294920 | tf_op jit(solution)/shard_map/ppermute | solution.py:36
  126.4 2.5 %collective-permute-start.10 = (bf16[2,2,1,2,48,128]{5,4,3,2,1,0:T(8,128)(2,1)S(1)}, bf16[2,2,1,2,48,128]{5,4,3,2,1,0:T(8,128)(2,1)S(1)}, u32[]{:S(2)}, u32[]{:S(2)}) collective-permute-start(bf16[2,2,1,2,48,128]{5,4,3,2,1,0:T(8,128)(2,1)S(1)} %copy-done.7), channel_id=1, source_target_pairs={{0,6},{2,4},{4,2},{6,0},{1,7},{3,5},{5,3},{7,1},{8,14},{10,12},{12... | collective-permute-start | bytes 294920 | tf_op jit(solution)/shard_map/ppermute | solution.py:36
  132.1 11.3 %all-to-all-start.4 = ((bf16[8,2,4,1536]{3,2,1,0:T(4,128)(2,1)}), bf16[8,2,4,1536]{3,2,1,0:T(4,128)(2,1)S(1)}, u32[]{:S(2)}, u32[]{:S(2)}) async-start(bf16[8,2,4,1536]{3,2,1,0:T(4,128)(2,1)} %plane_sums.1), calls=%async_computation.4 | async-start | bytes 393216 | tf_op jit(solution)/shard_map/all_to_all | solution.py:28
  143.7 1.9 %collective-permute-start.11 = (bf16[2,384,128]{2,1,0:T(8,128)(2,1)S(1)}, bf16[2,384,128]{2,1,0:T(8,128)(2,1)S(1)}, u32[]{:S(2)}, u32[]{:S(2)}) collective-permute-start(bf16[2,384,128]{2,1,0:T(8,128)(2,1)S(1)} %bitcast.24), channel_id=1, source_target_pairs={{0,8},{8,0},{1,9},{9,1},{2,10},{10,2},{3,11},{11,3},{4,12},{12,4},... | collective-permute-start | bytes 589832 | tf_op jit(solution)/shard_map/ppermute | solution.py:36
  150.1 11.0 %all-to-all-done.4 = bf16[8,2,4,1536]{3,2,1,0:T(4,128)(2,1)S(1)} async-done(((bf16[8,2,4,1536]{3,2,1,0:T(4,128)(2,1)}), bf16[8,2,4,1536]{3,2,1,0:T(4,128)(2,1)S(1)}, u32[]{:S(2)}, u32[]{:S(2)}) %all-to-all-start.4) | async-done | bytes 196640 | tf_op jit(solution)/shard_map/all_to_all | solution.py:28
  (44 shorter events, 18.3 us)
Async XLA Ops:
  2.1 33.8 %all-to-all-start = ((bf16[8,8,1536]{2,1,0:T(8,128)(2,1)}), bf16[8,8,1536]{2,1,0:T(8,128)(2,1)S(1)}, u32[]{:S(2)}, u32[]{:S(2)}) async-start(bf16[8,8,1536]{2,1,0:T(8,128)(2,1)} %broadcast_in_dim.4), calls=%async_computation | async-start | bytes 393216 | tf_op jit(solution)/shard_map/all_to_all | solution.py:28
  17.2 1.3 copy-start.1
  18.4 1.3 copy-start.2
  19.9 40.1 %copy-start = (bf16[2,48,3072]{2,1,0:T(8,128)(2,1)}, bf16[2,48,3072]{2,1,0:T(8,128)(2,1)S(1)}, u32[]{:S(2)}) copy-start(bf16[2,48,3072]{2,1,0:T(8,128)(2,1)S(1)} %get-tuple-element.19.refs_0_) | copy-start | bytes 1769476
  19.9 30.8 %collective-permute-start = (bf16[2,48,3072]{2,1,0:T(8,128)(2,1)S(1)}, bf16[2,48,3072]{2,1,0:T(8,128)(2,1)S(1)}, u32[]{:S(2)}, u32[]{:S(2)}) collective-permute-start(bf16[2,48,3072]{2,1,0:T(8,128)(2,1)S(1)} %get-tuple-element.20), channel_id=1, source_target_pairs={{0,128},{1,129},{128,0},{129,1},{2,130},{3,131},{130,2},{131,3},{4... | collective-permute-start | bytes 1769480 | tf_op jit(solution)/shard_map/ppermute | solution.py:36
  22.6 28.0 %collective-permute-start.1 = (bf16[2,48,3072]{2,1,0:T(8,128)(2,1)S(1)}, bf16[2,48,3072]{2,1,0:T(8,128)(2,1)}, u32[]{:S(2)}, u32[]{:S(2)}) collective-permute-start(bf16[2,48,3072]{2,1,0:T(8,128)(2,1)S(1)} %get-tuple-element.21), channel_id=1, source_target_pairs={{0,129},{1,128},{128,1},{129,0},{2,131},{3,130},{130,3},{131,2},{4... | collective-permute-start | bytes 1769480 | tf_op jit(solution)/shard_map/ppermute | solution.py:36
  26.2 27.9 %collective-permute-start.2 = (bf16[2,48,3072]{2,1,0:T(8,128)(2,1)S(1)}, bf16[2,48,3072]{2,1,0:T(8,128)(2,1)}, u32[]{:S(2)}, u32[]{:S(2)}) collective-permute-start(bf16[2,48,3072]{2,1,0:T(8,128)(2,1)S(1)} %get-tuple-element.22), channel_id=1, source_target_pairs={{0,1},{1,0},{128,129},{129,128},{2,3},{3,2},{130,131},{131,130},{4... | collective-permute-start | bytes 1769480 | tf_op jit(solution)/shard_map/ppermute | solution.py:36
  37.5 39.8 %all-to-all-start.1 = ((bf16[16,3,2,8,1536]{4,3,2,1,0:T(8,128)(2,1)}), bf16[16,3,2,8,1536]{4,3,2,1,0:T(8,128)(2,1)}, u32[]{:S(2)}, u32[]{:S(2)}) async-start(bf16[16,3,2,8,1536]{4,3,2,1,0:T(8,128)(2,1)} %lay_out_rows.1), calls=%async_computation.1 | async-start | bytes 4718592 | tf_op jit(solution)/shard_map/all_to_all | solution.py:28
  50.7 26.6 %copy-start.3 = (bf16[2,48,3072]{2,1,0:T(8,128)(2,1)}, bf16[2,48,3072]{2,1,0:T(8,128)(2,1)S(1)}, u32[]{:S(2)}) copy-start(bf16[2,48,3072]{2,1,0:T(8,128)(2,1)S(1)} %collective-permute-done.refs_1_) | copy-start | bytes 1769476
  54.1 3.9 %collective-permute-start.4 = (bf16[2,48,3072]{2,1,0:T(8,128)(2,1)S(1)}, bf16[2,48,3072]{2,1,0:T(8,128)(2,1)S(1)}, u32[]{:S(2)}, u32[]{:S(2)}) collective-permute-start(bf16[2,48,3072]{2,1,0:T(8,128)(2,1)S(1)} %collective-permute-done.refs_1_), channel_id=1, source_target_pairs={{0,8},{8,0},{1,9},{9,1},{2,10},{10,2},{3,11},{11,3},{4,12},{12,4},... | collective-permute-start | bytes 1769480 | tf_op jit(solution)/shard_map/ppermute | solution.py:36
  58.0 19.3 %copy-start.4 = (bf16[2,48,3072]{2,1,0:T(8,128)(2,1)}, bf16[2,48,3072]{2,1,0:T(8,128)(2,1)S(1)}, u32[]{:S(2)}) copy-start(bf16[2,48,3072]{2,1,0:T(8,128)(2,1)S(1)} %collective-permute-done.4.refs_5_) | copy-start | bytes 1769476
  58.0 4.3 %collective-permute-start.5 = (bf16[2,48,3072]{2,1,0:T(8,128)(2,1)}, bf16[2,48,3072]{2,1,0:T(8,128)(2,1)S(1)}, u32[]{:S(2)}, u32[]{:S(2)}) collective-permute-start(bf16[2,48,3072]{2,1,0:T(8,128)(2,1)} %collective-permute-done.1.refs_2_), channel_id=1, source_target_pairs={{0,8},{8,0},{1,9},{9,1},{2,10},{10,2},{3,11},{11,3},{4,12},{12,4},... | collective-permute-start | bytes 1769480 | tf_op jit(solution)/shard_map/ppermute | solution.py:36
  60.0 4.4 %collective-permute-start.3 = (bf16[2,48,3072]{2,1,0:T(8,128)(2,1)S(1)}, bf16[2,48,3072]{2,1,0:T(8,128)(2,1)S(1)}, u32[]{:S(2)}, u32[]{:S(2)}) collective-permute-start(bf16[2,48,3072]{2,1,0:T(8,128)(2,1)S(1)} %get-tuple-element.19.refs_0_), channel_id=1, source_target_pairs={{0,8},{8,0},{1,9},{9,1},{2,10},{10,2},{3,11},{11,3},{4,12},{12,4},... | collective-permute-start | bytes 1769480 | tf_op jit(solution)/shard_map/ppermute | solution.py:36
  62.3 15.0 %copy-start.5 = (bf16[2,48,3072]{2,1,0:T(8,128)(2,1)}, bf16[2,48,3072]{2,1,0:T(8,128)(2,1)S(1)}, u32[]{:S(2)}) copy-start(bf16[2,48,3072]{2,1,0:T(8,128)(2,1)S(1)} %collective-permute-done.5.refs_6_) | copy-start | bytes 1769476
  62.3 4.2 %collective-permute-start.6 = (bf16[2,48,3072]{2,1,0:T(8,128)(2,1)}, bf16[2,48,3072]{2,1,0:T(8,128)(2,1)}, u32[]{:S(2)}, u32[]{:S(2)}) collective-permute-start(bf16[2,48,3072]{2,1,0:T(8,128)(2,1)} %collective-permute-done.2.refs_3_), channel_id=1, source_target_pairs={{0,8},{8,0},{1,9},{9,1},{2,10},{10,2},{3,11},{11,3},{4,12},{12,4},... | collective-permute-start | bytes 1769480 | tf_op jit(solution)/shard_map/ppermute | solution.py:36
  64.4 12.9 %copy-start.6 = (bf16[2,48,3072]{2,1,0:T(8,128)(2,1)}, bf16[2,48,3072]{2,1,0:T(8,128)(2,1)S(1)}, u32[]{:S(2)}) copy-start(bf16[2,48,3072]{2,1,0:T(8,128)(2,1)S(1)} %collective-permute-done.3.refs_4_) | copy-start | bytes 1769476
  106.0 8.9 %copy-start.7 = (bf16[2,2,1,2,48,128]{5,4,3,2,1,0:T(8,128)(2,1)S(1)}, bf16[2,2,1,2,48,128]{5,4,3,2,1,0:T(8,128)(2,1)}, u32[]{:S(2)}) copy-start(bf16[2,2,1,2,48,128]{5,4,3,2,1,0:T(8,128)(2,1)} %get-tuple-element.30) | copy-start | bytes 294916
  106.0 25.3 %all-to-all-start.3 = ((bf16[16,2,8,3072]{3,2,1,0:T(8,128)(2,1)}), bf16[16,2,8,3072]{3,2,1,0:T(8,128)(2,1)S(1)}, u32[]{:S(2)}, u32[]{:S(2)}) async-start(bf16[16,2,8,3072]{3,2,1,0:T(8,128)(2,1)} %get-tuple-element.27), calls=%async_computation.3 | async-start | bytes 3145728 | tf_op jit(solution)/shard_map/all_to_all | solution.py:28
  112.9 32.7 %collective-permute-start.7 = (bf16[2,128,1536]{2,1,0:T(8,128)(2,1)}, bf16[2,128,1536]{2,1,0:T(8,128)(2,1)}, u32[]{:S(2)}, u32[]{:S(2)}) collective-permute-start(bf16[2,128,1536]{2,1,0:T(8,128)(2,1)} %get-tuple-element.28), channel_id=1, source_target_pairs={{0,8},{8,0},{1,9},{9,1},{2,10},{10,2},{3,11},{11,3},{4,12},{12,4},... | collective-permute-start | bytes 2359304 | tf_op jit(solution)/shard_map/ppermute | solution.py:36
  114.8 28.6 %collective-permute-start.8 = (bf16[2,2,1,2,48,128]{5,4,3,2,1,0:T(8,128)(2,1)S(1)}, bf16[2,2,1,2,48,128]{5,4,3,2,1,0:T(8,128)(2,1)S(1)}, u32[]{:S(2)}, u32[]{:S(2)}) collective-permute-start(bf16[2,2,1,2,48,128]{5,4,3,2,1,0:T(8,128)(2,1)S(1)} %copy-done.7), channel_id=1, source_target_pairs={{0,2},{2,0},{4,6},{6,4},{1,3},{3,1},{5,7},{7,5},{8,10},{10,8},{12,... | collective-permute-start | bytes 294920 | tf_op jit(solution)/shard_map/ppermute | solution.py:36
  119.1 24.3 %collective-permute-start.9 = (bf16[2,2,1,2,48,128]{5,4,3,2,1,0:T(8,128)(2,1)S(1)}, bf16[2,2,1,2,48,128]{5,4,3,2,1,0:T(8,128)(2,1)S(1)}, u32[]{:S(2)}, u32[]{:S(2)}) collective-permute-start(bf16[2,2,1,2,48,128]{5,4,3,2,1,0:T(8,128)(2,1)S(1)} %copy-done.7), channel_id=1, source_target_pairs={{0,4},{2,6},{4,0},{6,2},{1,5},{3,7},{5,1},{7,3},{8,12},{10,14},{12... | collective-permute-start | bytes 294920 | tf_op jit(solution)/shard_map/ppermute | solution.py:36
  126.4 17.1 %collective-permute-start.10 = (bf16[2,2,1,2,48,128]{5,4,3,2,1,0:T(8,128)(2,1)S(1)}, bf16[2,2,1,2,48,128]{5,4,3,2,1,0:T(8,128)(2,1)S(1)}, u32[]{:S(2)}, u32[]{:S(2)}) collective-permute-start(bf16[2,2,1,2,48,128]{5,4,3,2,1,0:T(8,128)(2,1)S(1)} %copy-done.7), channel_id=1, source_target_pairs={{0,6},{2,4},{4,2},{6,0},{1,7},{3,5},{5,3},{7,1},{8,14},{10,12},{12... | collective-permute-start | bytes 294920 | tf_op jit(solution)/shard_map/ppermute | solution.py:36
  132.1 29.0 %all-to-all-start.4 = ((bf16[8,2,4,1536]{3,2,1,0:T(4,128)(2,1)}), bf16[8,2,4,1536]{3,2,1,0:T(4,128)(2,1)S(1)}, u32[]{:S(2)}, u32[]{:S(2)}) async-start(bf16[8,2,4,1536]{3,2,1,0:T(4,128)(2,1)} %plane_sums.1), calls=%async_computation.4 | async-start | bytes 393216 | tf_op jit(solution)/shard_map/all_to_all | solution.py:28
  143.7 3.3 %collective-permute-start.11 = (bf16[2,384,128]{2,1,0:T(8,128)(2,1)S(1)}, bf16[2,384,128]{2,1,0:T(8,128)(2,1)S(1)}, u32[]{:S(2)}, u32[]{:S(2)}) collective-permute-start(bf16[2,384,128]{2,1,0:T(8,128)(2,1)S(1)} %bitcast.24), channel_id=1, source_target_pairs={{0,8},{8,0},{1,9},{9,1},{2,10},{10,2},{3,11},{11,3},{4,12},{12,4},... | collective-permute-start | bytes 589832 | tf_op jit(solution)/shard_map/ppermute | solution.py:36

commit v12 on v11

--- a/solution.py
+++ b/solution.py
@@ -12,7 +12,7 @@
 PLANE = ("xh", "xp", "y")
 COLUMN = ("zh", "z2", "z1")
 GROUP = ("xp", "zp")
-STEPS = (0, 2, 3, 1)
+STEPS = (0, 3, 2, 1)
 
 
 def activate(values):

time: 163 us -> 170 us (1.043)
  starting transfers between devices: 76.1 us -> 81.3 us
    all_to_all x4, starting transfers between devices: 40.7 us -> 45.5 us  [exchange(): return lax.all_to_all(value, axes, split_axis=0, concat_axis=0, tiled=True)]
    all_to_all x4, waiting for transfers between devices: 29.6 us -> 31.9 us  [exchange(): return lax.all_to_all(value, axes, split_axis=0, concat_axis=0, tiled=True)]
    ppermute x12, waiting for transfers between devices: 13.5 us -> 11.5 us  [partner(): return lax.ppermute(value, axes, [(at, at ^ step) for at in range(count)])]
where the time goes in v12:
time: 170 us; the launch traced here: 169 us
  starting transfers between devices  81.3 us (48%)
  waiting for transfers between devices  43.5 us (26%)
  blocking collectives  18.8 us (11%)
  Pallas kernels  13.7 us (8%)
  local copies, waits for them, and re-layouts  6.4 us (4%)
  matrix products  3.12 us (2%)
    all_to_all x4, starting transfers between devices, exchange(): return lax.all_to_all(value, axes, split_axis=0, concat_axis=0, tiled=True)  45.5 us
    ppermute x12, starting transfers between devices, partner(): return lax.ppermute(value, axes, [(at, at ^ step) for at in range(count)])  35.8 us
    all_to_all x4, waiting for transfers between devices, exchange(): return lax.all_to_all(value, axes, split_axis=0, concat_axis=0, tiled=True)  31.9 us
    all_to_all x1, blocking collectives, exchange(): return lax.all_to_all(value, axes, split_axis=0, concat_axis=0, tiled=True)  18.8 us
    ppermute x12, waiting for transfers between devices, partner(): return lax.ppermute(value, axes, [(at, at ^ step) for at in range(count)])  11.5 us
    pallas_call x1, Pallas kernels, output_parts(): pl.pallas_call(output_kernel, out_shape=[jax.ShapeDtypeStruct((count, 2,...  5.89 us
    pallas_call x1, Pallas kernels, hidden_parts(): pl.pallas_call(hidden_kernel, out_shape=[jax.ShapeDtypeStruct((4, 4, 3, 2...  5.06 us
    unnamed x17, local copies, waits for them, and re-layouts  3.75 us
  transfers between devices with their start and end apart: 16, of which 9 were waited for; matrix products, arithmetic and copies ran while one was open for 3% of the time, Pallas kernels for 2%

profile of v12, /device:TPU:6, one launch (start us, length us, event | category | flops | bytes accessed | tf_op | source)
XLA Modules:
  0.0 168.5 jit_solution(3650440674850779578)
XLA Ops:
  2.1 15.1 %all-to-all-start = ((bf16[8,8,1536]{2,1,0:T(8,128)(2,1)}), bf16[8,8,1536]{2,1,0:T(8,128)(2,1)S(1)}, u32[]{:S(2)}, u32[]{:S(2)}) async-start(bf16[8,8,1536]{2,1,0:T(8,128)(2,1)} %broadcast_in_dim.4), calls=%async_computation | async-start | bytes 393216 | tf_op jit(solution)/shard_map/all_to_all | solution.py:28
  19.9 3.2 %collective-permute-start = (bf16[2,48,3072]{2,1,0:T(8,128)(2,1)S(1)}, bf16[2,48,3072]{2,1,0:T(8,128)(2,1)S(1)}, u32[]{:S(2)}, u32[]{:S(2)}) collective-permute-start(bf16[2,48,3072]{2,1,0:T(8,128)(2,1)S(1)} %get-tuple-element.20), channel_id=1, source_target_pairs={{0,129},{1,128},{128,1},{129,0},{2,131},{3,130},{130,3},{131,2},{4... | collective-permute-start | bytes 1769480 | tf_op jit(solution)/shard_map/ppermute | solution.py:36
  23.1 3.1 %collective-permute-start.1 = (bf16[2,48,3072]{2,1,0:T(8,128)(2,1)S(1)}, bf16[2,48,3072]{2,1,0:T(8,128)(2,1)}, u32[]{:S(2)}, u32[]{:S(2)}) collective-permute-start(bf16[2,48,3072]{2,1,0:T(8,128)(2,1)S(1)} %get-tuple-element.21), channel_id=1, source_target_pairs={{0,128},{1,129},{128,0},{129,1},{2,130},{3,131},{130,2},{131,3},{4... | collective-permute-start | bytes 1769480 | tf_op jit(solution)/shard_map/ppermute | solution.py:36
  26.2 2.9 %collective-permute-start.2 = (bf16[2,48,3072]{2,1,0:T(8,128)(2,1)S(1)}, bf16[2,48,3072]{2,1,0:T(8,128)(2,1)}, u32[]{:S(2)}, u32[]{:S(2)}) collective-permute-start(bf16[2,48,3072]{2,1,0:T(8,128)(2,1)S(1)} %get-tuple-element.22), channel_id=1, source_target_pairs={{0,1},{1,0},{128,129},{129,128},{2,3},{3,2},{130,131},{131,130},{4... | collective-permute-start | bytes 1769480 | tf_op jit(solution)/shard_map/ppermute | solution.py:36
  29.1 7.5 %all-to-all-done.column_ref = bf16[8,8,1536]{2,1,0:T(8,128)(2,1)S(1)} async-done(((bf16[8,8,1536]{2,1,0:T(8,128)(2,1)}), bf16[8,8,1536]{2,1,0:T(8,128)(2,1)S(1)}, u32[]{:S(2)}, u32[]{:S(2)}) %all-to-all-start) | async-done | bytes 196640 | tf_op jit(solution)/shard_map/all_to_all | solution.py:28
  38.3 7.2 %all-to-all-start.1 = ((bf16[16,3,2,8,1536]{4,3,2,1,0:T(8,128)(2,1)}), bf16[16,3,2,8,1536]{4,3,2,1,0:T(8,128)(2,1)}, u32[]{:S(2)}, u32[]{:S(2)}) async-start(bf16[16,3,2,8,1536]{4,3,2,1,0:T(8,128)(2,1)} %lay_out_rows.1), calls=%async_computation.1 | async-start | bytes 4718592 | tf_op jit(solution)/shard_map/all_to_all | solution.py:28
  45.5 6.4 %collective-permute-done.1.refs_2_ = bf16[2,48,3072]{2,1,0:T(8,128)(2,1)} collective-permute-done((bf16[2,48,3072]{2,1,0:T(8,128)(2,1)S(1)}, bf16[2,48,3072]{2,1,0:T(8,128)(2,1)}, u32[]{:S(2)}, u32[]{:S(2)}) %collective-permute-start.1) | collective-permute-done | bytes 589856 | tf_op jit(solution)/shard_map/ppermute | solution.py:36
  54.6 2.0 %collective-permute-done.4.refs_5_ = bf16[2,48,3072]{2,1,0:T(8,128)(2,1)S(1)} collective-permute-done((bf16[2,48,3072]{2,1,0:T(8,128)(2,1)S(1)}, bf16[2,48,3072]{2,1,0:T(8,128)(2,1)S(1)}, u32[]{:S(2)}, u32[]{:S(2)}) %collective-permute-start.4) | collective-permute-done | bytes 589856 | tf_op jit(solution)/shard_map/ppermute | solution.py:36
  56.6 2.0 %collective-permute-start.5 = (bf16[2,48,3072]{2,1,0:T(8,128)(2,1)}, bf16[2,48,3072]{2,1,0:T(8,128)(2,1)S(1)}, u32[]{:S(2)}, u32[]{:S(2)}) collective-permute-start(bf16[2,48,3072]{2,1,0:T(8,128)(2,1)} %collective-permute-done.1.refs_2_), channel_id=1, source_target_pairs={{0,8},{8,0},{1,9},{9,1},{2,10},{10,2},{3,11},{11,3},{4,12},{12,4},... | collective-permute-start | bytes 1769480 | tf_op jit(solution)/shard_map/ppermute | solution.py:36
  58.6 2.3 %collective-permute-start.3 = (bf16[2,48,3072]{2,1,0:T(8,128)(2,1)S(1)}, bf16[2,48,3072]{2,1,0:T(8,128)(2,1)S(1)}, u32[]{:S(2)}, u32[]{:S(2)}) collective-permute-start(bf16[2,48,3072]{2,1,0:T(8,128)(2,1)S(1)} %get-tuple-element.19.refs_0_), channel_id=1, source_target_pairs={{0,8},{8,0},{1,9},{9,1},{2,10},{10,2},{3,11},{11,3},{4,12},{12,4},... | collective-permute-start | bytes 1769480 | tf_op jit(solution)/shard_map/ppermute | solution.py:36
  60.9 2.0 %collective-permute-start.6 = (bf16[2,48,3072]{2,1,0:T(8,128)(2,1)}, bf16[2,48,3072]{2,1,0:T(8,128)(2,1)}, u32[]{:S(2)}, u32[]{:S(2)}) collective-permute-start(bf16[2,48,3072]{2,1,0:T(8,128)(2,1)} %collective-permute-done.2.refs_3_), channel_id=1, source_target_pairs={{0,8},{8,0},{1,9},{9,1},{2,10},{10,2},{3,11},{11,3},{4,12},{12,4},... | collective-permute-start | bytes 1769480 | tf_op jit(solution)/shard_map/ppermute | solution.py:36
  63.0 2.2 %collective-permute-done.6.refs_7_ = bf16[2,48,3072]{2,1,0:T(8,128)(2,1)} collective-permute-done((bf16[2,48,3072]{2,1,0:T(8,128)(2,1)}, bf16[2,48,3072]{2,1,0:T(8,128)(2,1)}, u32[]{:S(2)}, u32[]{:S(2)}) %collective-permute-start.6) | collective-permute-done | bytes 589856 | tf_op jit(solution)/shard_map/ppermute | solution.py:36
  65.2 13.9 %all-to-all-done.1.source_ref = bf16[16,3,2,8,1536]{4,3,2,1,0:T(8,128)(2,1)} async-done(((bf16[16,3,2,8,1536]{4,3,2,1,0:T(8,128)(2,1)}), bf16[16,3,2,8,1536]{4,3,2,1,0:T(8,128)(2,1)}, u32[]{:S(2)}, u32[]{:S(2)}) %all-to-all-start.1) | async-done | bytes 2359328 | tf_op jit(solution)/shard_map/all_to_all | solution.py:28
  79.1 5.1 %hidden_parts.1 = (bf16[4,4,3,2,48,128]{5,4,3,2,1,0:T(8,128)(2,1)}, bf16[2,128,1536]{2,1,0:T(8,128)(2,1)}) custom-call(s32[1]{0:T(128)} %bitcast.member_ref, bf16[16,3,2,8,1536]{4,3,2,1,0:T(8,128)(2,1)} %all-to-all-done.1.source_ref, bf16[2,48,3072]{2,1,0:T(8,128)(2,1)} %copy-done, bf16[2,48,3072]{2,1,0:T(8,128)(2,1)} %copy-done.3, ...), custom_call_target="tpu_custom_call" | custom-call | flops 604000000 | bytes 6700000 | tf_op jit(solution)/shard_map/hidden_parts/pallas_call | solution.py:153
  84.1 18.8 %all_to_all.25.parts_ref = bf16[4,4,3,2,48,128]{5,4,3,2,1,0:T(8,128)(2,1)} all-to-all(bf16[4,4,3,2,48,128]{5,4,3,2,1,0:T(8,128)(2,1)} %get-tuple-element.26), channel_id=1, replica_groups=mesh['xh'=2,'xp'=2,'zh'=2,'y'=4,'c'=2,'z2'=2,'z1'=2,'zp'=2] {'xp','zp'}, dimensions={0} | all-to-all | bytes 2359296 | tf_op jit(solution)/shard_map/all_to_all | solution.py:28
  102.9 5.9 %output_parts.1 = (bf16[16,2,8,3072]{3,2,1,0:T(8,128)(2,1)}, bf16[2,2,1,2,48,128]{5,4,3,2,1,0:T(8,128)(2,1)}) custom-call(s32[1]{0:T(128)} %bitcast.member_ref, bf16[4,4,3,2,48,128]{5,4,3,2,1,0:T(8,128)(2,1)} %all_to_all.25.parts_ref, bf16[2,48,3072]{2,1,0:T(8,128)(2,1)} %copy-done, bf16[2,48,3072]{2,1,0:T(8,128)(2,1)} %copy-done.3, ...), custom_call_target="tpu_custom_call" | custom-call | flops 604000000 | bytes 6700000 | tf_op jit(solution)/shard_map/output_parts/pallas_call | solution.py:209
  108.9 8.8 %all-to-all-start.3 = ((bf16[16,2,8,3072]{3,2,1,0:T(8,128)(2,1)}), bf16[16,2,8,3072]{3,2,1,0:T(8,128)(2,1)S(1)}, u32[]{:S(2)}, u32[]{:S(2)}) async-start(bf16[16,2,8,3072]{3,2,1,0:T(8,128)(2,1)} %get-tuple-element.27), calls=%async_computation.3 | async-start | bytes 3145728 | tf_op jit(solution)/shard_map/all_to_all | solution.py:28
  117.7 1.9 %collective-permute-start.7 = (bf16[2,128,1536]{2,1,0:T(8,128)(2,1)}, bf16[2,128,1536]{2,1,0:T(8,128)(2,1)}, u32[]{:S(2)}, u32[]{:S(2)}) collective-permute-start(bf16[2,128,1536]{2,1,0:T(8,128)(2,1)} %get-tuple-element.28), channel_id=1, source_target_pairs={{0,8},{8,0},{1,9},{9,1},{2,10},{10,2},{3,11},{11,3},{4,12},{12,4},... | collective-permute-start | bytes 2359304 | tf_op jit(solution)/shard_map/ppermute | solution.py:36
  119.6 4.9 %collective-permute-start.8 = (bf16[2,2,1,2,48,128]{5,4,3,2,1,0:T(8,128)(2,1)S(1)}, bf16[2,2,1,2,48,128]{5,4,3,2,1,0:T(8,128)(2,1)S(1)}, u32[]{:S(2)}, u32[]{:S(2)}) collective-permute-start(bf16[2,2,1,2,48,128]{5,4,3,2,1,0:T(8,128)(2,1)S(1)} %copy-done.7), channel_id=1, source_target_pairs={{0,2},{2,0},{4,6},{6,4},{1,3},{3,1},{5,7},{7,5},{8,10},{10,8},{12,... | collective-permute-start | bytes 294920 | tf_op jit(solution)/shard_map/ppermute | solution.py:36
  124.5 7.6 %collective-permute-start.9 = (bf16[2,2,1,2,48,128]{5,4,3,2,1,0:T(8,128)(2,1)S(1)}, bf16[2,2,1,2,48,128]{5,4,3,2,1,0:T(8,128)(2,1)S(1)}, u32[]{:S(2)}, u32[]{:S(2)}) collective-permute-start(bf16[2,2,1,2,48,128]{5,4,3,2,1,0:T(8,128)(2,1)S(1)} %copy-done.7), channel_id=1, source_target_pairs={{0,4},{2,6},{4,0},{6,2},{1,5},{3,7},{5,1},{7,3},{8,12},{10,14},{12... | collective-permute-start | bytes 294920 | tf_op jit(solution)/shard_map/ppermute | solution.py:36
  132.1 2.0 %collective-permute-start.10 = (bf16[2,2,1,2,48,128]{5,4,3,2,1,0:T(8,128)(2,1)S(1)}, bf16[2,2,1,2,48,128]{5,4,3,2,1,0:T(8,128)(2,1)S(1)}, u32[]{:S(2)}, u32[]{:S(2)}) collective-permute-start(bf16[2,2,1,2,48,128]{5,4,3,2,1,0:T(8,128)(2,1)S(1)} %copy-done.7), channel_id=1, source_target_pairs={{0,6},{2,4},{4,2},{6,0},{1,7},{3,5},{5,3},{7,1},{8,14},{10,12},{12... | collective-permute-start | bytes 294920 | tf_op jit(solution)/shard_map/ppermute | solution.py:36
  137.7 14.3 %all-to-all-start.4 = ((bf16[8,2,4,1536]{3,2,1,0:T(4,128)(2,1)}), bf16[8,2,4,1536]{3,2,1,0:T(4,128)(2,1)S(1)}, u32[]{:S(2)}, u32[]{:S(2)}) async-start(bf16[8,2,4,1536]{3,2,1,0:T(4,128)(2,1)} %plane_sums.1), calls=%async_computation.4 | async-start | bytes 393216 | tf_op jit(solution)/shard_map/all_to_all | solution.py:28
  152.2 1.9 %collective-permute-start.11 = (bf16[2,384,128]{2,1,0:T(8,128)(2,1)S(1)}, bf16[2,384,128]{2,1,0:T(8,128)(2,1)S(1)}, u32[]{:S(2)}, u32[]{:S(2)}) collective-permute-start(bf16[2,384,128]{2,1,0:T(8,128)(2,1)S(1)} %bitcast.24), channel_id=1, source_target_pairs={{0,8},{8,0},{1,9},{9,1},{2,10},{10,2},{3,11},{11,3},{4,12},{12,4},... | collective-permute-start | bytes 589832 | tf_op jit(solution)/shard_map/ppermute | solution.py:36
  158.7 9.1 %all-to-all-done.4 = bf16[8,2,4,1536]{3,2,1,0:T(4,128)(2,1)S(1)} async-done(((bf16[8,2,4,1536]{3,2,1,0:T(4,128)(2,1)}), bf16[8,2,4,1536]{3,2,1,0:T(4,128)(2,1)S(1)}, u32[]{:S(2)}, u32[]{:S(2)}) %all-to-all-start.4) | async-done | bytes 196640 | tf_op jit(solution)/shard_map/all_to_all | solution.py:28
  (44 shorter events, 17.4 us)
Async XLA Ops:
  2.1 34.5 %all-to-all-start = ((bf16[8,8,1536]{2,1,0:T(8,128)(2,1)}), bf16[8,8,1536]{2,1,0:T(8,128)(2,1)S(1)}, u32[]{:S(2)}, u32[]{:S(2)}) async-start(bf16[8,8,1536]{2,1,0:T(8,128)(2,1)} %broadcast_in_dim.4), calls=%async_computation | async-start | bytes 393216 | tf_op jit(solution)/shard_map/all_to_all | solution.py:28
  17.2 1.3 copy-start.1
  18.4 1.3 copy-start.2
  19.9 38.8 %copy-start = (bf16[2,48,3072]{2,1,0:T(8,128)(2,1)}, bf16[2,48,3072]{2,1,0:T(8,128)(2,1)S(1)}, u32[]{:S(2)}) copy-start(bf16[2,48,3072]{2,1,0:T(8,128)(2,1)S(1)} %get-tuple-element.19.refs_0_) | copy-start | bytes 1769476
  19.9 25.6 %collective-permute-start = (bf16[2,48,3072]{2,1,0:T(8,128)(2,1)S(1)}, bf16[2,48,3072]{2,1,0:T(8,128)(2,1)S(1)}, u32[]{:S(2)}, u32[]{:S(2)}) collective-permute-start(bf16[2,48,3072]{2,1,0:T(8,128)(2,1)S(1)} %get-tuple-element.20), channel_id=1, source_target_pairs={{0,129},{1,128},{128,1},{129,0},{2,131},{3,130},{130,3},{131,2},{4... | collective-permute-start | bytes 1769480 | tf_op jit(solution)/shard_map/ppermute | solution.py:36
  23.1 28.9 %collective-permute-start.1 = (bf16[2,48,3072]{2,1,0:T(8,128)(2,1)S(1)}, bf16[2,48,3072]{2,1,0:T(8,128)(2,1)}, u32[]{:S(2)}, u32[]{:S(2)}) collective-permute-start(bf16[2,48,3072]{2,1,0:T(8,128)(2,1)S(1)} %get-tuple-element.21), channel_id=1, source_target_pairs={{0,128},{1,129},{128,0},{129,1},{2,130},{3,131},{130,2},{131,3},{4... | collective-permute-start | bytes 1769480 | tf_op jit(solution)/shard_map/ppermute | solution.py:36
  26.2 26.5 %collective-permute-start.2 = (bf16[2,48,3072]{2,1,0:T(8,128)(2,1)S(1)}, bf16[2,48,3072]{2,1,0:T(8,128)(2,1)}, u32[]{:S(2)}, u32[]{:S(2)}) collective-permute-start(bf16[2,48,3072]{2,1,0:T(8,128)(2,1)S(1)} %get-tuple-element.22), channel_id=1, source_target_pairs={{0,1},{1,0},{128,129},{129,128},{2,3},{3,2},{130,131},{131,130},{4... | collective-permute-start | bytes 1769480 | tf_op jit(solution)/shard_map/ppermute | solution.py:36
  38.3 40.8 %all-to-all-start.1 = ((bf16[16,3,2,8,1536]{4,3,2,1,0:T(8,128)(2,1)}), bf16[16,3,2,8,1536]{4,3,2,1,0:T(8,128)(2,1)}, u32[]{:S(2)}, u32[]{:S(2)}) async-start(bf16[16,3,2,8,1536]{4,3,2,1,0:T(8,128)(2,1)} %lay_out_rows.1), calls=%async_computation.1 | async-start | bytes 4718592 | tf_op jit(solution)/shard_map/all_to_all | solution.py:28
  45.5 33.5 %copy-start.3 = (bf16[2,48,3072]{2,1,0:T(8,128)(2,1)}, bf16[2,48,3072]{2,1,0:T(8,128)(2,1)S(1)}, u32[]{:S(2)}) copy-start(bf16[2,48,3072]{2,1,0:T(8,128)(2,1)S(1)} %collective-permute-done.refs_1_) | copy-start | bytes 1769476
  52.7 3.9 %collective-permute-start.4 = (bf16[2,48,3072]{2,1,0:T(8,128)(2,1)S(1)}, bf16[2,48,3072]{2,1,0:T(8,128)(2,1)S(1)}, u32[]{:S(2)}, u32[]{:S(2)}) collective-permute-start(bf16[2,48,3072]{2,1,0:T(8,128)(2,1)S(1)} %collective-permute-done.refs_1_), channel_id=1, source_target_pairs={{0,8},{8,0},{1,9},{9,1},{2,10},{10,2},{3,11},{11,3},{4,12},{12,4},... | collective-permute-start | bytes 1769480 | tf_op jit(solution)/shard_map/ppermute | solution.py:36
  56.6 22.5 %copy-start.4 = (bf16[2,48,3072]{2,1,0:T(8,128)(2,1)}, bf16[2,48,3072]{2,1,0:T(8,128)(2,1)S(1)}, u32[]{:S(2)}) copy-start(bf16[2,48,3072]{2,1,0:T(8,128)(2,1)S(1)} %collective-permute-done.4.refs_5_) | copy-start | bytes 1769476
  56.6 4.3 %collective-permute-start.5 = (bf16[2,48,3072]{2,1,0:T(8,128)(2,1)}, bf16[2,48,3072]{2,1,0:T(8,128)(2,1)S(1)}, u32[]{:S(2)}, u32[]{:S(2)}) collective-permute-start(bf16[2,48,3072]{2,1,0:T(8,128)(2,1)} %collective-permute-done.1.refs_2_), channel_id=1, source_target_pairs={{0,8},{8,0},{1,9},{9,1},{2,10},{10,2},{3,11},{11,3},{4,12},{12,4},... | collective-permute-start | bytes 1769480 | tf_op jit(solution)/shard_map/ppermute | solution.py:36
  58.6 4.4 %collective-permute-start.3 = (bf16[2,48,3072]{2,1,0:T(8,128)(2,1)S(1)}, bf16[2,48,3072]{2,1,0:T(8,128)(2,1)S(1)}, u32[]{:S(2)}, u32[]{:S(2)}) collective-permute-start(bf16[2,48,3072]{2,1,0:T(8,128)(2,1)S(1)} %get-tuple-element.19.refs_0_), channel_id=1, source_target_pairs={{0,8},{8,0},{1,9},{9,1},{2,10},{10,2},{3,11},{11,3},{4,12},{12,4},... | collective-permute-start | bytes 1769480 | tf_op jit(solution)/shard_map/ppermute | solution.py:36
  60.9 18.1 %copy-start.5 = (bf16[2,48,3072]{2,1,0:T(8,128)(2,1)}, bf16[2,48,3072]{2,1,0:T(8,128)(2,1)S(1)}, u32[]{:S(2)}) copy-start(bf16[2,48,3072]{2,1,0:T(8,128)(2,1)S(1)} %collective-permute-done.5.refs_6_) | copy-start | bytes 1769476
  60.9 4.2 %collective-permute-start.6 = (bf16[2,48,3072]{2,1,0:T(8,128)(2,1)}, bf16[2,48,3072]{2,1,0:T(8,128)(2,1)}, u32[]{:S(2)}, u32[]{:S(2)}) collective-permute-start(bf16[2,48,3072]{2,1,0:T(8,128)(2,1)} %collective-permute-done.2.refs_3_), channel_id=1, source_target_pairs={{0,8},{8,0},{1,9},{9,1},{2,10},{10,2},{3,11},{11,3},{4,12},{12,4},... | collective-permute-start | bytes 1769480 | tf_op jit(solution)/shard_map/ppermute | solution.py:36
  63.0 16.1 %copy-start.6 = (bf16[2,48,3072]{2,1,0:T(8,128)(2,1)}, bf16[2,48,3072]{2,1,0:T(8,128)(2,1)S(1)}, u32[]{:S(2)}) copy-start(bf16[2,48,3072]{2,1,0:T(8,128)(2,1)S(1)} %collective-permute-done.3.refs_4_) | copy-start | bytes 1769476
  108.8 10.8 %copy-start.7 = (bf16[2,2,1,2,48,128]{5,4,3,2,1,0:T(8,128)(2,1)S(1)}, bf16[2,2,1,2,48,128]{5,4,3,2,1,0:T(8,128)(2,1)}, u32[]{:S(2)}) copy-start(bf16[2,2,1,2,48,128]{5,4,3,2,1,0:T(8,128)(2,1)} %get-tuple-element.30) | copy-start | bytes 294916
  108.9 28.0 %all-to-all-start.3 = ((bf16[16,2,8,3072]{3,2,1,0:T(8,128)(2,1)}), bf16[16,2,8,3072]{3,2,1,0:T(8,128)(2,1)S(1)}, u32[]{:S(2)}, u32[]{:S(2)}) async-start(bf16[16,2,8,3072]{3,2,1,0:T(8,128)(2,1)} %get-tuple-element.27), calls=%async_computation.3 | async-start | bytes 3145728 | tf_op jit(solution)/shard_map/all_to_all | solution.py:28
  117.7 36.5 %collective-permute-start.7 = (bf16[2,128,1536]{2,1,0:T(8,128)(2,1)}, bf16[2,128,1536]{2,1,0:T(8,128)(2,1)}, u32[]{:S(2)}, u32[]{:S(2)}) collective-permute-start(bf16[2,128,1536]{2,1,0:T(8,128)(2,1)} %get-tuple-element.28), channel_id=1, source_target_pairs={{0,8},{8,0},{1,9},{9,1},{2,10},{10,2},{3,11},{11,3},{4,12},{12,4},... | collective-permute-start | bytes 2359304 | tf_op jit(solution)/shard_map/ppermute | solution.py:36
  119.6 32.4 %collective-permute-start.8 = (bf16[2,2,1,2,48,128]{5,4,3,2,1,0:T(8,128)(2,1)S(1)}, bf16[2,2,1,2,48,128]{5,4,3,2,1,0:T(8,128)(2,1)S(1)}, u32[]{:S(2)}, u32[]{:S(2)}) collective-permute-start(bf16[2,2,1,2,48,128]{5,4,3,2,1,0:T(8,128)(2,1)S(1)} %copy-done.7), channel_id=1, source_target_pairs={{0,2},{2,0},{4,6},{6,4},{1,3},{3,1},{5,7},{7,5},{8,10},{10,8},{12,... | collective-permute-start | bytes 294920 | tf_op jit(solution)/shard_map/ppermute | solution.py:36
  124.5 27.5 %collective-permute-start.9 = (bf16[2,2,1,2,48,128]{5,4,3,2,1,0:T(8,128)(2,1)S(1)}, bf16[2,2,1,2,48,128]{5,4,3,2,1,0:T(8,128)(2,1)S(1)}, u32[]{:S(2)}, u32[]{:S(2)}) collective-permute-start(bf16[2,2,1,2,48,128]{5,4,3,2,1,0:T(8,128)(2,1)S(1)} %copy-done.7), channel_id=1, source_target_pairs={{0,4},{2,6},{4,0},{6,2},{1,5},{3,7},{5,1},{7,3},{8,12},{10,14},{12... | collective-permute-start | bytes 294920 | tf_op jit(solution)/shard_map/ppermute | solution.py:36
  132.1 19.9 %collective-permute-start.10 = (bf16[2,2,1,2,48,128]{5,4,3,2,1,0:T(8,128)(2,1)S(1)}, bf16[2,2,1,2,48,128]{5,4,3,2,1,0:T(8,128)(2,1)S(1)}, u32[]{:S(2)}, u32[]{:S(2)}) collective-permute-start(bf16[2,2,1,2,48,128]{5,4,3,2,1,0:T(8,128)(2,1)S(1)} %copy-done.7), channel_id=1, source_target_pairs={{0,6},{2,4},{4,2},{6,0},{1,7},{3,5},{5,3},{7,1},{8,14},{10,12},{12... | collective-permute-start | bytes 294920 | tf_op jit(solution)/shard_map/ppermute | solution.py:36
  137.7 30.1 %all-to-all-start.4 = ((bf16[8,2,4,1536]{3,2,1,0:T(4,128)(2,1)}), bf16[8,2,4,1536]{3,2,1,0:T(4,128)(2,1)S(1)}, u32[]{:S(2)}, u32[]{:S(2)}) async-start(bf16[8,2,4,1536]{3,2,1,0:T(4,128)(2,1)} %plane_sums.1), calls=%async_computation.4 | async-start | bytes 393216 | tf_op jit(solution)/shard_map/all_to_all | solution.py:28
  152.2 3.3 %collective-permute-start.11 = (bf16[2,384,128]{2,1,0:T(8,128)(2,1)S(1)}, bf16[2,384,128]{2,1,0:T(8,128)(2,1)S(1)}, u32[]{:S(2)}, u32[]{:S(2)}) collective-permute-start(bf16[2,384,128]{2,1,0:T(8,128)(2,1)S(1)} %bitcast.24), channel_id=1, source_target_pairs={{0,8},{8,0},{1,9},{9,1},{2,10},{10,2},{3,11},{11,3},{4,12},{12,4},... | collective-permute-start | bytes 589832 | tf_op jit(solution)/shard_map/ppermute | solution.py:36
